TPU v7x, 256 devices: a whole 4x4x8 slice. The times are simulated.
256 devices in a mesh: row: 8 (over y_lo, x), col: 32 (over z, y_hi, core).
Axes of the slice: x: 4, y: 4 (y_hi: 2, y_lo: 2; y = y_hi * 2 + y_lo), z: 8, core: 2. Of those that a mesh axis runs over, the one named last changes fastest.
Arguments:
- volume: bfloat16 [16, 32, 32, 4096], P(None, None, 'row', 'col'), may hold values from -6 to 6
- cotangent: bfloat16 [16, 32, 32, 4096], P(None, None, 'row', 'col'), may hold values from -6 to 6
- w_half: bfloat16 [32, 16, 3, 3, 3], replicated, may hold values from -0.3125 to 0.3125
- w_quarter: bfloat16 [64, 32, 3, 3, 3], replicated, may hold values from -0.21875 to 0.21875
- w_back_half: bfloat16 [32, 64, 3, 3, 3], replicated, may hold values from -0.4375 to 0.4375
- w_back_full: bfloat16 [16, 32, 3, 3, 3], replicated, may hold values from -0.625 to 0.625
Outputs:
- grad_volume: bfloat16 [16, 32, 32, 4096], P(None, None, 'row', 'col')
- grad_w_half: float32 [32, 16, 3, 3, 3], replicated
- grad_w_quarter: float32 [64, 32, 3, 3, 3], replicated
- grad_w_back_half: float32 [32, 64, 3, 3, 3], replicated
- grad_w_back_full: float32 [16, 32, 3, 3, 3], replicated
All inputs are finite; a program needn't handle non-finite values.
Results may differ from a plain program's by a relative error of at most 0.013.
Values may be sent and summed in bfloat16 or wider, within the bound.
No kernel may reach another device: no remote copies, remote signals or barrier semaphores. Data moves between devices by JAX's collectives and lax.ppermute only.
A program may use at most 128 MiB of HBM per device.

v0:
```python
import math

import jax
import jax.numpy as jnp
from jax import lax
from jax.sharding import PartitionSpec as P

NUMBERS = ("NCDHW", "OIDHW", "NCDHW")


def shifted(value, axis, steps):
    count = lax.axis_size(axis)
    leading, last = (max(0, -steps), min(count, count - steps))
    return lax.ppermute(value, axis, [(source, source + steps) for source in range(leading, last)])


def down(extended, weight):
    result = lax.conv_general_dilated(
        extended[None],
        weight,
        (2, 2, 2),
        ((1, 1), (0, 0), (0, 0)),
        dimension_numbers=NUMBERS,
        preferred_element_type=jnp.float32,
    )
    return result[0]


def upsample(extended, weight):
    result = lax.conv_general_dilated(
        extended[None],
        weight,
        (1, 1, 1),
        ((1, 2), (1, 0), (1, 0)),
        lhs_dilation=(2, 2, 2),
        dimension_numbers=NUMBERS,
        preferred_element_type=jnp.float32,
    )
    return result[0]


def flipped(weight):
    return jnp.flip(weight, axis=(2, 3, 4)).transpose(1, 0, 2, 3, 4)


def silu_slope(pre):
    sigma = jax.nn.sigmoid(pre)
    return sigma * (1.0 + pre * (1.0 - sigma))


def down_wgrad(extended, grad_out):
    result = lax.conv_general_dilated(
        extended[:, None],
        grad_out[:, None],
        (1, 1, 1),
        ((1, 0), (0, 0), (0, 0)),
        rhs_dilation=(2, 2, 2),
        dimension_numbers=NUMBERS,
        preferred_element_type=jnp.float32,
    )
    return result.transpose(1, 0, 2, 3, 4)


def up_wgrad(source, grad_ext):
    result = lax.conv_general_dilated(
        grad_ext[:, None],
        source[:, None],
        (1, 1, 1),
        ((1, 0), (0, 0), (0, 0)),
        rhs_dilation=(2, 2, 2),
        dimension_numbers=NUMBERS,
        preferred_element_type=jnp.float32,
    )
    return jnp.flip(result, axis=(2, 3, 4))


def lower_rims(field):
    top_row = shifted(field[:, :, -1:, :], "row", 1)
    field = jnp.concatenate([top_row, field], axis=2)
    left_col = shifted(field[:, :, :, -1:], "col", 1)
    return jnp.concatenate([left_col, field], axis=3)


def upper_rims(field):
    below_row = shifted(field[:, :, :1, :], "row", -1)
    field = jnp.concatenate([field, below_row], axis=2)
    right_col = shifted(field[:, :, :, :1], "col", -1)
    return jnp.concatenate([field, right_col], axis=3)


def shards(volume, cotangent, w_half, w_quarter, w_back_half, w_back_full):
    cells = (
        volume.shape[1]
        * volume.shape[2]
        * volume.shape[3]
        * lax.axis_size("row")
        * lax.axis_size("col")
    )
    scale = 1.0 / math.sqrt(cells)
    volume_ext = lower_rims(volume)
    pre_h = down(volume_ext, w_half)
    half_act = jax.nn.silu(pre_h).astype(jnp.bfloat16)
    half_ext = lower_rims(half_act)
    pre_q = down(half_ext, w_quarter)
    quarter_act = jax.nn.silu(pre_q).astype(jnp.bfloat16)
    pre_m = upsample(upper_rims(quarter_act), w_back_half) + half_act.astype(jnp.float32)
    mixed_act = jax.nn.silu(pre_m).astype(jnp.bfloat16)
    cot_ext = lower_rims(cotangent)
    grad_mixed = (down(cot_ext, flipped(w_back_full)) * silu_slope(pre_m)).astype(jnp.bfloat16)
    grad_w4 = up_wgrad(mixed_act, cot_ext)
    mixed_ext = lower_rims(grad_mixed)
    grad_quarter = (down(mixed_ext, flipped(w_back_half)) * silu_slope(pre_q)).astype(jnp.bfloat16)
    grad_w3 = up_wgrad(quarter_act, mixed_ext)
    summed = upsample(upper_rims(grad_quarter), flipped(w_quarter)) + grad_mixed.astype(jnp.float32)
    grad_half = (summed * silu_slope(pre_h)).astype(jnp.bfloat16)
    grad_w2 = down_wgrad(half_ext, grad_quarter)
    grad_volume = (
        upsample(upper_rims(grad_half), flipped(w_half)) + cotangent.astype(jnp.float32)
    ).astype(jnp.bfloat16)
    grad_w1 = down_wgrad(volume_ext, grad_half)
    flat_one, flat_two, flat_three, flat_four = lax.psum(
        (grad_w1.reshape(-1), grad_w2.reshape(-1), grad_w3.reshape(-1), grad_w4.reshape(-1)),
        ("row", "col"),
    )
    grad_w1 = flat_one.reshape(grad_w1.shape) * scale
    grad_w2 = flat_two.reshape(grad_w2.shape) * scale
    grad_w3 = flat_three.reshape(grad_w3.shape) * scale
    grad_w4 = flat_four.reshape(grad_w4.shape) * scale
    return (grad_volume, grad_w1, grad_w2, grad_w3, grad_w4)


def solution(mesh):
    return jax.shard_map(
        shards,
        mesh=mesh,
        in_specs=(P(None, None, "row", "col"), P(None, None, "row", "col"), P(), P(), P(), P()),
        out_specs=(P(None, None, "row", "col"), P(), P(), P(), P()),
        check_vma=False,
    )
```

profile of v0, /device:TPU:1, one launch (start us, length us, event | category | flops | bytes accessed | tf_op | source)
XLA Modules:
  0.0 812.0 jit_solution(947734069271369304)
XLA Ops:
  9.9 4.0 collective-permute-start.2
  13.9 10.5 %collective-permute-done.2 = bf16[16,32,1,128]{1,0,3,2:T(8,128)(2,1)S(1)} collective-permute-done((bf16[16,32,1,128]{1,0,3,2:T(8,128)(2,1)S(1)}, bf16[16,32,1,128]{1,0,3,2:T(8,128)(2,1)S(1)}, u32[]{:S(2)}, u32[]{:S(2)}) %collective-permute-start.2) | collective-permute-done | bytes 131104 | tf_op jit(solution)/shard_map/ppermute | solution.py:14
  24.4 6.3 collective-permute-start.3
  34.3 5.2 copy.295
  40.8 5.7 fusion.17
  47.8 4.1 collective-permute-start.4
  58.0 6.3 collective-permute-start.5
  68.1 6.3 collective-permute-start.1
  86.7 7.0 copy.289
  97.0 5.7 fusion.20
  106.6 4.7 collective-permute-start.8
  113.4 6.5 collective-permute-start.9
  119.9 20.2 %copy.334 = bf16[16,1,32,5,129]{0,1,4,3,2:T(2,128)(2,1)} copy(bf16[16,1,32,5,129]{2,0,4,3,1:T(8,128)(2,1)} %get-tuple-element.39) | data formatting | bytes 1320960 | tf_op jit(solution)/shard_map/broadcast_in_dim | solution.py:66
  140.1 20.2 %copy.324 = bf16[16,1,32,5,129]{0,1,4,3,2:T(2,128)(2,1)} copy(bf16[16,1,32,5,129]{2,0,4,3,1:T(8,128)(2,1)} %get-tuple-element.41) | data formatting | bytes 1320960 | tf_op jit(solution)/shard_map/broadcast_in_dim | solution.py:53
  176.5 4.0 fusion.104
  194.6 25.3 %fusion.134 = f32[16,32,3,3,3]{1,0,4,3,2:T(8,128)S(1)} fusion(bf16[16,1,32,5,129]{0,1,4,3,2:T(2,128)(2,1)} %copy.334, bf16[32,1,16,2,64]{0,1,4,3,2:T(2,128)(2,1)S(1)} %copy.335), kind=kOutput, calls=%fused_computation.167 | convolution fusion | flops 55443456 | bytes 846848 | tf_op jit(solution)/shard_map/conv_general_dilated | solution.py:65
  224.1 25.2 %fusion.133 = f32[32,16,3,3,3]{0,1,4,3,2:T(8,128)S(1)} fusion(bf16[16,1,32,5,129]{0,1,4,3,2:T(2,128)(2,1)} %copy.324, bf16[32,1,16,2,64]{0,1,4,3,2:T(2,128)(2,1)} %copy.325), kind=kOutput, calls=%fused_computation.166 | convolution fusion | flops 55443456 | bytes 846848 | tf_op jit(solution)/shard_map/transpose | solution.py:61
  249.3 4.0 copy.326
  256.0 4.4 fusion.102
  260.4 9.1 %copy.332 = f32[32,64,3,3,3]{4,3,2,1,0:T(4,128)} copy(f32[32,64,3,3,3]{1,0,4,3,2:T(8,128)S(1)} %rev.16) | data formatting | bytes 442368 | tf_op jit(solution)/shard_map/jit(_flip)/rev | solution.py:74
  269.6 11.0 %reshape.323 = f32[55296]{0:T(1024)} reshape(f32[32,64,3,3,3]{4,3,2,1,0:T(4,128)} %copy.332) | data formatting | bytes 442368 | tf_op jit(solution)/shard_map/reshape | solution.py:122
  280.6 12.2 %copy.329 = f32[64,32,3,3,3]{4,3,2,1,0:T(4,128)} copy(f32[64,32,3,3,3]{0,1,4,3,2:T(8,128)S(1)} %copy-done.12) | data formatting | bytes 442368 | tf_op jit(solution)/shard_map/transpose | solution.py:61
  292.8 11.0 %reshape.322 = f32[55296]{0:T(1024)} reshape(f32[64,32,3,3,3]{4,3,2,1,0:T(4,128)} %copy.329) | data formatting | bytes 442368 | tf_op jit(solution)/shard_map/reshape | solution.py:122
  307.5 203.7 %all-reduce.5.cloned.1.call-done = (f32[13824]{0:T(1024)}, f32[13824]{0:T(1024)}) async-done(((f32[13824]{0:T(1024)}, f32[13824]{0:T(1024)}), (f32[13824]{0:T(1024)}, f32[13824]{0:T(1024)})) %all-reduce.5.cloned.1.call-update) | async-done | bytes 110608 | tf_op jit(solution)/shard_map/psum | solution.py:121
  523.0 6.6 broadcast_select_fusion
  529.6 9.2 %copy.318 = f32[32,4,8,18,16]{0,4,3,2,1:T(8,128)} copy(f32[32,4,8,18,16]{4,2,3,1,0:T(8,128)} %broadcast_select_fusion) | data formatting | bytes 2359296 | tf_op jit(solution)/shard_map/conv_general_dilated | solution.py:30
  538.8 4.2 fusion.11
  546.4 218.1 %all-reduce.7.cloned.1.call-done = (f32[55296]{0:T(1024)}, f32[55296]{0:T(1024)}) async-done(((f32[55296]{0:T(1024)}, f32[55296]{0:T(1024)}), (f32[55296]{0:T(1024)}, f32[55296]{0:T(1024)})) %all-reduce.7.cloned.1.call-update) | async-done | bytes 442384 | tf_op jit(solution)/shard_map/psum | solution.py:121
  765.6 8.5 %mul.241 = f32[32,64,3,3,3]{4,3,2,1,0:T(4,128)} reshape(f32[55296]{0:T(1024)S(1)} %get-tuple-element.53) | data formatting | bytes 442368 | tf_op jit(solution)/shard_map/mul | solution.py:127
  774.0 10.8 %copy.340 = f32[32,64,3,3,3]{1,0,4,3,2:T(8,128)} copy(f32[32,64,3,3,3]{4,3,2,1,0:T(4,128)} %mul.241) | data formatting | bytes 442368
  784.8 8.4 %mul.238 = f32[64,32,3,3,3]{4,3,2,1,0:T(4,128)} reshape(f32[55296]{0:T(1024)S(1)} %get-tuple-element.54) | data formatting | bytes 442368 | tf_op jit(solution)/shard_map/mul | solution.py:126
  793.3 11.7 %copy.339 = f32[64,32,3,3,3]{0,1,4,3,2:T(8,128)} copy(f32[64,32,3,3,3]{4,3,2,1,0:T(4,128)} %mul.238) | data formatting | bytes 442368
  (154 shorter events, 96.8 us)
Async XLA Ops:
  7.2 96.8 %copy-start = (bf16[32,64,3,3,3]{1,0,4,3,2:T(8,128)(2,1)S(1)}, bf16[32,64,3,3,3]{1,0,4,3,2:T(8,128)(2,1)}, u32[]{:S(2)}) copy-start(bf16[32,64,3,3,3]{1,0,4,3,2:T(8,128)(2,1)} %param.10) | copy-start | bytes 331780
  7.2 504.0 %all-reduce.5.cloned.1.call-start = ((), (), s32[]{:S(2)}) async-start(), calls=%async_computation | async-start | bytes 229376 | tf_op jit(solution)/shard_map/psum | solution.py:121
  9.9 14.5 %collective-permute-start.2 = (bf16[16,32,1,128]{1,0,3,2:T(8,128)(2,1)S(1)}, bf16[16,32,1,128]{1,0,3,2:T(8,128)(2,1)S(1)}, u32[]{:S(2)}, u32[]{:S(2)}) collective-permute-start(bf16[16,32,1,128]{1,0,3,2:T(8,128)(2,1)S(1)} %slice.65), channel_id=1, source_target_pairs={{0,32},{32,64},{64,96},{96,128},{128,160},{160,192},{192,224},{1,3... | collective-permute-start | bytes 393224 | tf_op jit(solution)/shard_map/ppermute | solution.py:14
  24.4 7.1 collective-permute-start.3
  34.3 6.5 copy-start.17
  34.3 6.5 copy-start.20
  47.8 9.9 %collective-permute-start.4 = (bf16[32,16,1,64]{3,1,2,0:T(8,128)(2,1)S(1)}, bf16[32,16,1,64]{3,1,2,0:T(8,128)(2,1)S(1)}, u32[]{:S(2)}, u32[]{:S(2)}) collective-permute-start(bf16[32,16,1,64]{3,1,2,0:T(8,128)(2,1)S(1)} %slice.68), channel_id=1, source_target_pairs={{0,32},{32,64},{64,96},{96,128},{128,160},{160,192},{192,224},{1,3... | collective-permute-start | bytes 196616 | tf_op jit(solution)/shard_map/ppermute | solution.py:14
  54.6 27.9 %copy-start.2 = (bf16[16,32,4,128]{1,0,3,2:T(8,128)(2,1)}, bf16[16,32,4,128]{1,0,3,2:T(8,128)(2,1)S(1)}, u32[]{:S(2)}) copy-start(bf16[16,32,4,128]{1,0,3,2:T(8,128)(2,1)S(1)} %copy.286) | copy-start | bytes 1572868
  54.6 12.1 %collective-permute-start = (bf16[16,32,1,128]{1,0,3,2:T(8,128)(2,1)S(1)}, bf16[16,32,1,128]{1,0,3,2:T(8,128)(2,1)S(1)}, u32[]{:S(2)}, u32[]{:S(2)}) collective-permute-start(bf16[16,32,1,128]{1,0,3,2:T(8,128)(2,1)S(1)} %slice.62), channel_id=1, source_target_pairs={{0,32},{32,64},{64,96},{96,128},{128,160},{160,192},{192,224},{1,3... | collective-permute-start | bytes 393224 | tf_op jit(solution)/shard_map/ppermute | solution.py:14
  57.8 16.7 %copy-start.11 = (bf16[32,16,1,64]{3,1,2,0:T(8,128)(2,1)}, bf16[32,16,1,64]{3,1,2,0:T(8,128)(2,1)S(1)}, u32[]{:S(2)}) copy-start(bf16[32,16,1,64]{3,1,2,0:T(8,128)(2,1)S(1)} %collective-permute-done.4) | copy-start | bytes 196612
  58.0 16.5 %collective-permute-start.5 = (bf16[32,16,3,1]{3,1,2,0:T(8,128)(2,1)S(1)}, bf16[32,16,3,1]{3,1,2,0:T(8,128)(2,1)S(1)}, u32[]{:S(2)}, u32[]{:S(2)}) collective-permute-start(bf16[32,16,3,1]{3,1,2,0:T(8,128)(2,1)S(1)} %pad_maximum_fusion.2), channel_id=1, source_target_pairs={{0,1},{1,2},{2,3},{3,4},{4,5},{5,6},{6,7},{7,8},{8,9},{9,10},{10,1... | collective-permute-start | bytes 9224 | tf_op jit(solution)/shard_map/ppermute | solution.py:14
  68.1 14.4 %collective-permute-start.1 = (bf16[16,32,5,1]{1,0,3,2:T(8,128)(2,1)}, bf16[16,32,5,1]{1,0,3,2:T(8,128)(2,1)S(1)}, u32[]{:S(2)}, u32[]{:S(2)}) collective-permute-start(bf16[16,32,5,1]{1,0,3,2:T(8,128)(2,1)} %pad_maximum_fusion.4), channel_id=1, source_target_pairs={{0,1},{1,2},{2,3},{3,4},{4,5},{5,6},{6,7},{7,8},{8,9},{9,10},{10,1... | collective-permute-start | bytes 15368 | tf_op jit(solution)/shard_map/ppermute | solution.py:14
  76.3 3.5 copy-start.21
  80.7 14.3 %collective-permute-start.6 = (bf16[64,8,1,32]{0,1,3,2:T(8,128)(2,1)S(1)}, bf16[64,8,1,32]{0,1,3,2:T(8,128)(2,1)S(1)}, u32[]{:S(2)}, u32[]{:S(2)}) collective-permute-start(bf16[64,8,1,32]{0,1,3,2:T(8,128)(2,1)S(1)} %fusion.99), channel_id=1, source_target_pairs={{32,0},{64,32},{96,64},{128,96},{160,128},{192,160},{224,192},{33,... | collective-permute-start | bytes 98312 | tf_op jit(solution)/shard_map/ppermute | solution.py:14
  86.7 10.3 %copy-start.16 = (bf16[16,32,3,3,3]{1,0,4,3,2:T(8,128)(2,1)S(1)}, bf16[16,32,3,3,3]{1,0,4,3,2:T(8,128)(2,1)}, u32[]{:S(2)}) copy-start(bf16[16,32,3,3,3]{1,0,4,3,2:T(8,128)(2,1)} %param.11) | copy-start | bytes 82948
  95.0 8.8 %collective-permute-start.7 = (bf16[64,8,2,1]{0,1,3,2:T(8,128)(2,1)S(1)}, bf16[64,8,2,1]{0,1,3,2:T(8,128)(2,1)S(1)}, u32[]{:S(2)}, u32[]{:S(2)}) collective-permute-start(bf16[64,8,2,1]{0,1,3,2:T(8,128)(2,1)S(1)} %pad_maximum_fusion.6), channel_id=1, source_target_pairs={{1,0},{2,1},{3,2},{4,3},{5,4},{6,5},{7,6},{8,7},{9,8},{10,9},{11,1... | collective-permute-start | bytes 6152 | tf_op jit(solution)/shard_map/ppermute | solution.py:14
  106.6 6.7 collective-permute-start.8
  113.4 49.9 %collective-permute-start.9 = (bf16[32,16,3,1]{3,1,2,0:T(8,128)(2,1)S(1)}, bf16[32,16,3,1]{3,1,2,0:T(8,128)(2,1)S(1)}, u32[]{:S(2)}, u32[]{:S(2)}) collective-permute-start(bf16[32,16,3,1]{3,1,2,0:T(8,128)(2,1)S(1)} %pad_maximum_fusion.1), channel_id=1, source_target_pairs={{0,1},{1,2},{2,3},{3,4},{4,5},{5,6},{6,7},{7,8},{8,9},{9,10},{10,1... | collective-permute-start | bytes 9224 | tf_op jit(solution)/shard_map/ppermute | solution.py:14
  140.1 20.2 %copy-start.9 = (bf16[32,1,16,3,65]{4,2,3,1,0:T(8,128)(2,1)S(1)}, bf16[32,1,16,3,65]{4,2,3,1,0:T(8,128)(2,1)}, u32[]{:S(2)}) copy-start(bf16[32,1,16,3,65]{4,2,3,1,0:T(8,128)(2,1)} %get-tuple-element.47) | copy-start | bytes 599044
  167.7 8.8 %copy-start.8 = (bf16[32,1,16,3,65]{0,1,4,3,2:T(2,128)(2,1)S(1)}, bf16[32,1,16,3,65]{0,1,4,3,2:T(2,128)(2,1)}, u32[]{:S(2)}) copy-start(bf16[32,1,16,3,65]{0,1,4,3,2:T(2,128)(2,1)} %copy.327) | copy-start | bytes 599044
  168.7 5.8 collective-permute-start.10
  174.4 9.2 %collective-permute-start.11 = (bf16[64,8,2,1]{0,1,3,2:T(8,128)(2,1)S(1)}, bf16[64,8,2,1]{0,1,3,2:T(8,128)(2,1)S(1)}, u32[]{:S(2)}, u32[]{:S(2)}) collective-permute-start(bf16[64,8,2,1]{0,1,3,2:T(8,128)(2,1)S(1)} %pad_maximum_fusion.5), channel_id=1, source_target_pairs={{1,0},{2,1},{3,2},{4,3},{5,4},{6,5},{7,6},{8,7},{9,8},{10,9},{11,1... | collective-permute-start | bytes 6152 | tf_op jit(solution)/shard_map/ppermute | solution.py:14
  176.5 4.0 copy-start.10
  189.7 30.2 %copy-start.4 = (bf16[32,16,2,64]{3,1,2,0:T(8,128)(2,1)}, bf16[32,16,2,64]{3,1,2,0:T(8,128)(2,1)S(1)}, u32[]{:S(2)}) copy-start(bf16[32,16,2,64]{3,1,2,0:T(8,128)(2,1)S(1)} %fusion.59) | copy-start | bytes 393220
  190.5 113.3 %collective-permute-start.12 = (bf16[32,16,1,64]{3,1,2,0:T(8,128)(2,1)}, bf16[32,16,1,64]{3,1,2,0:T(8,128)(2,1)}, u32[]{:S(2)}, u32[]{:S(2)}) collective-permute-start(bf16[32,16,1,64]{3,1,2,0:T(8,128)(2,1)} %slice.78), channel_id=1, source_target_pairs={{32,0},{64,32},{96,64},{128,96},{160,128},{192,160},{224,192},{33,... | collective-permute-start | bytes 196616 | tf_op jit(solution)/shard_map/ppermute | solution.py:14
  249.3 6.7 copy-start.14
  255.9 508.6 %all-reduce.7.cloned.1.call-start = ((), (), s32[]{:S(2)}) async-start(), calls=%async_computation.1 | async-start | bytes 884736 | tf_op jit(solution)/shard_map/psum | solution.py:121
  269.6 11.0 %copy-start.12 = (f32[64,32,3,3,3]{0,1,4,3,2:T(8,128)S(1)}, f32[64,32,3,3,3]{0,1,4,3,2:T(8,128)}, u32[]{:S(2)}) copy-start(f32[64,32,3,3,3]{0,1,4,3,2:T(8,128)} %fusion.104) | copy-start | bytes 663556
  292.8 11.1 %copy-start.5 = (bf16[32,16,2,64]{3,1,2,0:T(8,128)(2,1)S(1)}, bf16[32,16,2,64]{3,1,2,0:T(8,128)(2,1)}, u32[]{:S(2)}) copy-start(bf16[32,16,2,64]{3,1,2,0:T(8,128)(2,1)} %copy-done.4) | copy-start | bytes 393220
  305.6 214.8 %collective-permute-start.13 = (bf16[32,16,3,1]{3,1,2,0:T(8,128)(2,1)}, bf16[32,16,3,1]{3,1,2,0:T(8,128)(2,1)}, u32[]{:S(2)}, u32[]{:S(2)}) collective-permute-start(bf16[32,16,3,1]{3,1,2,0:T(8,128)(2,1)} %pad_maximum_fusion), channel_id=1, source_target_pairs={{1,0},{2,1},{3,2},{4,3},{5,4},{6,5},{7,6},{8,7},{9,8},{10,9},{11,1... | collective-permute-start | bytes 9224 | tf_op jit(solution)/shard_map/ppermute | solution.py:14
  529.6 9.2 %copy-start.3 = (bf16[16,32,4,128]{1,0,3,2:T(8,128)(2,1)S(1)}, bf16[16,32,4,128]{1,0,3,2:T(8,128)(2,1)}, u32[]{:S(2)}) copy-start(bf16[16,32,4,128]{1,0,3,2:T(8,128)(2,1)} %copy-done.2) | copy-start | bytes 1572868
  793.3 11.7 %copy-start.1 = (bf16[32,64,3,3,3]{1,0,4,3,2:T(8,128)(2,1)S(1)}, bf16[32,64,3,3,3]{1,0,4,3,2:T(8,128)(2,1)}, u32[]{:S(2)}) copy-start(bf16[32,64,3,3,3]{1,0,4,3,2:T(8,128)(2,1)} %param.10) | copy-start | bytes 331780
  (7 other events, 14.0 us)
Sparse Core Ops, SparseCore 0:
  256.0 255.1 all-reduce.4
  516.8 247.6 all-reduce.6
where the time goes:
time: 823 us; the launch traced here: 812 us
  waiting for transfers between devices  441 us (54%)
  local copies, waits for them, and re-layouts  204 us (25%)
  matrix products  80.7 us (10%)
  starting transfers between devices  51.6 us (6%)
  other arithmetic  19.3 us (2%)
  between operations  15.1 us (2%)
    psum x2, waiting for transfers between devices, shards(): lax.psum((grad_w1.reshape(-1), grad_w2.reshape(-1), grad_w3.reshape(-1),...  422 us
    ppermute x14, starting transfers between devices, shifted(): lax.ppermute(value, axis, [(source, source + steps) for source in range(l...  51.5 us
    unnamed x60, local copies, waits for them, and re-layouts  44.9 us
    conv_general_dilated x2, matrix products, up_wgrad(): lax.conv_general_dilated(grad_ext[:, None], source[:, None], (1, 1, 1), (...  29.7 us
    transpose x2, matrix products, down_wgrad(): return result.transpose(1, 0, 2, 3, 4)  29.1 us
    broadcast_in_dim x2, local copies, waits for them, and re-layouts, up_wgrad(): grad_ext[:, None]  23.3 us
    broadcast_in_dim x2, local copies, waits for them, and re-layouts, down_wgrad(): extended[:, None]  23.3 us
    ppermute x14, waiting for transfers between devices, shifted(): lax.ppermute(value, axis, [(source, source + steps) for source in range(l...  19.6 us
  transfers between devices with their start and end apart: 16, of which 7 were waited for; matrix products, arithmetic and copies ran while one was open for 28% of the time, Pallas kernels for 0%

commit v1 on v0

v1 whole, which is shorter than its diff:
```python
import functools
import math

import jax
import jax.numpy as jnp
import numpy as np
from jax import lax
from jax.experimental import pallas as pl
from jax.experimental.pallas import tpu as pltpu
from jax.sharding import PartitionSpec as P

BF = jnp.bfloat16
F32 = jnp.float32

QD, QC, HALO = 8, 32, 2
SPAN = QC + 2 * HALO
LANES = 384
PACK = 1152
LIMIT = 24 * 1024 * 1024


def lane_of(d, c):
    return SPAN * d + c + HALO


def constants():
    spread = np.zeros((QD * 128, 4 * 256), np.float32)
    rims = np.zeros((4 * LANES, 128), np.float32)
    place = np.zeros((2, 256, 4 * LANES), np.float32)
    for d in range(QD):
        for phase in range(4):
            for c in range(QC):
                spread[d * 128 + 4 * c + phase, phase * 256 + lane_of(d, c) - (0 if d < 6 else 128)] = 1
            for e in range(2):
                for side in range(2):
                    slot = phase * 16 + d * 2 + e
                    column = e if side == 0 else QC - 2 + e
                    rims[phase * LANES + lane_of(d, column), side * 64 + slot] = 1
                    outside = e - 2 if side == 0 else QC + e
                    for half in range(2):
                        place[half, side * 128 + half * 64 + slot, phase * LANES + lane_of(d, outside)] = 1
    order = np.zeros((256, 256), np.float32)
    for ch in range(16):
        for pd in range(4):
            for r in range(4):
                order[r * 64 + pd * 16 + ch, ch * 16 + pd * 4 + r] = 1
    return [np.asarray(a, BF) for a in (spread, rims, place, order)]


def dot(a, b):
    return lax.dot_general(a, b, (((1,), (0,)), ((), ())), preferred_element_type=F32)


def dot_nt(a, b):
    return lax.dot_general(a, b, (((1,), (1,)), ((), ())), preferred_element_type=F32)


def sigmoid(t):
    return 1.0 / (1.0 + jnp.exp(-t))


def slope(t):
    s = sigmoid(t)
    return s * (1.0 + t * (1.0 - s))


def relayout(x_ref, spread_ref, order_ref):
    wide = jnp.concatenate([x_ref[:, d].reshape(256, 128) for d in range(QD)], axis=1)
    rows = dot(order_ref[...], wide).astype(BF)
    early = dot(rows[:, :768], spread_ref[0:768])
    late = dot(rows[:, 768:], spread_ref[768:1024])
    pieces = []
    for pc in range(4):
        low, high = pc * 256, pc * 256 + 128
        pieces += [early[:, low:high], early[:, high : low + 256] + late[:, low:high], late[:, high : low + 256]]
    return jnp.concatenate(pieces, axis=1).astype(BF)


def own_kernel(vol_ref, cot_ref, spread_ref, order_ref, yv_ref, yc_ref, last_ref):
    yv_ref[...] = relayout(vol_ref, spread_ref, order_ref)
    yc_ref[...] = relayout(cot_ref, spread_ref, order_ref)
    last_ref[...] = yc_ref[192:256]


def parity(axis):
    return lax.axis_index(axis) & 1


def flag(condition):
    return jnp.where(condition, 1.0, 0.0).astype(F32)


def rows_kernel(xa_ref, xb_ref, yv_ref, yc_ref, ycrow_ref, spread_ref, order_ref, rims_ref, near_ref, yclo_ref, senda_ref, sendb_ref, edge_ref):
    odd = parity("row")
    near_ref[1 - odd] = relayout(xa_ref, spread_ref, order_ref)
    near_ref[odd] = relayout(xb_ref, spread_ref, order_ref)
    inner = flag(lax.axis_index("row") > 0)
    near_ref[0] = (near_ref[0].astype(F32) * inner).astype(BF)
    yclo_ref[...] = (ycrow_ref[...].astype(F32) * inner).astype(BF)
    rims = rims_ref[...]
    top = jnp.concatenate([dot(near_ref[0, 64:256], rims), dot(yv_ref[...], rims), dot(near_ref[1, 0:64], rims)], axis=0)
    bottom = jnp.concatenate([dot(near_ref[1, 64:256], rims), dot(yclo_ref[...], rims), dot(yc_ref[...], rims)], axis=0)
    edge_ref[0] = jnp.concatenate([top[:, :64], bottom[:, :64]], axis=1).astype(BF)
    edge_ref[1] = jnp.concatenate([top[:, 64:], bottom[:, 64:]], axis=1).astype(BF)
    odd = parity("col")
    senda_ref[...] = edge_ref[1 - odd]
    sendb_ref[...] = edge_ref[odd]


UP_TAP = {(0, 0): 1, (1, 0): 0, (1, 1): 2}
PAIRS = [(a, b, c) for a in range(2) for b in range(2) for c in range(2)]


def write_masks(mask_ref):
    lane = lax.broadcasted_iota(jnp.int32, (1, LANES), 1)
    c = lane
    for d in range(1, QD):
        c = jnp.where(lane >= d * SPAN, lane - d * SPAN, c)
    c = c - HALO
    inside = lane < QD * SPAN
    last_col = lax.axis_index("col") == lax.axis_size("col") - 1
    last_row = lax.axis_index("row") == lax.axis_size("row") - 1
    bound = jnp.where(last_col, QC, LANES)
    seen = jnp.where(inside & (c < bound), 1.0, 0.0).astype(F32)
    mask_ref[...] = jnp.zeros(mask_ref.shape, F32)
    mask_ref[0:1] = seen
    mask_ref[1:2] = seen * jnp.where(last_row, 0.0, 1.0)
    mask_ref[2:3] = jnp.where(inside & (c >= 0) & (c < QC), 1.0, 0.0).astype(F32)


def prepare_kernel(wh_ref, wq_ref, wbh_ref, wbf_ref, w1_ref, w2_ref, w3_ref, w4_ref, up1_ref, up2_ref, up3_ref, mask_ref):
    write_masks(mask_ref)
    for ref, out, eye, back in ((wh_ref, w1_ref, 32, False), (wq_ref, w2_ref, 64, False), (wbh_ref, w3_ref, 64, True), (wbf_ref, w4_ref, 32, True)):
        small, large = ref.shape[1], ref.shape[2]
        if back:
            flat = jnp.concatenate([ref[26 - k] for k in range(27)], axis=0)
        else:
            flat = ref[...].reshape(27 * small, large)
        rows = lax.broadcasted_iota(jnp.int32, (eye, eye), 0)
        cols = lax.broadcasted_iota(jnp.int32, (eye, eye), 1)
        unit = jnp.where(rows == cols, 1.0, 0.0).astype(BF)
        out[...] = dot_nt(unit, flat).astype(BF)
    for ref, out, back in ((wh_ref, up1_ref, True), (wq_ref, up2_ref, True), (wbh_ref, up3_ref, False)):
        small, large = ref.shape[1], ref.shape[2]
        out[...] = jnp.zeros(out.shape, BF)
        for p, (pr, pd, pc) in enumerate(PAIRS):
            for n, (nr, nd, nc) in enumerate(PAIRS):
                taps = [UP_TAP.get(key) for key in ((pd, nd), (pr, nr), (pc, nc))]
                if None in taps:
                    continue
                j = taps[0] * 9 + taps[1] * 3 + taps[2]
                out[p * small : (p + 1) * small, n * large : (n + 1) * large] = ref[26 - j if back else j]


def roll_up(x, steps):
    return pltpu.roll(x, steps % LANES, x.ndim - 1)


def fill_full(win_ref, y, base, count):
    pieces = [y[:, pc * LANES : (pc + 1) * LANES] for pc in range(4)]
    pieces = [roll_up(pieces[3], 1)] + pieces
    for c in range(5):
        piece = pieces[c].reshape(count, 4, 16, LANES)
        for pd in range(4):
            win_ref[1 + pd, base : base + count, c] = piece[:, pd].astype(BF)
        last = piece[:, 3].reshape(count * 16, LANES)
        win_ref[0, base : base + count, c] = roll_up(last, SPAN).reshape(count, 16, LANES).astype(BF)


def put_half(win_ref, row, pd, pc, value):
    win_ref[1 + pd, row, 1 + pc] = value.astype(BF)
    if pc == 1:
        left = roll_up(value, 1)
        win_ref[1 + pd, row, 0] = left.astype(BF)
    if pd == 1:
        above = roll_up(value, SPAN)
        win_ref[0, row, 1 + pc] = above.astype(BF)
        if pc == 1:
            win_ref[0, row, 0] = roll_up(left, SPAN).astype(BF)


def rounded(value):
    return value.astype(BF).astype(F32)


def neighbours(low, high):
    parts = []
    for value in (low, high):
        for nd in range(2):
            moved = roll_up(value, -SPAN) if nd else value
            parts.append(moved.astype(BF))
            parts.append(roll_up(moved, -1).astype(BF))
    return jnp.concatenate(parts, axis=0)


def forward_kernel(near_ref, yv_ref, yc_ref, yclo_ref, gota_ref, gotb_ref, mask_ref, place_ref, w1_ref, w2_ref, up3_ref, w4_ref, all_ref, cwin_ref, hwin_ref, preh_ref, preq_ref, q_ref, m_ref, gm_ref):
    seen = mask_ref[0:1]
    seen_next = mask_ref[1:2]
    own = mask_ref[2:3]
    odd = parity("col") == 1
    gota, gotb = gota_ref[...].astype(F32), gotb_ref[...].astype(F32)
    left = jnp.where(odd, gota, gotb) * flag(lax.axis_index("col") > 0)
    rims = jnp.concatenate([left, jnp.where(odd, gotb, gota)], axis=1).astype(BF)
    top, bottom = place_ref[0], place_ref[1]
    fill_full(all_ref, near_ref[0, 64:256].astype(F32) + dot(rims[0:192], top), 0, 3)
    fill_full(all_ref, yv_ref[...].astype(F32) + dot(rims[192:448], top), 3, 4)
    outside = jnp.concatenate([dot(rims[448:512], top), dot(rims[0:192], bottom)], axis=0)
    fill_full(all_ref, near_ref[1].astype(F32) + outside, 7, 4)
    w1 = w1_ref[...]
    for hr in range(5):
        for pd in range(2):
            for pc in range(2):
                col = all_ref[2 * pd : 2 * pd + 3, 2 * hr : 2 * hr + 3, 2 * pc : 2 * pc + 3].reshape(432, LANES)
                pre = dot(w1, col)
                if 1 <= hr <= 3:
                    preh_ref[hr - 1, pd, pc] = pre
                h = rounded(pre * sigmoid(pre)) * (seen if hr < 3 else seen_next)
                put_half(hwin_ref, hr, pd, pc, h)
    quarters = []
    for qr in range(2):
        col = hwin_ref[:, 2 * qr : 2 * qr + 3].reshape(864, LANES)
        pre = dot(w2_ref[...], col)
        preq_ref[qr] = pre
        quarters.append(rounded(pre * sigmoid(pre)) * (seen_next if qr else seen))
    q_ref[...] = (quarters[0] * own).astype(BF)
    up = dot(up3_ref[...], neighbours(quarters[0], quarters[1]))
    fill_full(cwin_ref, yclo_ref[...].astype(F32) + dot(rims[192:256], bottom), 0, 1)
    fill_full(cwin_ref, yc_ref[...].astype(F32) + dot(rims[256:512], bottom), 1, 4)
    w4 = w4_ref[...]
    for p, (pr, pd, pc) in enumerate(PAIRS):
        h = hwin_ref[1 + pd, 1 + pr, 1 + pc].astype(F32)
        pre = up[p * 32 : p * 32 + 32] + h
        m_ref[p] = (rounded(pre * sigmoid(pre)) * own).astype(BF)
        col = cwin_ref[2 * pd : 2 * pd + 3, 2 * pr : 2 * pr + 3, 2 * pc : 2 * pc + 3].reshape(432, LANES)
        gm = rounded(dot(w4, col) * slope(pre)) * seen
        gm_ref[pr, pd, pc] = gm.astype(BF)


def full_grad_kernel(cwin_ref, m_ref, out_ref):
    total = None
    for p, (pr, pd, pc) in enumerate(PAIRS):
        col = cwin_ref[2 * pd : 2 * pd + 3, 2 * pr : 2 * pr + 3, 2 * pc : 2 * pc + 3].reshape(432, LANES)
        part = dot_nt(col, m_ref[p])
        total = part if total is None else total + part
    store_groups(out_ref, total, 0, 112, 32)


def store_groups(out_ref, total, base, rows, width):
    size = total.shape[0]
    for group in range(128 // width):
        low, high = group * rows, min((group + 1) * rows, size)
        out_ref[base : base + high - low, group * width : (group + 1) * width] = total[low:high]
        if high - low < rows:
            out_ref[base + high - low : base + rows, group * width : (group + 1) * width] = jnp.zeros((rows - high + low, width), F32)


def backward_kernel(stage, gm_ref, gota_ref, gotb_ref, vwin_ref, hwin_ref, preh_ref, preq_ref, q_ref, g4_ref, mask_ref, w3_ref, up2_ref, ewin_ref, pack_ref, send_ref, mwin_ref):
    seen = mask_ref[0:1]
    seen_next = mask_ref[1:2]
    own = mask_ref[2:3]
    odd = parity("row") == 1
    inner = flag(lax.axis_index("row") > 0)
    for pd in range(2):
        for pc in range(2):
            last = [ref[1, pd, pc].astype(F32) for ref in (gota_ref, gotb_ref)]
            put_half(mwin_ref, 0, pd, pc, jnp.where(odd, last[0], last[1]) * inner)
            put_half(mwin_ref, 4, pd, pc, jnp.where(odd, last[1], last[0]))
            put_half(mwin_ref, 3, pd, pc, jnp.where(odd, gotb_ref[0, pd, pc].astype(F32), gota_ref[0, pd, pc].astype(F32)))
            for pr in range(2):
                put_half(mwin_ref, 1 + pr, pd, pc, gm_ref[pr, pd, pc].astype(F32))
    quarters = []
    for qr in range(2):
        col = mwin_ref[:, 2 * qr : 2 * qr + 3].reshape(864, LANES)
        gq = rounded(dot(w3_ref[...], col) * slope(preq_ref[qr])) * (seen_next if qr else seen)
        quarters.append(gq)
        if qr == 0:
            store_groups(pack_ref, dot_nt(col, q_ref[...]), 672, 448, 64)
    up = dot(up2_ref[...], neighbours(quarters[0], quarters[1]))
    up_next = dot(up2_ref[0:128, 0:256], neighbours(quarters[1], quarters[1])[0:256])
    total = None
    for p, (pr, pd, pc) in enumerate(PAIRS + [(2, 0, 0), (2, 0, 1), (2, 1, 0), (2, 1, 1)]):
        conv = up[p * 32 : p * 32 + 32] if pr < 2 else up_next[(p - 8) * 32 : (p - 8) * 32 + 32]
        gm = mwin_ref[1 + pd, 1 + pr, 1 + pc].astype(F32)
        gh = rounded((conv + gm) * slope(preh_ref[pr, pd, pc])) * (seen if pr < 2 else seen_next)
        ewin_ref[pd, pr, pc] = gh.astype(BF)
        if pc == 0:
            right = roll_up(gh, -1)
            ewin_ref[pd, pr, 2] = right.astype(BF)
        if pd == 0:
            below = roll_up(gh, -SPAN)
            ewin_ref[2, pr, pc] = below.astype(BF)
            if pc == 0:
                ewin_ref[2, pr, 2] = roll_up(right, -SPAN).astype(BF)
        if pr < 2:
            col = vwin_ref[2 * pd : 2 * pd + 3, 2 * pr + 2 : 2 * pr + 5, 2 * pc : 2 * pc + 3].reshape(432, LANES)
            part = dot_nt(col, (gh * own).astype(BF))
            total = part if total is None else total + part
    store_groups(pack_ref, total, 0, 112, 32)
    pack_ref[112:224] = g4_ref[...]
    col = hwin_ref[:, 0:3].reshape(864, LANES)
    store_groups(pack_ref, dot_nt(col, (quarters[0] * own).astype(BF)), 224, 448, 64)
    pack_ref[1120:PACK] = jnp.zeros((PACK - 1120, 128), F32)
    send_ref[...] = half(pack_ref, stage, False)[...].astype(BF)


def volume_kernel(ewin_ref, cwin_ref, up1_ref, spread_ref, order_ref, out_ref, z_ref):
    up1 = up1_ref[...]
    for pr, pd, pc in PAIRS:
        near = jnp.concatenate(
            [ewin_ref[pd + nd, pr + nr, pc + nc] for nr, nd, nc in PAIRS], axis=0
        )
        up = dot(up1, near)
        for f, (fr, fd, fc) in enumerate(PAIRS):
            r, d, c = 2 * pr + fr, 2 * pd + fd, 2 * pc + fc
            value = up[f * 16 : f * 16 + 16] + cwin_ref[1 + d, 1 + r, 1 + c].astype(F32)
            z_ref[r * 64 + d * 16 : r * 64 + d * 16 + 16, c * LANES : (c + 1) * LANES] = value.astype(BF)
    early = jnp.concatenate([z_ref[:, c * LANES : c * LANES + 256] for c in range(4)], axis=1)
    late = jnp.concatenate([z_ref[:, c * LANES + 128 : (c + 1) * LANES] for c in range(4)], axis=1)
    wide = jnp.concatenate([dot_nt(early, spread_ref[0:768]), dot_nt(late, spread_ref[768:1024])], axis=1).astype(BF)
    wide = lax.dot_general(order_ref[...], wide, (((0,), (0,)), ((), ())), preferred_element_type=F32).astype(BF)
    for d in range(QD):
        out_ref[:, d] = wide[:, d * 128 : (d + 1) * 128].reshape(16, 16, 128)


def side_of(axis, step):
    return jnp.where((lax.axis_index(axis) & step) != 0, 1, 0)


def half(ref, stage, mine):
    count = ref.shape[0] // 2
    side = side_of(*stage)
    return ref.at[pl.ds(pl.multiple_of((side if mine else 1 - side) * count, 16), count)]


def quarter_of(ref, parts, other):
    count = ref.shape[0] // parts
    place = (lax.axis_index("row") & (parts - 1)) ^ other
    return ref.at[pl.ds(pl.multiple_of(place * count, 16), count)]


def fold_kernel(stage, parts, kept_ref, got_ref, own_ref, *send_refs):
    total_ref = send_refs[-1]
    total_ref[...] = half(kept_ref, stage, True)[...] + got_ref[...].astype(F32)
    own_ref[...] = quarter_of(total_ref, parts, 0)[...]
    for other in range(1, parts):
        send_refs[other - 1][...] = quarter_of(total_ref, parts, other)[...].astype(BF)


def unfold_kernel(parts, *refs):
    out_ref = refs[-1]
    for other in range(parts):
        quarter_of(out_ref, parts, other)[...] = refs[other][...]


def finish_kernel(scale, stage, own_ref, got_ref, g1_ref, g2_ref, g3_ref, g4_ref, full_ref):
    half(full_ref, stage, True)[...] = own_ref[...].astype(F32)
    half(full_ref, stage, False)[...] = got_ref[...].astype(F32)
    for ref, base, rows, width in ((g1_ref, 0, 112, 32), (g4_ref, 112, 112, 32), (g2_ref, 224, 448, 64), (g3_ref, 672, 448, 64)):
        small = ref.shape[1]
        taps = rows // small
        back = ref is g3_ref or ref is g4_ref
        for group in range(128 // width):
            count = min(taps, 27 - group * taps)
            block = full_ref[base : base + count * small, group * width : (group + 1) * width] * scale
            block = block.reshape(count, small, width)
            if back:
                for t in range(count):
                    ref[26 - group * taps - t] = block[t]
            else:
                ref[group * taps : group * taps + count] = block


def call(kernel, outs, scratch=(), flops=0, name=None):
    shapes = [jax.ShapeDtypeStruct(shape, dtype) for shape, dtype in outs]
    return pl.pallas_call(
        kernel,
        out_shape=shapes,
        scratch_shapes=list(scratch),
        compiler_params=pltpu.CompilerParams(vmem_limit_bytes=LIMIT),
        cost_estimate=pl.CostEstimate(flops=flops, bytes_accessed=4000000, transcendentals=0),
        name=name,
    )


def swapped(value, row_step, col_step):
    rows, cols = lax.axis_size("row"), lax.axis_size("col")
    pairs = [(r * cols + c, (r ^ row_step) * cols + (c ^ col_step)) for r in range(rows) for c in range(cols)]
    return lax.ppermute(value, ("row", "col"), pairs)


def paired(value, axis, first):
    count = lax.axis_size(axis)
    pairs = []
    for low in range(first, count + first, 2):
        high = (low + 1) % count
        pairs += [(low, high), (high, low)]
    return lax.ppermute(value, axis, pairs)


def tree_sum(terms):
    terms = [term.astype(F32) for term in terms]
    while len(terms) > 1:
        terms = [low + high for low, high in zip(terms[::2], terms[1::2])]
    return terms[0]


def by_tap(weight, swap):
    order = (2, 3, 4, 1, 0) if swap else (2, 3, 4, 0, 1)
    moved = weight.transpose(order)
    return moved.reshape((27,) + moved.shape[3:])


def from_tap(grad, swap):
    cube = grad.reshape((3, 3, 3) + grad.shape[1:])
    return cube.transpose((4, 3, 0, 1, 2) if swap else (3, 4, 0, 1, 2))


def shards(volume, cotangent, w_half, w_quarter, w_back_half, w_back_full):
    rows, cols = lax.axis_size("row"), lax.axis_size("col")
    cells = volume.size // volume.shape[0] * rows * cols
    scale = 1.0 / math.sqrt(cells)
    spread, rims, place, order = [jnp.asarray(a) for a in constants()]
    vol = volume.reshape(16, QD, 16, 128)
    cot = cotangent.reshape(16, QD, 16, 128)
    vol_a, vol_b = paired(vol, "row", 0), paired(vol, "row", 1)
    yv, yc, cot_last = call(
        own_kernel,
        [((256, 4 * LANES), BF), ((256, 4 * LANES), BF), ((64, 4 * LANES), BF)],
        name="own",
    )(vol, cot, spread, order)
    cot_row = lax.ppermute(cot_last, "row", [(i, (i + 1) % rows) for i in range(rows)])
    w1, w2, w3, w4, up1, up2, up3, mask = call(
        prepare_kernel,
        [((32, 432), BF), ((64, 864), BF), ((64, 864), BF), ((32, 432), BF), ((128, 256), BF), ((256, 512), BF), ((256, 512), BF), ((8, LANES), F32)],
        name="prepare",
    )(by_tap(w_half, True), by_tap(w_quarter, True), by_tap(w_back_half, False), by_tap(w_back_full, False))
    near, cot_lo, send_a, send_b = call(
        rows_kernel,
        [((2, 256, 4 * LANES), BF), ((64, 4 * LANES), BF), ((512, 128), BF), ((512, 128), BF)],
        [pltpu.VMEM((2, 512, 128), BF)],
        name="rows",
    )(vol_a, vol_b, yv, yc, cot_row, spread, order, rims)
    rim_a, rim_b = paired(send_a, "col", 0), paired(send_b, "col", 1)
    vwin, cwin, hwin, preh, preq, quarter, mixed, gm = call(
        forward_kernel,
        [
            ((5, 11, 5, 16, LANES), BF),
            ((5, 5, 5, 16, LANES), BF),
            ((3, 5, 3, 32, LANES), BF),
            ((3, 2, 2, 32, LANES), F32),
            ((2, 64, LANES), F32),
            ((64, LANES), BF),
            ((8, 32, LANES), BF),
            ((2, 2, 2, 32, LANES), BF),
        ],
        name="forward",
    )(near, yv, yc, cot_lo, rim_a, rim_b, mask, place, w1, w2, up3, w4)
    gm_a, gm_b = paired(gm, "row", 0), paired(gm, "row", 1)
    (g4,) = call(full_grad_kernel, [((112, 128), F32)], flops=2 * 432 * 32 * LANES * 64, name="full_grad")(cwin, mixed)
    core = ("col", 1)
    parts = min(4, rows)
    ewin, kept, send = call(
        functools.partial(backward_kernel, core),
        [((3, 3, 3, 32, LANES), BF), ((PACK, 128), F32), ((PACK // 2, 128), BF)],
        [pltpu.VMEM((3, 5, 3, 32, LANES), BF)],
        name="backward",
    )(gm, gm_a, gm_b, vwin, hwin, preh, preq, quarter, g4, mask, w3, up2)
    share = PACK // 2 // parts
    kept, *sends = call(
        functools.partial(fold_kernel, core, parts),
        [((share, 128), F32)] + [((share, 128), BF)] * (parts - 1),
        [pltpu.VMEM((PACK // 2, 128), F32)],
        name="fold",
    )(kept, swapped(send, 0, 1))
    part = tree_sum([kept] + [swapped(send, other + 1, 0) for other, send in enumerate(sends)]).astype(BF)
    for group in ([("row", 4), ("col", 2)], [("col", 4), ("col", 8), ("col", 16)]):
        group = [(axis, step) for axis, step in group if step < lax.axis_size(axis)]
        terms = [part]
        for index in range(1, 2 ** len(group)):
            chosen = [stage for bit, stage in enumerate(group) if index >> bit & 1]
            moves = [sum(step for axis, step in chosen if axis == name) for name in ("row", "col")]
            terms.append(swapped(part, *moves))
        part = tree_sum(terms).astype(BF)
    (part,) = call(functools.partial(unfold_kernel, parts), [((PACK // 2, 128), BF)], name="unfold")(
        part, *[swapped(part, other, 0) for other in range(1, parts)]
    )
    (grad_volume,) = call(
        volume_kernel, [((16, QD, 16, 128), BF)], [pltpu.VMEM((256, 4 * LANES), BF)], flops=2 * 256 * 1024 * 4000, name="volume"
    )(ewin, cwin, up1, spread, order)
    g1, g2, g3, g4 = call(
        functools.partial(finish_kernel, scale, core),
        [((27, 16, 32), F32), ((27, 32, 64), F32), ((27, 32, 64), F32), ((27, 16, 32), F32)],
        [pltpu.VMEM((PACK, 128), F32)],
        name="finish",
    )(part, swapped(part, 0, 1))
    return (
        grad_volume.reshape(volume.shape),
        from_tap(g1, True),
        from_tap(g2, True),
        from_tap(g3, False),
        from_tap(g4, False),
    )


def solution(mesh):
    return jax.shard_map(
        shards,
        mesh=mesh,
        in_specs=(P(None, None, "row", "col"), P(None, None, "row", "col"), P(), P(), P(), P()),
        out_specs=(P(None, None, "row", "col"), P(), P(), P(), P()),
        check_vma=False,
    )
```

time: 823 us -> 96.4 us (0.12); the launches traced: 812 us -> 96.1 us
  waiting for transfers between devices: 441 us -> 24.4 us
  local copies, waits for them, and re-layouts: 204 us -> 4.62 us
  matrix products: 80.7 us -> 0 us
  other arithmetic: 19.3 us -> 0.1 us
  Pallas kernels: 0 us -> 15.7 us
  between operations: 15.1 us -> 0.79 us
    psum x2 -> x0, waiting for transfers between devices: 422 us -> none  [shards(): lax.psum((grad_w1.reshape(-1), grad_w2.reshape(-1), grad_w3.reshape(-1),...]
    broadcast_in_dim x11 -> x0, local copies, waits for them, and re-layouts: 52 us -> none  [the longest x2 23.3 us: up_wgrad(): grad_ext[:, None]]
    conv_general_dilated x9 -> x0, matrix products: 51.6 us -> none  [the longest x2 29.7 us: up_wgrad(): lax.conv_general_dilated(grad_ext[:, None], source[:, None], (1, 1, 1), (...]
    unnamed x60 -> x24, local copies, waits for them, and re-layouts: 44.9 us -> 4.62 us
    transpose x2 -> x0, matrix products: 29.1 us -> none  [down_wgrad(): return result.transpose(1, 0, 2, 3, 4)]
    conv_general_dilated x25 -> x0, local copies, waits for them, and re-layouts: 28.8 us -> none  [the longest x14 16.6 us: down(): lax.conv_general_dilated(extended[None], weight, (2, 2, 2), ((1, 1), (0,...]
    reshape x4 -> x0, local copies, waits for them, and re-layouts: 27.3 us -> none  [the longest x1 11 us: shards(): grad_w2.reshape(-1)]
    mul x4 -> x0, local copies, waits for them, and re-layouts: 20.2 us -> none  [the longest x1 8.47 us: shards(): grad_w3 = flat_three.reshape(grad_w3.shape) * scale]
  transfers between devices with their start and end apart: 16 -> 25, of which waited for: 7 -> 14; matrix products, arithmetic and copies ran while one was open for 28% -> 0% of each run, Pallas kernels for 0% -> 5%
where the time goes in v1:
time: 96.4 us; the launch traced here: 96.1 us
  starting transfers between devices  50.5 us (52%)
  waiting for transfers between devices  24.4 us (25%)
  Pallas kernels  15.7 us (16%)
  local copies, waits for them, and re-layouts  4.62 us (5%)
    ppermute x18, starting transfers between devices, swapped(): return lax.ppermute(value, ('row', 'col'), pairs)  37.7 us
    ppermute x6, starting transfers between devices, paired(): return lax.ppermute(value, axis, pairs)  11.3 us
    ppermute x18, waiting for transfers between devices, swapped(): return lax.ppermute(value, ('row', 'col'), pairs)  10.4 us
    ppermute x1, waiting for transfers between devices, shards(): lax.ppermute(cot_last, 'row', [(i, (i + 1) % rows) for i in range(rows)])  7.63 us
    ppermute x6, waiting for transfers between devices, paired(): return lax.ppermute(value, axis, pairs)  6.28 us
    unnamed x24, local copies, waits for them, and re-layouts  4.62 us
    pallas_call x1, Pallas kernels, shards(): call(forward_kernel, [((5, 11, 5, 16, LANES), BF), ((5, 5, 5, 16, LANES),...  3.96 us
    pallas_call x1, Pallas kernels, shards(): call(rows_kernel, [((2, 256, 4 * LANES), BF), ((64, 4 * LANES), BF), ((51...  2.79 us
  transfers between devices with their start and end apart: 25, of which 14 were waited for; matrix products, arithmetic and copies ran while one was open for 0% of the time, Pallas kernels for 5%

profile of v1, /device:TPU:1, one launch (start us, length us, event | category | flops | bytes accessed | tf_op | source)
XLA Modules:
  0.0 96.1 jit_solution(5621155422559644246)
XLA Ops:
  0.6 4.4 %collective-permute-start.1 = (bf16[16,8,16,128]{3,2,1,0:T(8,128)(2,1)}, bf16[16,8,16,128]{3,2,1,0:T(8,128)(2,1)S(1)}, u32[]{:S(2)}, u32[]{:S(2)}) collective-permute-start(bf16[16,8,16,128]{3,2,1,0:T(8,128)(2,1)} %bitcast.28), channel_id=1, source_target_pairs={{32,64},{64,32},{96,128},{128,96},{160,192},{192,160},{224,0},{0,2... | collective-permute-start | bytes 1572872 | tf_op jit(solution)/shard_map/ppermute | solution.py:397
  5.0 1.6 %copy-done = bf16[1024,1024]{1,0:T(8,128)(2,1)S(1)} copy-done((bf16[1024,1024]{1,0:T(8,128)(2,1)S(1)}, bf16[1024,1024]{1,0:T(8,128)(2,1)}, u32[]{:S(2)}) %copy-start) | copy-done | bytes 2097176
  6.6 1.0 %copy-done.3 = bf16[16,32,4,128]{3,2,1,0:T(4,128)(2,1)S(1)} copy-done((bf16[16,32,4,128]{3,2,1,0:T(4,128)(2,1)S(1)}, bf16[16,32,4,128]{3,2,1,0:T(4,128)(2,1)}, u32[]{:S(2)}) %copy-start.3) | copy-done | bytes 524312
  9.6 1.5 %own.1 = (bf16[256,1536]{1,0:T(8,128)(2,1)S(1)}, bf16[256,1536]{1,0:T(8,128)(2,1)S(1)}, bf16[64,1536]{1,0:T(8,128)(2,1)S(1)}) custom-call(bf16[16,8,16,128]{3,2,1,0:T(8,128)(2,1)S(1)} %bitcast.30, bf16[16,8,16,128]{3,2,1,0:T(8,128)(2,1)S(1)} %bitcast.27, bf16[1024,1024]{1,0:T(8,128)(2,1)S(1)} %copy-done, bf16[256,256]{1,0:T(8,128)(2,1)S(1)} %copy-done.5), custom_call_target="tpu_custom_call" | custom-call | bytes 4000000 | tf_op jit(solution)/shard_map/own/pallas_call | solution.py:426
  11.2 1.5 %collective-permute-start.2 = (bf16[64,1536]{1,0:T(8,128)(2,1)S(1)}, bf16[64,1536]{1,0:T(8,128)(2,1)S(1)}, u32[]{:S(2)}, u32[]{:S(2)}) collective-permute-start(bf16[64,1536]{1,0:T(8,128)(2,1)S(1)} %get-tuple-element.41), channel_id=1, source_target_pairs={{0,32},{32,64},{64,96},{96,128},{128,160},{160,192},{192,224},{224... | collective-permute-start | bytes 589832 | tf_op jit(solution)/shard_map/ppermute | solution.py:431
  12.7 7.6 %collective-permute-done.2.ycrow_ref = bf16[64,1536]{1,0:T(8,128)(2,1)S(1)} collective-permute-done((bf16[64,1536]{1,0:T(8,128)(2,1)S(1)}, bf16[64,1536]{1,0:T(8,128)(2,1)S(1)}, u32[]{:S(2)}, u32[]{:S(2)}) %collective-permute-start.2) | collective-permute-done | bytes 196640 | tf_op jit(solution)/shard_map/ppermute | solution.py:431
  20.4 2.8 %rows.1 = (bf16[2,256,1536]{2,1,0:T(8,128)(2,1)S(1)}, bf16[64,1536]{1,0:T(8,128)(2,1)S(1)}, bf16[512,128]{1,0:T(8,128)(2,1)S(1)}, bf16[512,128]{1,0:T(8,128)(2,1)S(1)}) custom-call(bf16[16,8,16,128]{3,2,1,0:T(8,128)(2,1)S(1)} %collective-permute-done.xa_ref, bf16[16,8,16,128]{3,2,1,0:T(8,128)(2,1)S(1)} %collective-permute-done.1.xb_ref, ...), custom_call_target="tpu_custom_call" | custom-call | bytes 4000000 | tf_op jit(solution)/shard_map/rows/pallas_call | solution.py:437
  23.2 2.1 %collective-permute-start.3 = (bf16[512,128]{1,0:T(8,128)(2,1)S(1)}, bf16[512,128]{1,0:T(8,128)(2,1)S(1)}, u32[]{:S(2)}, u32[]{:S(2)}) collective-permute-start(bf16[512,128]{1,0:T(8,128)(2,1)S(1)} %get-tuple-element.44), channel_id=1, source_target_pairs={{0,1},{1,0},{2,3},{3,2},{4,5},{5,4},{6,7},{7,6},{8,9},{9,8},{10,11... | collective-permute-start | bytes 393224 | tf_op jit(solution)/shard_map/ppermute | solution.py:397
  25.3 3.0 %collective-permute-start.4 = (bf16[512,128]{1,0:T(8,128)(2,1)S(1)}, bf16[512,128]{1,0:T(8,128)(2,1)S(1)}, u32[]{:S(2)}, u32[]{:S(2)}) collective-permute-start(bf16[512,128]{1,0:T(8,128)(2,1)S(1)} %get-tuple-element.45), channel_id=1, source_target_pairs={{1,2},{2,1},{3,4},{4,3},{5,6},{6,5},{7,8},{8,7},{9,10},{10,9},{11,... | collective-permute-start | bytes 393224 | tf_op jit(solution)/shard_map/ppermute | solution.py:397
  28.7 2.5 %collective-permute-done.4.gotb_ref = bf16[512,128]{1,0:T(8,128)(2,1)S(1)} collective-permute-done((bf16[512,128]{1,0:T(8,128)(2,1)S(1)}, bf16[512,128]{1,0:T(8,128)(2,1)S(1)}, u32[]{:S(2)}, u32[]{:S(2)}) %collective-permute-start.4) | collective-permute-done | bytes 131104 | tf_op jit(solution)/shard_map/ppermute | solution.py:397
  31.2 4.0 %forward.1 = (bf16[5,11,5,16,384]{4,3,2,1,0:T(8,128)(2,1)S(1)}, bf16[5,5,5,16,384]{4,3,2,1,0:T(8,128)(2,1)S(1)}, bf16[3,5,3,32,384]{4,3,2,1,0:T(8,128)(2,1)S(1)}...) custom-call(bf16[2,256,1536]{2,1,0:T(8,128)(2,1)S(1)} %get-tuple-ele, ...), custom_call_target="tpu_custom_call" | custom-call | bytes 4000000 | tf_op jit(solution)/shard_map/forward/pallas_call | solution.py:444
  35.2 1.7 %collective-permute-start.6 = (bf16[2,2,2,32,384]{4,3,2,1,0:T(8,128)(2,1)S(1)}, bf16[2,2,2,32,384]{4,3,2,1,0:T(8,128)(2,1)S(1)}, u32[]{:S(2)}, u32[]{:S(2)}) collective-permute-start(bf16[2,2,2,32,384]{4,3,2,1,0:T(8,128)(2,1)S(1)} %get-tuple-element.51.gm_ref), channel_id=1, source_target_pairs={{32,64},{64,32},{96,128},{128,96},{160,192},{192,160},{224,0},{0,2... | collective-permute-start | bytes 589832 | tf_op jit(solution)/shard_map/ppermute | solution.py:397
  37.0 1.1 %full_grad.1.g4_ref = f32[112,128]{1,0:T(8,128)S(1)} custom-call(bf16[5,5,5,16,384]{4,3,2,1,0:T(8,128)(2,1)S(1)} %get-tuple-element.57.cwin_ref, bf16[8,32,384]{2,1,0:T(8,128)(2,1)S(1)} %get-tuple-element.58.m_ref), custom_call_target="tpu_custom_call" | custom-call | flops 679477248 | bytes 4000000 | tf_op jit(solution)/shard_map/full_grad/pallas_call | solution.py:459
  38.1 3.7 %collective-permute-done.6.gotb_ref = bf16[2,2,2,32,384]{4,3,2,1,0:T(8,128)(2,1)S(1)} collective-permute-done((bf16[2,2,2,32,384]{4,3,2,1,0:T(8,128)(2,1)S(1)}, bf16[2,2,2,32,384]{4,3,2,1,0:T(8,128)(2,1)S(1)}, u32[]{:S(2)}, u32[]{:S(2)}) %collective-permute-start.6) | collective-permute-done | bytes 196640 | tf_op jit(solution)/shard_map/ppermute | solution.py:397
  41.9 2.6 %backward.1 = (bf16[3,3,3,32,384]{4,3,2,1,0:T(8,128)(2,1)S(1)}, f32[1152,128]{1,0:T(8,128)S(1)}, bf16[576,128]{1,0:T(8,128)(2,1)S(1)}) custom-call(bf16[2,2,2,32,384]{4,3,2,1,0:T(8,128)(2,1)S(1)} %get-tuple-element.51.gm_ref, bf16[2,2,2,32,384]{4,3,2,1,0:T(8,128)(2,1)S(1)} %collective-permute-done.5.gota_ref, ...), custom_call_target="tpu_custom_call" | custom-call | bytes 4000000 | tf_op jit(solution)/shard_map/backward/pallas_call | solution.py:462
  44.5 6.7 %collective-permute-start.7 = (bf16[576,128]{1,0:T(8,128)(2,1)S(1)}, bf16[576,128]{1,0:T(8,128)(2,1)S(1)}, u32[]{:S(2)}, u32[]{:S(2)}) collective-permute-start(bf16[576,128]{1,0:T(8,128)(2,1)S(1)} %get-tuple-element.64), channel_id=1, source_target_pairs={{0,1},{1,0},{2,3},{3,2},{4,5},{5,4},{6,7},{7,6},{8,9},{9,8},{10,11... | collective-permute-start | bytes 442376 | tf_op jit(solution)/shard_map/ppermute | solution.py:388
  52.4 2.5 %collective-permute-start.9 = (bf16[144,128]{1,0:T(8,128)(2,1)S(1)}, bf16[144,128]{1,0:T(8,128)(2,1)S(1)}, u32[]{:S(2)}, u32[]{:S(2)}) collective-permute-start(bf16[144,128]{1,0:T(8,128)(2,1)S(1)} %get-tuple-element.67), channel_id=1, source_target_pairs={{0,64},{1,65},{2,66},{3,67},{4,68},{5,69},{6,70},{7,71},{8,72},{9,... | collective-permute-start | bytes 110600 | tf_op jit(solution)/shard_map/ppermute | solution.py:388
  54.8 1.4 %collective-permute-start.10 = (bf16[144,128]{1,0:T(8,128)(2,1)S(1)}, bf16[144,128]{1,0:T(8,128)(2,1)S(1)}, u32[]{:S(2)}, u32[]{:S(2)}) collective-permute-start(bf16[144,128]{1,0:T(8,128)(2,1)S(1)} %get-tuple-element.68), channel_id=1, source_target_pairs={{0,96},{1,97},{2,98},{3,99},{4,100},{5,101},{6,102},{7,103},{8,104... | collective-permute-start | bytes 110600 | tf_op jit(solution)/shard_map/ppermute | solution.py:388
  56.9 1.9 %collective-permute-done.10 = bf16[144,128]{1,0:T(8,128)(2,1)S(1)} collective-permute-done((bf16[144,128]{1,0:T(8,128)(2,1)S(1)}, bf16[144,128]{1,0:T(8,128)(2,1)S(1)}, u32[]{:S(2)}, u32[]{:S(2)}) %collective-permute-start.10) | collective-permute-done | bytes 36896 | tf_op jit(solution)/shard_map/ppermute | solution.py:388
  59.0 2.5 %collective-permute-start.12 = (bf16[144,128]{1,0:T(8,128)(2,1)S(1)}, bf16[144,128]{1,0:T(8,128)(2,1)S(1)}, u32[]{:S(2)}, u32[]{:S(2)}) collective-permute-start(bf16[144,128]{1,0:T(8,128)(2,1)S(1)} %add_convert_fusion.2), channel_id=1, source_target_pairs={{0,2},{1,3},{2,0},{3,1},{4,6},{5,7},{6,4},{7,5},{8,10},{9,11},{10,... | collective-permute-start | bytes 110600 | tf_op jit(solution)/shard_map/ppermute | solution.py:388
  64.3 3.6 %collective-permute-start.20 = (bf16[144,128]{1,0:T(8,128)(2,1)S(1)}, bf16[144,128]{1,0:T(8,128)(2,1)S(1)}, u32[]{:S(2)}, u32[]{:S(2)}) collective-permute-start(bf16[144,128]{1,0:T(8,128)(2,1)S(1)} %add_convert_fusion.1), channel_id=1, source_target_pairs={{0,28},{1,29},{2,30},{3,31},{4,24},{5,25},{6,26},{7,27},{8,20},{9,... | collective-permute-start | bytes 110600 | tf_op jit(solution)/shard_map/ppermute | solution.py:388
  68.8 3.5 %collective-permute-start.18 = (bf16[144,128]{1,0:T(8,128)(2,1)S(1)}, bf16[144,128]{1,0:T(8,128)(2,1)S(1)}, u32[]{:S(2)}, u32[]{:S(2)}) collective-permute-start(bf16[144,128]{1,0:T(8,128)(2,1)S(1)} %add_convert_fusion.1), channel_id=1, source_target_pairs={{0,20},{1,21},{2,22},{3,23},{4,16},{5,17},{6,18},{7,19},{8,28},{9,... | collective-permute-start | bytes 110600 | tf_op jit(solution)/shard_map/ppermute | solution.py:388
  72.2 1.8 %collective-permute-start.17 = (bf16[144,128]{1,0:T(8,128)(2,1)S(1)}, bf16[144,128]{1,0:T(8,128)(2,1)S(1)}, u32[]{:S(2)}, u32[]{:S(2)}) collective-permute-start(bf16[144,128]{1,0:T(8,128)(2,1)S(1)} %add_convert_fusion.1), channel_id=1, source_target_pairs={{0,16},{1,17},{2,18},{3,19},{4,20},{5,21},{6,22},{7,23},{8,24},{9,... | collective-permute-start | bytes 110600 | tf_op jit(solution)/shard_map/ppermute | solution.py:388
  74.0 1.6 %collective-permute-start.16 = (bf16[144,128]{1,0:T(8,128)(2,1)S(1)}, bf16[144,128]{1,0:T(8,128)(2,1)S(1)}, u32[]{:S(2)}, u32[]{:S(2)}) collective-permute-start(bf16[144,128]{1,0:T(8,128)(2,1)S(1)} %add_convert_fusion.1), channel_id=1, source_target_pairs={{0,12},{1,13},{2,14},{3,15},{4,8},{5,9},{6,10},{7,11},{8,4},{9,5},... | collective-permute-start | bytes 110600 | tf_op jit(solution)/shard_map/ppermute | solution.py:388
  75.7 1.9 %collective-permute-start.14 = (bf16[144,128]{1,0:T(8,128)(2,1)S(1)}, bf16[144,128]{1,0:T(8,128)(2,1)S(1)}, u32[]{:S(2)}, u32[]{:S(2)}) collective-permute-start(bf16[144,128]{1,0:T(8,128)(2,1)S(1)} %add_convert_fusion.1), channel_id=1, source_target_pairs={{0,4},{1,5},{2,6},{3,7},{4,0},{5,1},{6,2},{7,3},{8,12},{9,13},{10,... | collective-permute-start | bytes 110600 | tf_op jit(solution)/shard_map/ppermute | solution.py:388
  77.6 1.6 %collective-permute-done.17 = bf16[144,128]{1,0:T(8,128)(2,1)S(1)} collective-permute-done((bf16[144,128]{1,0:T(8,128)(2,1)S(1)}, bf16[144,128]{1,0:T(8,128)(2,1)S(1)}, u32[]{:S(2)}, u32[]{:S(2)}) %collective-permute-start.17) | collective-permute-done | bytes 36896 | tf_op jit(solution)/shard_map/ppermute | solution.py:388
  80.1 1.1 %collective-permute-start.23 = (bf16[144,128]{1,0:T(8,128)(2,1)S(1)}, bf16[144,128]{1,0:T(8,128)(2,1)S(1)}, u32[]{:S(2)}, u32[]{:S(2)}) collective-permute-start(bf16[144,128]{1,0:T(8,128)(2,1)S(1)} %add_convert_fusion.refs_0_), channel_id=1, source_target_pairs={{0,96},{1,97},{2,98},{3,99},{4,100},{5,101},{6,102},{7,103},{8,104... | collective-permute-start | bytes 110600 | tf_op jit(solution)/shard_map/ppermute | solution.py:388
  81.3 1.6 %collective-permute-start.22 = (bf16[144,128]{1,0:T(8,128)(2,1)S(1)}, bf16[144,128]{1,0:T(8,128)(2,1)S(1)}, u32[]{:S(2)}, u32[]{:S(2)}) collective-permute-start(bf16[144,128]{1,0:T(8,128)(2,1)S(1)} %add_convert_fusion.refs_0_), channel_id=1, source_target_pairs={{0,64},{1,65},{2,66},{3,67},{4,68},{5,69},{6,70},{7,71},{8,72},{9,... | collective-permute-start | bytes 110600 | tf_op jit(solution)/shard_map/ppermute | solution.py:388
  84.4 1.2 %collective-permute-done.22.refs_2_ = bf16[144,128]{1,0:T(8,128)(2,1)S(1)} collective-permute-done((bf16[144,128]{1,0:T(8,128)(2,1)S(1)}, bf16[144,128]{1,0:T(8,128)(2,1)S(1)}, u32[]{:S(2)}, u32[]{:S(2)}) %collective-permute-start.22) | collective-permute-done | bytes 36896 | tf_op jit(solution)/shard_map/ppermute | solution.py:388
  85.7 7.1 %collective-permute-start.24 = (bf16[576,128]{1,0:T(8,128)(2,1)S(1)}, bf16[576,128]{1,0:T(8,128)(2,1)S(1)}, u32[]{:S(2)}, u32[]{:S(2)}) collective-permute-start(bf16[576,128]{1,0:T(8,128)(2,1)S(1)} %unfold.1.own_ref), channel_id=1, source_target_pairs={{0,1},{1,0},{2,3},{3,2},{4,5},{5,4},{6,7},{7,6},{8,9},{9,8},{10,11... | collective-permute-start | bytes 442376 | tf_op jit(solution)/shard_map/ppermute | solution.py:388
  92.8 2.0 %volume.1 = bf16[16,8,16,128]{3,2,1,0:T(8,128)(2,1)} custom-call(bf16[3,3,3,32,384]{4,3,2,1,0:T(8,128)(2,1)S(1)} %get-tuple-element.61.ewin_ref, bf16[5,5,5,16,384]{4,3,2,1,0:T(8,128)(2,1)S(1)} %get-tuple-element.57.cwin_ref, bf16[128,256]{1,0:T(8,128)(2,1)S(1)} %get-tuple-element.62.up1_ref, bf16[1024,1024]{1,0:T(8,128)(2,1)S(1)} %copy-done.1, ...), custom_call_target="tpu_custom_call" | custom-call | flops 2097152000 | bytes 4000000 | tf_op jit(solution)/shard_map/volume/pallas_call | solution.py:487
  94.9 1.2 %finish.1 = (f32[27,16,32]{2,1,0:T(8,128)}, f32[27,32,64]{2,1,0:T(8,128)}, f32[27,32,64]{2,1,0:T(8,128)}, f32[27,16,32]{2,1,0:T(8,128)}) custom-call(bf16[576,128]{1,0:T(8,128)(2,1)S(1)} %unfold.1.own_ref, bf16[576,128]{1,0:T(8,128)(2,1)S(1)} %collective-permute-done.24.got_ref), custom_call_target="tpu_custom_call" | custom-call | bytes 4000000 | tf_op jit(solution)/shard_map/finish/pallas_call | solution.py:490
  (55 shorter events, 10.8 us)
Async XLA Ops:
  0.6 19.7 %collective-permute-start.1 = (bf16[16,8,16,128]{3,2,1,0:T(8,128)(2,1)}, bf16[16,8,16,128]{3,2,1,0:T(8,128)(2,1)S(1)}, u32[]{:S(2)}, u32[]{:S(2)}) collective-permute-start(bf16[16,8,16,128]{3,2,1,0:T(8,128)(2,1)} %bitcast.28), channel_id=1, source_target_pairs={{32,64},{64,32},{96,128},{128,96},{160,192},{192,160},{224,0},{0,2... | collective-permute-start | bytes 1572872 | tf_op jit(solution)/shard_map/ppermute | solution.py:397
  5.0 15.3 %collective-permute-start = (bf16[16,8,16,128]{3,2,1,0:T(8,128)(2,1)}, bf16[16,8,16,128]{3,2,1,0:T(8,128)(2,1)S(1)}, u32[]{:S(2)}, u32[]{:S(2)}) collective-permute-start(bf16[16,8,16,128]{3,2,1,0:T(8,128)(2,1)} %bitcast.29), channel_id=1, source_target_pairs={{0,32},{32,0},{64,96},{96,64},{128,160},{160,128},{192,224},{224,1... | collective-permute-start | bytes 1572872 | tf_op jit(solution)/shard_map/ppermute | solution.py:397
  9.6 10.7 %copy-start.1 = (bf16[1024,1024]{1,0:T(8,128)(2,1)S(1)}, bf16[1024,1024]{1,0:T(8,128)(2,1)}, u32[]{:S(2)}) copy-start(bf16[1024,1024]{1,0:T(8,128)(2,1)} %constant.8.clone.spread_ref) | copy-start | bytes 6291460
  9.6 10.7 %copy-start.7 = (bf16[1536,128]{1,0:T(8,128)(2,1)S(1)}, bf16[1536,128]{1,0:T(8,128)(2,1)}, u32[]{:S(2)}) copy-start(bf16[1536,128]{1,0:T(8,128)(2,1)} %constant.9.clone.rims_ref) | copy-start | bytes 1179652
  11.2 9.2 %collective-permute-start.2 = (bf16[64,1536]{1,0:T(8,128)(2,1)S(1)}, bf16[64,1536]{1,0:T(8,128)(2,1)S(1)}, u32[]{:S(2)}, u32[]{:S(2)}) collective-permute-start(bf16[64,1536]{1,0:T(8,128)(2,1)S(1)} %get-tuple-element.41), channel_id=1, source_target_pairs={{0,32},{32,64},{64,96},{96,128},{128,160},{160,192},{192,224},{224... | collective-permute-start | bytes 589832 | tf_op jit(solution)/shard_map/ppermute | solution.py:431
  20.4 7.9 %copy-start.8 = (bf16[64,32,3,3,3]{0,1,4,3,2:T(8,128)(2,1)S(1)}, bf16[64,32,3,3,3]{0,1,4,3,2:T(8,128)(2,1)}, u32[]{:S(2)}) copy-start(bf16[64,32,3,3,3]{0,1,4,3,2:T(8,128)(2,1)} %param.13) | copy-start | bytes 331780
  20.4 7.9 %copy-start.9 = (bf16[32,64,3,3,3]{1,0,4,3,2:T(8,128)(2,1)S(1)}, bf16[32,64,3,3,3]{1,0,4,3,2:T(8,128)(2,1)}, u32[]{:S(2)}) copy-start(bf16[32,64,3,3,3]{1,0,4,3,2:T(8,128)(2,1)} %param.14) | copy-start | bytes 331780
  20.4 7.9 %copy-start.10 = (bf16[32,16,3,3,3]{0,1,4,3,2:T(8,128)(2,1)S(1)}, bf16[32,16,3,3,3]{0,1,4,3,2:T(8,128)(2,1)}, u32[]{:S(2)}) copy-start(bf16[32,16,3,3,3]{0,1,4,3,2:T(8,128)(2,1)} %param.12) | copy-start | bytes 82948
  20.4 10.8 %copy-start.2 = (bf16[2,256,1536]{2,1,0:T(8,128)(2,1)S(1)}, bf16[2,256,1536]{2,1,0:T(8,128)(2,1)}, u32[]{:S(2)}) copy-start(bf16[2,256,1536]{2,1,0:T(8,128)(2,1)} %constant.10.clone.place_ref) | copy-start | bytes 4718596
  23.2 5.4 %collective-permute-start.3 = (bf16[512,128]{1,0:T(8,128)(2,1)S(1)}, bf16[512,128]{1,0:T(8,128)(2,1)S(1)}, u32[]{:S(2)}, u32[]{:S(2)}) collective-permute-start(bf16[512,128]{1,0:T(8,128)(2,1)S(1)} %get-tuple-element.44), channel_id=1, source_target_pairs={{0,1},{1,0},{2,3},{3,2},{4,5},{5,4},{6,7},{7,6},{8,9},{9,8},{10,11... | collective-permute-start | bytes 393224 | tf_op jit(solution)/shard_map/ppermute | solution.py:397
  25.3 5.9 %collective-permute-start.4 = (bf16[512,128]{1,0:T(8,128)(2,1)S(1)}, bf16[512,128]{1,0:T(8,128)(2,1)S(1)}, u32[]{:S(2)}, u32[]{:S(2)}) collective-permute-start(bf16[512,128]{1,0:T(8,128)(2,1)S(1)} %get-tuple-element.45), channel_id=1, source_target_pairs={{1,2},{2,1},{3,4},{4,3},{5,6},{6,5},{7,8},{8,7},{9,10},{10,9},{11,... | collective-permute-start | bytes 393224 | tf_op jit(solution)/shard_map/ppermute | solution.py:397
  35.2 6.7 %collective-permute-start.6 = (bf16[2,2,2,32,384]{4,3,2,1,0:T(8,128)(2,1)S(1)}, bf16[2,2,2,32,384]{4,3,2,1,0:T(8,128)(2,1)S(1)}, u32[]{:S(2)}, u32[]{:S(2)}) collective-permute-start(bf16[2,2,2,32,384]{4,3,2,1,0:T(8,128)(2,1)S(1)} %get-tuple-element.51.gm_ref), channel_id=1, source_target_pairs={{32,64},{64,32},{96,128},{128,96},{160,192},{192,160},{224,0},{0,2... | collective-permute-start | bytes 589832 | tf_op jit(solution)/shard_map/ppermute | solution.py:397
  36.8 5.1 %collective-permute-start.5 = (bf16[2,2,2,32,384]{4,3,2,1,0:T(8,128)(2,1)S(1)}, bf16[2,2,2,32,384]{4,3,2,1,0:T(8,128)(2,1)S(1)}, u32[]{:S(2)}, u32[]{:S(2)}) collective-permute-start(bf16[2,2,2,32,384]{4,3,2,1,0:T(8,128)(2,1)S(1)} %get-tuple-element.51.gm_ref), channel_id=1, source_target_pairs={{0,32},{32,0},{64,96},{96,64},{128,160},{160,128},{192,224},{224,1... | collective-permute-start | bytes 589832 | tf_op jit(solution)/shard_map/ppermute | solution.py:397
  44.5 48.3 %copy-start.6 = (bf16[256,256]{1,0:T(8,128)(2,1)S(1)}, bf16[256,256]{1,0:T(8,128)(2,1)}, u32[]{:S(2)}) copy-start(bf16[256,256]{1,0:T(8,128)(2,1)} %constant.11.clone.order_ref) | copy-start | bytes 393220
  44.5 7.7 %collective-permute-start.7 = (bf16[576,128]{1,0:T(8,128)(2,1)S(1)}, bf16[576,128]{1,0:T(8,128)(2,1)S(1)}, u32[]{:S(2)}, u32[]{:S(2)}) collective-permute-start(bf16[576,128]{1,0:T(8,128)(2,1)S(1)} %get-tuple-element.64), channel_id=1, source_target_pairs={{0,1},{1,0},{2,3},{3,2},{4,5},{5,4},{6,7},{7,6},{8,9},{9,8},{10,11... | collective-permute-start | bytes 442376 | tf_op jit(solution)/shard_map/ppermute | solution.py:388
  52.3 3.9 %collective-permute-start.8 = (bf16[144,128]{1,0:T(8,128)(2,1)S(1)}, bf16[144,128]{1,0:T(8,128)(2,1)S(1)}, u32[]{:S(2)}, u32[]{:S(2)}) collective-permute-start(bf16[144,128]{1,0:T(8,128)(2,1)S(1)} %get-tuple-element.66), channel_id=1, source_target_pairs={{0,32},{1,33},{2,34},{3,35},{4,36},{5,37},{6,38},{7,39},{8,40},{9,... | collective-permute-start | bytes 110600 | tf_op jit(solution)/shard_map/ppermute | solution.py:388
  52.4 4.6 %collective-permute-start.9 = (bf16[144,128]{1,0:T(8,128)(2,1)S(1)}, bf16[144,128]{1,0:T(8,128)(2,1)S(1)}, u32[]{:S(2)}, u32[]{:S(2)}) collective-permute-start(bf16[144,128]{1,0:T(8,128)(2,1)S(1)} %get-tuple-element.67), channel_id=1, source_target_pairs={{0,64},{1,65},{2,66},{3,67},{4,68},{5,69},{6,70},{7,71},{8,72},{9,... | collective-permute-start | bytes 110600 | tf_op jit(solution)/shard_map/ppermute | solution.py:388
  54.8 4.0 %collective-permute-start.10 = (bf16[144,128]{1,0:T(8,128)(2,1)S(1)}, bf16[144,128]{1,0:T(8,128)(2,1)S(1)}, u32[]{:S(2)}, u32[]{:S(2)}) collective-permute-start(bf16[144,128]{1,0:T(8,128)(2,1)S(1)} %get-tuple-element.68), channel_id=1, source_target_pairs={{0,96},{1,97},{2,98},{3,99},{4,100},{5,101},{6,102},{7,103},{8,104... | collective-permute-start | bytes 110600 | tf_op jit(solution)/shard_map/ppermute | solution.py:388
  58.9 4.1 %collective-permute-start.13 = (bf16[144,128]{1,0:T(8,128)(2,1)S(1)}, bf16[144,128]{1,0:T(8,128)(2,1)S(1)}, u32[]{:S(2)}, u32[]{:S(2)}) collective-permute-start(bf16[144,128]{1,0:T(8,128)(2,1)S(1)} %add_convert_fusion.2), channel_id=1, source_target_pairs={{0,130},{1,131},{2,128},{3,129},{4,134},{5,135},{6,132},{7,133},{8... | collective-permute-start | bytes 110600 | tf_op jit(solution)/shard_map/ppermute | solution.py:388
  59.0 4.4 %collective-permute-start.12 = (bf16[144,128]{1,0:T(8,128)(2,1)S(1)}, bf16[144,128]{1,0:T(8,128)(2,1)S(1)}, u32[]{:S(2)}, u32[]{:S(2)}) collective-permute-start(bf16[144,128]{1,0:T(8,128)(2,1)S(1)} %add_convert_fusion.2), channel_id=1, source_target_pairs={{0,2},{1,3},{2,0},{3,1},{4,6},{5,7},{6,4},{7,5},{8,10},{9,11},{10,... | collective-permute-start | bytes 110600 | tf_op jit(solution)/shard_map/ppermute | solution.py:388
  61.5 2.8 %collective-permute-start.11 = (bf16[144,128]{1,0:T(8,128)(2,1)S(1)}, bf16[144,128]{1,0:T(8,128)(2,1)S(1)}, u32[]{:S(2)}, u32[]{:S(2)}) collective-permute-start(bf16[144,128]{1,0:T(8,128)(2,1)S(1)} %add_convert_fusion.2), channel_id=1, source_target_pairs={{0,128},{1,129},{2,130},{3,131},{4,132},{5,133},{6,134},{7,135},{8... | collective-permute-start | bytes 110600 | tf_op jit(solution)/shard_map/ppermute | solution.py:388
  64.3 11.4 %collective-permute-start.20 = (bf16[144,128]{1,0:T(8,128)(2,1)S(1)}, bf16[144,128]{1,0:T(8,128)(2,1)S(1)}, u32[]{:S(2)}, u32[]{:S(2)}) collective-permute-start(bf16[144,128]{1,0:T(8,128)(2,1)S(1)} %add_convert_fusion.1), channel_id=1, source_target_pairs={{0,28},{1,29},{2,30},{3,31},{4,24},{5,25},{6,26},{7,27},{8,20},{9,... | collective-permute-start | bytes 110600 | tf_op jit(solution)/shard_map/ppermute | solution.py:388
  67.9 7.7 %collective-permute-start.19 = (bf16[144,128]{1,0:T(8,128)(2,1)S(1)}, bf16[144,128]{1,0:T(8,128)(2,1)S(1)}, u32[]{:S(2)}, u32[]{:S(2)}) collective-permute-start(bf16[144,128]{1,0:T(8,128)(2,1)S(1)} %add_convert_fusion.1), channel_id=1, source_target_pairs={{0,24},{1,25},{2,26},{3,27},{4,28},{5,29},{6,30},{7,31},{8,16},{9,... | collective-permute-start | bytes 110600 | tf_op jit(solution)/shard_map/ppermute | solution.py:388
  68.8 8.8 %collective-permute-start.18 = (bf16[144,128]{1,0:T(8,128)(2,1)S(1)}, bf16[144,128]{1,0:T(8,128)(2,1)S(1)}, u32[]{:S(2)}, u32[]{:S(2)}) collective-permute-start(bf16[144,128]{1,0:T(8,128)(2,1)S(1)} %add_convert_fusion.1), channel_id=1, source_target_pairs={{0,20},{1,21},{2,22},{3,23},{4,16},{5,17},{6,18},{7,19},{8,28},{9,... | collective-permute-start | bytes 110600 | tf_op jit(solution)/shard_map/ppermute | solution.py:388
  72.2 6.9 %collective-permute-start.17 = (bf16[144,128]{1,0:T(8,128)(2,1)S(1)}, bf16[144,128]{1,0:T(8,128)(2,1)S(1)}, u32[]{:S(2)}, u32[]{:S(2)}) collective-permute-start(bf16[144,128]{1,0:T(8,128)(2,1)S(1)} %add_convert_fusion.1), channel_id=1, source_target_pairs={{0,16},{1,17},{2,18},{3,19},{4,20},{5,21},{6,22},{7,23},{8,24},{9,... | collective-permute-start | bytes 110600 | tf_op jit(solution)/shard_map/ppermute | solution.py:388
  74.0 5.1 %collective-permute-start.16 = (bf16[144,128]{1,0:T(8,128)(2,1)S(1)}, bf16[144,128]{1,0:T(8,128)(2,1)S(1)}, u32[]{:S(2)}, u32[]{:S(2)}) collective-permute-start(bf16[144,128]{1,0:T(8,128)(2,1)S(1)} %add_convert_fusion.1), channel_id=1, source_target_pairs={{0,12},{1,13},{2,14},{3,15},{4,8},{5,9},{6,10},{7,11},{8,4},{9,5},... | collective-permute-start | bytes 110600 | tf_op jit(solution)/shard_map/ppermute | solution.py:388
  75.7 4.4 %collective-permute-start.15 = (bf16[144,128]{1,0:T(8,128)(2,1)S(1)}, bf16[144,128]{1,0:T(8,128)(2,1)S(1)}, u32[]{:S(2)}, u32[]{:S(2)}) collective-permute-start(bf16[144,128]{1,0:T(8,128)(2,1)S(1)} %add_convert_fusion.1), channel_id=1, source_target_pairs={{0,8},{1,9},{2,10},{3,11},{4,12},{5,13},{6,14},{7,15},{8,0},{9,1},... | collective-permute-start | bytes 110600 | tf_op jit(solution)/shard_map/ppermute | solution.py:388
  75.7 4.4 %collective-permute-start.14 = (bf16[144,128]{1,0:T(8,128)(2,1)S(1)}, bf16[144,128]{1,0:T(8,128)(2,1)S(1)}, u32[]{:S(2)}, u32[]{:S(2)}) collective-permute-start(bf16[144,128]{1,0:T(8,128)(2,1)S(1)} %add_convert_fusion.1), channel_id=1, source_target_pairs={{0,4},{1,5},{2,6},{3,7},{4,0},{5,1},{6,2},{7,3},{8,12},{9,13},{10,... | collective-permute-start | bytes 110600 | tf_op jit(solution)/shard_map/ppermute | solution.py:388
  80.1 4.2 %collective-permute-start.23 = (bf16[144,128]{1,0:T(8,128)(2,1)S(1)}, bf16[144,128]{1,0:T(8,128)(2,1)S(1)}, u32[]{:S(2)}, u32[]{:S(2)}) collective-permute-start(bf16[144,128]{1,0:T(8,128)(2,1)S(1)} %add_convert_fusion.refs_0_), channel_id=1, source_target_pairs={{0,96},{1,97},{2,98},{3,99},{4,100},{5,101},{6,102},{7,103},{8,104... | collective-permute-start | bytes 110600 | tf_op jit(solution)/shard_map/ppermute | solution.py:388
  81.3 4.3 %collective-permute-start.22 = (bf16[144,128]{1,0:T(8,128)(2,1)S(1)}, bf16[144,128]{1,0:T(8,128)(2,1)S(1)}, u32[]{:S(2)}, u32[]{:S(2)}) collective-permute-start(bf16[144,128]{1,0:T(8,128)(2,1)S(1)} %add_convert_fusion.refs_0_), channel_id=1, source_target_pairs={{0,64},{1,65},{2,66},{3,67},{4,68},{5,69},{6,70},{7,71},{8,72},{9,... | collective-permute-start | bytes 110600 | tf_op jit(solution)/shard_map/ppermute | solution.py:388
  82.9 2.8 %collective-permute-start.21 = (bf16[144,128]{1,0:T(8,128)(2,1)S(1)}, bf16[144,128]{1,0:T(8,128)(2,1)S(1)}, u32[]{:S(2)}, u32[]{:S(2)}) collective-permute-start(bf16[144,128]{1,0:T(8,128)(2,1)S(1)} %add_convert_fusion.refs_0_), channel_id=1, source_target_pairs={{0,32},{1,33},{2,34},{3,35},{4,36},{5,37},{6,38},{7,39},{8,40},{9,... | collective-permute-start | bytes 110600 | tf_op jit(solution)/shard_map/ppermute | solution.py:388
  85.7 9.2 %collective-permute-start.24 = (bf16[576,128]{1,0:T(8,128)(2,1)S(1)}, bf16[576,128]{1,0:T(8,128)(2,1)S(1)}, u32[]{:S(2)}, u32[]{:S(2)}) collective-permute-start(bf16[576,128]{1,0:T(8,128)(2,1)S(1)} %unfold.1.own_ref), channel_id=1, source_target_pairs={{0,1},{1,0},{2,3},{3,2},{4,5},{5,4},{6,7},{7,6},{8,9},{9,8},{10,11... | collective-permute-start | bytes 442376 | tf_op jit(solution)/shard_map/ppermute | solution.py:388
  (5 other events, 12.5 us)

commit v2 on v1

--- a/solution.py
+++ b/solution.py
@@ -64,47 +64,38 @@
     return s * (1.0 + t * (1.0 - s))
 
 
-def relayout(x_ref, spread_ref, order_ref):
+def by_rows(x_ref, order_ref):
     wide = jnp.concatenate([x_ref[:, d].reshape(256, 128) for d in range(QD)], axis=1)
-    rows = dot(order_ref[...], wide).astype(BF)
+    return dot(order_ref[...], wide).astype(BF)
+
+
+def to_lanes(rows, spread_ref):
     early = dot(rows[:, :768], spread_ref[0:768])
     late = dot(rows[:, 768:], spread_ref[768:1024])
     pieces = []
     for pc in range(4):
         low, high = pc * 256, pc * 256 + 128
         pieces += [early[:, low:high], early[:, high : low + 256] + late[:, low:high], late[:, high : low + 256]]
-    return jnp.concatenate(pieces, axis=1).astype(BF)
-
-
-def own_kernel(vol_ref, cot_ref, spread_ref, order_ref, yv_ref, yc_ref, last_ref):
-    yv_ref[...] = relayout(vol_ref, spread_ref, order_ref)
-    yc_ref[...] = relayout(cot_ref, spread_ref, order_ref)
-    last_ref[...] = yc_ref[192:256]
-
-
-def parity(axis):
-    return lax.axis_index(axis) & 1
+    return jnp.concatenate(pieces, axis=1)
+
+
+def own_kernel(vol_ref, cot_ref, spread_ref, order_ref, rims_ref, yv_ref, yc_ref, cot_last_ref, first_ref, last_ref):
+    yv_ref[...] = to_lanes(by_rows(vol_ref, order_ref), spread_ref).astype(BF)
+    rows = by_rows(cot_ref, order_ref)
+    cot_last_ref[...] = rows[192:256]
+    yc_ref[...] = to_lanes(rows, spread_ref).astype(BF)
+    edges = [dot(ref[...], rims_ref[...]) for ref in (yv_ref, yc_ref)]
+    first_ref[...] = jnp.concatenate([edge[:, :64] for edge in edges], axis=1).astype(BF)
+    last_ref[...] = jnp.concatenate([edge[:, 64:] for edge in edges], axis=1).astype(BF)
 
 
 def flag(condition):
     return jnp.where(condition, 1.0, 0.0).astype(F32)
 
 
-def rows_kernel(xa_ref, xb_ref, yv_ref, yc_ref, ycrow_ref, spread_ref, order_ref, rims_ref, near_ref, yclo_ref, senda_ref, sendb_ref, edge_ref):
-    odd = parity("row")
-    near_ref[1 - odd] = relayout(xa_ref, spread_ref, order_ref)
-    near_ref[odd] = relayout(xb_ref, spread_ref, order_ref)
-    inner = flag(lax.axis_index("row") > 0)
-    near_ref[0] = (near_ref[0].astype(F32) * inner).astype(BF)
-    yclo_ref[...] = (ycrow_ref[...].astype(F32) * inner).astype(BF)
-    rims = rims_ref[...]
-    top = jnp.concatenate([dot(near_ref[0, 64:256], rims), dot(yv_ref[...], rims), dot(near_ref[1, 0:64], rims)], axis=0)
-    bottom = jnp.concatenate([dot(near_ref[1, 64:256], rims), dot(yclo_ref[...], rims), dot(yc_ref[...], rims)], axis=0)
-    edge_ref[0] = jnp.concatenate([top[:, :64], bottom[:, :64]], axis=1).astype(BF)
-    edge_ref[1] = jnp.concatenate([top[:, 64:], bottom[:, 64:]], axis=1).astype(BF)
-    odd = parity("col")
-    senda_ref[...] = edge_ref[1 - odd]
-    sendb_ref[...] = edge_ref[odd]
+def rim_kernel(left_ref, right_ref, out_ref):
+    out_ref[:, :128] = (left_ref[...].astype(F32) * flag(lax.axis_index("col") > 0)).astype(BF)
+    out_ref[:, 128:] = right_ref[...]
 
 
 UP_TAP = {(0, 0): 1, (1, 0): 0, (1, 1): 2}
@@ -193,19 +184,17 @@
     return jnp.concatenate(parts, axis=0)
 
 
-def forward_kernel(near_ref, yv_ref, yc_ref, yclo_ref, gota_ref, gotb_ref, mask_ref, place_ref, w1_ref, w2_ref, up3_ref, w4_ref, all_ref, cwin_ref, hwin_ref, preh_ref, preq_ref, q_ref, m_ref, gm_ref):
+def forward_kernel(xlo_ref, xhi_ref, yv_ref, yc_ref, cot_lo_ref, own_rim_ref, lo_rim_ref, hi_rim_ref, mask_ref, spread_ref, place_ref, order_ref, w1_ref, w2_ref, up3_ref, w4_ref, all_ref, cwin_ref, hwin_ref, preh_ref, preq_ref, q_ref, m_ref, gm_ref, gm_last_ref):
     seen = mask_ref[0:1]
     seen_next = mask_ref[1:2]
     own = mask_ref[2:3]
-    odd = parity("col") == 1
-    gota, gotb = gota_ref[...].astype(F32), gotb_ref[...].astype(F32)
-    left = jnp.where(odd, gota, gotb) * flag(lax.axis_index("col") > 0)
-    rims = jnp.concatenate([left, jnp.where(odd, gotb, gota)], axis=1).astype(BF)
-    top, bottom = place_ref[0], place_ref[1]
-    fill_full(all_ref, near_ref[0, 64:256].astype(F32) + dot(rims[0:192], top), 0, 3)
-    fill_full(all_ref, yv_ref[...].astype(F32) + dot(rims[192:448], top), 3, 4)
-    outside = jnp.concatenate([dot(rims[448:512], top), dot(rims[0:192], bottom)], axis=0)
-    fill_full(all_ref, near_ref[1].astype(F32) + outside, 7, 4)
+    inner = flag(lax.axis_index("row") > 0)
+    to_vol, to_cot = place_ref[0], place_ref[1]
+    y = to_lanes(by_rows(xlo_ref, order_ref)[64:256], spread_ref) + dot(lo_rim_ref[64:256], to_vol)
+    fill_full(all_ref, y * inner, 0, 3)
+    fill_full(all_ref, yv_ref[...].astype(F32) + dot(own_rim_ref[...], to_vol), 3, 4)
+    y = to_lanes(by_rows(xhi_ref, order_ref), spread_ref) + dot(hi_rim_ref[...], to_vol)
+    fill_full(all_ref, y, 7, 4)
     w1 = w1_ref[...]
     for hr in range(5):
         for pd in range(2):
@@ -224,8 +213,9 @@
         quarters.append(rounded(pre * sigmoid(pre)) * (seen_next if qr else seen))
     q_ref[...] = (quarters[0] * own).astype(BF)
     up = dot(up3_ref[...], neighbours(quarters[0], quarters[1]))
-    fill_full(cwin_ref, yclo_ref[...].astype(F32) + dot(rims[192:256], bottom), 0, 1)
-    fill_full(cwin_ref, yc_ref[...].astype(F32) + dot(rims[256:512], bottom), 1, 4)
+    y = to_lanes(cot_lo_ref[...], spread_ref) + dot(lo_rim_ref[192:256], to_cot)
+    fill_full(cwin_ref, y * inner, 0, 1)
+    fill_full(cwin_ref, yc_ref[...].astype(F32) + dot(own_rim_ref[...], to_cot), 1, 4)
     w4 = w4_ref[...]
     for p, (pr, pd, pc) in enumerate(PAIRS):
         h = hwin_ref[1 + pd, 1 + pr, 1 + pc].astype(F32)
@@ -234,6 +224,8 @@
         col = cwin_ref[2 * pd : 2 * pd + 3, 2 * pr : 2 * pr + 3, 2 * pc : 2 * pc + 3].reshape(432, LANES)
         gm = rounded(dot(w4, col) * slope(pre)) * seen
         gm_ref[pr, pd, pc] = gm.astype(BF)
+        if pr == 1:
+            gm_last_ref[pd, pc] = gm.astype(BF)
 
 
 def full_grad_kernel(cwin_ref, m_ref, out_ref):
@@ -254,20 +246,17 @@
             out_ref[base + high - low : base + rows, group * width : (group + 1) * width] = jnp.zeros((rows - high + low, width), F32)
 
 
-def backward_kernel(stage, gm_ref, gota_ref, gotb_ref, vwin_ref, hwin_ref, preh_ref, preq_ref, q_ref, g4_ref, mask_ref, w3_ref, up2_ref, ewin_ref, pack_ref, send_ref, mwin_ref):
+def backward_kernel(stage, gm_ref, gmlo_ref, gmhi_ref, vwin_ref, hwin_ref, preh_ref, preq_ref, q_ref, g4_ref, mask_ref, w3_ref, up2_ref, ewin_ref, pack_ref, send_ref, mwin_ref):
     seen = mask_ref[0:1]
     seen_next = mask_ref[1:2]
     own = mask_ref[2:3]
-    odd = parity("row") == 1
     inner = flag(lax.axis_index("row") > 0)
     for pd in range(2):
         for pc in range(2):
-            last = [ref[1, pd, pc].astype(F32) for ref in (gota_ref, gotb_ref)]
-            put_half(mwin_ref, 0, pd, pc, jnp.where(odd, last[0], last[1]) * inner)
-            put_half(mwin_ref, 4, pd, pc, jnp.where(odd, last[1], last[0]))
-            put_half(mwin_ref, 3, pd, pc, jnp.where(odd, gotb_ref[0, pd, pc].astype(F32), gota_ref[0, pd, pc].astype(F32)))
+            put_half(mwin_ref, 0, pd, pc, gmlo_ref[pd, pc].astype(F32) * inner)
             for pr in range(2):
                 put_half(mwin_ref, 1 + pr, pd, pc, gm_ref[pr, pd, pc].astype(F32))
+                put_half(mwin_ref, 3 + pr, pd, pc, gmhi_ref[pr, pd, pc].astype(F32))
     quarters = []
     for qr in range(2):
         col = mwin_ref[:, 2 * qr : 2 * qr + 3].reshape(864, LANES)
@@ -388,13 +377,9 @@
     return lax.ppermute(value, ("row", "col"), pairs)
 
 
-def paired(value, axis, first):
+def shifted(value, axis, steps):
     count = lax.axis_size(axis)
-    pairs = []
-    for low in range(first, count + first, 2):
-        high = (low + 1) % count
-        pairs += [(low, high), (high, low)]
-    return lax.ppermute(value, axis, pairs)
+    return lax.ppermute(value, axis, [(i, (i + steps) % count) for i in range(count)])
 
 
 def tree_sum(terms):
@@ -422,26 +407,22 @@
     spread, rims, place, order = [jnp.asarray(a) for a in constants()]
     vol = volume.reshape(16, QD, 16, 128)
     cot = cotangent.reshape(16, QD, 16, 128)
-    vol_a, vol_b = paired(vol, "row", 0), paired(vol, "row", 1)
-    yv, yc, cot_last = call(
+    vol_lo, vol_hi = shifted(vol, "row", 1), shifted(vol, "row", -1)
+    yv, yc, cot_last, first, last = call(
         own_kernel,
-        [((256, 4 * LANES), BF), ((256, 4 * LANES), BF), ((64, 4 * LANES), BF)],
+        [((256, 4 * LANES), BF), ((256, 4 * LANES), BF), ((64, 1024), BF), ((256, 128), BF), ((256, 128), BF)],
         name="own",
-    )(vol, cot, spread, order)
-    cot_row = lax.ppermute(cot_last, "row", [(i, (i + 1) % rows) for i in range(rows)])
+    )(vol, cot, spread, order, rims)
+    left, right = shifted(last, "col", 1), shifted(first, "col", -1)
+    cot_lo = shifted(cot_last, "row", 1)
+    (own_rim,) = call(rim_kernel, [((256, 256), BF)], name="rim")(left, right)
+    lo_rim, hi_rim = shifted(own_rim, "row", 1), shifted(own_rim, "row", -1)
     w1, w2, w3, w4, up1, up2, up3, mask = call(
         prepare_kernel,
         [((32, 432), BF), ((64, 864), BF), ((64, 864), BF), ((32, 432), BF), ((128, 256), BF), ((256, 512), BF), ((256, 512), BF), ((8, LANES), F32)],
         name="prepare",
     )(by_tap(w_half, True), by_tap(w_quarter, True), by_tap(w_back_half, False), by_tap(w_back_full, False))
-    near, cot_lo, send_a, send_b = call(
-        rows_kernel,
-        [((2, 256, 4 * LANES), BF), ((64, 4 * LANES), BF), ((512, 128), BF), ((512, 128), BF)],
-        [pltpu.VMEM((2, 512, 128), BF)],
-        name="rows",
-    )(vol_a, vol_b, yv, yc, cot_row, spread, order, rims)
-    rim_a, rim_b = paired(send_a, "col", 0), paired(send_b, "col", 1)
-    vwin, cwin, hwin, preh, preq, quarter, mixed, gm = call(
+    vwin, cwin, hwin, preh, preq, quarter, mixed, gm, gm_last = call(
         forward_kernel,
         [
             ((5, 11, 5, 16, LANES), BF),
@@ -452,10 +433,11 @@
             ((64, LANES), BF),
             ((8, 32, LANES), BF),
             ((2, 2, 2, 32, LANES), BF),
+            ((2, 2, 32, LANES), BF),
         ],
         name="forward",
-    )(near, yv, yc, cot_lo, rim_a, rim_b, mask, place, w1, w2, up3, w4)
-    gm_a, gm_b = paired(gm, "row", 0), paired(gm, "row", 1)
+    )(vol_lo, vol_hi, yv, yc, cot_lo, own_rim, lo_rim, hi_rim, mask, spread, place, order, w1, w2, up3, w4)
+    gm_lo, gm_hi = shifted(gm_last, "row", 1), shifted(gm, "row", -1)
     (g4,) = call(full_grad_kernel, [((112, 128), F32)], flops=2 * 432 * 32 * LANES * 64, name="full_grad")(cwin, mixed)
     core = ("col", 1)
     parts = min(4, rows)
@@ -464,7 +446,7 @@
         [((3, 3, 3, 32, LANES), BF), ((PACK, 128), F32), ((PACK // 2, 128), BF)],
         [pltpu.VMEM((3, 5, 3, 32, LANES), BF)],
         name="backward",
-    )(gm, gm_a, gm_b, vwin, hwin, preh, preq, quarter, g4, mask, w3, up2)
+    )(gm, gm_lo, gm_hi, vwin, hwin, preh, preq, quarter, g4, mask, w3, up2)
     share = PACK // 2 // parts
     kept, *sends = call(
         functools.partial(fold_kernel, core, parts),
@@ -473,7 +455,7 @@
         name="fold",
     )(kept, swapped(send, 0, 1))
     part = tree_sum([kept] + [swapped(send, other + 1, 0) for other, send in enumerate(sends)]).astype(BF)
-    for group in ([("row", 4), ("col", 2)], [("col", 4), ("col", 8), ("col", 16)]):
+    for group in ([("row", 4), ("col", 2)], [("col", 4), ("col", 8)], [("col", 16)]):
         group = [(axis, step) for axis, step in group if step < lax.axis_size(axis)]
         terms = [part]
         for index in range(1, 2 ** len(group)):

time: 96.4 us -> 96.6 us (level)
  starting transfers between devices: 50.5 us -> 38.8 us
  waiting for transfers between devices: 24.4 us -> 33.2 us
  local copies, waits for them, and re-layouts: 4.62 us -> 8.32 us
    ppermute x18 -> x15, starting transfers between devices: 37.7 us -> 27.8 us  [swapped(): return lax.ppermute(value, ('row', 'col'), pairs)]
    ppermute x18 -> x15, waiting for transfers between devices: 10.4 us -> 16 us  [swapped(): return lax.ppermute(value, ('row', 'col'), pairs)]
    unnamed x24, local copies, waits for them, and re-layouts: 4.62 us -> 8.32 us
    ppermute x7 -> x9, waiting for transfers between devices: 13.9 us -> 17.2 us  [shifted(): lax.ppermute(value, axis, [(i, (i + steps) % count) for i in range(count)])]
    pallas_call x2, Pallas kernels: 4.31 us -> 2.06 us  [the longest x1 2.03 us: shards(): call(own_kernel, [((256, 4 * LANES), BF), ((256, 4 * LANES), BF), ((64, 1...]
    ppermute x7 -> x9, starting transfers between devices: 12.9 us -> 11 us  [shifted(): lax.ppermute(value, axis, [(i, (i + steps) % count) for i in range(count)])]
    pallas_call x1, Pallas kernels: 3.96 us -> 5.59 us  [shards(): call(forward_kernel, [((5, 11, 5, 16, LANES), BF), ((5, 5, 5, 16, LANES),...]
  transfers between devices with their start and end apart: 25 -> 24, of which waited for: 14 -> 15; matrix products, arithmetic and copies ran while one was open for 0% -> 0% of each run, Pallas kernels for 5% -> 6%
where the time goes in v2:
time: 96.6 us; the launch traced here: 96.3 us
  starting transfers between devices  38.8 us (40%)
  waiting for transfers between devices  33.2 us (34%)
  Pallas kernels  15.1 us (16%)
  local copies, waits for them, and re-layouts  8.32 us (9%)
    ppermute x15, starting transfers between devices, swapped(): return lax.ppermute(value, ('row', 'col'), pairs)  27.8 us
    ppermute x9, waiting for transfers between devices, shifted(): lax.ppermute(value, axis, [(i, (i + steps) % count) for i in range(count)])  17.2 us
    ppermute x15, waiting for transfers between devices, swapped(): return lax.ppermute(value, ('row', 'col'), pairs)  16 us
    ppermute x9, starting transfers between devices, shifted(): lax.ppermute(value, axis, [(i, (i + steps) % count) for i in range(count)])  11 us
    unnamed x24, local copies, waits for them, and re-layouts  8.32 us
    pallas_call x1, Pallas kernels, shards(): call(forward_kernel, [((5, 11, 5, 16, LANES), BF), ((5, 5, 5, 16, LANES),...  5.59 us
    pallas_call x1, Pallas kernels, shards(): call(functools.partial(backward_kernel, core), [((3, 3, 3, 32, LANES), BF...  2.64 us
    pallas_call x1, Pallas kernels, shards(): call(volume_kernel, [((16, QD, 16, 128), BF)], [pltpu.VMEM((256, 4 * LANE...  2.05 us
  transfers between devices with their start and end apart: 24, of which 15 were waited for; matrix products, arithmetic and copies ran while one was open for 0% of the time, Pallas kernels for 6%

profile of v2, /device:TPU:1, one launch (start us, length us, event | category | flops | bytes accessed | tf_op | source)
XLA Modules:
  0.0 96.3 jit_solution(11070520511676452467)
XLA Ops:
  0.6 4.4 %collective-permute-start.1 = (bf16[16,8,16,128]{3,2,1,0:T(8,128)(2,1)}, bf16[16,8,16,128]{3,2,1,0:T(8,128)(2,1)S(1)}, u32[]{:S(2)}, u32[]{:S(2)}) collective-permute-start(bf16[16,8,16,128]{3,2,1,0:T(8,128)(2,1)} %bitcast.28), channel_id=1, source_target_pairs={{0,224},{32,0},{64,32},{96,64},{128,96},{160,128},{192,160},{224,1... | collective-permute-start | bytes 1572872 | tf_op jit(solution)/shard_map/ppermute | solution.py:382
  5.0 1.6 %copy-done = bf16[1024,1024]{1,0:T(8,128)(2,1)S(1)} copy-done((bf16[1024,1024]{1,0:T(8,128)(2,1)S(1)}, bf16[1024,1024]{1,0:T(8,128)(2,1)}, u32[]{:S(2)}) %copy-start) | copy-done | bytes 2097176
  7.5 1.0 %copy-done.5 = bf16[16,32,4,128]{3,2,1,0:T(4,128)(2,1)S(1)} copy-done((bf16[16,32,4,128]{3,2,1,0:T(4,128)(2,1)S(1)}, bf16[16,32,4,128]{3,2,1,0:T(4,128)(2,1)}, u32[]{:S(2)}) %copy-start.5) | copy-done | bytes 524312
  8.6 1.0 %copy-done.6 = bf16[16,32,4,128]{3,2,1,0:T(4,128)(2,1)S(1)} copy-done((bf16[16,32,4,128]{3,2,1,0:T(4,128)(2,1)S(1)}, bf16[16,32,4,128]{3,2,1,0:T(4,128)(2,1)}, u32[]{:S(2)}) %copy-start.6) | copy-done | bytes 524312
  10.6 2.0 %own.1 = (bf16[256,1536]{1,0:T(8,128)(2,1)S(1)}, bf16[256,1536]{1,0:T(8,128)(2,1)S(1)}, bf16[64,1024]{1,0:T(8,128)(2,1)S(1)}, bf16[256,128]{1,0:T(8,128)(2,1)S(1)}, bf16[256,128]{1,0:T(8,128)(2,1)S(1)}) custom-call(bf16[16,8,16,128]{3,2,1,0:T(8,128)(2,1)S(1)} %bitcast.30, bf16[16,8,16,128]{3,2,1,0:T(8,128)(2,1)S(1)} %bitcast.27, ...), custom_call_target="tpu_custom_call" | custom-call | bytes 4000000 | tf_op jit(solution)/shard_map/own/pallas_call | solution.py:411
  12.7 3.5 %collective-permute-start.3 = (bf16[256,128]{1,0:T(8,128)(2,1)S(1)}, bf16[256,128]{1,0:T(8,128)(2,1)S(1)}, u32[]{:S(2)}, u32[]{:S(2)}) collective-permute-start(bf16[256,128]{1,0:T(8,128)(2,1)S(1)} %get-tuple-element.41), channel_id=1, source_target_pairs={{0,1},{1,2},{2,3},{3,4},{4,5},{5,6},{6,7},{7,8},{8,9},{9,10},{10,1... | collective-permute-start | bytes 196616 | tf_op jit(solution)/shard_map/ppermute | solution.py:382
  16.2 5.9 %collective-permute-done.3.left_ref = bf16[256,128]{1,0:T(8,128)(2,1)S(1)} collective-permute-done((bf16[256,128]{1,0:T(8,128)(2,1)S(1)}, bf16[256,128]{1,0:T(8,128)(2,1)S(1)}, u32[]{:S(2)}, u32[]{:S(2)}) %collective-permute-start.3) | collective-permute-done | bytes 65568 | tf_op jit(solution)/shard_map/ppermute | solution.py:382
  22.1 5.1 %collective-permute-done.4.right_ref = bf16[256,128]{1,0:T(8,128)(2,1)S(1)} collective-permute-done((bf16[256,128]{1,0:T(8,128)(2,1)S(1)}, bf16[256,128]{1,0:T(8,128)(2,1)S(1)}, u32[]{:S(2)}, u32[]{:S(2)}) %collective-permute-start.4) | collective-permute-done | bytes 65568 | tf_op jit(solution)/shard_map/ppermute | solution.py:382
  27.2 1.5 %collective-permute-start.5 = (bf16[256,256]{1,0:T(8,128)(2,1)S(1)}, bf16[256,256]{1,0:T(8,128)(2,1)S(1)}, u32[]{:S(2)}, u32[]{:S(2)}) collective-permute-start(bf16[256,256]{1,0:T(8,128)(2,1)S(1)} %rim.1.own_rim_ref), channel_id=1, source_target_pairs={{0,32},{32,64},{64,96},{96,128},{128,160},{160,192},{192,224},{224... | collective-permute-start | bytes 393224 | tf_op jit(solution)/shard_map/ppermute | solution.py:382
  31.8 2.4 %collective-permute-done.5.lo_rim_ref = bf16[256,256]{1,0:T(8,128)(2,1)S(1)} collective-permute-done((bf16[256,256]{1,0:T(8,128)(2,1)S(1)}, bf16[256,256]{1,0:T(8,128)(2,1)S(1)}, u32[]{:S(2)}, u32[]{:S(2)}) %collective-permute-start.5) | collective-permute-done | bytes 131104 | tf_op jit(solution)/shard_map/ppermute | solution.py:382
  34.2 5.6 %forward.1 = (bf16[5,11,5,16,384]{4,3,2,1,0:T(8,128)(2,1)S(1)}, bf16[5,5,5,16,384]{4,3,2,1,0:T(8,128)(2,1)S(1)}, bf16[3,5,3,32,384]{4,3,2,1,0:T(8,128)(2,1)S(1)}...) custom-call(bf16[16,8,16,128]{3,2,1,0:T(8,128)(2,1)S(1)} %collective, ...), custom_call_target="tpu_custom_call" | custom-call | bytes 4000000 | tf_op jit(solution)/shard_map/forward/pallas_call | solution.py:425
  39.9 1.4 %collective-permute-start.7 = (bf16[2,2,32,384]{3,2,1,0:T(8,128)(2,1)S(1)}, bf16[2,2,32,384]{3,2,1,0:T(8,128)(2,1)S(1)}, u32[]{:S(2)}, u32[]{:S(2)}) collective-permute-start(bf16[2,2,32,384]{3,2,1,0:T(8,128)(2,1)S(1)} %get-tuple-element.49), channel_id=1, source_target_pairs={{0,32},{32,64},{64,96},{96,128},{128,160},{160,192},{192,224},{224... | collective-permute-start | bytes 294920 | tf_op jit(solution)/shard_map/ppermute | solution.py:382
  41.4 1.1 %full_grad.1.g4_ref = f32[112,128]{1,0:T(8,128)S(1)} custom-call(bf16[5,5,5,16,384]{4,3,2,1,0:T(8,128)(2,1)S(1)} %get-tuple-element.55.cwin_ref, bf16[8,32,384]{2,1,0:T(8,128)(2,1)S(1)} %get-tuple-element.56.m_ref), custom_call_target="tpu_custom_call" | custom-call | flops 679477248 | bytes 4000000 | tf_op jit(solution)/shard_map/full_grad/pallas_call | solution.py:441
  42.5 3.9 %collective-permute-done.7.gmlo_ref = bf16[2,2,32,384]{3,2,1,0:T(8,128)(2,1)S(1)} collective-permute-done((bf16[2,2,32,384]{3,2,1,0:T(8,128)(2,1)S(1)}, bf16[2,2,32,384]{3,2,1,0:T(8,128)(2,1)S(1)}, u32[]{:S(2)}, u32[]{:S(2)}) %collective-permute-start.7) | collective-permute-done | bytes 98336 | tf_op jit(solution)/shard_map/ppermute | solution.py:382
  46.4 2.6 %backward.1 = (bf16[3,3,3,32,384]{4,3,2,1,0:T(8,128)(2,1)S(1)}, f32[1152,128]{1,0:T(8,128)S(1)}, bf16[576,128]{1,0:T(8,128)(2,1)S(1)}) custom-call(bf16[2,2,2,32,384]{4,3,2,1,0:T(8,128)(2,1)S(1)} %get-tuple-element.48.gm_ref, bf16[2,2,32,384]{3,2,1,0:T(8,128)(2,1)S(1)} %collective-permute-done.7.gmlo_ref, ...), custom_call_target="tpu_custom_call" | custom-call | bytes 4000000 | tf_op jit(solution)/shard_map/backward/pallas_call | solution.py:444
  49.0 1.0 %collective-permute-start.9 = (bf16[576,128]{1,0:T(8,128)(2,1)S(1)}, bf16[576,128]{1,0:T(8,128)(2,1)S(1)}, u32[]{:S(2)}, u32[]{:S(2)}) collective-permute-start(bf16[576,128]{1,0:T(8,128)(2,1)S(1)} %get-tuple-element.62), channel_id=1, source_target_pairs={{0,1},{1,0},{2,3},{3,2},{4,5},{5,4},{6,7},{7,6},{8,9},{9,8},{10,11... | collective-permute-start | bytes 442376 | tf_op jit(solution)/shard_map/ppermute | solution.py:377
  51.2 3.3 %collective-permute-start.11 = (bf16[144,128]{1,0:T(8,128)(2,1)S(1)}, bf16[144,128]{1,0:T(8,128)(2,1)S(1)}, u32[]{:S(2)}, u32[]{:S(2)}) collective-permute-start(bf16[144,128]{1,0:T(8,128)(2,1)S(1)} %get-tuple-element.65), channel_id=1, source_target_pairs={{0,64},{1,65},{2,66},{3,67},{4,68},{5,69},{6,70},{7,71},{8,72},{9,... | collective-permute-start | bytes 110600 | tf_op jit(solution)/shard_map/ppermute | solution.py:377
  55.0 1.2 %collective-permute-done.11 = bf16[144,128]{1,0:T(8,128)(2,1)S(1)} collective-permute-done((bf16[144,128]{1,0:T(8,128)(2,1)S(1)}, bf16[144,128]{1,0:T(8,128)(2,1)S(1)}, u32[]{:S(2)}, u32[]{:S(2)}) %collective-permute-start.11) | collective-permute-done | bytes 36896 | tf_op jit(solution)/shard_map/ppermute | solution.py:377
  56.2 2.3 %collective-permute-done.12 = bf16[144,128]{1,0:T(8,128)(2,1)S(1)} collective-permute-done((bf16[144,128]{1,0:T(8,128)(2,1)S(1)}, bf16[144,128]{1,0:T(8,128)(2,1)S(1)}, u32[]{:S(2)}, u32[]{:S(2)}) %collective-permute-start.12) | collective-permute-done | bytes 36896 | tf_op jit(solution)/shard_map/ppermute | solution.py:377
  58.6 2.0 %collective-permute-start.14 = (bf16[144,128]{1,0:T(8,128)(2,1)S(1)}, bf16[144,128]{1,0:T(8,128)(2,1)S(1)}, u32[]{:S(2)}, u32[]{:S(2)}) collective-permute-start(bf16[144,128]{1,0:T(8,128)(2,1)S(1)} %add_convert_fusion.3), channel_id=1, source_target_pairs={{0,2},{1,3},{2,0},{3,1},{4,6},{5,7},{6,4},{7,5},{8,10},{9,11},{10,... | collective-permute-start | bytes 110600 | tf_op jit(solution)/shard_map/ppermute | solution.py:377
  60.6 1.2 %collective-permute-start.13 = (bf16[144,128]{1,0:T(8,128)(2,1)S(1)}, bf16[144,128]{1,0:T(8,128)(2,1)S(1)}, u32[]{:S(2)}, u32[]{:S(2)}) collective-permute-start(bf16[144,128]{1,0:T(8,128)(2,1)S(1)} %add_convert_fusion.3), channel_id=1, source_target_pairs={{0,128},{1,129},{2,130},{3,131},{4,132},{5,133},{6,134},{7,135},{8... | collective-permute-start | bytes 110600 | tf_op jit(solution)/shard_map/ppermute | solution.py:377
  63.6 4.8 %collective-permute-start.18 = (bf16[144,128]{1,0:T(8,128)(2,1)S(1)}, bf16[144,128]{1,0:T(8,128)(2,1)S(1)}, u32[]{:S(2)}, u32[]{:S(2)}) collective-permute-start(bf16[144,128]{1,0:T(8,128)(2,1)S(1)} %add_convert_fusion.2), channel_id=1, source_target_pairs={{0,12},{1,13},{2,14},{3,15},{4,8},{5,9},{6,10},{7,11},{8,4},{9,5},... | collective-permute-start | bytes 110600 | tf_op jit(solution)/shard_map/ppermute | solution.py:377
  69.8 2.5 %collective-permute-done.17 = bf16[144,128]{1,0:T(8,128)(2,1)S(1)} collective-permute-done((bf16[144,128]{1,0:T(8,128)(2,1)S(1)}, bf16[144,128]{1,0:T(8,128)(2,1)S(1)}, u32[]{:S(2)}, u32[]{:S(2)}) %collective-permute-start.17) | collective-permute-done | bytes 36896 | tf_op jit(solution)/shard_map/ppermute | solution.py:377
  72.3 3.2 %collective-permute-start.19 = (bf16[144,128]{1,0:T(8,128)(2,1)S(1)}, bf16[144,128]{1,0:T(8,128)(2,1)S(1)}, u32[]{:S(2)}, u32[]{:S(2)}) collective-permute-start(bf16[144,128]{1,0:T(8,128)(2,1)S(1)} %add_convert_fusion.1), channel_id=1, source_target_pairs={{0,16},{1,17},{2,18},{3,19},{4,20},{5,21},{6,22},{7,23},{8,24},{9,... | collective-permute-start | bytes 110600 | tf_op jit(solution)/shard_map/ppermute | solution.py:377
  75.6 3.7 %collective-permute-done.19 = bf16[144,128]{1,0:T(8,128)(2,1)S(1)} collective-permute-done((bf16[144,128]{1,0:T(8,128)(2,1)S(1)}, bf16[144,128]{1,0:T(8,128)(2,1)S(1)}, u32[]{:S(2)}, u32[]{:S(2)}) %collective-permute-start.19) | collective-permute-done | bytes 36896 | tf_op jit(solution)/shard_map/ppermute | solution.py:377
  79.3 1.7 %collective-permute-start.22 = (bf16[144,128]{1,0:T(8,128)(2,1)S(1)}, bf16[144,128]{1,0:T(8,128)(2,1)S(1)}, u32[]{:S(2)}, u32[]{:S(2)}) collective-permute-start(bf16[144,128]{1,0:T(8,128)(2,1)S(1)} %add_convert_fusion.refs_0_), channel_id=1, source_target_pairs={{0,96},{1,97},{2,98},{3,99},{4,100},{5,101},{6,102},{7,103},{8,104... | collective-permute-start | bytes 110600 | tf_op jit(solution)/shard_map/ppermute | solution.py:377
  81.0 1.6 %collective-permute-start.20 = (bf16[144,128]{1,0:T(8,128)(2,1)S(1)}, bf16[144,128]{1,0:T(8,128)(2,1)S(1)}, u32[]{:S(2)}, u32[]{:S(2)}) collective-permute-start(bf16[144,128]{1,0:T(8,128)(2,1)S(1)} %add_convert_fusion.refs_0_), channel_id=1, source_target_pairs={{0,32},{1,33},{2,34},{3,35},{4,36},{5,37},{6,38},{7,39},{8,40},{9,... | collective-permute-start | bytes 110600 | tf_op jit(solution)/shard_map/ppermute | solution.py:377
  82.6 1.1 %collective-permute-done.22.refs_3_ = bf16[144,128]{1,0:T(8,128)(2,1)S(1)} collective-permute-done((bf16[144,128]{1,0:T(8,128)(2,1)S(1)}, bf16[144,128]{1,0:T(8,128)(2,1)S(1)}, u32[]{:S(2)}, u32[]{:S(2)}) %collective-permute-start.22) | collective-permute-done | bytes 36896 | tf_op jit(solution)/shard_map/ppermute | solution.py:377
  83.7 1.6 %collective-permute-done.21.refs_2_ = bf16[144,128]{1,0:T(8,128)(2,1)S(1)} collective-permute-done((bf16[144,128]{1,0:T(8,128)(2,1)S(1)}, bf16[144,128]{1,0:T(8,128)(2,1)S(1)}, u32[]{:S(2)}, u32[]{:S(2)}) %collective-permute-start.21) | collective-permute-done | bytes 36896 | tf_op jit(solution)/shard_map/ppermute | solution.py:377
  85.3 7.7 %collective-permute-start.23 = (bf16[576,128]{1,0:T(8,128)(2,1)S(1)}, bf16[576,128]{1,0:T(8,128)(2,1)S(1)}, u32[]{:S(2)}, u32[]{:S(2)}) collective-permute-start(bf16[576,128]{1,0:T(8,128)(2,1)S(1)} %unfold.1.own_ref), channel_id=1, source_target_pairs={{0,1},{1,0},{2,3},{3,2},{4,5},{5,4},{6,7},{7,6},{8,9},{9,8},{10,11... | collective-permute-start | bytes 442376 | tf_op jit(solution)/shard_map/ppermute | solution.py:377
  93.0 2.1 %volume.1 = bf16[16,8,16,128]{3,2,1,0:T(8,128)(2,1)} custom-call(bf16[3,3,3,32,384]{4,3,2,1,0:T(8,128)(2,1)S(1)} %get-tuple-element.59.ewin_ref, bf16[5,5,5,16,384]{4,3,2,1,0:T(8,128)(2,1)S(1)} %get-tuple-element.55.cwin_ref, bf16[128,256]{1,0:T(8,128)(2,1)S(1)} %get-tuple-element.60.up1_ref, bf16[1024,1024]{1,0:T(8,128)(2,1)S(1)} %copy-done.1, ...), custom_call_target="tpu_custom_call" | custom-call | flops 2097152000 | bytes 4000000 | tf_op jit(solution)/shard_map/volume/pallas_call | solution.py:469
  95.0 1.2 %finish.1 = (f32[27,16,32]{2,1,0:T(8,128)}, f32[27,32,64]{2,1,0:T(8,128)}, f32[27,32,64]{2,1,0:T(8,128)}, f32[27,16,32]{2,1,0:T(8,128)}) custom-call(bf16[576,128]{1,0:T(8,128)(2,1)S(1)} %unfold.1.own_ref, bf16[576,128]{1,0:T(8,128)(2,1)S(1)} %collective-permute-done.23.got_ref), custom_call_target="tpu_custom_call" | custom-call | bytes 4000000 | tf_op jit(solution)/shard_map/finish/pallas_call | solution.py:472
  (54 shorter events, 10.2 us)
Async XLA Ops:
  0.6 33.6 %collective-permute-start.1 = (bf16[16,8,16,128]{3,2,1,0:T(8,128)(2,1)}, bf16[16,8,16,128]{3,2,1,0:T(8,128)(2,1)S(1)}, u32[]{:S(2)}, u32[]{:S(2)}) collective-permute-start(bf16[16,8,16,128]{3,2,1,0:T(8,128)(2,1)} %bitcast.28), channel_id=1, source_target_pairs={{0,224},{32,0},{64,32},{96,64},{128,96},{160,128},{192,160},{224,1... | collective-permute-start | bytes 1572872 | tf_op jit(solution)/shard_map/ppermute | solution.py:382
  5.0 29.2 %collective-permute-start = (bf16[16,8,16,128]{3,2,1,0:T(8,128)(2,1)}, bf16[16,8,16,128]{3,2,1,0:T(8,128)(2,1)S(1)}, u32[]{:S(2)}, u32[]{:S(2)}) collective-permute-start(bf16[16,8,16,128]{3,2,1,0:T(8,128)(2,1)} %bitcast.29), channel_id=1, source_target_pairs={{0,32},{32,64},{64,96},{96,128},{128,160},{160,192},{192,224},{224... | collective-permute-start | bytes 1572872 | tf_op jit(solution)/shard_map/ppermute | solution.py:382
  5.0 1.6 %copy-start = (bf16[1024,1024]{1,0:T(8,128)(2,1)S(1)}, bf16[1024,1024]{1,0:T(8,128)(2,1)}, u32[]{:S(2)}) copy-start(bf16[1024,1024]{1,0:T(8,128)(2,1)} %constant.8.clone.spread_ref) | copy-start | bytes 6291460
  7.5 1.0 %copy-start.5 = (bf16[16,32,4,128]{3,2,1,0:T(4,128)(2,1)S(1)}, bf16[16,32,4,128]{3,2,1,0:T(4,128)(2,1)}, u32[]{:S(2)}) copy-start(bf16[16,32,4,128]{3,2,1,0:T(4,128)(2,1)} %param.11) | copy-start | bytes 1572868
  8.6 1.0 %copy-start.6 = (bf16[16,32,4,128]{3,2,1,0:T(4,128)(2,1)S(1)}, bf16[16,32,4,128]{3,2,1,0:T(4,128)(2,1)}, u32[]{:S(2)}) copy-start(bf16[16,32,4,128]{3,2,1,0:T(4,128)(2,1)} %param.10) | copy-start | bytes 1572868
  9.6 1.0 %copy-start.7 = (bf16[1536,128]{1,0:T(8,128)(2,1)S(1)}, bf16[1536,128]{1,0:T(8,128)(2,1)}, u32[]{:S(2)}) copy-start(bf16[1536,128]{1,0:T(8,128)(2,1)} %constant.9.clone.rims_ref) | copy-start | bytes 1179652
  10.6 18.1 %copy-start.8 = (bf16[64,32,3,3,3]{0,1,4,3,2:T(8,128)(2,1)S(1)}, bf16[64,32,3,3,3]{0,1,4,3,2:T(8,128)(2,1)}, u32[]{:S(2)}) copy-start(bf16[64,32,3,3,3]{0,1,4,3,2:T(8,128)(2,1)} %param.13) | copy-start | bytes 331780
  10.6 23.6 %copy-start.1 = (bf16[1024,1024]{1,0:T(8,128)(2,1)S(1)}, bf16[1024,1024]{1,0:T(8,128)(2,1)}, u32[]{:S(2)}) copy-start(bf16[1024,1024]{1,0:T(8,128)(2,1)} %constant.8.clone.spread_ref) | copy-start | bytes 6291460
  10.6 23.6 %copy-start.2 = (bf16[2,256,1536]{2,1,0:T(8,128)(2,1)S(1)}, bf16[2,256,1536]{2,1,0:T(8,128)(2,1)}, u32[]{:S(2)}) copy-start(bf16[2,256,1536]{2,1,0:T(8,128)(2,1)} %constant.10.clone.place_ref) | copy-start | bytes 4718596
  12.7 9.4 %collective-permute-start.3 = (bf16[256,128]{1,0:T(8,128)(2,1)S(1)}, bf16[256,128]{1,0:T(8,128)(2,1)S(1)}, u32[]{:S(2)}, u32[]{:S(2)}) collective-permute-start(bf16[256,128]{1,0:T(8,128)(2,1)S(1)} %get-tuple-element.41), channel_id=1, source_target_pairs={{0,1},{1,2},{2,3},{3,4},{4,5},{5,6},{6,7},{7,8},{8,9},{9,10},{10,1... | collective-permute-start | bytes 196616 | tf_op jit(solution)/shard_map/ppermute | solution.py:382
  16.2 10.9 %collective-permute-start.4 = (bf16[256,128]{1,0:T(8,128)(2,1)S(1)}, bf16[256,128]{1,0:T(8,128)(2,1)S(1)}, u32[]{:S(2)}, u32[]{:S(2)}) collective-permute-start(bf16[256,128]{1,0:T(8,128)(2,1)S(1)} %get-tuple-element.42), channel_id=1, source_target_pairs={{0,31},{1,0},{2,1},{3,2},{4,3},{5,4},{6,5},{7,6},{8,7},{9,8},{10,9... | collective-permute-start | bytes 196616 | tf_op jit(solution)/shard_map/ppermute | solution.py:382
  16.2 15.6 %collective-permute-start.2 = (bf16[64,1024]{1,0:T(8,128)(2,1)S(1)}, bf16[64,1024]{1,0:T(8,128)(2,1)S(1)}, u32[]{:S(2)}, u32[]{:S(2)}) collective-permute-start(bf16[64,1024]{1,0:T(8,128)(2,1)S(1)} %get-tuple-element.40), channel_id=1, source_target_pairs={{0,32},{32,64},{64,96},{96,128},{128,160},{160,192},{192,224},{224... | collective-permute-start | bytes 393224 | tf_op jit(solution)/shard_map/ppermute | solution.py:382
  27.2 4.7 %collective-permute-start.6 = (bf16[256,256]{1,0:T(8,128)(2,1)S(1)}, bf16[256,256]{1,0:T(8,128)(2,1)S(1)}, u32[]{:S(2)}, u32[]{:S(2)}) collective-permute-start(bf16[256,256]{1,0:T(8,128)(2,1)S(1)} %rim.1.own_rim_ref), channel_id=1, source_target_pairs={{0,224},{32,0},{64,32},{96,64},{128,96},{160,128},{192,160},{224,1... | collective-permute-start | bytes 393224 | tf_op jit(solution)/shard_map/ppermute | solution.py:382
  27.2 7.0 %collective-permute-start.5 = (bf16[256,256]{1,0:T(8,128)(2,1)S(1)}, bf16[256,256]{1,0:T(8,128)(2,1)S(1)}, u32[]{:S(2)}, u32[]{:S(2)}) collective-permute-start(bf16[256,256]{1,0:T(8,128)(2,1)S(1)} %rim.1.own_rim_ref), channel_id=1, source_target_pairs={{0,32},{32,64},{64,96},{96,128},{128,160},{160,192},{192,224},{224... | collective-permute-start | bytes 393224 | tf_op jit(solution)/shard_map/ppermute | solution.py:382
  39.8 6.5 %collective-permute-start.8 = (bf16[2,2,2,32,384]{4,3,2,1,0:T(8,128)(2,1)S(1)}, bf16[2,2,2,32,384]{4,3,2,1,0:T(8,128)(2,1)S(1)}, u32[]{:S(2)}, u32[]{:S(2)}) collective-permute-start(bf16[2,2,2,32,384]{4,3,2,1,0:T(8,128)(2,1)S(1)} %get-tuple-element.48.gm_ref), channel_id=1, source_target_pairs={{0,224},{32,0},{64,32},{96,64},{128,96},{160,128},{192,160},{224,1... | collective-permute-start | bytes 589832 | tf_op jit(solution)/shard_map/ppermute | solution.py:382
  39.9 6.4 %collective-permute-start.7 = (bf16[2,2,32,384]{3,2,1,0:T(8,128)(2,1)S(1)}, bf16[2,2,32,384]{3,2,1,0:T(8,128)(2,1)S(1)}, u32[]{:S(2)}, u32[]{:S(2)}) collective-permute-start(bf16[2,2,32,384]{3,2,1,0:T(8,128)(2,1)S(1)} %get-tuple-element.49), channel_id=1, source_target_pairs={{0,32},{32,64},{64,96},{96,128},{128,160},{160,192},{192,224},{224... | collective-permute-start | bytes 294920 | tf_op jit(solution)/shard_map/ppermute | solution.py:382
  49.0 44.0 %copy-start.4 = (bf16[256,256]{1,0:T(8,128)(2,1)S(1)}, bf16[256,256]{1,0:T(8,128)(2,1)}, u32[]{:S(2)}) copy-start(bf16[256,256]{1,0:T(8,128)(2,1)} %constant.11.clone.order_ref) | copy-start | bytes 393220
  49.0 2.0 %collective-permute-start.9 = (bf16[576,128]{1,0:T(8,128)(2,1)S(1)}, bf16[576,128]{1,0:T(8,128)(2,1)S(1)}, u32[]{:S(2)}, u32[]{:S(2)}) collective-permute-start(bf16[576,128]{1,0:T(8,128)(2,1)S(1)} %get-tuple-element.62), channel_id=1, source_target_pairs={{0,1},{1,0},{2,3},{3,2},{4,5},{5,4},{6,7},{7,6},{8,9},{9,8},{10,11... | collective-permute-start | bytes 442376 | tf_op jit(solution)/shard_map/ppermute | solution.py:377
  51.1 3.9 %collective-permute-start.10 = (bf16[144,128]{1,0:T(8,128)(2,1)S(1)}, bf16[144,128]{1,0:T(8,128)(2,1)S(1)}, u32[]{:S(2)}, u32[]{:S(2)}) collective-permute-start(bf16[144,128]{1,0:T(8,128)(2,1)S(1)} %get-tuple-element.64), channel_id=1, source_target_pairs={{0,32},{1,33},{2,34},{3,35},{4,36},{5,37},{6,38},{7,39},{8,40},{9,... | collective-permute-start | bytes 110600 | tf_op jit(solution)/shard_map/ppermute | solution.py:377
  51.2 5.0 %collective-permute-start.11 = (bf16[144,128]{1,0:T(8,128)(2,1)S(1)}, bf16[144,128]{1,0:T(8,128)(2,1)S(1)}, u32[]{:S(2)}, u32[]{:S(2)}) collective-permute-start(bf16[144,128]{1,0:T(8,128)(2,1)S(1)} %get-tuple-element.65), channel_id=1, source_target_pairs={{0,64},{1,65},{2,66},{3,67},{4,68},{5,69},{6,70},{7,71},{8,72},{9,... | collective-permute-start | bytes 110600 | tf_op jit(solution)/shard_map/ppermute | solution.py:377
  54.5 4.0 %collective-permute-start.12 = (bf16[144,128]{1,0:T(8,128)(2,1)S(1)}, bf16[144,128]{1,0:T(8,128)(2,1)S(1)}, u32[]{:S(2)}, u32[]{:S(2)}) collective-permute-start(bf16[144,128]{1,0:T(8,128)(2,1)S(1)} %get-tuple-element.66), channel_id=1, source_target_pairs={{0,96},{1,97},{2,98},{3,99},{4,100},{5,101},{6,102},{7,103},{8,104... | collective-permute-start | bytes 110600 | tf_op jit(solution)/shard_map/ppermute | solution.py:377
  58.5 4.1 %collective-permute-start.15 = (bf16[144,128]{1,0:T(8,128)(2,1)S(1)}, bf16[144,128]{1,0:T(8,128)(2,1)S(1)}, u32[]{:S(2)}, u32[]{:S(2)}) collective-permute-start(bf16[144,128]{1,0:T(8,128)(2,1)S(1)} %add_convert_fusion.3), channel_id=1, source_target_pairs={{0,130},{1,131},{2,128},{3,129},{4,134},{5,135},{6,132},{7,133},{8... | collective-permute-start | bytes 110600 | tf_op jit(solution)/shard_map/ppermute | solution.py:377
  58.6 4.6 %collective-permute-start.14 = (bf16[144,128]{1,0:T(8,128)(2,1)S(1)}, bf16[144,128]{1,0:T(8,128)(2,1)S(1)}, u32[]{:S(2)}, u32[]{:S(2)}) collective-permute-start(bf16[144,128]{1,0:T(8,128)(2,1)S(1)} %add_convert_fusion.3), channel_id=1, source_target_pairs={{0,2},{1,3},{2,0},{3,1},{4,6},{5,7},{6,4},{7,5},{8,10},{9,11},{10,... | collective-permute-start | bytes 110600 | tf_op jit(solution)/shard_map/ppermute | solution.py:377
  60.6 3.0 %collective-permute-start.13 = (bf16[144,128]{1,0:T(8,128)(2,1)S(1)}, bf16[144,128]{1,0:T(8,128)(2,1)S(1)}, u32[]{:S(2)}, u32[]{:S(2)}) collective-permute-start(bf16[144,128]{1,0:T(8,128)(2,1)S(1)} %add_convert_fusion.3), channel_id=1, source_target_pairs={{0,128},{1,129},{2,130},{3,131},{4,132},{5,133},{6,134},{7,135},{8... | collective-permute-start | bytes 110600 | tf_op jit(solution)/shard_map/ppermute | solution.py:377
  63.6 6.2 %collective-permute-start.18 = (bf16[144,128]{1,0:T(8,128)(2,1)S(1)}, bf16[144,128]{1,0:T(8,128)(2,1)S(1)}, u32[]{:S(2)}, u32[]{:S(2)}) collective-permute-start(bf16[144,128]{1,0:T(8,128)(2,1)S(1)} %add_convert_fusion.2), channel_id=1, source_target_pairs={{0,12},{1,13},{2,14},{3,15},{4,8},{5,9},{6,10},{7,11},{8,4},{9,5},... | collective-permute-start | bytes 110600 | tf_op jit(solution)/shard_map/ppermute | solution.py:377
  68.4 3.8 %collective-permute-start.17 = (bf16[144,128]{1,0:T(8,128)(2,1)S(1)}, bf16[144,128]{1,0:T(8,128)(2,1)S(1)}, u32[]{:S(2)}, u32[]{:S(2)}) collective-permute-start(bf16[144,128]{1,0:T(8,128)(2,1)S(1)} %add_convert_fusion.2), channel_id=1, source_target_pairs={{0,8},{1,9},{2,10},{3,11},{4,12},{5,13},{6,14},{7,15},{8,0},{9,1},... | collective-permute-start | bytes 110600 | tf_op jit(solution)/shard_map/ppermute | solution.py:377
  68.4 3.8 %collective-permute-start.16 = (bf16[144,128]{1,0:T(8,128)(2,1)S(1)}, bf16[144,128]{1,0:T(8,128)(2,1)S(1)}, u32[]{:S(2)}, u32[]{:S(2)}) collective-permute-start(bf16[144,128]{1,0:T(8,128)(2,1)S(1)} %add_convert_fusion.2), channel_id=1, source_target_pairs={{0,4},{1,5},{2,6},{3,7},{4,0},{5,1},{6,2},{7,3},{8,12},{9,13},{10,... | collective-permute-start | bytes 110600 | tf_op jit(solution)/shard_map/ppermute | solution.py:377
  72.3 6.9 %collective-permute-start.19 = (bf16[144,128]{1,0:T(8,128)(2,1)S(1)}, bf16[144,128]{1,0:T(8,128)(2,1)S(1)}, u32[]{:S(2)}, u32[]{:S(2)}) collective-permute-start(bf16[144,128]{1,0:T(8,128)(2,1)S(1)} %add_convert_fusion.1), channel_id=1, source_target_pairs={{0,16},{1,17},{2,18},{3,19},{4,20},{5,21},{6,22},{7,23},{8,24},{9,... | collective-permute-start | bytes 110600 | tf_op jit(solution)/shard_map/ppermute | solution.py:377
  79.3 4.4 %collective-permute-start.22 = (bf16[144,128]{1,0:T(8,128)(2,1)S(1)}, bf16[144,128]{1,0:T(8,128)(2,1)S(1)}, u32[]{:S(2)}, u32[]{:S(2)}) collective-permute-start(bf16[144,128]{1,0:T(8,128)(2,1)S(1)} %add_convert_fusion.refs_0_), channel_id=1, source_target_pairs={{0,96},{1,97},{2,98},{3,99},{4,100},{5,101},{6,102},{7,103},{8,104... | collective-permute-start | bytes 110600 | tf_op jit(solution)/shard_map/ppermute | solution.py:377
  81.0 4.3 %collective-permute-start.21 = (bf16[144,128]{1,0:T(8,128)(2,1)S(1)}, bf16[144,128]{1,0:T(8,128)(2,1)S(1)}, u32[]{:S(2)}, u32[]{:S(2)}) collective-permute-start(bf16[144,128]{1,0:T(8,128)(2,1)S(1)} %add_convert_fusion.refs_0_), channel_id=1, source_target_pairs={{0,64},{1,65},{2,66},{3,67},{4,68},{5,69},{6,70},{7,71},{8,72},{9,... | collective-permute-start | bytes 110600 | tf_op jit(solution)/shard_map/ppermute | solution.py:377
  81.0 4.3 %collective-permute-start.20 = (bf16[144,128]{1,0:T(8,128)(2,1)S(1)}, bf16[144,128]{1,0:T(8,128)(2,1)S(1)}, u32[]{:S(2)}, u32[]{:S(2)}) collective-permute-start(bf16[144,128]{1,0:T(8,128)(2,1)S(1)} %add_convert_fusion.refs_0_), channel_id=1, source_target_pairs={{0,32},{1,33},{2,34},{3,35},{4,36},{5,37},{6,38},{7,39},{8,40},{9,... | collective-permute-start | bytes 110600 | tf_op jit(solution)/shard_map/ppermute | solution.py:377
  85.3 9.7 %collective-permute-start.23 = (bf16[576,128]{1,0:T(8,128)(2,1)S(1)}, bf16[576,128]{1,0:T(8,128)(2,1)S(1)}, u32[]{:S(2)}, u32[]{:S(2)}) collective-permute-start(bf16[576,128]{1,0:T(8,128)(2,1)S(1)} %unfold.1.own_ref), channel_id=1, source_target_pairs={{0,1},{1,0},{2,3},{3,2},{4,5},{5,4},{6,7},{7,6},{8,9},{9,8},{10,11... | collective-permute-start | bytes 442376 | tf_op jit(solution)/shard_map/ppermute | solution.py:377
  (4 other events, 3.6 us)

commit v3 on v2

--- a/solution.py
+++ b/solution.py
@@ -3,7 +3,6 @@
 
 import jax
 import jax.numpy as jnp
-import numpy as np
 from jax import lax
 from jax.experimental import pallas as pl
 from jax.experimental.pallas import tpu as pltpu
@@ -15,7 +14,7 @@
 QD, QC, HALO = 8, 32, 2
 SPAN = QC + 2 * HALO
 LANES = 384
-PACK = 1152
+PACK = 1536
 LIMIT = 24 * 1024 * 1024
 
 
@@ -23,28 +22,36 @@
     return SPAN * d + c + HALO
 
 
-def constants():
-    spread = np.zeros((QD * 128, 4 * 256), np.float32)
-    rims = np.zeros((4 * LANES, 128), np.float32)
-    place = np.zeros((2, 256, 4 * LANES), np.float32)
-    for d in range(QD):
-        for phase in range(4):
-            for c in range(QC):
-                spread[d * 128 + 4 * c + phase, phase * 256 + lane_of(d, c) - (0 if d < 6 else 128)] = 1
-            for e in range(2):
-                for side in range(2):
-                    slot = phase * 16 + d * 2 + e
-                    column = e if side == 0 else QC - 2 + e
-                    rims[phase * LANES + lane_of(d, column), side * 64 + slot] = 1
-                    outside = e - 2 if side == 0 else QC + e
-                    for half in range(2):
-                        place[half, side * 128 + half * 64 + slot, phase * LANES + lane_of(d, outside)] = 1
-    order = np.zeros((256, 256), np.float32)
-    for ch in range(16):
-        for pd in range(4):
-            for r in range(4):
-                order[r * 64 + pd * 16 + ch, ch * 16 + pd * 4 + r] = 1
-    return [np.asarray(a, BF) for a in (spread, rims, place, order)]
+def iota(shape, dim):
+    return lax.broadcasted_iota(jnp.int32, shape, dim)
+
+
+def ones_where(condition):
+    return jnp.where(condition, 1.0, 0.0).astype(BF)
+
+
+def tables_kernel(spread_ref, rims_ref, place_ref, order_ref):
+    w, lane = iota((128, 256), 0), iota((128, 256), 1)
+    for phase in range(4):
+        apart = jnp.where((w & 3) == phase, lane - (w >> 2), -LANES)
+        for d in range(QD):
+            block = ones_where(apart == lane_of(d, 0) - (0 if d < 6 else 128))
+            spread_ref[d * 128 : (d + 1) * 128, phase * 256 : (phase + 1) * 256] = block
+    slot, lane = iota((LANES, 128), 1), iota((LANES, 128), 0)
+    column = (slot & 1) + jnp.where(slot >= 64, QC - 2, 0)
+    target = SPAN * ((slot >> 1) & 7) + HALO + column
+    for phase in range(4):
+        rims_ref[phase * LANES : (phase + 1) * LANES] = ones_where((lane == target) & (((slot >> 4) & 3) == phase))
+    place_ref[...] = jnp.zeros(place_ref.shape, BF)
+    slot, lane = iota((16, LANES), 0), iota((16, LANES), 1)
+    for side in range(2):
+        block = ones_where(lane == SPAN * (slot >> 1) + HALO + (slot & 1) + (QC if side else -2))
+        for array in range(2):
+            for phase in range(4):
+                row = side * 128 + array * 64 + phase * 16
+                place_ref[array, row : row + 16, phase * LANES : (phase + 1) * LANES] = block
+    row, column = iota((256, 256), 0), iota((256, 256), 1)
+    order_ref[...] = ones_where(column == (row & 15) * 16 + ((row >> 4) & 3) * 4 + (row >> 6))
 
 
 def dot(a, b):
@@ -79,9 +86,19 @@
     return jnp.concatenate(pieces, axis=1)
 
 
-def own_kernel(vol_ref, cot_ref, spread_ref, order_ref, rims_ref, yv_ref, yc_ref, cot_last_ref, first_ref, last_ref):
-    yv_ref[...] = to_lanes(by_rows(vol_ref, order_ref), spread_ref).astype(BF)
-    rows = by_rows(cot_ref, order_ref)
+def fetch(pairs, sems):
+    copies = [pltpu.make_async_copy(source, target, sems.at[i]) for i, (source, target) in enumerate(pairs)]
+    for copy in copies:
+        copy.start()
+    return copies
+
+
+def own_kernel(vol_ref, cot_ref, spread_ref, order_ref, rims_ref, yv_ref, yc_ref, cot_last_ref, first_ref, last_ref, vol_here, cot_here, sems):
+    copies = fetch(((vol_ref, vol_here), (cot_ref, cot_here)), sems)
+    copies[0].wait()
+    yv_ref[...] = to_lanes(by_rows(vol_here, order_ref), spread_ref).astype(BF)
+    copies[1].wait()
+    rows = by_rows(cot_here, order_ref)
     cot_last_ref[...] = rows[192:256]
     yc_ref[...] = to_lanes(rows, spread_ref).astype(BF)
     edges = [dot(ref[...], rims_ref[...]) for ref in (yv_ref, yc_ref)]
@@ -119,8 +136,14 @@
     mask_ref[2:3] = jnp.where(inside & (c >= 0) & (c < QC), 1.0, 0.0).astype(F32)
 
 
-def prepare_kernel(wh_ref, wq_ref, wbh_ref, wbf_ref, w1_ref, w2_ref, w3_ref, w4_ref, up1_ref, up2_ref, up3_ref, mask_ref):
-    write_masks(mask_ref)
+def prepare_kernel(*refs):
+    sources, outs, here, sems = refs[0:4], refs[4:12], refs[12:16], refs[16]
+    copies = fetch(list(zip(sources, here)), sems)
+    write_masks(outs[7])
+    for copy in copies:
+        copy.wait()
+    wh_ref, wq_ref, wbh_ref, wbf_ref = here
+    w1_ref, w2_ref, w3_ref, w4_ref, up1_ref, up2_ref, up3_ref = outs[:7]
     for ref, out, eye, back in ((wh_ref, w1_ref, 32, False), (wq_ref, w2_ref, 64, False), (wbh_ref, w3_ref, 64, True), (wbf_ref, w4_ref, 32, True)):
         small, large = ref.shape[1], ref.shape[2]
         if back:
@@ -321,24 +344,18 @@
     return ref.at[pl.ds(pl.multiple_of((side if mine else 1 - side) * count, 16), count)]
 
 
-def quarter_of(ref, parts, other):
-    count = ref.shape[0] // parts
-    place = (lax.axis_index("row") & (parts - 1)) ^ other
-    return ref.at[pl.ds(pl.multiple_of(place * count, 16), count)]
-
-
-def fold_kernel(stage, parts, kept_ref, got_ref, own_ref, *send_refs):
-    total_ref = send_refs[-1]
-    total_ref[...] = half(kept_ref, stage, True)[...] + got_ref[...].astype(F32)
-    own_ref[...] = quarter_of(total_ref, parts, 0)[...]
-    for other in range(1, parts):
-        send_refs[other - 1][...] = quarter_of(total_ref, parts, other)[...].astype(BF)
-
-
-def unfold_kernel(parts, *refs):
-    out_ref = refs[-1]
-    for other in range(parts):
-        quarter_of(out_ref, parts, other)[...] = refs[other][...]
+def fold_kernel(stage, kept_ref, got_ref, out_ref):
+    out_ref[...] = (half(kept_ref, stage, True)[...] + got_ref[...].astype(F32)).astype(BF)
+
+
+def sum_kernel(terms, copies, x_ref, out_ref):
+    size = x_ref.shape[0] // terms
+    total = x_ref[0:size].astype(F32)
+    for i in range(1, terms):
+        total = total + x_ref[i * size : (i + 1) * size].astype(F32)
+    total = total.astype(BF)
+    for i in range(copies):
+        out_ref[i * size : (i + 1) * size] = total
 
 
 def finish_kernel(scale, stage, own_ref, got_ref, g1_ref, g2_ref, g3_ref, g4_ref, full_ref):
@@ -359,12 +376,16 @@
                 ref[group * taps : group * taps + count] = block
 
 
-def call(kernel, outs, scratch=(), flops=0, name=None):
+def call(kernel, outs, scratch=(), flops=0, far=None, name=None):
     shapes = [jax.ShapeDtypeStruct(shape, dtype) for shape, dtype in outs]
+    specs = {}
+    if far:
+        specs["in_specs"] = [pl.BlockSpec(memory_space=pltpu.HBM)] * far[0] + [pl.BlockSpec(memory_space=pltpu.VMEM)] * far[1]
     return pl.pallas_call(
         kernel,
         out_shape=shapes,
         scratch_shapes=list(scratch),
+        **specs,
         compiler_params=pltpu.CompilerParams(vmem_limit_bytes=LIMIT),
         cost_estimate=pl.CostEstimate(flops=flops, bytes_accessed=4000000, transcendentals=0),
         name=name,
@@ -382,11 +403,19 @@
     return lax.ppermute(value, axis, [(i, (i + steps) % count) for i in range(count)])
 
 
-def tree_sum(terms):
-    terms = [term.astype(F32) for term in terms]
-    while len(terms) > 1:
-        terms = [low + high for low, high in zip(terms[::2], terms[1::2])]
-    return terms[0]
+def exchanged(value, row_bits, col_bits):
+    rows, cols = lax.axis_size("row"), lax.axis_size("col")
+    if not row_bits and not col_bits:
+        return value
+    groups = {}
+    for r in range(rows):
+        for c in range(cols):
+            groups.setdefault((r & ~row_bits, c & ~col_bits), []).append(r * cols + c)
+    return lax.all_to_all(value, ("row", "col"), 0, 0, axis_index_groups=list(groups.values()), tiled=True)
+
+
+def held(value):
+    return pltpu.with_memory_space_constraint(value, pltpu.HBM)
 
 
 def by_tap(weight, swap):
@@ -404,24 +433,33 @@
     rows, cols = lax.axis_size("row"), lax.axis_size("col")
     cells = volume.size // volume.shape[0] * rows * cols
     scale = 1.0 / math.sqrt(cells)
-    spread, rims, place, order = [jnp.asarray(a) for a in constants()]
+    spread, rims, place, order = call(
+        tables_kernel,
+        [((QD * 128, 1024), BF), ((4 * LANES, 128), BF), ((2, 256, 4 * LANES), BF), ((256, 256), BF)],
+        name="tables",
+    )()
     vol = volume.reshape(16, QD, 16, 128)
     cot = cotangent.reshape(16, QD, 16, 128)
     vol_lo, vol_hi = shifted(vol, "row", 1), shifted(vol, "row", -1)
     yv, yc, cot_last, first, last = call(
         own_kernel,
         [((256, 4 * LANES), BF), ((256, 4 * LANES), BF), ((64, 1024), BF), ((256, 128), BF), ((256, 128), BF)],
+        [pltpu.VMEM(vol.shape, BF), pltpu.VMEM(cot.shape, BF), pltpu.SemaphoreType.DMA((2,))],
+        far=(2, 3),
         name="own",
-    )(vol, cot, spread, order, rims)
+    )(held(vol), held(cot), spread, order, rims)
     left, right = shifted(last, "col", 1), shifted(first, "col", -1)
     cot_lo = shifted(cot_last, "row", 1)
     (own_rim,) = call(rim_kernel, [((256, 256), BF)], name="rim")(left, right)
     lo_rim, hi_rim = shifted(own_rim, "row", 1), shifted(own_rim, "row", -1)
+    weights = by_tap(w_half, True), by_tap(w_quarter, True), by_tap(w_back_half, False), by_tap(w_back_full, False)
     w1, w2, w3, w4, up1, up2, up3, mask = call(
         prepare_kernel,
         [((32, 432), BF), ((64, 864), BF), ((64, 864), BF), ((32, 432), BF), ((128, 256), BF), ((256, 512), BF), ((256, 512), BF), ((8, LANES), F32)],
+        [pltpu.VMEM(weight.shape, BF) for weight in weights] + [pltpu.SemaphoreType.DMA((4,))],
+        far=(4, 0),
         name="prepare",
-    )(by_tap(w_half, True), by_tap(w_quarter, True), by_tap(w_back_half, False), by_tap(w_back_full, False))
+    )(*[held(weight) for weight in weights])
     vwin, cwin, hwin, preh, preq, quarter, mixed, gm, gm_last = call(
         forward_kernel,
         [
@@ -440,32 +478,20 @@
     gm_lo, gm_hi = shifted(gm_last, "row", 1), shifted(gm, "row", -1)
     (g4,) = call(full_grad_kernel, [((112, 128), F32)], flops=2 * 432 * 32 * LANES * 64, name="full_grad")(cwin, mixed)
     core = ("col", 1)
-    parts = min(4, rows)
     ewin, kept, send = call(
         functools.partial(backward_kernel, core),
         [((3, 3, 3, 32, LANES), BF), ((PACK, 128), F32), ((PACK // 2, 128), BF)],
         [pltpu.VMEM((3, 5, 3, 32, LANES), BF)],
         name="backward",
     )(gm, gm_lo, gm_hi, vwin, hwin, preh, preq, quarter, g4, mask, w3, up2)
-    share = PACK // 2 // parts
-    kept, *sends = call(
-        functools.partial(fold_kernel, core, parts),
-        [((share, 128), F32)] + [((share, 128), BF)] * (parts - 1),
-        [pltpu.VMEM((PACK // 2, 128), F32)],
-        name="fold",
-    )(kept, swapped(send, 0, 1))
-    part = tree_sum([kept] + [swapped(send, other + 1, 0) for other, send in enumerate(sends)]).astype(BF)
-    for group in ([("row", 4), ("col", 2)], [("col", 4), ("col", 8)], [("col", 16)]):
-        group = [(axis, step) for axis, step in group if step < lax.axis_size(axis)]
-        terms = [part]
-        for index in range(1, 2 ** len(group)):
-            chosen = [stage for bit, stage in enumerate(group) if index >> bit & 1]
-            moves = [sum(step for axis, step in chosen if axis == name) for name in ("row", "col")]
-            terms.append(swapped(part, *moves))
-        part = tree_sum(terms).astype(BF)
-    (part,) = call(functools.partial(unfold_kernel, parts), [((PACK // 2, 128), BF)], name="unfold")(
-        part, *[swapped(part, other, 0) for other in range(1, parts)]
-    )
+    (part,) = call(functools.partial(fold_kernel, core), [((PACK // 2, 128), BF)], name="fold")(kept, swapped(send, 0, 1))
+    along = [(7 & (rows - 1), 2 & (cols - 1)), (0, 28 & (cols - 1))]
+    sizes = [2 ** (r.bit_count() + c.bit_count()) for r, c in along]
+    share = PACK // 2 // sizes[0]
+    for bits, size, later in zip(along, sizes, sizes[::-1]):
+        part = exchanged(part.reshape(size, share, 128), *bits).reshape(size * share, 128)
+        (part,) = call(functools.partial(sum_kernel, size, later), [((later * share, 128), BF)], name="sum")(part)
+    part = exchanged(part.reshape(sizes[0], share, 128), *along[0]).reshape(PACK // 2, 128)
     (grad_volume,) = call(
         volume_kernel, [((16, QD, 16, 128), BF)], [pltpu.VMEM((256, 4 * LANES), BF)], flops=2 * 256 * 1024 * 4000, name="volume"
     )(ewin, cwin, up1, spread, order)

time: 96.6 us -> 95 us (0.983)
  blocking collectives: 0 us -> 38.4 us
  starting transfers between devices: 38.8 us -> 15.4 us
  waiting for transfers between devices: 33.2 us -> 22 us
  local copies, waits for them, and re-layouts: 8.32 us -> 0 us
  Pallas kernels: 15.1 us -> 18.3 us
    all_to_all x0 -> x3, blocking collectives: none -> 38.4 us  [exchanged(): lax.all_to_all(value, ('row', 'col'), 0, 0, axis_index_groups=list(groups...]
    ppermute x15 -> x2, starting transfers between devices: 27.8 us -> 4.4 us  [swapped(): return lax.ppermute(value, ('row', 'col'), pairs)]
    ppermute x15 -> x2, waiting for transfers between devices: 16 us -> 1.43 us  [swapped(): return lax.ppermute(value, ('row', 'col'), pairs)]
    unnamed x24 -> x0, local copies, waits for them, and re-layouts: 8.32 us -> none
    ppermute x9, waiting for transfers between devices: 17.2 us -> 20.6 us  [shifted(): lax.ppermute(value, axis, [(i, (i + steps) % count) for i in range(count)])]
    pallas_call x1, Pallas kernels: 0.36 us -> 1.61 us  [shards(): call(prepare_kernel, [((32, 432), BF), ((64, 864), BF), ((64, 864), BF),...]
    pallas_call x1, Pallas kernels: 2.03 us -> 3.27 us  [shards(): call(own_kernel, [((256, 4 * LANES), BF), ((256, 4 * LANES), BF), ((64, 1...]
  transfers between devices with their start and end apart: 24 -> 11, of which waited for: 15 -> 6; matrix products, arithmetic and copies ran while one was open for 0% -> 0% of each run, Pallas kernels for 6% -> 9%
where the time goes in v3:
time: 95 us; the launch traced here: 94.8 us
  blocking collectives  38.4 us (40%)
  waiting for transfers between devices  22 us (23%)
  Pallas kernels  18.3 us (19%)
  starting transfers between devices  15.4 us (16%)
    all_to_all x3, blocking collectives, exchanged(): lax.all_to_all(value, ('row', 'col'), 0, 0, axis_index_groups=list(groups...  38.4 us
    ppermute x9, waiting for transfers between devices, shifted(): lax.ppermute(value, axis, [(i, (i + steps) % count) for i in range(count)])  20.6 us
    ppermute x9, starting transfers between devices, shifted(): lax.ppermute(value, axis, [(i, (i + steps) % count) for i in range(count)])  11 us
    pallas_call x1, Pallas kernels, shards(): call(forward_kernel, [((5, 11, 5, 16, LANES), BF), ((5, 5, 5, 16, LANES),...  5.56 us
    ppermute x2, starting transfers between devices, swapped(): return lax.ppermute(value, ('row', 'col'), pairs)  4.4 us
    pallas_call x1, Pallas kernels, shards(): call(own_kernel, [((256, 4 * LANES), BF), ((256, 4 * LANES), BF), ((64, 1...  3.27 us
    pallas_call x1, Pallas kernels, shards(): call(functools.partial(backward_kernel, core), [((3, 3, 3, 32, LANES), BF...  2.63 us
    pallas_call x1, Pallas kernels, shards(): call(volume_kernel, [((16, QD, 16, 128), BF)], [pltpu.VMEM((256, 4 * LANE...  2.04 us
  transfers between devices with their start and end apart: 11, of which 6 were waited for; matrix products, arithmetic and copies ran while one was open for 0% of the time, Pallas kernels for 9%

profile of v3, /device:TPU:1, one launch (start us, length us, event | category | flops | bytes accessed | tf_op | source)
XLA Modules:
  0.0 94.8 jit_solution(7000007023657798091)
XLA Ops:
  0.6 4.4 %collective-permute-start.1 = (bf16[16,8,16,128]{3,2,1,0:T(8,128)(2,1)}, bf16[16,8,16,128]{3,2,1,0:T(8,128)(2,1)S(1)}, u32[]{:S(2)}, u32[]{:S(2)}) collective-permute-start(bf16[16,8,16,128]{3,2,1,0:T(8,128)(2,1)} %bitcast.41), channel_id=1, source_target_pairs={{0,224},{32,0},{64,32},{96,64},{128,96},{160,128},{192,160},{224,1... | collective-permute-start | bytes 1572872 | tf_op jit(solution)/shard_map/ppermute | solution.py:403
  5.0 0.0 collective-permute-start
  5.0 0.6 tables.1
  5.7 3.3 %own.1 = (bf16[256,1536]{1,0:T(8,128)(2,1)S(1)}, bf16[256,1536]{1,0:T(8,128)(2,1)S(1)}, bf16[64,1024]{1,0:T(8,128)(2,1)S(1)}, bf16[256,128]{1,0:T(8,128)(2,1)S(1)}, bf16[256,128]{1,0:T(8,128)(2,1)S(1)}) custom-call(bf16[16,8,16,128]{3,2,1,0:T(8,128)(2,1)} %bitcast.43, bf16[16,8,16,128]{3,2,1,0:T(8,128)(2,1)} %bitcast.40, ...), custom_call_target="tpu_custom_call" | custom-call | bytes 4000000 | tf_op jit(solution)/shard_map/own/pallas_call | solution.py:444
  8.9 3.5 %collective-permute-start.3 = (bf16[256,128]{1,0:T(8,128)(2,1)S(1)}, bf16[256,128]{1,0:T(8,128)(2,1)S(1)}, u32[]{:S(2)}, u32[]{:S(2)}) collective-permute-start(bf16[256,128]{1,0:T(8,128)(2,1)S(1)} %get-tuple-element.44), channel_id=1, source_target_pairs={{0,1},{1,2},{2,3},{3,4},{4,5},{5,6},{6,7},{7,8},{8,9},{9,10},{10,1... | collective-permute-start | bytes 196616 | tf_op jit(solution)/shard_map/ppermute | solution.py:403
  12.5 0.0 collective-permute-start.4
  12.5 0.0 collective-permute-start.2
  12.5 11.0 %collective-permute-done.3.left_ref = bf16[256,128]{1,0:T(8,128)(2,1)S(1)} collective-permute-done((bf16[256,128]{1,0:T(8,128)(2,1)S(1)}, bf16[256,128]{1,0:T(8,128)(2,1)S(1)}, u32[]{:S(2)}, u32[]{:S(2)}) %collective-permute-start.3) | collective-permute-done | bytes 65568 | tf_op jit(solution)/shard_map/ppermute | solution.py:403
  23.5 3.4 %collective-permute-done.4.right_ref = bf16[256,128]{1,0:T(8,128)(2,1)S(1)} collective-permute-done((bf16[256,128]{1,0:T(8,128)(2,1)S(1)}, bf16[256,128]{1,0:T(8,128)(2,1)S(1)}, u32[]{:S(2)}, u32[]{:S(2)}) %collective-permute-start.4) | collective-permute-done | bytes 65568 | tf_op jit(solution)/shard_map/ppermute | solution.py:403
  26.9 0.1 collective-permute-start.6
  26.9 1.5 %collective-permute-start.5 = (bf16[256,256]{1,0:T(8,128)(2,1)S(1)}, bf16[256,256]{1,0:T(8,128)(2,1)S(1)}, u32[]{:S(2)}, u32[]{:S(2)}) collective-permute-start(bf16[256,256]{1,0:T(8,128)(2,1)S(1)} %rim.1.own_rim_ref), channel_id=1, source_target_pairs={{0,32},{32,64},{64,96},{96,128},{128,160},{160,192},{192,224},{224... | collective-permute-start | bytes 393224 | tf_op jit(solution)/shard_map/ppermute | solution.py:403
  28.4 1.6 %prepare.1 = (bf16[32,432]{1,0:T(8,128)(2,1)S(1)}, bf16[64,864]{1,0:T(8,128)(2,1)S(1)}, bf16[64,864]{1,0:T(8,128)(2,1)S(1)}, bf16[32,432]{1,0:T(8,128)(2,1)S(1)}...) custom-call(bf16[27,16,32]{2,1,0:T(8,128)(2,1)} %bitcast.46, ...), custom_call_target="tpu_custom_call" | custom-call | bytes 4000000 | tf_op jit(solution)/shard_map/prepare/pallas_call | solution.py:456
  30.0 0.0 collective-permute-done.2.cot_lo_ref
  30.0 0.7 collective-permute-done.6.hi_rim_ref
  30.8 2.4 %collective-permute-done.5.lo_rim_ref = bf16[256,256]{1,0:T(8,128)(2,1)S(1)} collective-permute-done((bf16[256,256]{1,0:T(8,128)(2,1)S(1)}, bf16[256,256]{1,0:T(8,128)(2,1)S(1)}, u32[]{:S(2)}, u32[]{:S(2)}) %collective-permute-start.5) | collective-permute-done | bytes 131104 | tf_op jit(solution)/shard_map/ppermute | solution.py:403
  33.1 0.0 collective-permute-done.1.xhi_ref
  33.1 0.0 collective-permute-done.xlo_ref
  33.1 5.6 %forward.1 = (bf16[5,11,5,16,384]{4,3,2,1,0:T(8,128)(2,1)S(1)}, bf16[5,5,5,16,384]{4,3,2,1,0:T(8,128)(2,1)S(1)}, bf16[3,5,3,32,384]{4,3,2,1,0:T(8,128)(2,1)S(1)}...) custom-call(bf16[16,8,16,128]{3,2,1,0:T(8,128)(2,1)S(1)} %collective, ...), custom_call_target="tpu_custom_call" | custom-call | bytes 4000000 | tf_op jit(solution)/shard_map/forward/pallas_call | solution.py:463
  38.7 0.1 collective-permute-start.8
  38.8 1.5 %collective-permute-start.7 = (bf16[2,2,32,384]{3,2,1,0:T(8,128)(2,1)S(1)}, bf16[2,2,32,384]{3,2,1,0:T(8,128)(2,1)S(1)}, u32[]{:S(2)}, u32[]{:S(2)}) collective-permute-start(bf16[2,2,32,384]{3,2,1,0:T(8,128)(2,1)S(1)} %get-tuple-element.53), channel_id=1, source_target_pairs={{0,32},{32,64},{64,96},{96,128},{128,160},{160,192},{192,224},{224... | collective-permute-start | bytes 294920 | tf_op jit(solution)/shard_map/ppermute | solution.py:403
  40.3 1.1 %full_grad.1.g4_ref = f32[112,128]{1,0:T(8,128)S(1)} custom-call(bf16[5,5,5,16,384]{4,3,2,1,0:T(8,128)(2,1)S(1)} %get-tuple-element.59.cwin_ref, bf16[8,32,384]{2,1,0:T(8,128)(2,1)S(1)} %get-tuple-element.60.m_ref), custom_call_target="tpu_custom_call" | custom-call | flops 679477248 | bytes 4000000 | tf_op jit(solution)/shard_map/full_grad/pallas_call | solution.py:479
  41.4 3.1 %collective-permute-done.7.gmlo_ref = bf16[2,2,32,384]{3,2,1,0:T(8,128)(2,1)S(1)} collective-permute-done((bf16[2,2,32,384]{3,2,1,0:T(8,128)(2,1)S(1)}, bf16[2,2,32,384]{3,2,1,0:T(8,128)(2,1)S(1)}, u32[]{:S(2)}, u32[]{:S(2)}) %collective-permute-start.7) | collective-permute-done | bytes 98336 | tf_op jit(solution)/shard_map/ppermute | solution.py:403
  44.5 0.0 collective-permute-done.8.gmhi_ref
  44.5 2.6 %backward.1 = (bf16[3,3,3,32,384]{4,3,2,1,0:T(8,128)(2,1)S(1)}, f32[1536,128]{1,0:T(8,128)S(1)}, bf16[768,128]{1,0:T(8,128)(2,1)S(1)}) custom-call(bf16[2,2,2,32,384]{4,3,2,1,0:T(8,128)(2,1)S(1)} %get-tuple-element.52.gm_ref, bf16[2,2,32,384]{3,2,1,0:T(8,128)(2,1)S(1)} %collective-permute-done.7.gmlo_ref, ...), custom_call_target="tpu_custom_call" | custom-call | bytes 4000000 | tf_op jit(solution)/shard_map/backward/pallas_call | solution.py:481
  47.1 0.1 collective-permute-start.9
  47.2 1.4 %collective-permute-done.9.got_ref = bf16[768,128]{1,0:T(8,128)(2,1)S(1)} collective-permute-done((bf16[768,128]{1,0:T(8,128)(2,1)S(1)}, bf16[768,128]{1,0:T(8,128)(2,1)S(1)}, u32[]{:S(2)}, u32[]{:S(2)}) %collective-permute-start.9) | collective-permute-done | bytes 196640 | tf_op jit(solution)/shard_map/ppermute | solution.py:398
  48.7 12.4 %all_to_all.15 = bf16[16,48,128]{2,1,0:T(8,128)(2,1)S(1)} all-to-all(bf16[16,48,128]{2,1,0:T(8,128)(2,1)S(1)} %bitcast.33), channel_id=1, replica_groups={{0,2,32,34,64,66,96,98,128,130,160,162,192,194,224,226},{1,3,33,35,65,6..., dimensions={0} | all-to-all | bytes 393216 | tf_op jit(solution)/shard_map/all_to_all | solution.py:414
  61.1 15.7 %all_to_all.16 = bf16[8,48,128]{2,1,0:T(8,128)(2,1)S(1)} all-to-all(bf16[8,48,128]{2,1,0:T(8,128)(2,1)S(1)} %bitcast.38), channel_id=1, replica_groups={{0,4,8,12,16,20,24,28},{1,5,9,13,17,21,25,29},{2,6,10,14,18,22,26,30},{..., dimensions={0} | all-to-all | bytes 196608 | tf_op jit(solution)/shard_map/all_to_all | solution.py:414
  76.8 10.4 %all_to_all.17 = bf16[16,48,128]{2,1,0:T(8,128)(2,1)S(1)} all-to-all(bf16[16,48,128]{2,1,0:T(8,128)(2,1)S(1)} %bitcast.37), channel_id=1, replica_groups={{0,2,32,34,64,66,96,98,128,130,160,162,192,194,224,226},{1,3,33,35,65,6..., dimensions={0} | all-to-all | bytes 393216 | tf_op jit(solution)/shard_map/all_to_all | solution.py:414
  87.1 4.3 %collective-permute-start.10 = (bf16[768,128]{1,0:T(8,128)(2,1)S(1)}, bf16[768,128]{1,0:T(8,128)(2,1)S(1)}, u32[]{:S(2)}, u32[]{:S(2)}) collective-permute-start(bf16[768,128]{1,0:T(8,128)(2,1)S(1)} %bitcast.34), channel_id=1, source_target_pairs={{0,1},{1,0},{2,3},{3,2},{4,5},{5,4},{6,7},{7,6},{8,9},{9,8},{10,11... | collective-permute-start | bytes 589832 | tf_op jit(solution)/shard_map/ppermute | solution.py:398
  91.4 2.0 %volume.1 = bf16[16,8,16,128]{3,2,1,0:T(8,128)(2,1)} custom-call(bf16[3,3,3,32,384]{4,3,2,1,0:T(8,128)(2,1)S(1)} %get-tuple-element.63.ewin_ref, bf16[5,5,5,16,384]{4,3,2,1,0:T(8,128)(2,1)S(1)} %get-tuple-element.59.cwin_ref, bf16[128,256]{1,0:T(8,128)(2,1)S(1)} %get-tuple-element.64.up1_ref, bf16[1024,1024]{1,0:T(8,128)(2,1)S(1)} %get-tuple-element.38.spread_ref, ...), custom_call_target="tpu_custom_call" | custom-call | flops 2097152000 | bytes 4000000 | tf_op jit(solution)/shard_map/volume/pallas_call | solution.py:495
  93.5 1.3 %finish.1 = (f32[27,16,32]{2,1,0:T(8,128)}, f32[27,32,64]{2,1,0:T(8,128)}, f32[27,32,64]{2,1,0:T(8,128)}, f32[27,16,32]{2,1,0:T(8,128)}) custom-call(bf16[768,128]{1,0:T(8,128)(2,1)S(1)} %bitcast.35, bf16[768,128]{1,0:T(8,128)(2,1)S(1)} %collective-permute-done.10.got_ref), custom_call_target="tpu_custom_call" | custom-call | bytes 4000000 | tf_op jit(solution)/shard_map/finish/pallas_call | solution.py:498
  (5 shorter events, 0.1 us)
Async XLA Ops:
  0.6 32.5 %collective-permute-start.1 = (bf16[16,8,16,128]{3,2,1,0:T(8,128)(2,1)}, bf16[16,8,16,128]{3,2,1,0:T(8,128)(2,1)S(1)}, u32[]{:S(2)}, u32[]{:S(2)}) collective-permute-start(bf16[16,8,16,128]{3,2,1,0:T(8,128)(2,1)} %bitcast.41), channel_id=1, source_target_pairs={{0,224},{32,0},{64,32},{96,64},{128,96},{160,128},{192,160},{224,1... | collective-permute-start | bytes 1572872 | tf_op jit(solution)/shard_map/ppermute | solution.py:403
  5.0 28.1 %collective-permute-start = (bf16[16,8,16,128]{3,2,1,0:T(8,128)(2,1)}, bf16[16,8,16,128]{3,2,1,0:T(8,128)(2,1)S(1)}, u32[]{:S(2)}, u32[]{:S(2)}) collective-permute-start(bf16[16,8,16,128]{3,2,1,0:T(8,128)(2,1)} %bitcast.42), channel_id=1, source_target_pairs={{0,32},{32,64},{64,96},{96,128},{128,160},{160,192},{192,224},{224... | collective-permute-start | bytes 1572872 | tf_op jit(solution)/shard_map/ppermute | solution.py:403
  8.9 14.5 %collective-permute-start.3 = (bf16[256,128]{1,0:T(8,128)(2,1)S(1)}, bf16[256,128]{1,0:T(8,128)(2,1)S(1)}, u32[]{:S(2)}, u32[]{:S(2)}) collective-permute-start(bf16[256,128]{1,0:T(8,128)(2,1)S(1)} %get-tuple-element.44), channel_id=1, source_target_pairs={{0,1},{1,2},{2,3},{3,4},{4,5},{5,6},{6,7},{7,8},{8,9},{9,10},{10,1... | collective-permute-start | bytes 196616 | tf_op jit(solution)/shard_map/ppermute | solution.py:403
  12.5 14.4 %collective-permute-start.4 = (bf16[256,128]{1,0:T(8,128)(2,1)S(1)}, bf16[256,128]{1,0:T(8,128)(2,1)S(1)}, u32[]{:S(2)}, u32[]{:S(2)}) collective-permute-start(bf16[256,128]{1,0:T(8,128)(2,1)S(1)} %get-tuple-element.45), channel_id=1, source_target_pairs={{0,31},{1,0},{2,1},{3,2},{4,3},{5,4},{6,5},{7,6},{8,7},{9,8},{10,9... | collective-permute-start | bytes 196616 | tf_op jit(solution)/shard_map/ppermute | solution.py:403
  12.5 17.5 %collective-permute-start.2 = (bf16[64,1024]{1,0:T(8,128)(2,1)S(1)}, bf16[64,1024]{1,0:T(8,128)(2,1)S(1)}, u32[]{:S(2)}, u32[]{:S(2)}) collective-permute-start(bf16[64,1024]{1,0:T(8,128)(2,1)S(1)} %get-tuple-element.43), channel_id=1, source_target_pairs={{0,32},{32,64},{64,96},{96,128},{128,160},{160,192},{192,224},{224... | collective-permute-start | bytes 393224 | tf_op jit(solution)/shard_map/ppermute | solution.py:403
  26.9 3.9 %collective-permute-start.6 = (bf16[256,256]{1,0:T(8,128)(2,1)S(1)}, bf16[256,256]{1,0:T(8,128)(2,1)S(1)}, u32[]{:S(2)}, u32[]{:S(2)}) collective-permute-start(bf16[256,256]{1,0:T(8,128)(2,1)S(1)} %rim.1.own_rim_ref), channel_id=1, source_target_pairs={{0,224},{32,0},{64,32},{96,64},{128,96},{160,128},{192,160},{224,1... | collective-permute-start | bytes 393224 | tf_op jit(solution)/shard_map/ppermute | solution.py:403
  26.9 6.2 %collective-permute-start.5 = (bf16[256,256]{1,0:T(8,128)(2,1)S(1)}, bf16[256,256]{1,0:T(8,128)(2,1)S(1)}, u32[]{:S(2)}, u32[]{:S(2)}) collective-permute-start(bf16[256,256]{1,0:T(8,128)(2,1)S(1)} %rim.1.own_rim_ref), channel_id=1, source_target_pairs={{0,32},{32,64},{64,96},{96,128},{128,160},{160,192},{192,224},{224... | collective-permute-start | bytes 393224 | tf_op jit(solution)/shard_map/ppermute | solution.py:403
  38.7 5.7 %collective-permute-start.8 = (bf16[2,2,2,32,384]{4,3,2,1,0:T(8,128)(2,1)S(1)}, bf16[2,2,2,32,384]{4,3,2,1,0:T(8,128)(2,1)S(1)}, u32[]{:S(2)}, u32[]{:S(2)}) collective-permute-start(bf16[2,2,2,32,384]{4,3,2,1,0:T(8,128)(2,1)S(1)} %get-tuple-element.52.gm_ref), channel_id=1, source_target_pairs={{0,224},{32,0},{64,32},{96,64},{128,96},{160,128},{192,160},{224,1... | collective-permute-start | bytes 589832 | tf_op jit(solution)/shard_map/ppermute | solution.py:403
  38.8 5.7 %collective-permute-start.7 = (bf16[2,2,32,384]{3,2,1,0:T(8,128)(2,1)S(1)}, bf16[2,2,32,384]{3,2,1,0:T(8,128)(2,1)S(1)}, u32[]{:S(2)}, u32[]{:S(2)}) collective-permute-start(bf16[2,2,32,384]{3,2,1,0:T(8,128)(2,1)S(1)} %get-tuple-element.53), channel_id=1, source_target_pairs={{0,32},{32,64},{64,96},{96,128},{128,160},{160,192},{192,224},{224... | collective-permute-start | bytes 294920 | tf_op jit(solution)/shard_map/ppermute | solution.py:403
  47.1 1.5 %collective-permute-start.9 = (bf16[768,128]{1,0:T(8,128)(2,1)S(1)}, bf16[768,128]{1,0:T(8,128)(2,1)S(1)}, u32[]{:S(2)}, u32[]{:S(2)}) collective-permute-start(bf16[768,128]{1,0:T(8,128)(2,1)S(1)} %get-tuple-element.66), channel_id=1, source_target_pairs={{0,1},{1,0},{2,3},{3,2},{4,5},{5,4},{6,7},{7,6},{8,9},{9,8},{10,11... | collective-permute-start | bytes 589832 | tf_op jit(solution)/shard_map/ppermute | solution.py:398
  87.1 6.4 %collective-permute-start.10 = (bf16[768,128]{1,0:T(8,128)(2,1)S(1)}, bf16[768,128]{1,0:T(8,128)(2,1)S(1)}, u32[]{:S(2)}, u32[]{:S(2)}) collective-permute-start(bf16[768,128]{1,0:T(8,128)(2,1)S(1)} %bitcast.34), channel_id=1, source_target_pairs={{0,1},{1,0},{2,3},{3,2},{4,5},{5,4},{6,7},{7,6},{8,9},{9,8},{10,11... | collective-permute-start | bytes 589832 | tf_op jit(solution)/shard_map/ppermute | solution.py:398

commit v4 on v3

--- a/solution.py
+++ b/solution.py
@@ -93,13 +93,15 @@
     return copies
 
 
-def own_kernel(vol_ref, cot_ref, spread_ref, order_ref, rims_ref, yv_ref, yc_ref, cot_last_ref, first_ref, last_ref, vol_here, cot_here, sems):
+def own_kernel(vol_ref, cot_ref, spread_ref, order_ref, rims_ref, yv_ref, yc_ref, main_ref, first_ref, last_ref, vol_here, cot_here, sems):
     copies = fetch(((vol_ref, vol_here), (cot_ref, cot_here)), sems)
     copies[0].wait()
-    yv_ref[...] = to_lanes(by_rows(vol_here, order_ref), spread_ref).astype(BF)
+    rows = by_rows(vol_here, order_ref)
+    main_ref[0:64] = rows[192:256]
+    yv_ref[...] = to_lanes(rows, spread_ref).astype(BF)
     copies[1].wait()
     rows = by_rows(cot_here, order_ref)
-    cot_last_ref[...] = rows[192:256]
+    main_ref[64:128] = rows[192:256]
     yc_ref[...] = to_lanes(rows, spread_ref).astype(BF)
     edges = [dot(ref[...], rims_ref[...]) for ref in (yv_ref, yc_ref)]
     first_ref[...] = jnp.concatenate([edge[:, :64] for edge in edges], axis=1).astype(BF)
@@ -110,9 +112,10 @@
     return jnp.where(condition, 1.0, 0.0).astype(F32)
 
 
-def rim_kernel(left_ref, right_ref, out_ref):
+def rim_kernel(left_ref, right_ref, out_ref, corner_ref):
     out_ref[:, :128] = (left_ref[...].astype(F32) * flag(lax.axis_index("col") > 0)).astype(BF)
     out_ref[:, 128:] = right_ref[...]
+    corner_ref[...] = out_ref[192:256]
 
 
 UP_TAP = {(0, 0): 1, (1, 0): 0, (1, 1): 2}
@@ -207,27 +210,44 @@
     return jnp.concatenate(parts, axis=0)
 
 
-def forward_kernel(xlo_ref, xhi_ref, yv_ref, yc_ref, cot_lo_ref, own_rim_ref, lo_rim_ref, hi_rim_ref, mask_ref, spread_ref, place_ref, order_ref, w1_ref, w2_ref, up3_ref, w4_ref, all_ref, cwin_ref, hwin_ref, preh_ref, preq_ref, q_ref, m_ref, gm_ref, gm_last_ref):
+def half_kernel(main_ref, yv_ref, own_rim_ref, lo_rim_ref, mask_ref, spread_ref, place_ref, w1_ref, vwin_ref, preh_ref, h_ref, h_last_ref):
+    seen = mask_ref[0:1]
+    to_vol = place_ref[0]
+    y = to_lanes(main_ref[0:64], spread_ref) + dot(lo_rim_ref[...], to_vol)
+    fill_full(vwin_ref, y * flag(lax.axis_index("row") > 0), 0, 1)
+    fill_full(vwin_ref, yv_ref[...].astype(F32) + dot(own_rim_ref[...], to_vol), 1, 4)
+    w1 = w1_ref[...]
+    for pr, pd, pc in PAIRS:
+        col = vwin_ref[2 * pd : 2 * pd + 3, 2 * pr : 2 * pr + 3, 2 * pc : 2 * pc + 3].reshape(432, LANES)
+        pre = dot(w1, col)
+        preh_ref[pr, pd, pc] = pre
+        h_ref[pr, pd, pc] = (pre * sigmoid(pre) * seen).astype(BF)
+        if pr == 1:
+            h_last_ref[pd, pc] = h_ref[pr, pd, pc]
+
+
+def cotangent_kernel(main_ref, yc_ref, own_rim_ref, lo_rim_ref, spread_ref, place_ref, w4_ref, cwin_ref, pull_ref):
+    to_cot = place_ref[1]
+    y = to_lanes(main_ref[64:128], spread_ref) + dot(lo_rim_ref[...], to_cot)
+    fill_full(cwin_ref, y * flag(lax.axis_index("row") > 0), 0, 1)
+    fill_full(cwin_ref, yc_ref[...].astype(F32) + dot(own_rim_ref[...], to_cot), 1, 4)
+    w4 = w4_ref[...]
+    for p, (pr, pd, pc) in enumerate(PAIRS):
+        col = cwin_ref[2 * pd : 2 * pd + 3, 2 * pr : 2 * pr + 3, 2 * pc : 2 * pc + 3].reshape(432, LANES)
+        pull_ref[p] = dot(w4, col)
+
+
+def middle_kernel(h_ref, hlo_ref, hhi_ref, pull_ref, mask_ref, w2_ref, up3_ref, hwin_ref, preq_ref, q_ref, m_ref, gm_ref, gm_last_ref):
     seen = mask_ref[0:1]
     seen_next = mask_ref[1:2]
     own = mask_ref[2:3]
     inner = flag(lax.axis_index("row") > 0)
-    to_vol, to_cot = place_ref[0], place_ref[1]
-    y = to_lanes(by_rows(xlo_ref, order_ref)[64:256], spread_ref) + dot(lo_rim_ref[64:256], to_vol)
-    fill_full(all_ref, y * inner, 0, 3)
-    fill_full(all_ref, yv_ref[...].astype(F32) + dot(own_rim_ref[...], to_vol), 3, 4)
-    y = to_lanes(by_rows(xhi_ref, order_ref), spread_ref) + dot(hi_rim_ref[...], to_vol)
-    fill_full(all_ref, y, 7, 4)
-    w1 = w1_ref[...]
-    for hr in range(5):
-        for pd in range(2):
-            for pc in range(2):
-                col = all_ref[2 * pd : 2 * pd + 3, 2 * hr : 2 * hr + 3, 2 * pc : 2 * pc + 3].reshape(432, LANES)
-                pre = dot(w1, col)
-                if 1 <= hr <= 3:
-                    preh_ref[hr - 1, pd, pc] = pre
-                h = rounded(pre * sigmoid(pre)) * (seen if hr < 3 else seen_next)
-                put_half(hwin_ref, hr, pd, pc, h)
+    for pd in range(2):
+        for pc in range(2):
+            put_half(hwin_ref, 0, pd, pc, hlo_ref[pd, pc].astype(F32) * inner)
+            for pr in range(2):
+                put_half(hwin_ref, 1 + pr, pd, pc, h_ref[pr, pd, pc].astype(F32))
+                put_half(hwin_ref, 3 + pr, pd, pc, hhi_ref[pr, pd, pc].astype(F32) * seen_next)
     quarters = []
     for qr in range(2):
         col = hwin_ref[:, 2 * qr : 2 * qr + 3].reshape(864, LANES)
@@ -236,16 +256,10 @@
         quarters.append(rounded(pre * sigmoid(pre)) * (seen_next if qr else seen))
     q_ref[...] = (quarters[0] * own).astype(BF)
     up = dot(up3_ref[...], neighbours(quarters[0], quarters[1]))
-    y = to_lanes(cot_lo_ref[...], spread_ref) + dot(lo_rim_ref[192:256], to_cot)
-    fill_full(cwin_ref, y * inner, 0, 1)
-    fill_full(cwin_ref, yc_ref[...].astype(F32) + dot(own_rim_ref[...], to_cot), 1, 4)
-    w4 = w4_ref[...]
     for p, (pr, pd, pc) in enumerate(PAIRS):
-        h = hwin_ref[1 + pd, 1 + pr, 1 + pc].astype(F32)
-        pre = up[p * 32 : p * 32 + 32] + h
+        pre = up[p * 32 : p * 32 + 32] + h_ref[pr, pd, pc].astype(F32)
         m_ref[p] = (rounded(pre * sigmoid(pre)) * own).astype(BF)
-        col = cwin_ref[2 * pd : 2 * pd + 3, 2 * pr : 2 * pr + 3, 2 * pc : 2 * pc + 3].reshape(432, LANES)
-        gm = rounded(dot(w4, col) * slope(pre)) * seen
+        gm = rounded(pull_ref[p] * slope(pre)) * seen
         gm_ref[pr, pd, pc] = gm.astype(BF)
         if pr == 1:
             gm_last_ref[pd, pc] = gm.astype(BF)
@@ -269,7 +283,18 @@
             out_ref[base + high - low : base + rows, group * width : (group + 1) * width] = jnp.zeros((rows - high + low, width), F32)
 
 
-def backward_kernel(stage, gm_ref, gmlo_ref, gmhi_ref, vwin_ref, hwin_ref, preh_ref, preq_ref, q_ref, g4_ref, mask_ref, w3_ref, up2_ref, ewin_ref, pack_ref, send_ref, mwin_ref):
+def put_upper(win_ref, pd, pc, value):
+    win_ref[pd, pc] = value.astype(BF)
+    if pc == 0:
+        right = roll_up(value, -1)
+        win_ref[pd, 2] = right.astype(BF)
+    if pd == 0:
+        win_ref[2, pc] = roll_up(value, -SPAN).astype(BF)
+        if pc == 0:
+            win_ref[2, 2] = roll_up(right, -SPAN).astype(BF)
+
+
+def backward_kernel(stage, gm_ref, gmlo_ref, gmhi_ref, vwin_ref, hwin_ref, preh_ref, preq_ref, q_ref, g4_ref, mask_ref, w3_ref, up2_ref, ewin_ref, gh_first_ref, pack_ref, send_ref, mwin_ref):
     seen = mask_ref[0:1]
     seen_next = mask_ref[1:2]
     own = mask_ref[2:3]
@@ -288,25 +313,17 @@
         if qr == 0:
             store_groups(pack_ref, dot_nt(col, q_ref[...]), 672, 448, 64)
     up = dot(up2_ref[...], neighbours(quarters[0], quarters[1]))
-    up_next = dot(up2_ref[0:128, 0:256], neighbours(quarters[1], quarters[1])[0:256])
     total = None
-    for p, (pr, pd, pc) in enumerate(PAIRS + [(2, 0, 0), (2, 0, 1), (2, 1, 0), (2, 1, 1)]):
-        conv = up[p * 32 : p * 32 + 32] if pr < 2 else up_next[(p - 8) * 32 : (p - 8) * 32 + 32]
+    for p, (pr, pd, pc) in enumerate(PAIRS):
+        conv = up[p * 32 : p * 32 + 32]
         gm = mwin_ref[1 + pd, 1 + pr, 1 + pc].astype(F32)
-        gh = rounded((conv + gm) * slope(preh_ref[pr, pd, pc])) * (seen if pr < 2 else seen_next)
-        ewin_ref[pd, pr, pc] = gh.astype(BF)
-        if pc == 0:
-            right = roll_up(gh, -1)
-            ewin_ref[pd, pr, 2] = right.astype(BF)
-        if pd == 0:
-            below = roll_up(gh, -SPAN)
-            ewin_ref[2, pr, pc] = below.astype(BF)
-            if pc == 0:
-                ewin_ref[2, pr, 2] = roll_up(right, -SPAN).astype(BF)
-        if pr < 2:
-            col = vwin_ref[2 * pd : 2 * pd + 3, 2 * pr + 2 : 2 * pr + 5, 2 * pc : 2 * pc + 3].reshape(432, LANES)
-            part = dot_nt(col, (gh * own).astype(BF))
-            total = part if total is None else total + part
+        gh = rounded((conv + gm) * slope(preh_ref[pr, pd, pc])) * seen
+        put_upper(ewin_ref.at[:, pr], pd, pc, gh)
+        if pr == 0:
+            gh_first_ref[pd, pc] = gh.astype(BF)
+        col = vwin_ref[2 * pd : 2 * pd + 3, 2 * pr : 2 * pr + 3, 2 * pc : 2 * pc + 3].reshape(432, LANES)
+        part = dot_nt(col, (gh * own).astype(BF))
+        total = part if total is None else total + part
     store_groups(pack_ref, total, 0, 112, 32)
     pack_ref[112:224] = g4_ref[...]
     col = hwin_ref[:, 0:3].reshape(864, LANES)
@@ -315,11 +332,19 @@
     send_ref[...] = half(pack_ref, stage, False)[...].astype(BF)
 
 
-def volume_kernel(ewin_ref, cwin_ref, up1_ref, spread_ref, order_ref, out_ref, z_ref):
+def volume_kernel(ewin_ref, next_ref, cwin_ref, up1_ref, spread_ref, order_ref, out_ref, z_ref, ext_ref):
+    below = flag(lax.axis_index("row") < lax.axis_size("row") - 1)
+    for pd in range(2):
+        for pc in range(2):
+            put_upper(ext_ref, pd, pc, next_ref[pd, pc].astype(F32) * below)
     up1 = up1_ref[...]
     for pr, pd, pc in PAIRS:
         near = jnp.concatenate(
-            [ewin_ref[pd + nd, pr + nr, pc + nc] for nr, nd, nc in PAIRS], axis=0
+            [
+                ewin_ref[pd + nd, pr + nr, pc + nc] if pr + nr < 2 else ext_ref[pd + nd, pc + nc]
+                for nr, nd, nc in PAIRS
+            ],
+            axis=0,
         )
         up = dot(up1, near)
         for f, (fr, fd, fc) in enumerate(PAIRS):
@@ -440,18 +465,17 @@
     )()
     vol = volume.reshape(16, QD, 16, 128)
     cot = cotangent.reshape(16, QD, 16, 128)
-    vol_lo, vol_hi = shifted(vol, "row", 1), shifted(vol, "row", -1)
-    yv, yc, cot_last, first, last = call(
+    yv, yc, main, first, last = call(
         own_kernel,
-        [((256, 4 * LANES), BF), ((256, 4 * LANES), BF), ((64, 1024), BF), ((256, 128), BF), ((256, 128), BF)],
+        [((256, 4 * LANES), BF), ((256, 4 * LANES), BF), ((128, 1024), BF), ((256, 128), BF), ((256, 128), BF)],
         [pltpu.VMEM(vol.shape, BF), pltpu.VMEM(cot.shape, BF), pltpu.SemaphoreType.DMA((2,))],
         far=(2, 3),
         name="own",
     )(held(vol), held(cot), spread, order, rims)
     left, right = shifted(last, "col", 1), shifted(first, "col", -1)
-    cot_lo = shifted(cot_last, "row", 1)
-    (own_rim,) = call(rim_kernel, [((256, 256), BF)], name="rim")(left, right)
-    lo_rim, hi_rim = shifted(own_rim, "row", 1), shifted(own_rim, "row", -1)
+    main_lo = shifted(main, "row", 1)
+    own_rim, corner = call(rim_kernel, [((256, 256), BF), ((64, 256), BF)], name="rim")(left, right)
+    lo_rim = shifted(corner, "row", 1)
     weights = by_tap(w_half, True), by_tap(w_quarter, True), by_tap(w_back_half, False), by_tap(w_back_full, False)
     w1, w2, w3, w4, up1, up2, up3, mask = call(
         prepare_kernel,
@@ -460,27 +484,27 @@
         far=(4, 0),
         name="prepare",
     )(*[held(weight) for weight in weights])
-    vwin, cwin, hwin, preh, preq, quarter, mixed, gm, gm_last = call(
-        forward_kernel,
-        [
-            ((5, 11, 5, 16, LANES), BF),
-            ((5, 5, 5, 16, LANES), BF),
-            ((3, 5, 3, 32, LANES), BF),
-            ((3, 2, 2, 32, LANES), F32),
-            ((2, 64, LANES), F32),
-            ((64, LANES), BF),
-            ((8, 32, LANES), BF),
-            ((2, 2, 2, 32, LANES), BF),
-            ((2, 2, 32, LANES), BF),
-        ],
-        name="forward",
-    )(vol_lo, vol_hi, yv, yc, cot_lo, own_rim, lo_rim, hi_rim, mask, spread, place, order, w1, w2, up3, w4)
+    full_window, half_rows = (5, 5, 5, 16, LANES), (2, 2, 2, 32, LANES)
+    vwin, preh, half_act, half_last = call(
+        half_kernel,
+        [(full_window, BF), (half_rows, F32), (half_rows, BF), (half_rows[1:], BF)],
+        name="half",
+    )(main_lo, yv, own_rim, lo_rim, mask, spread, place, w1)
+    half_lo, half_hi = shifted(half_last, "row", 1), shifted(half_act, "row", -1)
+    cwin, pull = call(
+        cotangent_kernel, [(full_window, BF), ((8, 32, LANES), F32)], flops=2 * 432 * 32 * LANES * 64, name="cotangent"
+    )(main_lo, yc, own_rim, lo_rim, spread, place, w4)
+    hwin, preq, quarter, mixed, gm, gm_last = call(
+        middle_kernel,
+        [((3, 5, 3, 32, LANES), BF), ((2, 64, LANES), F32), ((64, LANES), BF), ((8, 32, LANES), BF), (half_rows, BF), (half_rows[1:], BF)],
+        name="middle",
+    )(half_act, half_lo, half_hi, pull, mask, w2, up3)
     gm_lo, gm_hi = shifted(gm_last, "row", 1), shifted(gm, "row", -1)
     (g4,) = call(full_grad_kernel, [((112, 128), F32)], flops=2 * 432 * 32 * LANES * 64, name="full_grad")(cwin, mixed)
     core = ("col", 1)
-    ewin, kept, send = call(
+    ewin, gh_first, kept, send = call(
         functools.partial(backward_kernel, core),
-        [((3, 3, 3, 32, LANES), BF), ((PACK, 128), F32), ((PACK // 2, 128), BF)],
+        [((3, 2, 3, 32, LANES), BF), (half_rows[1:], BF), ((PACK, 128), F32), ((PACK // 2, 128), BF)],
         [pltpu.VMEM((3, 5, 3, 32, LANES), BF)],
         name="backward",
     )(gm, gm_lo, gm_hi, vwin, hwin, preh, preq, quarter, g4, mask, w3, up2)
@@ -493,8 +517,8 @@
         (part,) = call(functools.partial(sum_kernel, size, later), [((later * share, 128), BF)], name="sum")(part)
     part = exchanged(part.reshape(sizes[0], share, 128), *along[0]).reshape(PACK // 2, 128)
     (grad_volume,) = call(
-        volume_kernel, [((16, QD, 16, 128), BF)], [pltpu.VMEM((256, 4 * LANES), BF)], flops=2 * 256 * 1024 * 4000, name="volume"
-    )(ewin, cwin, up1, spread, order)
+        volume_kernel, [((16, QD, 16, 128), BF)], [pltpu.VMEM((256, 4 * LANES), BF), pltpu.VMEM((3, 3, 32, LANES), BF)], flops=2 * 256 * 1024 * 4000, name="volume"
+    )(ewin, shifted(gh_first, "row", -1), cwin, up1, spread, order)
     g1, g2, g3, g4 = call(
         functools.partial(finish_kernel, scale, core),
         [((27, 16, 32), F32), ((27, 32, 64), F32), ((27, 32, 64), F32), ((27, 16, 32), F32)],

time: 95 us -> 92.8 us (0.977)
  blocking collectives: 38.4 us -> 25 us
  starting transfers between devices: 15.4 us -> 22.1 us
  waiting for transfers between devices: 22 us -> 25.7 us
  local copies, waits for them, and re-layouts: 0 us -> 1.4 us
    all_to_all x3 -> x2, blocking collectives: 38.4 us -> 25 us  [exchanged(): lax.all_to_all(value, ('row', 'col'), 0, 0, axis_index_groups=list(groups...]
    all_to_all x0 -> x1, waiting for transfers between devices: none -> 3.81 us  [exchanged(): lax.all_to_all(value, ('row', 'col'), 0, 0, axis_index_groups=list(groups...]
    all_to_all x0 -> x1, starting transfers between devices: none -> 3.52 us  [exchanged(): lax.all_to_all(value, ('row', 'col'), 0, 0, axis_index_groups=list(groups...]
    ppermute x2, starting transfers between devices: 4.4 us -> 6.08 us  [swapped(): return lax.ppermute(value, ('row', 'col'), pairs)]
    ppermute x9, starting transfers between devices: 11 us -> 12.5 us  [shifted(): lax.ppermute(value, axis, [(i, (i + steps) % count) for i in range(count)])]
    pallas_call x4 -> x6, Pallas kernels: 11.5 us -> 10.1 us  [the longest x1 3.27 us: shards(): call(own_kernel, [((256, 4 * LANES), BF), ((256, 4 * LANES), BF), ((128,...]
    unnamed x0 -> x4, local copies, waits for them, and re-layouts: none -> 1.4 us
  transfers between devices with their start and end apart: 11 -> 12, of which waited for: 6 -> 7; matrix products, arithmetic and copies ran while one was open for 0% -> 0% of each run, Pallas kernels for 9% -> 7%
where the time goes in v4:
time: 92.8 us; the launch traced here: 92.5 us
  waiting for transfers between devices  25.7 us (28%)
  blocking collectives  25 us (27%)
  starting transfers between devices  22.1 us (24%)
  Pallas kernels  17.5 us (19%)
  local copies, waits for them, and re-layouts  1.4 us (2%)
    all_to_all x2, blocking collectives, exchanged(): lax.all_to_all(value, ('row', 'col'), 0, 0, axis_index_groups=list(groups...  25 us
    ppermute x9, waiting for transfers between devices, shifted(): lax.ppermute(value, axis, [(i, (i + steps) % count) for i in range(count)])  20.8 us
    ppermute x9, starting transfers between devices, shifted(): lax.ppermute(value, axis, [(i, (i + steps) % count) for i in range(count)])  12.5 us
    ppermute x2, starting transfers between devices, swapped(): return lax.ppermute(value, ('row', 'col'), pairs)  6.08 us
    all_to_all x1, waiting for transfers between devices, exchanged(): lax.all_to_all(value, ('row', 'col'), 0, 0, axis_index_groups=list(groups...  3.81 us
    all_to_all x1, starting transfers between devices, exchanged(): lax.all_to_all(value, ('row', 'col'), 0, 0, axis_index_groups=list(groups...  3.52 us
    pallas_call x1, Pallas kernels, shards(): call(own_kernel, [((256, 4 * LANES), BF), ((256, 4 * LANES), BF), ((128,...  3.27 us
    pallas_call x1, Pallas kernels, shards(): call(functools.partial(backward_kernel, core), [((3, 2, 3, 32, LANES), BF...  2.53 us
  transfers between devices with their start and end apart: 12, of which 7 were waited for; matrix products, arithmetic and copies ran while one was open for 0% of the time, Pallas kernels for 7%

profile of v4, /device:TPU:1, one launch (start us, length us, event | category | flops | bytes accessed | tf_op | source)
XLA Modules:
  0.0 92.5 jit_solution(334826037071013633)
XLA Ops:
  0.6 0.6 tables.1
  1.3 3.3 %own.1 = (bf16[256,1536]{1,0:T(8,128)(2,1)S(1)}, bf16[256,1536]{1,0:T(8,128)(2,1)S(1)}, bf16[128,1024]{1,0:T(8,128)(2,1)S(1)}, bf16[256,128]{1,0:T(8,128)(2,1)S(1)}, bf16[256,128]{1,0:T(8,128)(2,1)S(1)}) custom-call(bf16[16,8,16,128]{3,2,1,0:T(8,128)(2,1)} %bitcast.39, bf16[16,8,16,128]{3,2,1,0:T(8,128)(2,1)} %bitcast.40, ...), custom_call_target="tpu_custom_call" | custom-call | bytes 4000000 | tf_op jit(solution)/shard_map/own/pallas_call | solution.py:468
  4.5 2.1 %collective-permute-start = (bf16[128,1024]{1,0:T(8,128)(2,1)S(1)}, bf16[128,1024]{1,0:T(8,128)(2,1)S(1)}, u32[]{:S(2)}, u32[]{:S(2)}) collective-permute-start(bf16[128,1024]{1,0:T(8,128)(2,1)S(1)} %get-tuple-element.47), channel_id=1, source_target_pairs={{0,32},{32,64},{64,96},{96,128},{128,160},{160,192},{192,224},{224... | collective-permute-start | bytes 786440 | tf_op jit(solution)/shard_map/ppermute | solution.py:428
  6.7 3.8 %collective-permute-start.1 = (bf16[256,128]{1,0:T(8,128)(2,1)S(1)}, bf16[256,128]{1,0:T(8,128)(2,1)S(1)}, u32[]{:S(2)}, u32[]{:S(2)}) collective-permute-start(bf16[256,128]{1,0:T(8,128)(2,1)S(1)} %get-tuple-element.49), channel_id=1, source_target_pairs={{0,1},{1,2},{2,3},{3,4},{4,5},{5,6},{6,7},{7,8},{8,9},{9,10},{10,1... | collective-permute-start | bytes 196616 | tf_op jit(solution)/shard_map/ppermute | solution.py:428
  10.4 6.0 %collective-permute-done.1.left_ref = bf16[256,128]{1,0:T(8,128)(2,1)S(1)} collective-permute-done((bf16[256,128]{1,0:T(8,128)(2,1)S(1)}, bf16[256,128]{1,0:T(8,128)(2,1)S(1)}, u32[]{:S(2)}, u32[]{:S(2)}) %collective-permute-start.1) | collective-permute-done | bytes 65568 | tf_op jit(solution)/shard_map/ppermute | solution.py:428
  16.4 3.1 %collective-permute-done.2.right_ref = bf16[256,128]{1,0:T(8,128)(2,1)S(1)} collective-permute-done((bf16[256,128]{1,0:T(8,128)(2,1)S(1)}, bf16[256,128]{1,0:T(8,128)(2,1)S(1)}, u32[]{:S(2)}, u32[]{:S(2)}) %collective-permute-start.2) | collective-permute-done | bytes 65568 | tf_op jit(solution)/shard_map/ppermute | solution.py:428
  19.5 0.1 collective-permute-start.3
  19.6 1.6 %prepare.1 = (bf16[32,432]{1,0:T(8,128)(2,1)S(1)}, bf16[64,864]{1,0:T(8,128)(2,1)S(1)}, bf16[64,864]{1,0:T(8,128)(2,1)S(1)}, bf16[32,432]{1,0:T(8,128)(2,1)S(1)}...) custom-call(bf16[27,16,32]{2,1,0:T(8,128)(2,1)} %bitcast.43, ...), custom_call_target="tpu_custom_call" | custom-call | bytes 4000000 | tf_op jit(solution)/shard_map/prepare/pallas_call | solution.py:480
  21.2 3.2 %collective-permute-done.3.lo_rim_ref = bf16[64,256]{1,0:T(8,128)(2,1)S(1)} collective-permute-done((bf16[64,256]{1,0:T(8,128)(2,1)S(1)}, bf16[64,256]{1,0:T(8,128)(2,1)S(1)}, u32[]{:S(2)}, u32[]{:S(2)}) %collective-permute-start.3) | collective-permute-done | bytes 32800 | tf_op jit(solution)/shard_map/ppermute | solution.py:428
  24.4 1.6 %half.1 = (bf16[5,5,5,16,384]{4,3,2,1,0:T(8,128)(2,1)S(1)}, f32[2,2,2,32,384]{4,3,2,1,0:T(8,128)S(1)}, bf16[2,2,2,32,384]{4,3,2,1,0:T(8,128)(2,1)S(1)}, bf16[2,2,32,384]{3,2,1,0:T(8,128)(2,1)S(1)}) custom-call(bf16[128,1024]{1,0:T(8,128)(2,1)S(1)} %collective-permute-done.main_ref, bf16[256,1536]{1,0:T(8,128)(2,1)S(1)} %get-tuple-element.48.yv_ref, ...), custom_call_target="tpu_custom_call" | custom-call | bytes 4000000 | tf_op jit(solution)/shard_map/half/pallas_call | solution.py:488
  26.0 0.4 collective-permute-start.5
  26.4 1.1 %collective-permute-start.4 = (bf16[2,2,32,384]{3,2,1,0:T(8,128)(2,1)S(1)}, bf16[2,2,32,384]{3,2,1,0:T(8,128)(2,1)S(1)}, u32[]{:S(2)}, u32[]{:S(2)}) collective-permute-start(bf16[2,2,32,384]{3,2,1,0:T(8,128)(2,1)S(1)} %get-tuple-element.57), channel_id=1, source_target_pairs={{0,32},{32,64},{64,96},{96,128},{128,160},{160,192},{192,224},{224... | collective-permute-start | bytes 294920 | tf_op jit(solution)/shard_map/ppermute | solution.py:428
  27.5 1.5 %cotangent.1 = (bf16[5,5,5,16,384]{4,3,2,1,0:T(8,128)(2,1)S(1)}, f32[8,32,384]{2,1,0:T(8,128)S(1)}) custom-call(bf16[128,1024]{1,0:T(8,128)(2,1)S(1)} %collective-permute-done.main_ref, bf16[256,1536]{1,0:T(8,128)(2,1)S(1)} %get-tuple-element.58.yc_ref, bf16[256,256]{1,0:T(8,128)(2,1)S(1)} %get-tuple-element.51.own_rim_ref, ...), custom_call_target="tpu_custom_call" | custom-call | flops 679477248 | bytes 4000000 | tf_op jit(solution)/shard_map/cotangent/pallas_call | solution.py:494
  29.1 4.1 %collective-permute-done.4.hlo_ref = bf16[2,2,32,384]{3,2,1,0:T(8,128)(2,1)S(1)} collective-permute-done((bf16[2,2,32,384]{3,2,1,0:T(8,128)(2,1)S(1)}, bf16[2,2,32,384]{3,2,1,0:T(8,128)(2,1)S(1)}, u32[]{:S(2)}, u32[]{:S(2)}) %collective-permute-start.4) | collective-permute-done | bytes 98336 | tf_op jit(solution)/shard_map/ppermute | solution.py:428
  33.2 1.2 %middle.1 = (bf16[3,5,3,32,384]{4,3,2,1,0:T(8,128)(2,1)S(1)}, f32[2,64,384]{2,1,0:T(8,128)S(1)}, bf16[64,384]{1,0:T(8,128)(2,1)S(1)}, bf16[8,32,384]{2,1,0:T(8,1...) custom-call(bf16[2,2,2,32,384]{4,3,2,1,0:T(8,128)(2,1)S(1)} %get-tuple-element.56.h_ref, ...), custom_call_target="tpu_custom_call" | custom-call | bytes 4000000 | tf_op jit(solution)/shard_map/middle/pallas_call | solution.py:497
  34.4 1.6 %collective-permute-start.7 = (bf16[2,2,2,32,384]{4,3,2,1,0:T(8,128)(2,1)S(1)}, bf16[2,2,2,32,384]{4,3,2,1,0:T(8,128)(2,1)S(1)}, u32[]{:S(2)}, u32[]{:S(2)}) collective-permute-start(bf16[2,2,2,32,384]{4,3,2,1,0:T(8,128)(2,1)S(1)} %get-tuple-element.63.gm_ref), channel_id=1, source_target_pairs={{0,224},{32,0},{64,32},{96,64},{128,96},{160,128},{192,160},{224,1... | collective-permute-start | bytes 589832 | tf_op jit(solution)/shard_map/ppermute | solution.py:428
  35.9 0.0 collective-permute-start.6
  35.9 1.1 %full_grad.1.g4_ref = f32[112,128]{1,0:T(8,128)S(1)} custom-call(bf16[5,5,5,16,384]{4,3,2,1,0:T(8,128)(2,1)S(1)} %get-tuple-element.70.cwin_ref, bf16[8,32,384]{2,1,0:T(8,128)(2,1)S(1)} %get-tuple-element.71.m_ref), custom_call_target="tpu_custom_call" | custom-call | flops 679477248 | bytes 4000000 | tf_op jit(solution)/shard_map/full_grad/pallas_call | solution.py:503
  37.1 4.5 %collective-permute-done.6.gmlo_ref = bf16[2,2,32,384]{3,2,1,0:T(8,128)(2,1)S(1)} collective-permute-done((bf16[2,2,32,384]{3,2,1,0:T(8,128)(2,1)S(1)}, bf16[2,2,32,384]{3,2,1,0:T(8,128)(2,1)S(1)}, u32[]{:S(2)}, u32[]{:S(2)}) %collective-permute-start.6) | collective-permute-done | bytes 98336 | tf_op jit(solution)/shard_map/ppermute | solution.py:428
  41.5 2.5 %backward.1 = (bf16[3,2,3,32,384]{4,3,2,1,0:T(8,128)(2,1)S(1)}, bf16[2,2,32,384]{3,2,1,0:T(8,128)(2,1)S(1)}, f32[1536,128]{1,0:T(8,128)S(1)}, bf16[768,128]{1,0:T(8,128)(2,1)S(1)}) custom-call(bf16[2,2,2,32,384]{4,3,2,1,0:T(8,128)(2,1)S(1)} %get-tuple-element.63.gm_ref, bf16[2,2,32,384]{3,2,1,0:T(8,128)(2,1)S(1)} %collective-permute-done.6.gmlo_ref, ...), custom_call_target="tpu_custom_call" | custom-call | bytes 4000000 | tf_op jit(solution)/shard_map/backward/pallas_call | solution.py:505
  44.1 1.8 %collective-permute-start.9 = (bf16[768,128]{1,0:T(8,128)(2,1)S(1)}, bf16[768,128]{1,0:T(8,128)(2,1)S(1)}, u32[]{:S(2)}, u32[]{:S(2)}) collective-permute-start(bf16[768,128]{1,0:T(8,128)(2,1)S(1)} %get-tuple-element.78), channel_id=1, source_target_pairs={{0,1},{1,0},{2,3},{3,2},{4,5},{5,4},{6,7},{7,6},{8,9},{9,8},{10,11... | collective-permute-start | bytes 589832 | tf_op jit(solution)/shard_map/ppermute | solution.py:423
  45.9 1.1 %collective-permute-done.9.got_ref = bf16[768,128]{1,0:T(8,128)(2,1)S(1)} collective-permute-done((bf16[768,128]{1,0:T(8,128)(2,1)S(1)}, bf16[768,128]{1,0:T(8,128)(2,1)S(1)}, u32[]{:S(2)}, u32[]{:S(2)}) %collective-permute-start.9) | collective-permute-done | bytes 196640 | tf_op jit(solution)/shard_map/ppermute | solution.py:423
  47.0 10.6 %all_to_all.15 = bf16[16,48,128]{2,1,0:T(8,128)(2,1)S(1)} all-to-all(bf16[16,48,128]{2,1,0:T(8,128)(2,1)S(1)} %bitcast.33), channel_id=1, replica_groups={{0,2,32,34,64,66,96,98,128,130,160,162,192,194,224,226},{1,3,33,35,65,6..., dimensions={0} | all-to-all | bytes 393216 | tf_op jit(solution)/shard_map/all_to_all | solution.py:439
  57.7 14.4 %all_to_all.16 = bf16[8,48,128]{2,1,0:T(8,128)(2,1)S(1)} all-to-all(bf16[8,48,128]{2,1,0:T(8,128)(2,1)S(1)} %bitcast.37), channel_id=1, replica_groups={{0,4,8,12,16,20,24,28},{1,5,9,13,17,21,25,29},{2,6,10,14,18,22,26,30},{..., dimensions={0} | all-to-all | bytes 196608 | tf_op jit(solution)/shard_map/all_to_all | solution.py:439
  72.1 0.7 sum.3
  72.8 3.5 %all-to-all-start.2 = ((bf16[16,48,128]{2,1,0:T(8,128)(2,1)}), bf16[16,48,128]{2,1,0:T(8,128)(2,1)S(1)}, u32[]{:S(2)}, u32[]{:S(2)}) async-start(bf16[16,48,128]{2,1,0:T(8,128)(2,1)} %bitcast.15), calls=%async_computation.2 | async-start | bytes 393216 | tf_op jit(solution)/shard_map/all_to_all | solution.py:439
  76.3 3.4 %collective-permute-start.8 = (bf16[2,2,32,384]{3,2,1,0:T(8,128)(2,1)S(1)}, bf16[2,2,32,384]{3,2,1,0:T(8,128)(2,1)S(1)}, u32[]{:S(2)}, u32[]{:S(2)}) collective-permute-start(bf16[2,2,32,384]{3,2,1,0:T(8,128)(2,1)S(1)} %get-tuple-element.75), channel_id=1, source_target_pairs={{0,224},{32,0},{64,32},{96,64},{128,96},{160,128},{192,160},{224,1... | collective-permute-start | bytes 294920 | tf_op jit(solution)/shard_map/ppermute | solution.py:428
  79.7 3.8 %all-to-all-done.2 = bf16[16,48,128]{2,1,0:T(8,128)(2,1)S(1)} async-done(((bf16[16,48,128]{2,1,0:T(8,128)(2,1)}), bf16[16,48,128]{2,1,0:T(8,128)(2,1)S(1)}, u32[]{:S(2)}, u32[]{:S(2)}) %all-to-all-start.2) | async-done | bytes 196640 | tf_op jit(solution)/shard_map/all_to_all | solution.py:439
  83.6 4.2 %collective-permute-start.10 = (bf16[768,128]{1,0:T(8,128)(2,1)S(1)}, bf16[768,128]{1,0:T(8,128)(2,1)S(1)}, u32[]{:S(2)}, u32[]{:S(2)}) collective-permute-start(bf16[768,128]{1,0:T(8,128)(2,1)S(1)} %bitcast.34), channel_id=1, source_target_pairs={{0,1},{1,0},{2,3},{3,2},{4,5},{5,4},{6,7},{7,6},{8,9},{9,8},{10,11... | collective-permute-start | bytes 589832 | tf_op jit(solution)/shard_map/ppermute | solution.py:423
  87.8 1.4 %copy-done.1 = bf16[5,5,5,16,384]{4,3,2,1,0:T(8,128)(2,1)S(1)} copy-done((bf16[5,5,5,16,384]{4,3,2,1,0:T(8,128)(2,1)S(1)}, bf16[5,5,5,16,384]{4,3,2,1,0:T(8,128)(2,1)}, u32[]{:S(2)}) %copy-start.1) | copy-done | bytes 1536024
  89.2 2.0 %volume.1 = bf16[16,8,16,128]{3,2,1,0:T(8,128)(2,1)} custom-call(bf16[3,2,3,32,384]{4,3,2,1,0:T(8,128)(2,1)S(1)} %get-tuple-element.74.ewin_ref, bf16[2,2,32,384]{3,2,1,0:T(8,128)(2,1)S(1)} %collective-permute-done.8.next_ref, bf16[5,5,5,16,384]{4,3,2,1,0:T(8,128)(2,1)S(1)} %copy-done.1, bf16[128,256]{1,0:T(8,128)(2,1)S(1)} %get-tuple-element.76.up1_ref, ...), custom_call_target="tpu_custom_call" | custom-call | flops 2097152000 | bytes 4000000 | tf_op jit(solution)/shard_map/volume/pallas_call | solution.py:519
  91.2 1.3 %finish.1 = (f32[27,16,32]{2,1,0:T(8,128)}, f32[27,32,64]{2,1,0:T(8,128)}, f32[27,32,64]{2,1,0:T(8,128)}, f32[27,16,32]{2,1,0:T(8,128)}) custom-call(bf16[768,128]{1,0:T(8,128)(2,1)S(1)} %bitcast.35, bf16[768,128]{1,0:T(8,128)(2,1)S(1)} %collective-permute-done.10.got_ref), custom_call_target="tpu_custom_call" | custom-call | bytes 4000000 | tf_op jit(solution)/shard_map/finish/pallas_call | solution.py:522
  (12 shorter events, 0.1 us)
Async XLA Ops:
  4.5 19.9 %collective-permute-start = (bf16[128,1024]{1,0:T(8,128)(2,1)S(1)}, bf16[128,1024]{1,0:T(8,128)(2,1)S(1)}, u32[]{:S(2)}, u32[]{:S(2)}) collective-permute-start(bf16[128,1024]{1,0:T(8,128)(2,1)S(1)} %get-tuple-element.47), channel_id=1, source_target_pairs={{0,32},{32,64},{64,96},{96,128},{128,160},{160,192},{192,224},{224... | collective-permute-start | bytes 786440 | tf_op jit(solution)/shard_map/ppermute | solution.py:428
  6.7 9.7 %collective-permute-start.1 = (bf16[256,128]{1,0:T(8,128)(2,1)S(1)}, bf16[256,128]{1,0:T(8,128)(2,1)S(1)}, u32[]{:S(2)}, u32[]{:S(2)}) collective-permute-start(bf16[256,128]{1,0:T(8,128)(2,1)S(1)} %get-tuple-element.49), channel_id=1, source_target_pairs={{0,1},{1,2},{2,3},{3,4},{4,5},{5,6},{6,7},{7,8},{8,9},{9,10},{10,1... | collective-permute-start | bytes 196616 | tf_op jit(solution)/shard_map/ppermute | solution.py:428
  10.4 9.0 %collective-permute-start.2 = (bf16[256,128]{1,0:T(8,128)(2,1)S(1)}, bf16[256,128]{1,0:T(8,128)(2,1)S(1)}, u32[]{:S(2)}, u32[]{:S(2)}) collective-permute-start(bf16[256,128]{1,0:T(8,128)(2,1)S(1)} %get-tuple-element.50), channel_id=1, source_target_pairs={{0,31},{1,0},{2,1},{3,2},{4,3},{5,4},{6,5},{7,6},{8,7},{9,8},{10,9... | collective-permute-start | bytes 196616 | tf_op jit(solution)/shard_map/ppermute | solution.py:428
  19.5 5.0 %collective-permute-start.3 = (bf16[64,256]{1,0:T(8,128)(2,1)S(1)}, bf16[64,256]{1,0:T(8,128)(2,1)S(1)}, u32[]{:S(2)}, u32[]{:S(2)}) collective-permute-start(bf16[64,256]{1,0:T(8,128)(2,1)S(1)} %get-tuple-element.52), channel_id=1, source_target_pairs={{0,32},{32,64},{64,96},{96,128},{128,160},{160,192},{192,224},{224... | collective-permute-start | bytes 98312 | tf_op jit(solution)/shard_map/ppermute | solution.py:428
  26.0 7.2 %collective-permute-start.5 = (bf16[2,2,2,32,384]{4,3,2,1,0:T(8,128)(2,1)S(1)}, bf16[2,2,2,32,384]{4,3,2,1,0:T(8,128)(2,1)S(1)}, u32[]{:S(2)}, u32[]{:S(2)}) collective-permute-start(bf16[2,2,2,32,384]{4,3,2,1,0:T(8,128)(2,1)S(1)} %get-tuple-element.56.h_ref), channel_id=1, source_target_pairs={{0,224},{32,0},{64,32},{96,64},{128,96},{160,128},{192,160},{224,1... | collective-permute-start | bytes 589832 | tf_op jit(solution)/shard_map/ppermute | solution.py:428
  26.4 6.8 %collective-permute-start.4 = (bf16[2,2,32,384]{3,2,1,0:T(8,128)(2,1)S(1)}, bf16[2,2,32,384]{3,2,1,0:T(8,128)(2,1)S(1)}, u32[]{:S(2)}, u32[]{:S(2)}) collective-permute-start(bf16[2,2,32,384]{3,2,1,0:T(8,128)(2,1)S(1)} %get-tuple-element.57), channel_id=1, source_target_pairs={{0,32},{32,64},{64,96},{96,128},{128,160},{160,192},{192,224},{224... | collective-permute-start | bytes 294920 | tf_op jit(solution)/shard_map/ppermute | solution.py:428
  29.1 8.0 %copy-start = (bf16[5,5,5,16,384]{4,3,2,1,0:T(8,128)(2,1)}, bf16[5,5,5,16,384]{4,3,2,1,0:T(8,128)(2,1)S(1)}, u32[]{:S(2)}) copy-start(bf16[5,5,5,16,384]{4,3,2,1,0:T(8,128)(2,1)S(1)} %get-tuple-element.70.cwin_ref) | copy-start | bytes 4608004
  34.4 7.2 %collective-permute-start.7 = (bf16[2,2,2,32,384]{4,3,2,1,0:T(8,128)(2,1)S(1)}, bf16[2,2,2,32,384]{4,3,2,1,0:T(8,128)(2,1)S(1)}, u32[]{:S(2)}, u32[]{:S(2)}) collective-permute-start(bf16[2,2,2,32,384]{4,3,2,1,0:T(8,128)(2,1)S(1)} %get-tuple-element.63.gm_ref), channel_id=1, source_target_pairs={{0,224},{32,0},{64,32},{96,64},{128,96},{160,128},{192,160},{224,1... | collective-permute-start | bytes 589832 | tf_op jit(solution)/shard_map/ppermute | solution.py:428
  35.9 5.6 %collective-permute-start.6 = (bf16[2,2,32,384]{3,2,1,0:T(8,128)(2,1)S(1)}, bf16[2,2,32,384]{3,2,1,0:T(8,128)(2,1)S(1)}, u32[]{:S(2)}, u32[]{:S(2)}) collective-permute-start(bf16[2,2,32,384]{3,2,1,0:T(8,128)(2,1)S(1)} %get-tuple-element.64), channel_id=1, source_target_pairs={{0,32},{32,64},{64,96},{96,128},{128,160},{160,192},{192,224},{224... | collective-permute-start | bytes 294920 | tf_op jit(solution)/shard_map/ppermute | solution.py:428
  44.1 2.9 %collective-permute-start.9 = (bf16[768,128]{1,0:T(8,128)(2,1)S(1)}, bf16[768,128]{1,0:T(8,128)(2,1)S(1)}, u32[]{:S(2)}, u32[]{:S(2)}) collective-permute-start(bf16[768,128]{1,0:T(8,128)(2,1)S(1)} %get-tuple-element.78), channel_id=1, source_target_pairs={{0,1},{1,0},{2,3},{3,2},{4,5},{5,4},{6,7},{7,6},{8,9},{9,8},{10,11... | collective-permute-start | bytes 589832 | tf_op jit(solution)/shard_map/ppermute | solution.py:423
  72.8 10.8 %all-to-all-start.2 = ((bf16[16,48,128]{2,1,0:T(8,128)(2,1)}), bf16[16,48,128]{2,1,0:T(8,128)(2,1)S(1)}, u32[]{:S(2)}, u32[]{:S(2)}) async-start(bf16[16,48,128]{2,1,0:T(8,128)(2,1)} %bitcast.15), calls=%async_computation.2 | async-start | bytes 393216 | tf_op jit(solution)/shard_map/all_to_all | solution.py:439
  76.3 11.5 %collective-permute-start.8 = (bf16[2,2,32,384]{3,2,1,0:T(8,128)(2,1)S(1)}, bf16[2,2,32,384]{3,2,1,0:T(8,128)(2,1)S(1)}, u32[]{:S(2)}, u32[]{:S(2)}) collective-permute-start(bf16[2,2,32,384]{3,2,1,0:T(8,128)(2,1)S(1)} %get-tuple-element.75), channel_id=1, source_target_pairs={{0,224},{32,0},{64,32},{96,64},{128,96},{160,128},{192,160},{224,1... | collective-permute-start | bytes 294920 | tf_op jit(solution)/shard_map/ppermute | solution.py:428
  83.6 7.7 %collective-permute-start.10 = (bf16[768,128]{1,0:T(8,128)(2,1)S(1)}, bf16[768,128]{1,0:T(8,128)(2,1)S(1)}, u32[]{:S(2)}, u32[]{:S(2)}) collective-permute-start(bf16[768,128]{1,0:T(8,128)(2,1)S(1)} %bitcast.34), channel_id=1, source_target_pairs={{0,1},{1,0},{2,3},{3,2},{4,5},{5,4},{6,7},{7,6},{8,9},{9,8},{10,11... | collective-permute-start | bytes 589832 | tf_op jit(solution)/shard_map/ppermute | solution.py:423
  87.8 1.4 %copy-start.1 = (bf16[5,5,5,16,384]{4,3,2,1,0:T(8,128)(2,1)S(1)}, bf16[5,5,5,16,384]{4,3,2,1,0:T(8,128)(2,1)}, u32[]{:S(2)}) copy-start(bf16[5,5,5,16,384]{4,3,2,1,0:T(8,128)(2,1)} %copy-done) | copy-start | bytes 4608004

commit v5 on v4

--- a/solution.py
+++ b/solution.py
@@ -37,11 +37,9 @@
         for d in range(QD):
             block = ones_where(apart == lane_of(d, 0) - (0 if d < 6 else 128))
             spread_ref[d * 128 : (d + 1) * 128, phase * 256 : (phase + 1) * 256] = block
-    slot, lane = iota((LANES, 128), 1), iota((LANES, 128), 0)
+    slot, row = iota((QD * 128, 128), 1), iota((QD * 128, 128), 0)
     column = (slot & 1) + jnp.where(slot >= 64, QC - 2, 0)
-    target = SPAN * ((slot >> 1) & 7) + HALO + column
-    for phase in range(4):
-        rims_ref[phase * LANES : (phase + 1) * LANES] = ones_where((lane == target) & (((slot >> 4) & 3) == phase))
+    rims_ref[...] = ones_where(row == ((slot >> 1) & 7) * 128 + 4 * column + ((slot >> 4) & 3))
     place_ref[...] = jnp.zeros(place_ref.shape, BF)
     slot, lane = iota((16, LANES), 0), iota((16, LANES), 1)
     for side in range(2):
@@ -93,29 +91,33 @@
     return copies
 
 
-def own_kernel(vol_ref, cot_ref, spread_ref, order_ref, rims_ref, yv_ref, yc_ref, main_ref, first_ref, last_ref, vol_here, cot_here, sems):
+def edge_kernel(vol_ref, cot_ref, order_ref, rims_ref, vol_rows_ref, cot_rows_ref, main_ref, first_ref, last_ref, first_low_ref, last_low_ref, vol_here, cot_here, sems):
     copies = fetch(((vol_ref, vol_here), (cot_ref, cot_here)), sems)
-    copies[0].wait()
-    rows = by_rows(vol_here, order_ref)
-    main_ref[0:64] = rows[192:256]
-    yv_ref[...] = to_lanes(rows, spread_ref).astype(BF)
-    copies[1].wait()
-    rows = by_rows(cot_here, order_ref)
-    main_ref[64:128] = rows[192:256]
-    yc_ref[...] = to_lanes(rows, spread_ref).astype(BF)
-    edges = [dot(ref[...], rims_ref[...]) for ref in (yv_ref, yc_ref)]
+    edges = []
+    for i, (here, rows_ref) in enumerate(((vol_here, vol_rows_ref), (cot_here, cot_rows_ref))):
+        copies[i].wait()
+        rows = by_rows(here, order_ref)
+        rows_ref[...] = rows
+        main_ref[i * 64 : i * 64 + 64] = rows[192:256]
+        edges.append(dot(rows, rims_ref[...]))
     first_ref[...] = jnp.concatenate([edge[:, :64] for edge in edges], axis=1).astype(BF)
     last_ref[...] = jnp.concatenate([edge[:, 64:] for edge in edges], axis=1).astype(BF)
+    first_low_ref[...] = first_ref[192:256]
+    last_low_ref[...] = last_ref[192:256]
+
+
+def own_kernel(vol_rows_ref, cot_rows_ref, spread_ref, yv_ref, yc_ref):
+    yv_ref[...] = to_lanes(vol_rows_ref[...], spread_ref).astype(BF)
+    yc_ref[...] = to_lanes(cot_rows_ref[...], spread_ref).astype(BF)
 
 
 def flag(condition):
     return jnp.where(condition, 1.0, 0.0).astype(F32)
 
 
-def rim_kernel(left_ref, right_ref, out_ref, corner_ref):
-    out_ref[:, :128] = (left_ref[...].astype(F32) * flag(lax.axis_index("col") > 0)).astype(BF)
-    out_ref[:, 128:] = right_ref[...]
-    corner_ref[...] = out_ref[192:256]
+def rims_of(left_ref, right_ref):
+    left = left_ref[...].astype(F32) * flag(lax.axis_index("col") > 0)
+    return jnp.concatenate([left.astype(BF), right_ref[...]], axis=1)
 
 
 UP_TAP = {(0, 0): 1, (1, 0): 0, (1, 1): 2}
@@ -210,12 +212,12 @@
     return jnp.concatenate(parts, axis=0)
 
 
-def half_kernel(main_ref, yv_ref, own_rim_ref, lo_rim_ref, mask_ref, spread_ref, place_ref, w1_ref, vwin_ref, preh_ref, h_ref, h_last_ref):
+def half_kernel(main_ref, yv_ref, left_ref, right_ref, low_left_ref, low_right_ref, mask_ref, spread_ref, place_ref, w1_ref, vwin_ref, preh_ref, h_ref, h_last_ref):
     seen = mask_ref[0:1]
     to_vol = place_ref[0]
-    y = to_lanes(main_ref[0:64], spread_ref) + dot(lo_rim_ref[...], to_vol)
+    y = to_lanes(main_ref[0:64], spread_ref) + dot(rims_of(low_left_ref, low_right_ref), to_vol)
     fill_full(vwin_ref, y * flag(lax.axis_index("row") > 0), 0, 1)
-    fill_full(vwin_ref, yv_ref[...].astype(F32) + dot(own_rim_ref[...], to_vol), 1, 4)
+    fill_full(vwin_ref, yv_ref[...].astype(F32) + dot(rims_of(left_ref, right_ref), to_vol), 1, 4)
     w1 = w1_ref[...]
     for pr, pd, pc in PAIRS:
         col = vwin_ref[2 * pd : 2 * pd + 3, 2 * pr : 2 * pr + 3, 2 * pc : 2 * pc + 3].reshape(432, LANES)
@@ -226,11 +228,11 @@
             h_last_ref[pd, pc] = h_ref[pr, pd, pc]
 
 
-def cotangent_kernel(main_ref, yc_ref, own_rim_ref, lo_rim_ref, spread_ref, place_ref, w4_ref, cwin_ref, pull_ref):
+def cotangent_kernel(main_ref, yc_ref, left_ref, right_ref, low_left_ref, low_right_ref, spread_ref, place_ref, w4_ref, cwin_ref, pull_ref):
     to_cot = place_ref[1]
-    y = to_lanes(main_ref[64:128], spread_ref) + dot(lo_rim_ref[...], to_cot)
+    y = to_lanes(main_ref[64:128], spread_ref) + dot(rims_of(low_left_ref, low_right_ref), to_cot)
     fill_full(cwin_ref, y * flag(lax.axis_index("row") > 0), 0, 1)
-    fill_full(cwin_ref, yc_ref[...].astype(F32) + dot(own_rim_ref[...], to_cot), 1, 4)
+    fill_full(cwin_ref, yc_ref[...].astype(F32) + dot(rims_of(left_ref, right_ref), to_cot), 1, 4)
     w4 = w4_ref[...]
     for p, (pr, pd, pc) in enumerate(PAIRS):
         col = cwin_ref[2 * pd : 2 * pd + 3, 2 * pr : 2 * pr + 3, 2 * pc : 2 * pc + 3].reshape(432, LANES)
@@ -428,6 +430,12 @@
     return lax.ppermute(value, axis, [(i, (i + steps) % count) for i in range(count)])
 
 
+def diagonal(value, row_step, col_step):
+    rows, cols = lax.axis_size("row"), lax.axis_size("col")
+    pairs = [(r * cols + c, (r + row_step) % rows * cols + (c + col_step) % cols) for r in range(rows) for c in range(cols)]
+    return lax.ppermute(value, ("row", "col"), pairs)
+
+
 def exchanged(value, row_bits, col_bits):
     rows, cols = lax.axis_size("row"), lax.axis_size("col")
     if not row_bits and not col_bits:
@@ -460,22 +468,21 @@
     scale = 1.0 / math.sqrt(cells)
     spread, rims, place, order = call(
         tables_kernel,
-        [((QD * 128, 1024), BF), ((4 * LANES, 128), BF), ((2, 256, 4 * LANES), BF), ((256, 256), BF)],
+        [((QD * 128, 1024), BF), ((QD * 128, 128), BF), ((2, 256, 4 * LANES), BF), ((256, 256), BF)],
         name="tables",
     )()
     vol = volume.reshape(16, QD, 16, 128)
     cot = cotangent.reshape(16, QD, 16, 128)
-    yv, yc, main, first, last = call(
-        own_kernel,
-        [((256, 4 * LANES), BF), ((256, 4 * LANES), BF), ((128, 1024), BF), ((256, 128), BF), ((256, 128), BF)],
+    vol_rows, cot_rows, main, first, last, first_low, last_low = call(
+        edge_kernel,
+        [((256, 1024), BF), ((256, 1024), BF), ((128, 1024), BF), ((256, 128), BF), ((256, 128), BF), ((64, 128), BF), ((64, 128), BF)],
         [pltpu.VMEM(vol.shape, BF), pltpu.VMEM(cot.shape, BF), pltpu.SemaphoreType.DMA((2,))],
-        far=(2, 3),
-        name="own",
-    )(held(vol), held(cot), spread, order, rims)
-    left, right = shifted(last, "col", 1), shifted(first, "col", -1)
+        far=(2, 2),
+        name="edge",
+    )(held(vol), held(cot), order, rims)
     main_lo = shifted(main, "row", 1)
-    own_rim, corner = call(rim_kernel, [((256, 256), BF), ((64, 256), BF)], name="rim")(left, right)
-    lo_rim = shifted(corner, "row", 1)
+    edges = [shifted(last, "col", 1), shifted(first, "col", -1), diagonal(last_low, 1, 1), diagonal(first_low, 1, -1)]
+    yv, yc = call(own_kernel, [((256, 4 * LANES), BF), ((256, 4 * LANES), BF)], flops=2 * 256 * 1024 * 4000, name="own")(vol_rows, cot_rows, spread)
     weights = by_tap(w_half, True), by_tap(w_quarter, True), by_tap(w_back_half, False), by_tap(w_back_full, False)
     w1, w2, w3, w4, up1, up2, up3, mask = call(
         prepare_kernel,
@@ -489,11 +496,11 @@
         half_kernel,
         [(full_window, BF), (half_rows, F32), (half_rows, BF), (half_rows[1:], BF)],
         name="half",
-    )(main_lo, yv, own_rim, lo_rim, mask, spread, place, w1)
+    )(main_lo, yv, *edges, mask, spread, place, w1)
     half_lo, half_hi = shifted(half_last, "row", 1), shifted(half_act, "row", -1)
     cwin, pull = call(
         cotangent_kernel, [(full_window, BF), ((8, 32, LANES), F32)], flops=2 * 432 * 32 * LANES * 64, name="cotangent"
-    )(main_lo, yc, own_rim, lo_rim, spread, place, w4)
+    )(main_lo, yc, *edges, spread, place, w4)
     hwin, preq, quarter, mixed, gm, gm_last = call(
         middle_kernel,
         [((3, 5, 3, 32, LANES), BF), ((2, 64, LANES), F32), ((64, LANES), BF), ((8, 32, LANES), BF), (half_rows, BF), (half_rows[1:], BF)],
@@ -509,6 +516,7 @@
         name="backward",
     )(gm, gm_lo, gm_hi, vwin, hwin, preh, preq, quarter, g4, mask, w3, up2)
     (part,) = call(functools.partial(fold_kernel, core), [((PACK // 2, 128), BF)], name="fold")(kept, swapped(send, 0, 1))
+    part, gh_next = lax.optimization_barrier((part, shifted(gh_first, "row", -1)))
     along = [(7 & (rows - 1), 2 & (cols - 1)), (0, 28 & (cols - 1))]
     sizes = [2 ** (r.bit_count() + c.bit_count()) for r, c in along]
     share = PACK // 2 // sizes[0]
@@ -518,7 +526,8 @@
     part = exchanged(part.reshape(sizes[0], share, 128), *along[0]).reshape(PACK // 2, 128)
     (grad_volume,) = call(
         volume_kernel, [((16, QD, 16, 128), BF)], [pltpu.VMEM((256, 4 * LANES), BF), pltpu.VMEM((3, 3, 32, LANES), BF)], flops=2 * 256 * 1024 * 4000, name="volume"
-    )(ewin, shifted(gh_first, "row", -1), cwin, up1, spread, order)
+    )(ewin, gh_next, cwin, up1, spread, order)
+    part, grad_volume = lax.optimization_barrier((part, grad_volume))
     g1, g2, g3, g4 = call(
         functools.partial(finish_kernel, scale, core),
         [((27, 16, 32), F32), ((27, 32, 64), F32), ((27, 32, 64), F32), ((27, 16, 32), F32)],

time: 92.8 us -> 95.6 us (1.030)
  starting transfers between devices: 22.1 us -> 30.2 us
  waiting for transfers between devices: 25.7 us -> 17.8 us
  blocking collectives: 25 us -> 27.6 us
    ppermute x9 -> x8, waiting for transfers between devices: 20.8 us -> 12.6 us  [shifted(): lax.ppermute(value, axis, [(i, (i + steps) % count) for i in range(count)])]
    ppermute x0 -> x2, starting transfers between devices: none -> 4.69 us  [diagonal(): return lax.ppermute(value, ('row', 'col'), pairs)]
    ppermute x2, starting transfers between devices: 6.08 us -> 10.7 us  [swapped(): return lax.ppermute(value, ('row', 'col'), pairs)]
    all_to_all x2, blocking collectives: 25 us -> 27.6 us  [exchanged(): lax.all_to_all(value, ('row', 'col'), 0, 0, axis_index_groups=list(groups...]
    ppermute x9 -> x8, starting transfers between devices: 12.5 us -> 11.3 us  [shifted(): lax.ppermute(value, axis, [(i, (i + steps) % count) for i in range(count)])]
  transfers between devices with their start and end apart: 12 -> 13, of which waited for: 7 -> 7; matrix products, arithmetic and copies ran while one was open for 0% -> 0% of each run, Pallas kernels for 7% -> 8%
where the time goes in v5:
time: 95.6 us; the launch traced here: 95.2 us
  starting transfers between devices  30.2 us (32%)
  blocking collectives  27.6 us (29%)
  waiting for transfers between devices  17.8 us (19%)
  Pallas kernels  17.5 us (18%)
  local copies, waits for them, and re-layouts  1.39 us (1%)
    all_to_all x2, blocking collectives, exchanged(): lax.all_to_all(value, ('row', 'col'), 0, 0, axis_index_groups=list(groups...  27.6 us
    ppermute x8, waiting for transfers between devices, shifted(): lax.ppermute(value, axis, [(i, (i + steps) % count) for i in range(count)])  12.6 us
    ppermute x8, starting transfers between devices, shifted(): lax.ppermute(value, axis, [(i, (i + steps) % count) for i in range(count)])  11.3 us
    ppermute x2, starting transfers between devices, swapped(): return lax.ppermute(value, ('row', 'col'), pairs)  10.7 us
    ppermute x2, starting transfers between devices, diagonal(): return lax.ppermute(value, ('row', 'col'), pairs)  4.69 us
    all_to_all x1, waiting for transfers between devices, exchanged(): lax.all_to_all(value, ('row', 'col'), 0, 0, axis_index_groups=list(groups...  3.85 us
    all_to_all x1, starting transfers between devices, exchanged(): lax.all_to_all(value, ('row', 'col'), 0, 0, axis_index_groups=list(groups...  3.52 us
    pallas_call x1, Pallas kernels, shards(): call(functools.partial(backward_kernel, core), [((3, 2, 3, 32, LANES), BF...  2.53 us
  transfers between devices with their start and end apart: 13, of which 7 were waited for; matrix products, arithmetic and copies ran while one was open for 0% of the time, Pallas kernels for 8%

profile of v5, /device:TPU:1, one launch (start us, length us, event | category | flops | bytes accessed | tf_op | source)
XLA Modules:
  0.0 95.2 jit_solution(4560596187161979050)
XLA Ops:
  0.6 0.6 tables.1
  1.2 2.0 %edge.1 = (bf16[256,1024]{1,0:T(8,128)(2,1)S(1)}, bf16[256,1024]{1,0:T(8,128)(2,1)S(1)}, bf16[128,1024]{1,0:T(8,128)(2,1)S(1)}, bf16[256,128]{1,0:T(8,128)(2,1)S...) custom-call(bf16[16,8,16,128]{3,2,1,0:T(8,128)(2,1)} %bitcast.39, ...), custom_call_target="tpu_custom_call" | custom-call | bytes 4000000 | tf_op jit(solution)/shard_map/edge/pallas_call | solution.py:476
  3.3 2.1 %collective-permute-start = (bf16[128,1024]{1,0:T(8,128)(2,1)S(1)}, bf16[128,1024]{1,0:T(8,128)(2,1)S(1)}, u32[]{:S(2)}, u32[]{:S(2)}) collective-permute-start(bf16[128,1024]{1,0:T(8,128)(2,1)S(1)} %get-tuple-element.52), channel_id=1, source_target_pairs={{0,32},{32,64},{64,96},{96,128},{128,160},{160,192},{192,224},{224... | collective-permute-start | bytes 786440 | tf_op jit(solution)/shard_map/ppermute | solution.py:430
  5.4 4.7 %collective-permute-start.3 = (bf16[64,128]{1,0:T(8,128)(2,1)S(1)}, bf16[64,128]{1,0:T(8,128)(2,1)S(1)}, u32[]{:S(2)}, u32[]{:S(2)}) collective-permute-start(bf16[64,128]{1,0:T(8,128)(2,1)S(1)} %get-tuple-element.59), channel_id=1, source_target_pairs={{0,33},{1,34},{2,35},{3,36},{4,37},{5,38},{6,39},{7,40},{8,41},{9,... | collective-permute-start | bytes 49160 | tf_op jit(solution)/shard_map/ppermute | solution.py:436
  10.1 3.9 %collective-permute-start.1 = (bf16[256,128]{1,0:T(8,128)(2,1)S(1)}, bf16[256,128]{1,0:T(8,128)(2,1)S(1)}, u32[]{:S(2)}, u32[]{:S(2)}) collective-permute-start(bf16[256,128]{1,0:T(8,128)(2,1)S(1)} %get-tuple-element.57), channel_id=1, source_target_pairs={{0,1},{1,2},{2,3},{3,4},{4,5},{5,6},{6,7},{7,8},{8,9},{9,10},{10,1... | collective-permute-start | bytes 196616 | tf_op jit(solution)/shard_map/ppermute | solution.py:430
  14.0 1.0 %collective-permute-start.2 = (bf16[256,128]{1,0:T(8,128)(2,1)S(1)}, bf16[256,128]{1,0:T(8,128)(2,1)S(1)}, u32[]{:S(2)}, u32[]{:S(2)}) collective-permute-start(bf16[256,128]{1,0:T(8,128)(2,1)S(1)} %get-tuple-element.58), channel_id=1, source_target_pairs={{0,31},{1,0},{2,1},{3,2},{4,3},{5,4},{6,5},{7,6},{8,7},{9,8},{10,9... | collective-permute-start | bytes 196616 | tf_op jit(solution)/shard_map/ppermute | solution.py:430
  14.9 1.3 %own.1 = (bf16[256,1536]{1,0:T(8,128)(2,1)S(1)}, bf16[256,1536]{1,0:T(8,128)(2,1)S(1)}) custom-call(bf16[256,1024]{1,0:T(8,128)(2,1)S(1)} %get-tuple-element.53.vol_rows_ref, bf16[256,1024]{1,0:T(8,128)(2,1)S(1)} %get-tuple-element.54.cot_rows_ref, bf16[1024,1024]{1,0:T(8,128)(2,1)S(1)} %get-tuple-element.55.spread_ref), custom_call_target="tpu_custom_call" | custom-call | flops 2097152000 | bytes 4000000 | tf_op jit(solution)/shard_map/own/pallas_call | solution.py:485
  16.2 1.6 %prepare.1 = (bf16[32,432]{1,0:T(8,128)(2,1)S(1)}, bf16[64,864]{1,0:T(8,128)(2,1)S(1)}, bf16[64,864]{1,0:T(8,128)(2,1)S(1)}, bf16[32,432]{1,0:T(8,128)(2,1)S(1)}...) custom-call(bf16[27,16,32]{2,1,0:T(8,128)(2,1)} %bitcast.43, ...), custom_call_target="tpu_custom_call" | custom-call | bytes 4000000 | tf_op jit(solution)/shard_map/prepare/pallas_call | solution.py:487
  17.9 1.3 %collective-permute-done.2.right_ref = bf16[256,128]{1,0:T(8,128)(2,1)S(1)} collective-permute-done((bf16[256,128]{1,0:T(8,128)(2,1)S(1)}, bf16[256,128]{1,0:T(8,128)(2,1)S(1)}, u32[]{:S(2)}, u32[]{:S(2)}) %collective-permute-start.2) | collective-permute-done | bytes 65568 | tf_op jit(solution)/shard_map/ppermute | solution.py:430
  19.2 1.6 %half.1 = (bf16[5,5,5,16,384]{4,3,2,1,0:T(8,128)(2,1)S(1)}, f32[2,2,2,32,384]{4,3,2,1,0:T(8,128)S(1)}, bf16[2,2,2,32,384]{4,3,2,1,0:T(8,128)(2,1)S(1)}, bf16[2,2,32,384]{3,2,1,0:T(8,128)(2,1)S(1)}) custom-call(bf16[128,1024]{1,0:T(8,128)(2,1)S(1)} %collective-permute-done.main_ref, bf16[256,1536]{1,0:T(8,128)(2,1)S(1)} %get-tuple-element.56.yv_ref, ...), custom_call_target="tpu_custom_call" | custom-call | bytes 4000000 | tf_op jit(solution)/shard_map/half/pallas_call | solution.py:495
  20.7 1.8 %collective-permute-start.6 = (bf16[2,2,2,32,384]{4,3,2,1,0:T(8,128)(2,1)S(1)}, bf16[2,2,2,32,384]{4,3,2,1,0:T(8,128)(2,1)S(1)}, u32[]{:S(2)}, u32[]{:S(2)}) collective-permute-start(bf16[2,2,2,32,384]{4,3,2,1,0:T(8,128)(2,1)S(1)} %get-tuple-element.64.h_ref), channel_id=1, source_target_pairs={{0,224},{32,0},{64,32},{96,64},{128,96},{160,128},{192,160},{224,1... | collective-permute-start | bytes 589832 | tf_op jit(solution)/shard_map/ppermute | solution.py:430
  22.6 1.5 %cotangent.1 = (bf16[5,5,5,16,384]{4,3,2,1,0:T(8,128)(2,1)S(1)}, f32[8,32,384]{2,1,0:T(8,128)S(1)}) custom-call(bf16[128,1024]{1,0:T(8,128)(2,1)S(1)} %collective-permute-done.main_ref, bf16[256,1536]{1,0:T(8,128)(2,1)S(1)} %get-tuple-element.66.yc_ref, bf16[256,128]{1,0:T(8,128)(2,1)S(1)} %collective-permute-done.1.left_ref, ...), custom_call_target="tpu_custom_call" | custom-call | flops 679477248 | bytes 4000000 | tf_op jit(solution)/shard_map/cotangent/pallas_call | solution.py:501
  24.1 4.0 %collective-permute-done.5.hlo_ref = bf16[2,2,32,384]{3,2,1,0:T(8,128)(2,1)S(1)} collective-permute-done((bf16[2,2,32,384]{3,2,1,0:T(8,128)(2,1)S(1)}, bf16[2,2,32,384]{3,2,1,0:T(8,128)(2,1)S(1)}, u32[]{:S(2)}, u32[]{:S(2)}) %collective-permute-start.5) | collective-permute-done | bytes 98336 | tf_op jit(solution)/shard_map/ppermute | solution.py:430
  28.1 1.2 %middle.1 = (bf16[3,5,3,32,384]{4,3,2,1,0:T(8,128)(2,1)S(1)}, f32[2,64,384]{2,1,0:T(8,128)S(1)}, bf16[64,384]{1,0:T(8,128)(2,1)S(1)}, bf16[8,32,384]{2,1,0:T(8,1...) custom-call(bf16[2,2,2,32,384]{4,3,2,1,0:T(8,128)(2,1)S(1)} %get-tuple-element.64.h_ref, ...), custom_call_target="tpu_custom_call" | custom-call | bytes 4000000 | tf_op jit(solution)/shard_map/middle/pallas_call | solution.py:504
  29.3 1.3 %collective-permute-start.8 = (bf16[2,2,2,32,384]{4,3,2,1,0:T(8,128)(2,1)S(1)}, bf16[2,2,2,32,384]{4,3,2,1,0:T(8,128)(2,1)S(1)}, u32[]{:S(2)}, u32[]{:S(2)}) collective-permute-start(bf16[2,2,2,32,384]{4,3,2,1,0:T(8,128)(2,1)S(1)} %get-tuple-element.71.gm_ref), channel_id=1, source_target_pairs={{0,224},{32,0},{64,32},{96,64},{128,96},{160,128},{192,160},{224,1... | collective-permute-start | bytes 589832 | tf_op jit(solution)/shard_map/ppermute | solution.py:430
  30.6 0.4 collective-permute-start.7
  31.0 1.1 %full_grad.1.g4_ref = f32[112,128]{1,0:T(8,128)S(1)} custom-call(bf16[5,5,5,16,384]{4,3,2,1,0:T(8,128)(2,1)S(1)} %get-tuple-element.78.cwin_ref, bf16[8,32,384]{2,1,0:T(8,128)(2,1)S(1)} %get-tuple-element.79.m_ref), custom_call_target="tpu_custom_call" | custom-call | flops 679477248 | bytes 4000000 | tf_op jit(solution)/shard_map/full_grad/pallas_call | solution.py:510
  32.2 4.0 %collective-permute-done.7.gmlo_ref = bf16[2,2,32,384]{3,2,1,0:T(8,128)(2,1)S(1)} collective-permute-done((bf16[2,2,32,384]{3,2,1,0:T(8,128)(2,1)S(1)}, bf16[2,2,32,384]{3,2,1,0:T(8,128)(2,1)S(1)}, u32[]{:S(2)}, u32[]{:S(2)}) %collective-permute-start.7) | collective-permute-done | bytes 98336 | tf_op jit(solution)/shard_map/ppermute | solution.py:430
  36.2 2.5 %backward.1 = (bf16[3,2,3,32,384]{4,3,2,1,0:T(8,128)(2,1)S(1)}, bf16[2,2,32,384]{3,2,1,0:T(8,128)(2,1)S(1)}, f32[1536,128]{1,0:T(8,128)S(1)}, bf16[768,128]{1,0:T(8,128)(2,1)S(1)}) custom-call(bf16[2,2,2,32,384]{4,3,2,1,0:T(8,128)(2,1)S(1)} %get-tuple-element.71.gm_ref, bf16[2,2,32,384]{3,2,1,0:T(8,128)(2,1)S(1)} %collective-permute-done.7.gmlo_ref, ...), custom_call_target="tpu_custom_call" | custom-call | bytes 4000000 | tf_op jit(solution)/shard_map/backward/pallas_call | solution.py:512
  38.7 5.8 %collective-permute-start.9 = (bf16[768,128]{1,0:T(8,128)(2,1)S(1)}, bf16[768,128]{1,0:T(8,128)(2,1)S(1)}, u32[]{:S(2)}, u32[]{:S(2)}) collective-permute-start(bf16[768,128]{1,0:T(8,128)(2,1)S(1)} %get-tuple-element.83), channel_id=1, source_target_pairs={{0,1},{1,0},{2,3},{3,2},{4,5},{5,4},{6,7},{7,6},{8,9},{9,8},{10,11... | collective-permute-start | bytes 589832 | tf_op jit(solution)/shard_map/ppermute | solution.py:425
  44.6 0.8 collective-permute-start.10
  45.7 3.2 %collective-permute-done.10.next_ref = bf16[2,2,32,384]{3,2,1,0:T(8,128)(2,1)S(1)} collective-permute-done((bf16[2,2,32,384]{3,2,1,0:T(8,128)(2,1)S(1)}, bf16[2,2,32,384]{3,2,1,0:T(8,128)(2,1)S(1)}, u32[]{:S(2)}, u32[]{:S(2)}) %collective-permute-start.10) | collective-permute-done | bytes 98336 | tf_op jit(solution)/shard_map/ppermute | solution.py:430
  48.9 11.8 %all_to_all.15 = bf16[16,48,128]{2,1,0:T(8,128)(2,1)S(1)} all-to-all(bf16[16,48,128]{2,1,0:T(8,128)(2,1)S(1)} %bitcast.33), channel_id=1, replica_groups={{0,2,32,34,64,66,96,98,128,130,160,162,192,194,224,226},{1,3,33,35,65,6..., dimensions={0} | all-to-all | bytes 393216 | tf_op jit(solution)/shard_map/all_to_all | solution.py:447
  60.8 15.7 %all_to_all.16 = bf16[8,48,128]{2,1,0:T(8,128)(2,1)S(1)} all-to-all(bf16[8,48,128]{2,1,0:T(8,128)(2,1)S(1)} %bitcast.37), channel_id=1, replica_groups={{0,4,8,12,16,20,24,28},{1,5,9,13,17,21,25,29},{2,6,10,14,18,22,26,30},{..., dimensions={0} | all-to-all | bytes 196608 | tf_op jit(solution)/shard_map/all_to_all | solution.py:447
  76.5 0.7 sum.3
  77.2 3.5 %all-to-all-start.2 = ((bf16[16,48,128]{2,1,0:T(8,128)(2,1)}), bf16[16,48,128]{2,1,0:T(8,128)(2,1)S(1)}, u32[]{:S(2)}, u32[]{:S(2)}) async-start(bf16[16,48,128]{2,1,0:T(8,128)(2,1)} %bitcast.14), calls=%async_computation.2 | async-start | bytes 393216 | tf_op jit(solution)/shard_map/all_to_all | solution.py:447
  80.7 1.4 %copy-done.1 = bf16[5,5,5,16,384]{4,3,2,1,0:T(8,128)(2,1)S(1)} copy-done((bf16[5,5,5,16,384]{4,3,2,1,0:T(8,128)(2,1)S(1)}, bf16[5,5,5,16,384]{4,3,2,1,0:T(8,128)(2,1)}, u32[]{:S(2)}) %copy-start.1) | copy-done | bytes 1536024
  82.1 2.0 %volume.1 = bf16[16,8,16,128]{3,2,1,0:T(8,128)(2,1)} custom-call(bf16[3,2,3,32,384]{4,3,2,1,0:T(8,128)(2,1)S(1)} %get-tuple-element.86.ewin_ref, bf16[2,2,32,384]{3,2,1,0:T(8,128)(2,1)S(1)} %collective-permute-done.10.next_ref, bf16[5,5,5,16,384]{4,3,2,1,0:T(8,128)(2,1)S(1)} %copy-done.1, bf16[128,256]{1,0:T(8,128)(2,1)S(1)} %get-tuple-element.88.up1_ref, ...), custom_call_target="tpu_custom_call" | custom-call | flops 2097152000 | bytes 4000000 | tf_op jit(solution)/shard_map/volume/pallas_call | solution.py:527
  84.1 3.8 %all-to-all-done.2 = bf16[16,48,128]{2,1,0:T(8,128)(2,1)S(1)} async-done(((bf16[16,48,128]{2,1,0:T(8,128)(2,1)}), bf16[16,48,128]{2,1,0:T(8,128)(2,1)S(1)}, u32[]{:S(2)}, u32[]{:S(2)}) %all-to-all-start.2) | async-done | bytes 196640 | tf_op jit(solution)/shard_map/all_to_all | solution.py:447
  88.0 4.9 %collective-permute-start.11 = (bf16[768,128]{1,0:T(8,128)(2,1)S(1)}, bf16[768,128]{1,0:T(8,128)(2,1)S(1)}, u32[]{:S(2)}, u32[]{:S(2)}) collective-permute-start(bf16[768,128]{1,0:T(8,128)(2,1)S(1)} %bitcast.34), channel_id=1, source_target_pairs={{0,1},{1,0},{2,3},{3,2},{4,5},{5,4},{6,7},{7,6},{8,9},{9,8},{10,11... | collective-permute-start | bytes 589832 | tf_op jit(solution)/shard_map/ppermute | solution.py:425
  92.9 1.1 %collective-permute-done.11.got_ref = bf16[768,128]{1,0:T(8,128)(2,1)S(1)} collective-permute-done((bf16[768,128]{1,0:T(8,128)(2,1)S(1)}, bf16[768,128]{1,0:T(8,128)(2,1)S(1)}, u32[]{:S(2)}, u32[]{:S(2)}) %collective-permute-start.11) | collective-permute-done | bytes 196640 | tf_op jit(solution)/shard_map/ppermute | solution.py:425
  93.9 1.3 %finish.1 = (f32[27,16,32]{2,1,0:T(8,128)}, f32[27,32,64]{2,1,0:T(8,128)}, f32[27,32,64]{2,1,0:T(8,128)}, f32[27,16,32]{2,1,0:T(8,128)}) custom-call(bf16[768,128]{1,0:T(8,128)(2,1)S(1)} %bitcast.35, bf16[768,128]{1,0:T(8,128)(2,1)S(1)} %collective-permute-done.11.got_ref), custom_call_target="tpu_custom_call" | custom-call | bytes 4000000 | tf_op jit(solution)/shard_map/finish/pallas_call | solution.py:531
  (14 shorter events, 0.4 us)
Async XLA Ops:
  3.3 15.9 %collective-permute-start = (bf16[128,1024]{1,0:T(8,128)(2,1)S(1)}, bf16[128,1024]{1,0:T(8,128)(2,1)S(1)}, u32[]{:S(2)}, u32[]{:S(2)}) collective-permute-start(bf16[128,1024]{1,0:T(8,128)(2,1)S(1)} %get-tuple-element.52), channel_id=1, source_target_pairs={{0,32},{32,64},{64,96},{96,128},{128,160},{160,192},{192,224},{224... | collective-permute-start | bytes 786440 | tf_op jit(solution)/shard_map/ppermute | solution.py:430
  5.4 12.4 %collective-permute-start.3 = (bf16[64,128]{1,0:T(8,128)(2,1)S(1)}, bf16[64,128]{1,0:T(8,128)(2,1)S(1)}, u32[]{:S(2)}, u32[]{:S(2)}) collective-permute-start(bf16[64,128]{1,0:T(8,128)(2,1)S(1)} %get-tuple-element.59), channel_id=1, source_target_pairs={{0,33},{1,34},{2,35},{3,36},{4,37},{5,38},{6,39},{7,40},{8,41},{9,... | collective-permute-start | bytes 49160 | tf_op jit(solution)/shard_map/ppermute | solution.py:436
  10.1 7.8 %collective-permute-start.4 = (bf16[64,128]{1,0:T(8,128)(2,1)S(1)}, bf16[64,128]{1,0:T(8,128)(2,1)S(1)}, u32[]{:S(2)}, u32[]{:S(2)}) collective-permute-start(bf16[64,128]{1,0:T(8,128)(2,1)S(1)} %get-tuple-element.60), channel_id=1, source_target_pairs={{0,63},{1,32},{2,33},{3,34},{4,35},{5,36},{6,37},{7,38},{8,39},{9,... | collective-permute-start | bytes 49160 | tf_op jit(solution)/shard_map/ppermute | solution.py:436
  10.1 7.8 %collective-permute-start.1 = (bf16[256,128]{1,0:T(8,128)(2,1)S(1)}, bf16[256,128]{1,0:T(8,128)(2,1)S(1)}, u32[]{:S(2)}, u32[]{:S(2)}) collective-permute-start(bf16[256,128]{1,0:T(8,128)(2,1)S(1)} %get-tuple-element.57), channel_id=1, source_target_pairs={{0,1},{1,2},{2,3},{3,4},{4,5},{5,6},{6,7},{7,8},{8,9},{9,10},{10,1... | collective-permute-start | bytes 196616 | tf_op jit(solution)/shard_map/ppermute | solution.py:430
  14.0 5.2 %collective-permute-start.2 = (bf16[256,128]{1,0:T(8,128)(2,1)S(1)}, bf16[256,128]{1,0:T(8,128)(2,1)S(1)}, u32[]{:S(2)}, u32[]{:S(2)}) collective-permute-start(bf16[256,128]{1,0:T(8,128)(2,1)S(1)} %get-tuple-element.58), channel_id=1, source_target_pairs={{0,31},{1,0},{2,1},{3,2},{4,3},{5,4},{6,5},{7,6},{8,7},{9,8},{10,9... | collective-permute-start | bytes 196616 | tf_op jit(solution)/shard_map/ppermute | solution.py:430
  20.7 7.4 %collective-permute-start.6 = (bf16[2,2,2,32,384]{4,3,2,1,0:T(8,128)(2,1)S(1)}, bf16[2,2,2,32,384]{4,3,2,1,0:T(8,128)(2,1)S(1)}, u32[]{:S(2)}, u32[]{:S(2)}) collective-permute-start(bf16[2,2,2,32,384]{4,3,2,1,0:T(8,128)(2,1)S(1)} %get-tuple-element.64.h_ref), channel_id=1, source_target_pairs={{0,224},{32,0},{64,32},{96,64},{128,96},{160,128},{192,160},{224,1... | collective-permute-start | bytes 589832 | tf_op jit(solution)/shard_map/ppermute | solution.py:430
  22.6 5.6 %collective-permute-start.5 = (bf16[2,2,32,384]{3,2,1,0:T(8,128)(2,1)S(1)}, bf16[2,2,32,384]{3,2,1,0:T(8,128)(2,1)S(1)}, u32[]{:S(2)}, u32[]{:S(2)}) collective-permute-start(bf16[2,2,32,384]{3,2,1,0:T(8,128)(2,1)S(1)} %get-tuple-element.65), channel_id=1, source_target_pairs={{0,32},{32,64},{64,96},{96,128},{128,160},{160,192},{192,224},{224... | collective-permute-start | bytes 294920 | tf_op jit(solution)/shard_map/ppermute | solution.py:430
  24.1 8.1 %copy-start = (bf16[5,5,5,16,384]{4,3,2,1,0:T(8,128)(2,1)}, bf16[5,5,5,16,384]{4,3,2,1,0:T(8,128)(2,1)S(1)}, u32[]{:S(2)}) copy-start(bf16[5,5,5,16,384]{4,3,2,1,0:T(8,128)(2,1)S(1)} %get-tuple-element.78.cwin_ref) | copy-start | bytes 4608004
  29.3 6.9 %collective-permute-start.8 = (bf16[2,2,2,32,384]{4,3,2,1,0:T(8,128)(2,1)S(1)}, bf16[2,2,2,32,384]{4,3,2,1,0:T(8,128)(2,1)S(1)}, u32[]{:S(2)}, u32[]{:S(2)}) collective-permute-start(bf16[2,2,2,32,384]{4,3,2,1,0:T(8,128)(2,1)S(1)} %get-tuple-element.71.gm_ref), channel_id=1, source_target_pairs={{0,224},{32,0},{64,32},{96,64},{128,96},{160,128},{192,160},{224,1... | collective-permute-start | bytes 589832 | tf_op jit(solution)/shard_map/ppermute | solution.py:430
  30.6 5.6 %collective-permute-start.7 = (bf16[2,2,32,384]{3,2,1,0:T(8,128)(2,1)S(1)}, bf16[2,2,32,384]{3,2,1,0:T(8,128)(2,1)S(1)}, u32[]{:S(2)}, u32[]{:S(2)}) collective-permute-start(bf16[2,2,32,384]{3,2,1,0:T(8,128)(2,1)S(1)} %get-tuple-element.72), channel_id=1, source_target_pairs={{0,32},{32,64},{64,96},{96,128},{128,160},{160,192},{192,224},{224... | collective-permute-start | bytes 294920 | tf_op jit(solution)/shard_map/ppermute | solution.py:430
  38.7 6.9 %collective-permute-start.9 = (bf16[768,128]{1,0:T(8,128)(2,1)S(1)}, bf16[768,128]{1,0:T(8,128)(2,1)S(1)}, u32[]{:S(2)}, u32[]{:S(2)}) collective-permute-start(bf16[768,128]{1,0:T(8,128)(2,1)S(1)} %get-tuple-element.83), channel_id=1, source_target_pairs={{0,1},{1,0},{2,3},{3,2},{4,5},{5,4},{6,7},{7,6},{8,9},{9,8},{10,11... | collective-permute-start | bytes 589832 | tf_op jit(solution)/shard_map/ppermute | solution.py:425
  44.6 4.4 %collective-permute-start.10 = (bf16[2,2,32,384]{3,2,1,0:T(8,128)(2,1)S(1)}, bf16[2,2,32,384]{3,2,1,0:T(8,128)(2,1)S(1)}, u32[]{:S(2)}, u32[]{:S(2)}) collective-permute-start(bf16[2,2,32,384]{3,2,1,0:T(8,128)(2,1)S(1)} %get-tuple-element.84), channel_id=1, source_target_pairs={{0,224},{32,0},{64,32},{96,64},{128,96},{160,128},{192,160},{224,1... | collective-permute-start | bytes 294920 | tf_op jit(solution)/shard_map/ppermute | solution.py:430
  77.2 10.8 %all-to-all-start.2 = ((bf16[16,48,128]{2,1,0:T(8,128)(2,1)}), bf16[16,48,128]{2,1,0:T(8,128)(2,1)S(1)}, u32[]{:S(2)}, u32[]{:S(2)}) async-start(bf16[16,48,128]{2,1,0:T(8,128)(2,1)} %bitcast.14), calls=%async_computation.2 | async-start | bytes 393216 | tf_op jit(solution)/shard_map/all_to_all | solution.py:447
  80.7 1.4 %copy-start.1 = (bf16[5,5,5,16,384]{4,3,2,1,0:T(8,128)(2,1)S(1)}, bf16[5,5,5,16,384]{4,3,2,1,0:T(8,128)(2,1)}, u32[]{:S(2)}) copy-start(bf16[5,5,5,16,384]{4,3,2,1,0:T(8,128)(2,1)} %copy-done) | copy-start | bytes 4608004
  88.0 5.9 %collective-permute-start.11 = (bf16[768,128]{1,0:T(8,128)(2,1)S(1)}, bf16[768,128]{1,0:T(8,128)(2,1)S(1)}, u32[]{:S(2)}, u32[]{:S(2)}) collective-permute-start(bf16[768,128]{1,0:T(8,128)(2,1)S(1)} %bitcast.34), channel_id=1, source_target_pairs={{0,1},{1,0},{2,3},{3,2},{4,5},{5,4},{6,7},{7,6},{8,9},{9,8},{10,11... | collective-permute-start | bytes 589832 | tf_op jit(solution)/shard_map/ppermute | solution.py:425

commit v6 on v5

--- a/solution.py
+++ b/solution.py
@@ -14,7 +14,7 @@
 QD, QC, HALO = 8, 32, 2
 SPAN = QC + 2 * HALO
 LANES = 384
-PACK = 1536
+PACK = 1280
 LIMIT = 24 * 1024 * 1024
 
 
@@ -198,6 +198,19 @@
             win_ref[0, row, 0] = roll_up(left, SPAN).astype(BF)
 
 
+def packed(values):
+    tails = [pltpu.roll(value[:, 256:], 32 * i, 1) if i else value[:, 256:] for i, value in enumerate(values)]
+    tail = (tails[0] + tails[1]) + (tails[2] + tails[3])
+    return jnp.concatenate([value[:, :256] for value in values] + [tail], axis=1).astype(BF)
+
+
+def unpacked(value, i):
+    tail = value[:, 1024:]
+    tail = pltpu.roll(tail, 128 - 32 * i, 1) if i else tail
+    tail = jnp.where(iota(tail.shape, 1) < 32, tail, 0.0)
+    return jnp.concatenate([value[:, 256 * i : 256 * i + 256], tail], axis=1)
+
+
 def rounded(value):
     return value.astype(BF).astype(F32)
 
@@ -212,7 +225,7 @@
     return jnp.concatenate(parts, axis=0)
 
 
-def half_kernel(main_ref, yv_ref, left_ref, right_ref, low_left_ref, low_right_ref, mask_ref, spread_ref, place_ref, w1_ref, vwin_ref, preh_ref, h_ref, h_last_ref):
+def half_kernel(main_ref, yv_ref, left_ref, right_ref, low_left_ref, low_right_ref, mask_ref, spread_ref, place_ref, w1_ref, vwin_ref, preh_ref, h_ref, h_all_ref, h_last_ref):
     seen = mask_ref[0:1]
     to_vol = place_ref[0]
     y = to_lanes(main_ref[0:64], spread_ref) + dot(rims_of(low_left_ref, low_right_ref), to_vol)
@@ -224,8 +237,9 @@
         pre = dot(w1, col)
         preh_ref[pr, pd, pc] = pre
         h_ref[pr, pd, pc] = (pre * sigmoid(pre) * seen).astype(BF)
-        if pr == 1:
-            h_last_ref[pd, pc] = h_ref[pr, pd, pc]
+    for pr in range(2):
+        h_all_ref[pr] = packed([h_ref[pr, pd, pc].astype(F32) for pd in range(2) for pc in range(2)])
+    h_last_ref[...] = h_all_ref[1]
 
 
 def cotangent_kernel(main_ref, yc_ref, left_ref, right_ref, low_left_ref, low_right_ref, spread_ref, place_ref, w4_ref, cwin_ref, pull_ref):
@@ -239,17 +253,18 @@
         pull_ref[p] = dot(w4, col)
 
 
-def middle_kernel(h_ref, hlo_ref, hhi_ref, pull_ref, mask_ref, w2_ref, up3_ref, hwin_ref, preq_ref, q_ref, m_ref, gm_ref, gm_last_ref):
+def middle_kernel(h_ref, hlo_ref, hhi_ref, pull_ref, mask_ref, w2_ref, up3_ref, hwin_ref, preq_ref, q_ref, m_ref, gm_ref, gm_all_ref, gm_last_ref):
     seen = mask_ref[0:1]
     seen_next = mask_ref[1:2]
     own = mask_ref[2:3]
     inner = flag(lax.axis_index("row") > 0)
     for pd in range(2):
         for pc in range(2):
-            put_half(hwin_ref, 0, pd, pc, hlo_ref[pd, pc].astype(F32) * inner)
+            phase = 2 * pd + pc
+            put_half(hwin_ref, 0, pd, pc, unpacked(hlo_ref[...].astype(F32), phase) * inner)
             for pr in range(2):
                 put_half(hwin_ref, 1 + pr, pd, pc, h_ref[pr, pd, pc].astype(F32))
-                put_half(hwin_ref, 3 + pr, pd, pc, hhi_ref[pr, pd, pc].astype(F32) * seen_next)
+                put_half(hwin_ref, 3 + pr, pd, pc, unpacked(hhi_ref[pr].astype(F32), phase) * seen_next)
     quarters = []
     for qr in range(2):
         col = hwin_ref[:, 2 * qr : 2 * qr + 3].reshape(864, LANES)
@@ -263,8 +278,9 @@
         m_ref[p] = (rounded(pre * sigmoid(pre)) * own).astype(BF)
         gm = rounded(pull_ref[p] * slope(pre)) * seen
         gm_ref[pr, pd, pc] = gm.astype(BF)
-        if pr == 1:
-            gm_last_ref[pd, pc] = gm.astype(BF)
+    for pr in range(2):
+        gm_all_ref[pr] = packed([gm_ref[pr, pd, pc].astype(F32) for pd in range(2) for pc in range(2)])
+    gm_last_ref[...] = gm_all_ref[1]
 
 
 def full_grad_kernel(cwin_ref, m_ref, out_ref):
@@ -303,10 +319,11 @@
     inner = flag(lax.axis_index("row") > 0)
     for pd in range(2):
         for pc in range(2):
-            put_half(mwin_ref, 0, pd, pc, gmlo_ref[pd, pc].astype(F32) * inner)
+            phase = 2 * pd + pc
+            put_half(mwin_ref, 0, pd, pc, unpacked(gmlo_ref[...].astype(F32), phase) * inner)
             for pr in range(2):
                 put_half(mwin_ref, 1 + pr, pd, pc, gm_ref[pr, pd, pc].astype(F32))
-                put_half(mwin_ref, 3 + pr, pd, pc, gmhi_ref[pr, pd, pc].astype(F32))
+                put_half(mwin_ref, 3 + pr, pd, pc, unpacked(gmhi_ref[pr].astype(F32), phase))
     quarters = []
     for qr in range(2):
         col = mwin_ref[:, 2 * qr : 2 * qr + 3].reshape(864, LANES)
@@ -316,16 +333,18 @@
             store_groups(pack_ref, dot_nt(col, q_ref[...]), 672, 448, 64)
     up = dot(up2_ref[...], neighbours(quarters[0], quarters[1]))
     total = None
+    first_row = []
     for p, (pr, pd, pc) in enumerate(PAIRS):
         conv = up[p * 32 : p * 32 + 32]
         gm = mwin_ref[1 + pd, 1 + pr, 1 + pc].astype(F32)
         gh = rounded((conv + gm) * slope(preh_ref[pr, pd, pc])) * seen
         put_upper(ewin_ref.at[:, pr], pd, pc, gh)
         if pr == 0:
-            gh_first_ref[pd, pc] = gh.astype(BF)
+            first_row.append(gh)
         col = vwin_ref[2 * pd : 2 * pd + 3, 2 * pr : 2 * pr + 3, 2 * pc : 2 * pc + 3].reshape(432, LANES)
         part = dot_nt(col, (gh * own).astype(BF))
         total = part if total is None else total + part
+    gh_first_ref[...] = packed(first_row)
     store_groups(pack_ref, total, 0, 112, 32)
     pack_ref[112:224] = g4_ref[...]
     col = hwin_ref[:, 0:3].reshape(864, LANES)
@@ -338,7 +357,7 @@
     below = flag(lax.axis_index("row") < lax.axis_size("row") - 1)
     for pd in range(2):
         for pc in range(2):
-            put_upper(ext_ref, pd, pc, next_ref[pd, pc].astype(F32) * below)
+            put_upper(ext_ref, pd, pc, unpacked(next_ref[...].astype(F32), 2 * pd + pc) * below)
     up1 = up1_ref[...]
     for pr, pd, pc in PAIRS:
         near = jnp.concatenate(
@@ -377,12 +396,8 @@
 
 def sum_kernel(terms, copies, x_ref, out_ref):
     size = x_ref.shape[0] // terms
-    total = x_ref[0:size].astype(F32)
-    for i in range(1, terms):
-        total = total + x_ref[i * size : (i + 1) * size].astype(F32)
-    total = total.astype(BF)
-    for i in range(copies):
-        out_ref[i * size : (i + 1) * size] = total
+    total = jnp.sum(x_ref[...].astype(F32).reshape(terms, size, 128), axis=0, keepdims=True)
+    out_ref[...] = jnp.broadcast_to(total, (copies, size, 128)).reshape(copies * size, 128).astype(BF)
 
 
 def finish_kernel(scale, stage, own_ref, got_ref, g1_ref, g2_ref, g3_ref, g4_ref, full_ref):
@@ -492,37 +507,38 @@
         name="prepare",
     )(*[held(weight) for weight in weights])
     full_window, half_rows = (5, 5, 5, 16, LANES), (2, 2, 2, 32, LANES)
-    vwin, preh, half_act, half_last = call(
+    vwin, preh, half_act, half_all, half_last = call(
         half_kernel,
-        [(full_window, BF), (half_rows, F32), (half_rows, BF), (half_rows[1:], BF)],
+        [(full_window, BF), (half_rows, F32), (half_rows, BF), ((2, 32, 1152), BF), ((32, 1152), BF)],
         name="half",
     )(main_lo, yv, *edges, mask, spread, place, w1)
-    half_lo, half_hi = shifted(half_last, "row", 1), shifted(half_act, "row", -1)
+    half_lo, half_hi = shifted(half_last, "row", 1), shifted(half_all, "row", -1)
     cwin, pull = call(
         cotangent_kernel, [(full_window, BF), ((8, 32, LANES), F32)], flops=2 * 432 * 32 * LANES * 64, name="cotangent"
     )(main_lo, yc, *edges, spread, place, w4)
-    hwin, preq, quarter, mixed, gm, gm_last = call(
+    hwin, preq, quarter, mixed, gm, gm_all, gm_last = call(
         middle_kernel,
-        [((3, 5, 3, 32, LANES), BF), ((2, 64, LANES), F32), ((64, LANES), BF), ((8, 32, LANES), BF), (half_rows, BF), (half_rows[1:], BF)],
+        [((3, 5, 3, 32, LANES), BF), ((2, 64, LANES), F32), ((64, LANES), BF), ((8, 32, LANES), BF), (half_rows, BF), ((2, 32, 1152), BF), ((32, 1152), BF)],
         name="middle",
     )(half_act, half_lo, half_hi, pull, mask, w2, up3)
-    gm_lo, gm_hi = shifted(gm_last, "row", 1), shifted(gm, "row", -1)
+    gm_lo, gm_hi = shifted(gm_last, "row", 1), shifted(gm_all, "row", -1)
     (g4,) = call(full_grad_kernel, [((112, 128), F32)], flops=2 * 432 * 32 * LANES * 64, name="full_grad")(cwin, mixed)
     core = ("col", 1)
     ewin, gh_first, kept, send = call(
         functools.partial(backward_kernel, core),
-        [((3, 2, 3, 32, LANES), BF), (half_rows[1:], BF), ((PACK, 128), F32), ((PACK // 2, 128), BF)],
+        [((3, 2, 3, 32, LANES), BF), ((32, 1152), BF), ((PACK, 128), F32), ((PACK // 2, 128), BF)],
         [pltpu.VMEM((3, 5, 3, 32, LANES), BF)],
         name="backward",
     )(gm, gm_lo, gm_hi, vwin, hwin, preh, preq, quarter, g4, mask, w3, up2)
     (part,) = call(functools.partial(fold_kernel, core), [((PACK // 2, 128), BF)], name="fold")(kept, swapped(send, 0, 1))
-    part, gh_next = lax.optimization_barrier((part, shifted(gh_first, "row", -1)))
+    gh_next = shifted(gh_first, "row", -1)
     along = [(7 & (rows - 1), 2 & (cols - 1)), (0, 28 & (cols - 1))]
     sizes = [2 ** (r.bit_count() + c.bit_count()) for r, c in along]
     share = PACK // 2 // sizes[0]
     for bits, size, later in zip(along, sizes, sizes[::-1]):
         part = exchanged(part.reshape(size, share, 128), *bits).reshape(size * share, 128)
         (part,) = call(functools.partial(sum_kernel, size, later), [((later * share, 128), BF)], name="sum")(part)
+    part, gh_next = lax.optimization_barrier((part, gh_next))
     part = exchanged(part.reshape(sizes[0], share, 128), *along[0]).reshape(PACK // 2, 128)
     (grad_volume,) = call(
         volume_kernel, [((16, QD, 16, 128), BF)], [pltpu.VMEM((256, 4 * LANES), BF), pltpu.VMEM((3, 3, 32, LANES), BF)], flops=2 * 256 * 1024 * 4000, name="volume"

time: 95.6 us -> 89.2 us (0.933)
  blocking collectives: 27.6 us -> 10.1 us
  starting transfers between devices: 30.2 us -> 37.2 us
  waiting for transfers between devices: 17.8 us -> 21.1 us
    all_to_all x2 -> x1, blocking collectives: 27.6 us -> 10.1 us  [exchanged(): lax.all_to_all(value, ('row', 'col'), 0, 0, axis_index_groups=list(groups...]
    all_to_all x1 -> x2, starting transfers between devices: 3.52 us -> 11.3 us  [exchanged(): lax.all_to_all(value, ('row', 'col'), 0, 0, axis_index_groups=list(groups...]
    all_to_all x1 -> x2, waiting for transfers between devices: 3.85 us -> 10.5 us  [exchanged(): lax.all_to_all(value, ('row', 'col'), 0, 0, axis_index_groups=list(groups...]
    ppermute x8, waiting for transfers between devices: 12.6 us -> 8.58 us  [shifted(): lax.ppermute(value, axis, [(i, (i + steps) % count) for i in range(count)])]
  transfers between devices with their start and end apart: 13 -> 14, of which waited for: 7 -> 7; matrix products, arithmetic and copies ran while one was open for 0% -> 0% of each run, Pallas kernels for 8% -> 9%
where the time goes in v6:
time: 89.2 us; the launch traced here: 88.8 us
  starting transfers between devices  37.2 us (42%)
  waiting for transfers between devices  21.1 us (24%)
  Pallas kernels  18.3 us (21%)
  blocking collectives  10.1 us (11%)
  local copies, waits for them, and re-layouts  1.39 us (2%)
    all_to_all x2, starting transfers between devices, exchanged(): lax.all_to_all(value, ('row', 'col'), 0, 0, axis_index_groups=list(groups...  11.3 us
    ppermute x8, starting transfers between devices, shifted(): lax.ppermute(value, axis, [(i, (i + steps) % count) for i in range(count)])  11.2 us
    all_to_all x2, waiting for transfers between devices, exchanged(): lax.all_to_all(value, ('row', 'col'), 0, 0, axis_index_groups=list(groups...  10.5 us
    all_to_all x1, blocking collectives, exchanged(): lax.all_to_all(value, ('row', 'col'), 0, 0, axis_index_groups=list(groups...  10.1 us
    ppermute x2, starting transfers between devices, swapped(): return lax.ppermute(value, ('row', 'col'), pairs)  10 us
    ppermute x8, waiting for transfers between devices, shifted(): lax.ppermute(value, axis, [(i, (i + steps) % count) for i in range(count)])  8.58 us
    ppermute x2, starting transfers between devices, diagonal(): return lax.ppermute(value, ('row', 'col'), pairs)  4.69 us
    pallas_call x1, Pallas kernels, shards(): call(functools.partial(backward_kernel, core), [((3, 2, 3, 32, LANES), BF...  2.59 us
  transfers between devices with their start and end apart: 14, of which 7 were waited for; matrix products, arithmetic and copies ran while one was open for 0% of the time, Pallas kernels for 9%

profile of v6, /device:TPU:1, one launch (start us, length us, event | category | flops | bytes accessed | tf_op | source)
XLA Modules:
  0.0 88.8 jit_solution(5839497171923333936)
XLA Ops:
  1.2 2.0 %edge.1 = (bf16[256,1024]{1,0:T(8,128)(2,1)S(1)}, bf16[256,1024]{1,0:T(8,128)(2,1)S(1)}, bf16[128,1024]{1,0:T(8,128)(2,1)S(1)}, bf16[256,128]{1,0:T(8,128)(2,1)S...) custom-call(bf16[16,8,16,128]{3,2,1,0:T(8,128)(2,1)} %bitcast.38, ...), custom_call_target="tpu_custom_call" | custom-call | bytes 4000000 | tf_op jit(solution)/shard_map/edge/pallas_call | solution.py:491
  3.3 2.1 %collective-permute-start = (bf16[128,1024]{1,0:T(8,128)(2,1)S(1)}, bf16[128,1024]{1,0:T(8,128)(2,1)S(1)}, u32[]{:S(2)}, u32[]{:S(2)}) collective-permute-start(bf16[128,1024]{1,0:T(8,128)(2,1)S(1)} %get-tuple-element.54), channel_id=1, source_target_pairs={{0,32},{32,64},{64,96},{96,128},{128,160},{160,192},{192,224},{224... | collective-permute-start | bytes 786440 | tf_op jit(solution)/shard_map/ppermute | solution.py:445
  5.4 4.7 %collective-permute-start.3 = (bf16[64,128]{1,0:T(8,128)(2,1)S(1)}, bf16[64,128]{1,0:T(8,128)(2,1)S(1)}, u32[]{:S(2)}, u32[]{:S(2)}) collective-permute-start(bf16[64,128]{1,0:T(8,128)(2,1)S(1)} %get-tuple-element.61), channel_id=1, source_target_pairs={{0,33},{1,34},{2,35},{3,36},{4,37},{5,38},{6,39},{7,40},{8,41},{9,... | collective-permute-start | bytes 49160 | tf_op jit(solution)/shard_map/ppermute | solution.py:451
  10.1 3.9 %collective-permute-start.1 = (bf16[256,128]{1,0:T(8,128)(2,1)S(1)}, bf16[256,128]{1,0:T(8,128)(2,1)S(1)}, u32[]{:S(2)}, u32[]{:S(2)}) collective-permute-start(bf16[256,128]{1,0:T(8,128)(2,1)S(1)} %get-tuple-element.59), channel_id=1, source_target_pairs={{0,1},{1,2},{2,3},{3,4},{4,5},{5,6},{6,7},{7,8},{8,9},{9,10},{10,1... | collective-permute-start | bytes 196616 | tf_op jit(solution)/shard_map/ppermute | solution.py:445
  14.0 1.0 %collective-permute-start.2 = (bf16[256,128]{1,0:T(8,128)(2,1)S(1)}, bf16[256,128]{1,0:T(8,128)(2,1)S(1)}, u32[]{:S(2)}, u32[]{:S(2)}) collective-permute-start(bf16[256,128]{1,0:T(8,128)(2,1)S(1)} %get-tuple-element.60), channel_id=1, source_target_pairs={{0,31},{1,0},{2,1},{3,2},{4,3},{5,4},{6,5},{7,6},{8,7},{9,8},{10,9... | collective-permute-start | bytes 196616 | tf_op jit(solution)/shard_map/ppermute | solution.py:445
  14.9 1.3 %own.1 = (bf16[256,1536]{1,0:T(8,128)(2,1)S(1)}, bf16[256,1536]{1,0:T(8,128)(2,1)S(1)}) custom-call(bf16[256,1024]{1,0:T(8,128)(2,1)S(1)} %get-tuple-element.55.vol_rows_ref, bf16[256,1024]{1,0:T(8,128)(2,1)S(1)} %get-tuple-element.56.cot_rows_ref, bf16[1024,1024]{1,0:T(8,128)(2,1)S(1)} %get-tuple-element.57.spread_ref), custom_call_target="tpu_custom_call" | custom-call | flops 2097152000 | bytes 4000000 | tf_op jit(solution)/shard_map/own/pallas_call | solution.py:500
  16.2 1.6 %prepare.1 = (bf16[32,432]{1,0:T(8,128)(2,1)S(1)}, bf16[64,864]{1,0:T(8,128)(2,1)S(1)}, bf16[64,864]{1,0:T(8,128)(2,1)S(1)}, bf16[32,432]{1,0:T(8,128)(2,1)S(1)}...) custom-call(bf16[27,16,32]{2,1,0:T(8,128)(2,1)} %bitcast.42, ...), custom_call_target="tpu_custom_call" | custom-call | bytes 4000000 | tf_op jit(solution)/shard_map/prepare/pallas_call | solution.py:502
  17.9 1.3 %collective-permute-done.2.right_ref = bf16[256,128]{1,0:T(8,128)(2,1)S(1)} collective-permute-done((bf16[256,128]{1,0:T(8,128)(2,1)S(1)}, bf16[256,128]{1,0:T(8,128)(2,1)S(1)}, u32[]{:S(2)}, u32[]{:S(2)}) %collective-permute-start.2) | collective-permute-done | bytes 65568 | tf_op jit(solution)/shard_map/ppermute | solution.py:445
  19.2 1.6 %half.1 = (bf16[5,5,5,16,384]{4,3,2,1,0:T(8,128)(2,1)S(1)}, f32[2,2,2,32,384]{4,3,2,1,0:T(8,128)S(1)}, bf16[2,2,2,32,384]{4,3,2,1,0:T(8,128)(2,1)S(1)}, bf16[2,3...) custom-call(bf16[128,1024]{1,0:T(8,128)(2,1)S(1)} %collective-permute-done.main_ref, ...), custom_call_target="tpu_custom_call" | custom-call | bytes 4000000 | tf_op jit(solution)/shard_map/half/pallas_call | solution.py:510
  20.8 1.8 %collective-permute-start.6 = (bf16[2,32,1152]{2,1,0:T(8,128)(2,1)S(1)}, bf16[2,32,1152]{2,1,0:T(8,128)(2,1)S(1)}, u32[]{:S(2)}, u32[]{:S(2)}) collective-permute-start(bf16[2,32,1152]{2,1,0:T(8,128)(2,1)S(1)} %get-tuple-element.68), channel_id=1, source_target_pairs={{0,224},{32,0},{64,32},{96,64},{128,96},{160,128},{192,160},{224,1... | collective-permute-start | bytes 442376 | tf_op jit(solution)/shard_map/ppermute | solution.py:445
  22.6 1.5 %cotangent.1 = (bf16[5,5,5,16,384]{4,3,2,1,0:T(8,128)(2,1)S(1)}, f32[8,32,384]{2,1,0:T(8,128)S(1)}) custom-call(bf16[128,1024]{1,0:T(8,128)(2,1)S(1)} %collective-permute-done.main_ref, bf16[256,1536]{1,0:T(8,128)(2,1)S(1)} %get-tuple-element.69.yc_ref, bf16[256,128]{1,0:T(8,128)(2,1)S(1)} %collective-permute-done.1.left_ref, ...), custom_call_target="tpu_custom_call" | custom-call | flops 679477248 | bytes 4000000 | tf_op jit(solution)/shard_map/cotangent/pallas_call | solution.py:516
  24.2 3.8 %collective-permute-done.5.hlo_ref = bf16[32,1152]{1,0:T(8,128)(2,1)S(1)} collective-permute-done((bf16[32,1152]{1,0:T(8,128)(2,1)S(1)}, bf16[32,1152]{1,0:T(8,128)(2,1)S(1)}, u32[]{:S(2)}, u32[]{:S(2)}) %collective-permute-start.5) | collective-permute-done | bytes 73760 | tf_op jit(solution)/shard_map/ppermute | solution.py:445
  27.9 1.3 %middle.1 = (bf16[3,5,3,32,384]{4,3,2,1,0:T(8,128)(2,1)S(1)}, f32[2,64,384]{2,1,0:T(8,128)S(1)}, bf16[64,384]{1,0:T(8,128)(2,1)S(1)}, bf16[8,32,384]{2,1,0:T(8,1...) custom-call(bf16[2,2,2,32,384]{4,3,2,1,0:T(8,128)(2,1)S(1)} %get-tup, ...), custom_call_target="tpu_custom_call" | custom-call | bytes 4000000 | tf_op jit(solution)/shard_map/middle/pallas_call | solution.py:519
  29.2 1.0 %collective-permute-start.8 = (bf16[2,32,1152]{2,1,0:T(8,128)(2,1)S(1)}, bf16[2,32,1152]{2,1,0:T(8,128)(2,1)S(1)}, u32[]{:S(2)}, u32[]{:S(2)}) collective-permute-start(bf16[2,32,1152]{2,1,0:T(8,128)(2,1)S(1)} %get-tuple-element.76), channel_id=1, source_target_pairs={{0,224},{32,0},{64,32},{96,64},{128,96},{160,128},{192,160},{224,1... | collective-permute-start | bytes 442376 | tf_op jit(solution)/shard_map/ppermute | solution.py:445
  30.3 0.7 collective-permute-start.7
  31.0 1.1 %full_grad.1.g4_ref = f32[112,128]{1,0:T(8,128)S(1)} custom-call(bf16[5,5,5,16,384]{4,3,2,1,0:T(8,128)(2,1)S(1)} %get-tuple-element.82.cwin_ref, bf16[8,32,384]{2,1,0:T(8,128)(2,1)S(1)} %get-tuple-element.83.m_ref), custom_call_target="tpu_custom_call" | custom-call | flops 679477248 | bytes 4000000 | tf_op jit(solution)/shard_map/full_grad/pallas_call | solution.py:525
  32.1 3.5 %collective-permute-done.7.gmlo_ref = bf16[32,1152]{1,0:T(8,128)(2,1)S(1)} collective-permute-done((bf16[32,1152]{1,0:T(8,128)(2,1)S(1)}, bf16[32,1152]{1,0:T(8,128)(2,1)S(1)}, u32[]{:S(2)}, u32[]{:S(2)}) %collective-permute-start.7) | collective-permute-done | bytes 73760 | tf_op jit(solution)/shard_map/ppermute | solution.py:445
  35.6 2.6 %backward.1 = (bf16[3,2,3,32,384]{4,3,2,1,0:T(8,128)(2,1)S(1)}, bf16[32,1152]{1,0:T(8,128)(2,1)S(1)}, f32[1280,128]{1,0:T(8,128)S(1)}, bf16[640,128]{1,0:T(8,128)(2,1)S(1)}) custom-call(bf16[2,2,2,32,384]{4,3,2,1,0:T(8,128)(2,1)S(1)} %get-tuple-element.74.gm_ref, bf16[32,1152]{1,0:T(8,128)(2,1)S(1)} %collective-permute-done.7.gmlo_ref, ...), custom_call_target="tpu_custom_call" | custom-call | bytes 4000000 | tf_op jit(solution)/shard_map/backward/pallas_call | solution.py:527
  38.2 5.8 %collective-permute-start.9 = (bf16[640,128]{1,0:T(8,128)(2,1)S(1)}, bf16[640,128]{1,0:T(8,128)(2,1)S(1)}, u32[]{:S(2)}, u32[]{:S(2)}) collective-permute-start(bf16[640,128]{1,0:T(8,128)(2,1)S(1)} %get-tuple-element.87), channel_id=1, source_target_pairs={{0,1},{1,0},{2,3},{3,2},{4,5},{5,4},{6,7},{7,6},{8,9},{9,8},{10,11... | collective-permute-start | bytes 491528 | tf_op jit(solution)/shard_map/ppermute | solution.py:440
  44.0 1.0 %collective-permute-done.9.got_ref = bf16[640,128]{1,0:T(8,128)(2,1)S(1)} collective-permute-done((bf16[640,128]{1,0:T(8,128)(2,1)S(1)}, bf16[640,128]{1,0:T(8,128)(2,1)S(1)}, u32[]{:S(2)}, u32[]{:S(2)}) %collective-permute-start.9) | collective-permute-done | bytes 163872 | tf_op jit(solution)/shard_map/ppermute | solution.py:440
  45.1 10.1 %all_to_all.15 = bf16[16,40,128]{2,1,0:T(8,128)(2,1)S(1)} all-to-all(bf16[16,40,128]{2,1,0:T(8,128)(2,1)S(1)} %bitcast.36), channel_id=1, replica_groups={{0,2,32,34,64,66,96,98,128,130,160,162,192,194,224,226},{1,3,33,35,65,6..., dimensions={0} | all-to-all | bytes 327680 | tf_op jit(solution)/shard_map/all_to_all | solution.py:462
  55.8 7.7 %all-to-all-start.1 = ((bf16[8,40,128]{2,1,0:T(8,128)(2,1)}), bf16[8,40,128]{2,1,0:T(8,128)(2,1)S(1)}, u32[]{:S(2)}, u32[]{:S(2)}) async-start(bf16[8,40,128]{2,1,0:T(8,128)(2,1)} %bitcast.12), calls=%async_computation.1 | async-start | bytes 163840 | tf_op jit(solution)/shard_map/all_to_all | solution.py:462
  63.6 0.7 collective-permute-start.10
  64.3 6.8 %all-to-all-done.1 = bf16[8,40,128]{2,1,0:T(8,128)(2,1)S(1)} async-done(((bf16[8,40,128]{2,1,0:T(8,128)(2,1)}), bf16[8,40,128]{2,1,0:T(8,128)(2,1)S(1)}, u32[]{:S(2)}, u32[]{:S(2)}) %all-to-all-start.1) | async-done | bytes 81952 | tf_op jit(solution)/shard_map/all_to_all | solution.py:462
  71.1 0.7 sum.3
  71.8 3.5 %all-to-all-start.2 = ((bf16[16,40,128]{2,1,0:T(8,128)(2,1)}), bf16[16,40,128]{2,1,0:T(8,128)(2,1)S(1)}, u32[]{:S(2)}, u32[]{:S(2)}) async-start(bf16[16,40,128]{2,1,0:T(8,128)(2,1)} %bitcast.14), calls=%async_computation.2 | async-start | bytes 327680 | tf_op jit(solution)/shard_map/all_to_all | solution.py:462
  75.3 1.4 %copy-done.1 = bf16[5,5,5,16,384]{4,3,2,1,0:T(8,128)(2,1)S(1)} copy-done((bf16[5,5,5,16,384]{4,3,2,1,0:T(8,128)(2,1)S(1)}, bf16[5,5,5,16,384]{4,3,2,1,0:T(8,128)(2,1)}, u32[]{:S(2)}) %copy-start.1) | copy-done | bytes 1536024
  76.7 2.0 %volume.1 = bf16[16,8,16,128]{3,2,1,0:T(8,128)(2,1)} custom-call(bf16[3,2,3,32,384]{4,3,2,1,0:T(8,128)(2,1)S(1)} %get-tuple-element.90.ewin_ref, bf16[32,1152]{1,0:T(8,128)(2,1)S(1)} %collective-permute-done.10.next_ref, bf16[5,5,5,16,384]{4,3,2,1,0:T(8,128)(2,1)S(1)} %copy-done.1, bf16[128,256]{1,0:T(8,128)(2,1)S(1)} %get-tuple-element.92.up1_ref, ...), custom_call_target="tpu_custom_call" | custom-call | flops 2097152000 | bytes 4000000 | tf_op jit(solution)/shard_map/volume/pallas_call | solution.py:543
  78.7 3.7 %all-to-all-done.2 = bf16[16,40,128]{2,1,0:T(8,128)(2,1)S(1)} async-done(((bf16[16,40,128]{2,1,0:T(8,128)(2,1)}), bf16[16,40,128]{2,1,0:T(8,128)(2,1)S(1)}, u32[]{:S(2)}, u32[]{:S(2)}) %all-to-all-start.2) | async-done | bytes 163872 | tf_op jit(solution)/shard_map/all_to_all | solution.py:462
  82.4 4.2 %collective-permute-start.11 = (bf16[640,128]{1,0:T(8,128)(2,1)S(1)}, bf16[640,128]{1,0:T(8,128)(2,1)S(1)}, u32[]{:S(2)}, u32[]{:S(2)}) collective-permute-start(bf16[640,128]{1,0:T(8,128)(2,1)S(1)} %bitcast.33), channel_id=1, source_target_pairs={{0,1},{1,0},{2,3},{3,2},{4,5},{5,4},{6,7},{7,6},{8,9},{9,8},{10,11... | collective-permute-start | bytes 491528 | tf_op jit(solution)/shard_map/ppermute | solution.py:440
  86.6 1.0 %collective-permute-done.11.got_ref = bf16[640,128]{1,0:T(8,128)(2,1)S(1)} collective-permute-done((bf16[640,128]{1,0:T(8,128)(2,1)S(1)}, bf16[640,128]{1,0:T(8,128)(2,1)S(1)}, u32[]{:S(2)}, u32[]{:S(2)}) %collective-permute-start.11) | collective-permute-done | bytes 163872 | tf_op jit(solution)/shard_map/ppermute | solution.py:440
  87.6 1.2 %finish.1 = (f32[27,16,32]{2,1,0:T(8,128)}, f32[27,32,64]{2,1,0:T(8,128)}, f32[27,32,64]{2,1,0:T(8,128)}, f32[27,16,32]{2,1,0:T(8,128)}) custom-call(bf16[640,128]{1,0:T(8,128)(2,1)S(1)} %bitcast.34, bf16[640,128]{1,0:T(8,128)(2,1)S(1)} %collective-permute-done.11.got_ref), custom_call_target="tpu_custom_call" | custom-call | bytes 4000000 | tf_op jit(solution)/shard_map/finish/pallas_call | solution.py:547
  (15 shorter events, 1.3 us)
Async XLA Ops:
  3.3 15.9 %collective-permute-start = (bf16[128,1024]{1,0:T(8,128)(2,1)S(1)}, bf16[128,1024]{1,0:T(8,128)(2,1)S(1)}, u32[]{:S(2)}, u32[]{:S(2)}) collective-permute-start(bf16[128,1024]{1,0:T(8,128)(2,1)S(1)} %get-tuple-element.54), channel_id=1, source_target_pairs={{0,32},{32,64},{64,96},{96,128},{128,160},{160,192},{192,224},{224... | collective-permute-start | bytes 786440 | tf_op jit(solution)/shard_map/ppermute | solution.py:445
  5.4 12.5 %collective-permute-start.3 = (bf16[64,128]{1,0:T(8,128)(2,1)S(1)}, bf16[64,128]{1,0:T(8,128)(2,1)S(1)}, u32[]{:S(2)}, u32[]{:S(2)}) collective-permute-start(bf16[64,128]{1,0:T(8,128)(2,1)S(1)} %get-tuple-element.61), channel_id=1, source_target_pairs={{0,33},{1,34},{2,35},{3,36},{4,37},{5,38},{6,39},{7,40},{8,41},{9,... | collective-permute-start | bytes 49160 | tf_op jit(solution)/shard_map/ppermute | solution.py:451
  10.1 7.8 %collective-permute-start.4 = (bf16[64,128]{1,0:T(8,128)(2,1)S(1)}, bf16[64,128]{1,0:T(8,128)(2,1)S(1)}, u32[]{:S(2)}, u32[]{:S(2)}) collective-permute-start(bf16[64,128]{1,0:T(8,128)(2,1)S(1)} %get-tuple-element.62), channel_id=1, source_target_pairs={{0,63},{1,32},{2,33},{3,34},{4,35},{5,36},{6,37},{7,38},{8,39},{9,... | collective-permute-start | bytes 49160 | tf_op jit(solution)/shard_map/ppermute | solution.py:451
  10.1 7.8 %collective-permute-start.1 = (bf16[256,128]{1,0:T(8,128)(2,1)S(1)}, bf16[256,128]{1,0:T(8,128)(2,1)S(1)}, u32[]{:S(2)}, u32[]{:S(2)}) collective-permute-start(bf16[256,128]{1,0:T(8,128)(2,1)S(1)} %get-tuple-element.59), channel_id=1, source_target_pairs={{0,1},{1,2},{2,3},{3,4},{4,5},{5,6},{6,7},{7,8},{8,9},{9,10},{10,1... | collective-permute-start | bytes 196616 | tf_op jit(solution)/shard_map/ppermute | solution.py:445
  14.0 5.2 %collective-permute-start.2 = (bf16[256,128]{1,0:T(8,128)(2,1)S(1)}, bf16[256,128]{1,0:T(8,128)(2,1)S(1)}, u32[]{:S(2)}, u32[]{:S(2)}) collective-permute-start(bf16[256,128]{1,0:T(8,128)(2,1)S(1)} %get-tuple-element.60), channel_id=1, source_target_pairs={{0,31},{1,0},{2,1},{3,2},{4,3},{5,4},{6,5},{7,6},{8,7},{9,8},{10,9... | collective-permute-start | bytes 196616 | tf_op jit(solution)/shard_map/ppermute | solution.py:445
  20.8 7.2 %collective-permute-start.6 = (bf16[2,32,1152]{2,1,0:T(8,128)(2,1)S(1)}, bf16[2,32,1152]{2,1,0:T(8,128)(2,1)S(1)}, u32[]{:S(2)}, u32[]{:S(2)}) collective-permute-start(bf16[2,32,1152]{2,1,0:T(8,128)(2,1)S(1)} %get-tuple-element.68), channel_id=1, source_target_pairs={{0,224},{32,0},{64,32},{96,64},{128,96},{160,128},{192,160},{224,1... | collective-permute-start | bytes 442376 | tf_op jit(solution)/shard_map/ppermute | solution.py:445
  22.6 5.3 %collective-permute-start.5 = (bf16[32,1152]{1,0:T(8,128)(2,1)S(1)}, bf16[32,1152]{1,0:T(8,128)(2,1)S(1)}, u32[]{:S(2)}, u32[]{:S(2)}) collective-permute-start(bf16[32,1152]{1,0:T(8,128)(2,1)S(1)} %get-tuple-element.67), channel_id=1, source_target_pairs={{0,32},{32,64},{64,96},{96,128},{128,160},{160,192},{192,224},{224... | collective-permute-start | bytes 221192 | tf_op jit(solution)/shard_map/ppermute | solution.py:445
  24.1 7.9 %copy-start = (bf16[5,5,5,16,384]{4,3,2,1,0:T(8,128)(2,1)}, bf16[5,5,5,16,384]{4,3,2,1,0:T(8,128)(2,1)S(1)}, u32[]{:S(2)}) copy-start(bf16[5,5,5,16,384]{4,3,2,1,0:T(8,128)(2,1)S(1)} %get-tuple-element.82.cwin_ref) | copy-start | bytes 4608004
  29.2 6.4 %collective-permute-start.8 = (bf16[2,32,1152]{2,1,0:T(8,128)(2,1)S(1)}, bf16[2,32,1152]{2,1,0:T(8,128)(2,1)S(1)}, u32[]{:S(2)}, u32[]{:S(2)}) collective-permute-start(bf16[2,32,1152]{2,1,0:T(8,128)(2,1)S(1)} %get-tuple-element.76), channel_id=1, source_target_pairs={{0,224},{32,0},{64,32},{96,64},{128,96},{160,128},{192,160},{224,1... | collective-permute-start | bytes 442376 | tf_op jit(solution)/shard_map/ppermute | solution.py:445
  30.3 5.3 %collective-permute-start.7 = (bf16[32,1152]{1,0:T(8,128)(2,1)S(1)}, bf16[32,1152]{1,0:T(8,128)(2,1)S(1)}, u32[]{:S(2)}, u32[]{:S(2)}) collective-permute-start(bf16[32,1152]{1,0:T(8,128)(2,1)S(1)} %get-tuple-element.75), channel_id=1, source_target_pairs={{0,32},{32,64},{64,96},{96,128},{128,160},{160,192},{192,224},{224... | collective-permute-start | bytes 221192 | tf_op jit(solution)/shard_map/ppermute | solution.py:445
  38.2 6.9 %collective-permute-start.9 = (bf16[640,128]{1,0:T(8,128)(2,1)S(1)}, bf16[640,128]{1,0:T(8,128)(2,1)S(1)}, u32[]{:S(2)}, u32[]{:S(2)}) collective-permute-start(bf16[640,128]{1,0:T(8,128)(2,1)S(1)} %get-tuple-element.87), channel_id=1, source_target_pairs={{0,1},{1,0},{2,3},{3,2},{4,5},{5,4},{6,7},{7,6},{8,9},{9,8},{10,11... | collective-permute-start | bytes 491528 | tf_op jit(solution)/shard_map/ppermute | solution.py:440
  55.8 15.2 %all-to-all-start.1 = ((bf16[8,40,128]{2,1,0:T(8,128)(2,1)}), bf16[8,40,128]{2,1,0:T(8,128)(2,1)S(1)}, u32[]{:S(2)}, u32[]{:S(2)}) async-start(bf16[8,40,128]{2,1,0:T(8,128)(2,1)} %bitcast.12), calls=%async_computation.1 | async-start | bytes 163840 | tf_op jit(solution)/shard_map/all_to_all | solution.py:462
  63.6 8.2 %collective-permute-start.10 = (bf16[32,1152]{1,0:T(8,128)(2,1)S(1)}, bf16[32,1152]{1,0:T(8,128)(2,1)S(1)}, u32[]{:S(2)}, u32[]{:S(2)}) collective-permute-start(bf16[32,1152]{1,0:T(8,128)(2,1)S(1)} %get-tuple-element.88), channel_id=1, source_target_pairs={{0,224},{32,0},{64,32},{96,64},{128,96},{160,128},{192,160},{224,1... | collective-permute-start | bytes 221192 | tf_op jit(solution)/shard_map/ppermute | solution.py:445
  71.8 10.6 %all-to-all-start.2 = ((bf16[16,40,128]{2,1,0:T(8,128)(2,1)}), bf16[16,40,128]{2,1,0:T(8,128)(2,1)S(1)}, u32[]{:S(2)}, u32[]{:S(2)}) async-start(bf16[16,40,128]{2,1,0:T(8,128)(2,1)} %bitcast.14), calls=%async_computation.2 | async-start | bytes 327680 | tf_op jit(solution)/shard_map/all_to_all | solution.py:462
  75.3 1.4 %copy-start.1 = (bf16[5,5,5,16,384]{4,3,2,1,0:T(8,128)(2,1)S(1)}, bf16[5,5,5,16,384]{4,3,2,1,0:T(8,128)(2,1)}, u32[]{:S(2)}) copy-start(bf16[5,5,5,16,384]{4,3,2,1,0:T(8,128)(2,1)} %copy-done) | copy-start | bytes 4608004
  82.4 5.2 %collective-permute-start.11 = (bf16[640,128]{1,0:T(8,128)(2,1)S(1)}, bf16[640,128]{1,0:T(8,128)(2,1)S(1)}, u32[]{:S(2)}, u32[]{:S(2)}) collective-permute-start(bf16[640,128]{1,0:T(8,128)(2,1)S(1)} %bitcast.33), channel_id=1, source_target_pairs={{0,1},{1,0},{2,3},{3,2},{4,5},{5,4},{6,7},{7,6},{8,9},{9,8},{10,11... | collective-permute-start | bytes 491528 | tf_op jit(solution)/shard_map/ppermute | solution.py:440

commit v7 on v6

--- a/solution.py
+++ b/solution.py
@@ -30,16 +30,13 @@
     return jnp.where(condition, 1.0, 0.0).astype(BF)
 
 
-def tables_kernel(spread_ref, rims_ref, place_ref, order_ref):
+def lane_tables(spread_ref, place_ref):
     w, lane = iota((128, 256), 0), iota((128, 256), 1)
     for phase in range(4):
         apart = jnp.where((w & 3) == phase, lane - (w >> 2), -LANES)
         for d in range(QD):
             block = ones_where(apart == lane_of(d, 0) - (0 if d < 6 else 128))
             spread_ref[d * 128 : (d + 1) * 128, phase * 256 : (phase + 1) * 256] = block
-    slot, row = iota((QD * 128, 128), 1), iota((QD * 128, 128), 0)
-    column = (slot & 1) + jnp.where(slot >= 64, QC - 2, 0)
-    rims_ref[...] = ones_where(row == ((slot >> 1) & 7) * 128 + 4 * column + ((slot >> 4) & 3))
     place_ref[...] = jnp.zeros(place_ref.shape, BF)
     slot, lane = iota((16, LANES), 0), iota((16, LANES), 1)
     for side in range(2):
@@ -48,6 +45,12 @@
             for phase in range(4):
                 row = side * 128 + array * 64 + phase * 16
                 place_ref[array, row : row + 16, phase * LANES : (phase + 1) * LANES] = block
+
+
+def row_tables(rims_ref, order_ref):
+    slot, row = iota((QD * 128, 128), 1), iota((QD * 128, 128), 0)
+    column = (slot & 1) + jnp.where(slot >= 64, QC - 2, 0)
+    rims_ref[...] = ones_where(row == ((slot >> 1) & 7) * 128 + 4 * column + ((slot >> 4) & 3))
     row, column = iota((256, 256), 0), iota((256, 256), 1)
     order_ref[...] = ones_where(column == (row & 15) * 16 + ((row >> 4) & 3) * 4 + (row >> 6))
 
@@ -91,8 +94,9 @@
     return copies
 
 
-def edge_kernel(vol_ref, cot_ref, order_ref, rims_ref, vol_rows_ref, cot_rows_ref, main_ref, first_ref, last_ref, first_low_ref, last_low_ref, vol_here, cot_here, sems):
+def edge_kernel(vol_ref, cot_ref, order_ref, vol_rows_ref, cot_rows_ref, main_ref, first_ref, last_ref, first_low_ref, last_low_ref, vol_here, cot_here, rims_ref, sems):
     copies = fetch(((vol_ref, vol_here), (cot_ref, cot_here)), sems)
+    row_tables(rims_ref, order_ref)
     edges = []
     for i, (here, rows_ref) in enumerate(((vol_here, vol_rows_ref), (cot_here, cot_rows_ref))):
         copies[i].wait()
@@ -106,7 +110,8 @@
     last_low_ref[...] = last_ref[192:256]
 
 
-def own_kernel(vol_rows_ref, cot_rows_ref, spread_ref, yv_ref, yc_ref):
+def own_kernel(vol_rows_ref, cot_rows_ref, yv_ref, yc_ref, spread_ref, place_ref):
+    lane_tables(spread_ref, place_ref)
     yv_ref[...] = to_lanes(vol_rows_ref[...], spread_ref).astype(BF)
     yc_ref[...] = to_lanes(cot_rows_ref[...], spread_ref).astype(BF)
 
@@ -445,6 +450,13 @@
     return lax.ppermute(value, axis, [(i, (i + steps) % count) for i in range(count)])
 
 
+def tree_sum(terms):
+    terms = [term.astype(F32) for term in terms]
+    while len(terms) > 1:
+        terms = [low + high for low, high in zip(terms[::2], terms[1::2])]
+    return terms[0]
+
+
 def diagonal(value, row_step, col_step):
     rows, cols = lax.axis_size("row"), lax.axis_size("col")
     pairs = [(r * cols + c, (r + row_step) % rows * cols + (c + col_step) % cols) for r in range(rows) for c in range(cols)]
@@ -481,23 +493,23 @@
     rows, cols = lax.axis_size("row"), lax.axis_size("col")
     cells = volume.size // volume.shape[0] * rows * cols
     scale = 1.0 / math.sqrt(cells)
-    spread, rims, place, order = call(
-        tables_kernel,
-        [((QD * 128, 1024), BF), ((QD * 128, 128), BF), ((2, 256, 4 * LANES), BF), ((256, 256), BF)],
-        name="tables",
-    )()
     vol = volume.reshape(16, QD, 16, 128)
     cot = cotangent.reshape(16, QD, 16, 128)
-    vol_rows, cot_rows, main, first, last, first_low, last_low = call(
+    order, vol_rows, cot_rows, main, first, last, first_low, last_low = call(
         edge_kernel,
-        [((256, 1024), BF), ((256, 1024), BF), ((128, 1024), BF), ((256, 128), BF), ((256, 128), BF), ((64, 128), BF), ((64, 128), BF)],
-        [pltpu.VMEM(vol.shape, BF), pltpu.VMEM(cot.shape, BF), pltpu.SemaphoreType.DMA((2,))],
-        far=(2, 2),
+        [((256, 256), BF), ((256, 1024), BF), ((256, 1024), BF), ((128, 1024), BF), ((256, 128), BF), ((256, 128), BF), ((64, 128), BF), ((64, 128), BF)],
+        [pltpu.VMEM(vol.shape, BF), pltpu.VMEM(cot.shape, BF), pltpu.VMEM((QD * 128, 128), BF), pltpu.SemaphoreType.DMA((2,))],
+        far=(2, 0),
         name="edge",
-    )(held(vol), held(cot), order, rims)
+    )(held(vol), held(cot))
     main_lo = shifted(main, "row", 1)
     edges = [shifted(last, "col", 1), shifted(first, "col", -1), diagonal(last_low, 1, 1), diagonal(first_low, 1, -1)]
-    yv, yc = call(own_kernel, [((256, 4 * LANES), BF), ((256, 4 * LANES), BF)], flops=2 * 256 * 1024 * 4000, name="own")(vol_rows, cot_rows, spread)
+    yv, yc, spread, place = call(
+        own_kernel,
+        [((256, 4 * LANES), BF), ((256, 4 * LANES), BF), ((QD * 128, 1024), BF), ((2, 256, 4 * LANES), BF)],
+        flops=2 * 256 * 1024 * 4000,
+        name="own",
+    )(vol_rows, cot_rows)
     weights = by_tap(w_half, True), by_tap(w_quarter, True), by_tap(w_back_half, False), by_tap(w_back_full, False)
     w1, w2, w3, w4, up1, up2, up3, mask = call(
         prepare_kernel,
@@ -532,14 +544,17 @@
     )(gm, gm_lo, gm_hi, vwin, hwin, preh, preq, quarter, g4, mask, w3, up2)
     (part,) = call(functools.partial(fold_kernel, core), [((PACK // 2, 128), BF)], name="fold")(kept, swapped(send, 0, 1))
     gh_next = shifted(gh_first, "row", -1)
-    along = [(7 & (rows - 1), 2 & (cols - 1)), (0, 28 & (cols - 1))]
-    sizes = [2 ** (r.bit_count() + c.bit_count()) for r, c in along]
-    share = PACK // 2 // sizes[0]
-    for bits, size, later in zip(along, sizes, sizes[::-1]):
-        part = exchanged(part.reshape(size, share, 128), *bits).reshape(size * share, 128)
-        (part,) = call(functools.partial(sum_kernel, size, later), [((later * share, 128), BF)], name="sum")(part)
+    near = (7 & (rows - 1), 2 & (cols - 1))
+    size = 2 ** sum(bits.bit_count() for bits in near)
+    share = PACK // 2 // size
+    part = exchanged(part.reshape(size, share, 128), *near).reshape(size * share, 128)
+    (part,) = call(functools.partial(sum_kernel, size, 1), [((share, 128), BF)], name="sum")(part)
+    for steps in ((4,), (8, 16, 24)):
+        if max(steps) < cols:
+            part = tree_sum([part] + [swapped(part, 0, step) for step in steps]).astype(BF)
+    (part,) = call(functools.partial(sum_kernel, 1, size), [((size * share, 128), BF)], name="copies")(part)
     part, gh_next = lax.optimization_barrier((part, gh_next))
-    part = exchanged(part.reshape(sizes[0], share, 128), *along[0]).reshape(PACK // 2, 128)
+    part = exchanged(part.reshape(size, share, 128), *near).reshape(PACK // 2, 128)
     (grad_volume,) = call(
         volume_kernel, [((16, QD, 16, 128), BF)], [pltpu.VMEM((256, 4 * LANES), BF), pltpu.VMEM((3, 3, 32, LANES), BF)], flops=2 * 256 * 1024 * 4000, name="volume"
     )(ewin, gh_next, cwin, up1, spread, order)

time: 89.2 us -> 88 us (0.987)
  waiting for transfers between devices: 21.1 us -> 19.7 us
  starting transfers between devices: 37.2 us -> 38.5 us
  Pallas kernels: 18.3 us -> 17.2 us
    ppermute x2 -> x6, starting transfers between devices: 10 us -> 18.9 us  [swapped(): return lax.ppermute(value, ('row', 'col'), pairs)]
    all_to_all x2 -> x1, starting transfers between devices: 11.3 us -> 3.63 us  [exchanged(): lax.all_to_all(value, ('row', 'col'), 0, 0, axis_index_groups=list(groups...]
    all_to_all x2 -> x1, waiting for transfers between devices: 10.5 us -> 3.77 us  [exchanged(): lax.all_to_all(value, ('row', 'col'), 0, 0, axis_index_groups=list(groups...]
    ppermute x2 -> x6, waiting for transfers between devices: 2.06 us -> 7.53 us  [swapped(): return lax.ppermute(value, ('row', 'col'), pairs)]
    pallas_call x5 -> x4, Pallas kernels: 5.26 us -> 4.18 us  [the longest x1 2.03 us: shards(): call(edge_kernel, [((256, 256), BF), ((256, 1024), BF), ((256, 1024), BF)...]
  transfers between devices with their start and end apart: 14 -> 17, of which waited for: 7 -> 8; matrix products, arithmetic and copies ran while one was open for 0% -> 0% of each run, Pallas kernels for 9% -> 10%
where the time goes in v7:
time: 88 us; the launch traced here: 87.8 us
  starting transfers between devices  38.5 us (44%)
  waiting for transfers between devices  19.7 us (22%)
  Pallas kernels  17.2 us (20%)
  blocking collectives  10.1 us (11%)
  local copies, waits for them, and re-layouts  1.39 us (2%)
    ppermute x6, starting transfers between devices, swapped(): return lax.ppermute(value, ('row', 'col'), pairs)  18.9 us
    ppermute x8, starting transfers between devices, shifted(): lax.ppermute(value, axis, [(i, (i + steps) % count) for i in range(count)])  11.3 us
    all_to_all x1, blocking collectives, exchanged(): lax.all_to_all(value, ('row', 'col'), 0, 0, axis_index_groups=list(groups...  10.1 us
    ppermute x8, waiting for transfers between devices, shifted(): lax.ppermute(value, axis, [(i, (i + steps) % count) for i in range(count)])  8.43 us
    ppermute x6, waiting for transfers between devices, swapped(): return lax.ppermute(value, ('row', 'col'), pairs)  7.53 us
    ppermute x2, starting transfers between devices, diagonal(): return lax.ppermute(value, ('row', 'col'), pairs)  4.69 us
    all_to_all x1, waiting for transfers between devices, exchanged(): lax.all_to_all(value, ('row', 'col'), 0, 0, axis_index_groups=list(groups...  3.77 us
    all_to_all x1, starting transfers between devices, exchanged(): lax.all_to_all(value, ('row', 'col'), 0, 0, axis_index_groups=list(groups...  3.63 us
  transfers between devices with their start and end apart: 17, of which 8 were waited for; matrix products, arithmetic and copies ran while one was open for 0% of the time, Pallas kernels for 10%

profile of v7, /device:TPU:1, one launch (start us, length us, event | category | flops | bytes accessed | tf_op | source)
XLA Modules:
  0.0 87.8 jit_solution(1692590268609541585)
XLA Ops:
  0.6 2.0 %edge.1 = (bf16[256,256]{1,0:T(8,128)(2,1)S(1)}, bf16[256,1024]{1,0:T(8,128)(2,1)S(1)}, bf16[256,1024]{1,0:T(8,128)(2,1)S(1)}, bf16[128,1024]{1,0:T(8,128)(2,1)S...) custom-call(bf16[16,8,16,128]{3,2,1,0:T(8,128)(2,1)} %bitcast.35, ...), custom_call_target="tpu_custom_call" | custom-call | bytes 4000000 | tf_op jit(solution)/shard_map/edge/pallas_call | solution.py:498
  2.7 2.1 %collective-permute-start = (bf16[128,1024]{1,0:T(8,128)(2,1)S(1)}, bf16[128,1024]{1,0:T(8,128)(2,1)S(1)}, u32[]{:S(2)}, u32[]{:S(2)}) collective-permute-start(bf16[128,1024]{1,0:T(8,128)(2,1)S(1)} %get-tuple-element.51), channel_id=1, source_target_pairs={{0,32},{32,64},{64,96},{96,128},{128,160},{160,192},{192,224},{224... | collective-permute-start | bytes 786440 | tf_op jit(solution)/shard_map/ppermute | solution.py:450
  4.8 4.7 %collective-permute-start.3 = (bf16[64,128]{1,0:T(8,128)(2,1)S(1)}, bf16[64,128]{1,0:T(8,128)(2,1)S(1)}, u32[]{:S(2)}, u32[]{:S(2)}) collective-permute-start(bf16[64,128]{1,0:T(8,128)(2,1)S(1)} %get-tuple-element.57), channel_id=1, source_target_pairs={{0,33},{1,34},{2,35},{3,36},{4,37},{5,38},{6,39},{7,40},{8,41},{9,... | collective-permute-start | bytes 49160 | tf_op jit(solution)/shard_map/ppermute | solution.py:463
  9.5 3.9 %collective-permute-start.1 = (bf16[256,128]{1,0:T(8,128)(2,1)S(1)}, bf16[256,128]{1,0:T(8,128)(2,1)S(1)}, u32[]{:S(2)}, u32[]{:S(2)}) collective-permute-start(bf16[256,128]{1,0:T(8,128)(2,1)S(1)} %get-tuple-element.55), channel_id=1, source_target_pairs={{0,1},{1,2},{2,3},{3,4},{4,5},{5,6},{6,7},{7,8},{8,9},{9,10},{10,1... | collective-permute-start | bytes 196616 | tf_op jit(solution)/shard_map/ppermute | solution.py:450
  13.4 1.0 %collective-permute-start.2 = (bf16[256,128]{1,0:T(8,128)(2,1)S(1)}, bf16[256,128]{1,0:T(8,128)(2,1)S(1)}, u32[]{:S(2)}, u32[]{:S(2)}) collective-permute-start(bf16[256,128]{1,0:T(8,128)(2,1)S(1)} %get-tuple-element.56), channel_id=1, source_target_pairs={{0,31},{1,0},{2,1},{3,2},{4,3},{5,4},{6,5},{7,6},{8,7},{9,8},{10,9... | collective-permute-start | bytes 196616 | tf_op jit(solution)/shard_map/ppermute | solution.py:450
  14.3 1.4 %own.1 = (bf16[256,1536]{1,0:T(8,128)(2,1)S(1)}, bf16[256,1536]{1,0:T(8,128)(2,1)S(1)}, bf16[1024,1024]{1,0:T(8,128)(2,1)S(1)}, bf16[2,256,1536]{2,1,0:T(8,128)(2,1)S(1)}) custom-call(bf16[256,1024]{1,0:T(8,128)(2,1)S(1)} %get-tuple-element.52.vol_rows_ref, bf16[256,1024]{1,0:T(8,128)(2,1)S(1)} %get-tuple-element.53.cot_rows_ref), custom_call_target="tpu_custom_call" | custom-call | flops 2097152000 | bytes 4000000 | tf_op jit(solution)/shard_map/own/pallas_call | solution.py:507
  15.8 1.6 %prepare.1 = (bf16[32,432]{1,0:T(8,128)(2,1)S(1)}, bf16[64,864]{1,0:T(8,128)(2,1)S(1)}, bf16[64,864]{1,0:T(8,128)(2,1)S(1)}, bf16[32,432]{1,0:T(8,128)(2,1)S(1)}...) custom-call(bf16[27,16,32]{2,1,0:T(8,128)(2,1)} %bitcast.39, ...), custom_call_target="tpu_custom_call" | custom-call | bytes 4000000 | tf_op jit(solution)/shard_map/prepare/pallas_call | solution.py:514
  17.4 1.1 %collective-permute-done.2.right_ref = bf16[256,128]{1,0:T(8,128)(2,1)S(1)} collective-permute-done((bf16[256,128]{1,0:T(8,128)(2,1)S(1)}, bf16[256,128]{1,0:T(8,128)(2,1)S(1)}, u32[]{:S(2)}, u32[]{:S(2)}) %collective-permute-start.2) | collective-permute-done | bytes 65568 | tf_op jit(solution)/shard_map/ppermute | solution.py:450
  18.6 1.6 %half.1 = (bf16[5,5,5,16,384]{4,3,2,1,0:T(8,128)(2,1)S(1)}, f32[2,2,2,32,384]{4,3,2,1,0:T(8,128)S(1)}, bf16[2,2,2,32,384]{4,3,2,1,0:T(8,128)(2,1)S(1)}, bf16[2,3...) custom-call(bf16[128,1024]{1,0:T(8,128)(2,1)S(1)} %collective-permute-done.main_ref, ...), custom_call_target="tpu_custom_call" | custom-call | bytes 4000000 | tf_op jit(solution)/shard_map/half/pallas_call | solution.py:522
  20.2 1.8 %collective-permute-start.6 = (bf16[2,32,1152]{2,1,0:T(8,128)(2,1)S(1)}, bf16[2,32,1152]{2,1,0:T(8,128)(2,1)S(1)}, u32[]{:S(2)}, u32[]{:S(2)}) collective-permute-start(bf16[2,32,1152]{2,1,0:T(8,128)(2,1)S(1)} %get-tuple-element.65), channel_id=1, source_target_pairs={{0,224},{32,0},{64,32},{96,64},{128,96},{160,128},{192,160},{224,1... | collective-permute-start | bytes 442376 | tf_op jit(solution)/shard_map/ppermute | solution.py:450
  22.0 1.5 %cotangent.1 = (bf16[5,5,5,16,384]{4,3,2,1,0:T(8,128)(2,1)S(1)}, f32[8,32,384]{2,1,0:T(8,128)S(1)}) custom-call(bf16[128,1024]{1,0:T(8,128)(2,1)S(1)} %collective-permute-done.main_ref, bf16[256,1536]{1,0:T(8,128)(2,1)S(1)} %get-tuple-element.66.yc_ref, bf16[256,128]{1,0:T(8,128)(2,1)S(1)} %collective-permute-done.1.left_ref, ...), custom_call_target="tpu_custom_call" | custom-call | flops 679477248 | bytes 4000000 | tf_op jit(solution)/shard_map/cotangent/pallas_call | solution.py:528
  23.5 3.8 %collective-permute-done.5.hlo_ref = bf16[32,1152]{1,0:T(8,128)(2,1)S(1)} collective-permute-done((bf16[32,1152]{1,0:T(8,128)(2,1)S(1)}, bf16[32,1152]{1,0:T(8,128)(2,1)S(1)}, u32[]{:S(2)}, u32[]{:S(2)}) %collective-permute-start.5) | collective-permute-done | bytes 73760 | tf_op jit(solution)/shard_map/ppermute | solution.py:450
  27.3 1.3 %middle.1 = (bf16[3,5,3,32,384]{4,3,2,1,0:T(8,128)(2,1)S(1)}, f32[2,64,384]{2,1,0:T(8,128)S(1)}, bf16[64,384]{1,0:T(8,128)(2,1)S(1)}, bf16[8,32,384]{2,1,0:T(8,1...) custom-call(bf16[2,2,2,32,384]{4,3,2,1,0:T(8,128)(2,1)S(1)} %get-tup, ...), custom_call_target="tpu_custom_call" | custom-call | bytes 4000000 | tf_op jit(solution)/shard_map/middle/pallas_call | solution.py:531
  28.6 1.0 %collective-permute-start.8 = (bf16[2,32,1152]{2,1,0:T(8,128)(2,1)S(1)}, bf16[2,32,1152]{2,1,0:T(8,128)(2,1)S(1)}, u32[]{:S(2)}, u32[]{:S(2)}) collective-permute-start(bf16[2,32,1152]{2,1,0:T(8,128)(2,1)S(1)} %get-tuple-element.73), channel_id=1, source_target_pairs={{0,224},{32,0},{64,32},{96,64},{128,96},{160,128},{192,160},{224,1... | collective-permute-start | bytes 442376 | tf_op jit(solution)/shard_map/ppermute | solution.py:450
  30.3 1.1 %full_grad.1.g4_ref = f32[112,128]{1,0:T(8,128)S(1)} custom-call(bf16[5,5,5,16,384]{4,3,2,1,0:T(8,128)(2,1)S(1)} %get-tuple-element.79.cwin_ref, bf16[8,32,384]{2,1,0:T(8,128)(2,1)S(1)} %get-tuple-element.80.m_ref), custom_call_target="tpu_custom_call" | custom-call | flops 679477248 | bytes 4000000 | tf_op jit(solution)/shard_map/full_grad/pallas_call | solution.py:537
  31.5 3.5 %collective-permute-done.7.gmlo_ref = bf16[32,1152]{1,0:T(8,128)(2,1)S(1)} collective-permute-done((bf16[32,1152]{1,0:T(8,128)(2,1)S(1)}, bf16[32,1152]{1,0:T(8,128)(2,1)S(1)}, u32[]{:S(2)}, u32[]{:S(2)}) %collective-permute-start.7) | collective-permute-done | bytes 73760 | tf_op jit(solution)/shard_map/ppermute | solution.py:450
  35.0 2.6 %backward.1 = (bf16[3,2,3,32,384]{4,3,2,1,0:T(8,128)(2,1)S(1)}, bf16[32,1152]{1,0:T(8,128)(2,1)S(1)}, f32[1280,128]{1,0:T(8,128)S(1)}, bf16[640,128]{1,0:T(8,128)(2,1)S(1)}) custom-call(bf16[2,2,2,32,384]{4,3,2,1,0:T(8,128)(2,1)S(1)} %get-tuple-element.71.gm_ref, bf16[32,1152]{1,0:T(8,128)(2,1)S(1)} %collective-permute-done.7.gmlo_ref, ...), custom_call_target="tpu_custom_call" | custom-call | bytes 4000000 | tf_op jit(solution)/shard_map/backward/pallas_call | solution.py:539
  37.6 6.0 %collective-permute-start.9 = (bf16[640,128]{1,0:T(8,128)(2,1)S(1)}, bf16[640,128]{1,0:T(8,128)(2,1)S(1)}, u32[]{:S(2)}, u32[]{:S(2)}) collective-permute-start(bf16[640,128]{1,0:T(8,128)(2,1)S(1)} %get-tuple-element.84), channel_id=1, source_target_pairs={{0,1},{1,0},{2,3},{3,2},{4,5},{5,4},{6,7},{7,6},{8,9},{9,8},{10,11... | collective-permute-start | bytes 491528 | tf_op jit(solution)/shard_map/ppermute | solution.py:445
  43.6 1.0 %collective-permute-done.9.got_ref = bf16[640,128]{1,0:T(8,128)(2,1)S(1)} collective-permute-done((bf16[640,128]{1,0:T(8,128)(2,1)S(1)}, bf16[640,128]{1,0:T(8,128)(2,1)S(1)}, u32[]{:S(2)}, u32[]{:S(2)}) %collective-permute-start.9) | collective-permute-done | bytes 163872 | tf_op jit(solution)/shard_map/ppermute | solution.py:445
  44.6 10.1 %all_to_all.10 = bf16[16,40,128]{2,1,0:T(8,128)(2,1)S(1)} all-to-all(bf16[16,40,128]{2,1,0:T(8,128)(2,1)S(1)} %bitcast.34), channel_id=1, replica_groups={{0,2,32,34,64,66,96,98,128,130,160,162,192,194,224,226},{1,3,33,35,65,6..., dimensions={0} | all-to-all | bytes 327680 | tf_op jit(solution)/shard_map/all_to_all | solution.py:474
  54.8 2.5 %collective-permute-done.10 = bf16[40,128]{1,0:T(8,128)(2,1)S(1)} collective-permute-done((bf16[40,128]{1,0:T(8,128)(2,1)S(1)}, bf16[40,128]{1,0:T(8,128)(2,1)S(1)}, u32[]{:S(2)}, u32[]{:S(2)}) %collective-permute-start.10) | collective-permute-done | bytes 10272 | tf_op jit(solution)/shard_map/ppermute | solution.py:445
  57.4 4.6 %collective-permute-start.13 = (bf16[40,128]{1,0:T(8,128)(2,1)S(1)}, bf16[40,128]{1,0:T(8,128)(2,1)S(1)}, u32[]{:S(2)}, u32[]{:S(2)}) collective-permute-start(bf16[40,128]{1,0:T(8,128)(2,1)S(1)} %add_convert_fusion.1), channel_id=1, source_target_pairs={{0,24},{1,25},{2,26},{3,27},{4,28},{5,29},{6,30},{7,31},{8,16},{9,... | collective-permute-start | bytes 30728 | tf_op jit(solution)/shard_map/ppermute | solution.py:445
  61.9 2.8 %collective-permute-start.12 = (bf16[40,128]{1,0:T(8,128)(2,1)S(1)}, bf16[40,128]{1,0:T(8,128)(2,1)S(1)}, u32[]{:S(2)}, u32[]{:S(2)}) collective-permute-start(bf16[40,128]{1,0:T(8,128)(2,1)S(1)} %add_convert_fusion.1), channel_id=1, source_target_pairs={{0,16},{1,17},{2,18},{3,19},{4,20},{5,21},{6,22},{7,23},{8,24},{9,... | collective-permute-start | bytes 30728 | tf_op jit(solution)/shard_map/ppermute | solution.py:445
  64.8 0.7 collective-permute-start.14
  65.5 3.0 %collective-permute-done.12 = bf16[40,128]{1,0:T(8,128)(2,1)S(1)} collective-permute-done((bf16[40,128]{1,0:T(8,128)(2,1)S(1)}, bf16[40,128]{1,0:T(8,128)(2,1)S(1)}, u32[]{:S(2)}, u32[]{:S(2)}) %collective-permute-start.12) | collective-permute-done | bytes 10272 | tf_op jit(solution)/shard_map/ppermute | solution.py:445
  69.2 3.6 %all-to-all-start.1 = ((bf16[16,40,128]{2,1,0:T(8,128)(2,1)}), bf16[16,40,128]{2,1,0:T(8,128)(2,1)S(1)}, u32[]{:S(2)}, u32[]{:S(2)}) async-start(bf16[16,40,128]{2,1,0:T(8,128)(2,1)} %bitcast.12), calls=%async_computation.1 | async-start | bytes 327680 | tf_op jit(solution)/shard_map/all_to_all | solution.py:474
  72.8 1.4 %copy-done.1 = bf16[5,5,5,16,384]{4,3,2,1,0:T(8,128)(2,1)S(1)} copy-done((bf16[5,5,5,16,384]{4,3,2,1,0:T(8,128)(2,1)S(1)}, bf16[5,5,5,16,384]{4,3,2,1,0:T(8,128)(2,1)}, u32[]{:S(2)}) %copy-start.1) | copy-done | bytes 1536024
  74.2 2.0 %volume.1 = bf16[16,8,16,128]{3,2,1,0:T(8,128)(2,1)} custom-call(bf16[3,2,3,32,384]{4,3,2,1,0:T(8,128)(2,1)S(1)} %get-tuple-element.87.ewin_ref, bf16[32,1152]{1,0:T(8,128)(2,1)S(1)} %collective-permute-done.14.next_ref, bf16[5,5,5,16,384]{4,3,2,1,0:T(8,128)(2,1)S(1)} %copy-done.1, bf16[128,256]{1,0:T(8,128)(2,1)S(1)} %get-tuple-element.89.up1_ref, ...), custom_call_target="tpu_custom_call" | custom-call | flops 2097152000 | bytes 4000000 | tf_op jit(solution)/shard_map/volume/pallas_call | solution.py:558
  76.2 3.8 %all-to-all-done.1 = bf16[16,40,128]{2,1,0:T(8,128)(2,1)S(1)} async-done(((bf16[16,40,128]{2,1,0:T(8,128)(2,1)}), bf16[16,40,128]{2,1,0:T(8,128)(2,1)S(1)}, u32[]{:S(2)}, u32[]{:S(2)}) %all-to-all-start.1) | async-done | bytes 163872 | tf_op jit(solution)/shard_map/all_to_all | solution.py:474
  80.0 5.5 %collective-permute-start.15 = (bf16[640,128]{1,0:T(8,128)(2,1)S(1)}, bf16[640,128]{1,0:T(8,128)(2,1)S(1)}, u32[]{:S(2)}, u32[]{:S(2)}) collective-permute-start(bf16[640,128]{1,0:T(8,128)(2,1)S(1)} %bitcast.31), channel_id=1, source_target_pairs={{0,1},{1,0},{2,3},{3,2},{4,5},{5,4},{6,7},{7,6},{8,9},{9,8},{10,11... | collective-permute-start | bytes 491528 | tf_op jit(solution)/shard_map/ppermute | solution.py:445
  85.5 1.0 %collective-permute-done.15.got_ref = bf16[640,128]{1,0:T(8,128)(2,1)S(1)} collective-permute-done((bf16[640,128]{1,0:T(8,128)(2,1)S(1)}, bf16[640,128]{1,0:T(8,128)(2,1)S(1)}, u32[]{:S(2)}, u32[]{:S(2)}) %collective-permute-start.15) | collective-permute-done | bytes 163872 | tf_op jit(solution)/shard_map/ppermute | solution.py:445
  86.5 1.2 %finish.1 = (f32[27,16,32]{2,1,0:T(8,128)}, f32[27,32,64]{2,1,0:T(8,128)}, f32[27,32,64]{2,1,0:T(8,128)}, f32[27,16,32]{2,1,0:T(8,128)}) custom-call(bf16[640,128]{1,0:T(8,128)(2,1)S(1)} %bitcast.32, bf16[640,128]{1,0:T(8,128)(2,1)S(1)} %collective-permute-done.15.got_ref), custom_call_target="tpu_custom_call" | custom-call | bytes 4000000 | tf_op jit(solution)/shard_map/finish/pallas_call | solution.py:562
  (22 shorter events, 1.6 us)
Async XLA Ops:
  2.7 15.9 %collective-permute-start = (bf16[128,1024]{1,0:T(8,128)(2,1)S(1)}, bf16[128,1024]{1,0:T(8,128)(2,1)S(1)}, u32[]{:S(2)}, u32[]{:S(2)}) collective-permute-start(bf16[128,1024]{1,0:T(8,128)(2,1)S(1)} %get-tuple-element.51), channel_id=1, source_target_pairs={{0,32},{32,64},{64,96},{96,128},{128,160},{160,192},{192,224},{224... | collective-permute-start | bytes 786440 | tf_op jit(solution)/shard_map/ppermute | solution.py:450
  4.8 12.6 %collective-permute-start.3 = (bf16[64,128]{1,0:T(8,128)(2,1)S(1)}, bf16[64,128]{1,0:T(8,128)(2,1)S(1)}, u32[]{:S(2)}, u32[]{:S(2)}) collective-permute-start(bf16[64,128]{1,0:T(8,128)(2,1)S(1)} %get-tuple-element.57), channel_id=1, source_target_pairs={{0,33},{1,34},{2,35},{3,36},{4,37},{5,38},{6,39},{7,40},{8,41},{9,... | collective-permute-start | bytes 49160 | tf_op jit(solution)/shard_map/ppermute | solution.py:463
  9.5 7.9 %collective-permute-start.4 = (bf16[64,128]{1,0:T(8,128)(2,1)S(1)}, bf16[64,128]{1,0:T(8,128)(2,1)S(1)}, u32[]{:S(2)}, u32[]{:S(2)}) collective-permute-start(bf16[64,128]{1,0:T(8,128)(2,1)S(1)} %get-tuple-element.58), channel_id=1, source_target_pairs={{0,63},{1,32},{2,33},{3,34},{4,35},{5,36},{6,37},{7,38},{8,39},{9,... | collective-permute-start | bytes 49160 | tf_op jit(solution)/shard_map/ppermute | solution.py:463
  9.5 7.9 %collective-permute-start.1 = (bf16[256,128]{1,0:T(8,128)(2,1)S(1)}, bf16[256,128]{1,0:T(8,128)(2,1)S(1)}, u32[]{:S(2)}, u32[]{:S(2)}) collective-permute-start(bf16[256,128]{1,0:T(8,128)(2,1)S(1)} %get-tuple-element.55), channel_id=1, source_target_pairs={{0,1},{1,2},{2,3},{3,4},{4,5},{5,6},{6,7},{7,8},{8,9},{9,10},{10,1... | collective-permute-start | bytes 196616 | tf_op jit(solution)/shard_map/ppermute | solution.py:450
  13.4 5.2 %collective-permute-start.2 = (bf16[256,128]{1,0:T(8,128)(2,1)S(1)}, bf16[256,128]{1,0:T(8,128)(2,1)S(1)}, u32[]{:S(2)}, u32[]{:S(2)}) collective-permute-start(bf16[256,128]{1,0:T(8,128)(2,1)S(1)} %get-tuple-element.56), channel_id=1, source_target_pairs={{0,31},{1,0},{2,1},{3,2},{4,3},{5,4},{6,5},{7,6},{8,7},{9,8},{10,9... | collective-permute-start | bytes 196616 | tf_op jit(solution)/shard_map/ppermute | solution.py:450
  20.2 7.2 %collective-permute-start.6 = (bf16[2,32,1152]{2,1,0:T(8,128)(2,1)S(1)}, bf16[2,32,1152]{2,1,0:T(8,128)(2,1)S(1)}, u32[]{:S(2)}, u32[]{:S(2)}) collective-permute-start(bf16[2,32,1152]{2,1,0:T(8,128)(2,1)S(1)} %get-tuple-element.65), channel_id=1, source_target_pairs={{0,224},{32,0},{64,32},{96,64},{128,96},{160,128},{192,160},{224,1... | collective-permute-start | bytes 442376 | tf_op jit(solution)/shard_map/ppermute | solution.py:450
  22.0 5.3 %collective-permute-start.5 = (bf16[32,1152]{1,0:T(8,128)(2,1)S(1)}, bf16[32,1152]{1,0:T(8,128)(2,1)S(1)}, u32[]{:S(2)}, u32[]{:S(2)}) collective-permute-start(bf16[32,1152]{1,0:T(8,128)(2,1)S(1)} %get-tuple-element.64), channel_id=1, source_target_pairs={{0,32},{32,64},{64,96},{96,128},{128,160},{160,192},{192,224},{224... | collective-permute-start | bytes 221192 | tf_op jit(solution)/shard_map/ppermute | solution.py:450
  23.5 7.9 %copy-start = (bf16[5,5,5,16,384]{4,3,2,1,0:T(8,128)(2,1)}, bf16[5,5,5,16,384]{4,3,2,1,0:T(8,128)(2,1)S(1)}, u32[]{:S(2)}) copy-start(bf16[5,5,5,16,384]{4,3,2,1,0:T(8,128)(2,1)S(1)} %get-tuple-element.79.cwin_ref) | copy-start | bytes 4608004
  28.6 6.4 %collective-permute-start.8 = (bf16[2,32,1152]{2,1,0:T(8,128)(2,1)S(1)}, bf16[2,32,1152]{2,1,0:T(8,128)(2,1)S(1)}, u32[]{:S(2)}, u32[]{:S(2)}) collective-permute-start(bf16[2,32,1152]{2,1,0:T(8,128)(2,1)S(1)} %get-tuple-element.73), channel_id=1, source_target_pairs={{0,224},{32,0},{64,32},{96,64},{128,96},{160,128},{192,160},{224,1... | collective-permute-start | bytes 442376 | tf_op jit(solution)/shard_map/ppermute | solution.py:450
  29.7 5.3 %collective-permute-start.7 = (bf16[32,1152]{1,0:T(8,128)(2,1)S(1)}, bf16[32,1152]{1,0:T(8,128)(2,1)S(1)}, u32[]{:S(2)}, u32[]{:S(2)}) collective-permute-start(bf16[32,1152]{1,0:T(8,128)(2,1)S(1)} %get-tuple-element.72), channel_id=1, source_target_pairs={{0,32},{32,64},{64,96},{96,128},{128,160},{160,192},{192,224},{224... | collective-permute-start | bytes 221192 | tf_op jit(solution)/shard_map/ppermute | solution.py:450
  37.6 7.0 %collective-permute-start.9 = (bf16[640,128]{1,0:T(8,128)(2,1)S(1)}, bf16[640,128]{1,0:T(8,128)(2,1)S(1)}, u32[]{:S(2)}, u32[]{:S(2)}) collective-permute-start(bf16[640,128]{1,0:T(8,128)(2,1)S(1)} %get-tuple-element.84), channel_id=1, source_target_pairs={{0,1},{1,0},{2,3},{3,2},{4,5},{5,4},{6,7},{7,6},{8,9},{9,8},{10,11... | collective-permute-start | bytes 491528 | tf_op jit(solution)/shard_map/ppermute | solution.py:445
  54.7 2.6 %collective-permute-start.10 = (bf16[40,128]{1,0:T(8,128)(2,1)S(1)}, bf16[40,128]{1,0:T(8,128)(2,1)S(1)}, u32[]{:S(2)}, u32[]{:S(2)}) collective-permute-start(bf16[40,128]{1,0:T(8,128)(2,1)S(1)} %sum.1), channel_id=1, source_target_pairs={{0,4},{1,5},{2,6},{3,7},{4,0},{5,1},{6,2},{7,3},{8,12},{9,13},{10,... | collective-permute-start | bytes 30728 | tf_op jit(solution)/shard_map/ppermute | solution.py:445
  57.4 8.1 %collective-permute-start.13 = (bf16[40,128]{1,0:T(8,128)(2,1)S(1)}, bf16[40,128]{1,0:T(8,128)(2,1)S(1)}, u32[]{:S(2)}, u32[]{:S(2)}) collective-permute-start(bf16[40,128]{1,0:T(8,128)(2,1)S(1)} %add_convert_fusion.1), channel_id=1, source_target_pairs={{0,24},{1,25},{2,26},{3,27},{4,28},{5,29},{6,30},{7,31},{8,16},{9,... | collective-permute-start | bytes 30728 | tf_op jit(solution)/shard_map/ppermute | solution.py:445
  61.9 6.5 %collective-permute-start.12 = (bf16[40,128]{1,0:T(8,128)(2,1)S(1)}, bf16[40,128]{1,0:T(8,128)(2,1)S(1)}, u32[]{:S(2)}, u32[]{:S(2)}) collective-permute-start(bf16[40,128]{1,0:T(8,128)(2,1)S(1)} %add_convert_fusion.1), channel_id=1, source_target_pairs={{0,16},{1,17},{2,18},{3,19},{4,20},{5,21},{6,22},{7,23},{8,24},{9,... | collective-permute-start | bytes 30728 | tf_op jit(solution)/shard_map/ppermute | solution.py:445
  64.7 3.7 %collective-permute-start.11 = (bf16[40,128]{1,0:T(8,128)(2,1)S(1)}, bf16[40,128]{1,0:T(8,128)(2,1)S(1)}, u32[]{:S(2)}, u32[]{:S(2)}) collective-permute-start(bf16[40,128]{1,0:T(8,128)(2,1)S(1)} %add_convert_fusion.1), channel_id=1, source_target_pairs={{0,8},{1,9},{2,10},{3,11},{4,12},{5,13},{6,14},{7,15},{8,0},{9,1},... | collective-permute-start | bytes 30728 | tf_op jit(solution)/shard_map/ppermute | solution.py:445
  64.8 4.4 %collective-permute-start.14 = (bf16[32,1152]{1,0:T(8,128)(2,1)S(1)}, bf16[32,1152]{1,0:T(8,128)(2,1)S(1)}, u32[]{:S(2)}, u32[]{:S(2)}) collective-permute-start(bf16[32,1152]{1,0:T(8,128)(2,1)S(1)} %get-tuple-element.85), channel_id=1, source_target_pairs={{0,224},{32,0},{64,32},{96,64},{128,96},{160,128},{192,160},{224,1... | collective-permute-start | bytes 221192 | tf_op jit(solution)/shard_map/ppermute | solution.py:450
  69.2 10.8 %all-to-all-start.1 = ((bf16[16,40,128]{2,1,0:T(8,128)(2,1)}), bf16[16,40,128]{2,1,0:T(8,128)(2,1)S(1)}, u32[]{:S(2)}, u32[]{:S(2)}) async-start(bf16[16,40,128]{2,1,0:T(8,128)(2,1)} %bitcast.12), calls=%async_computation.1 | async-start | bytes 327680 | tf_op jit(solution)/shard_map/all_to_all | solution.py:474
  72.8 1.4 %copy-start.1 = (bf16[5,5,5,16,384]{4,3,2,1,0:T(8,128)(2,1)S(1)}, bf16[5,5,5,16,384]{4,3,2,1,0:T(8,128)(2,1)}, u32[]{:S(2)}) copy-start(bf16[5,5,5,16,384]{4,3,2,1,0:T(8,128)(2,1)} %copy-done) | copy-start | bytes 4608004
  80.0 6.5 %collective-permute-start.15 = (bf16[640,128]{1,0:T(8,128)(2,1)S(1)}, bf16[640,128]{1,0:T(8,128)(2,1)S(1)}, u32[]{:S(2)}, u32[]{:S(2)}) collective-permute-start(bf16[640,128]{1,0:T(8,128)(2,1)S(1)} %bitcast.31), channel_id=1, source_target_pairs={{0,1},{1,0},{2,3},{3,2},{4,5},{5,4},{6,7},{7,6},{8,9},{9,8},{10,11... | collective-permute-start | bytes 491528 | tf_op jit(solution)/shard_map/ppermute | solution.py:445

commit v8 on v7

--- a/solution.py
+++ b/solution.py
@@ -146,34 +146,46 @@
     mask_ref[2:3] = jnp.where(inside & (c >= 0) & (c < QC), 1.0, 0.0).astype(F32)
 
 
-def prepare_kernel(*refs):
-    sources, outs, here, sems = refs[0:4], refs[4:12], refs[12:16], refs[16]
-    copies = fetch(list(zip(sources, here)), sems)
-    write_masks(outs[7])
+def as_conv(ref, out_ref, back):
+    small, large = ref.shape[1], ref.shape[2]
+    if back:
+        flat = jnp.concatenate([ref[26 - k] for k in range(27)], axis=0)
+    else:
+        flat = ref[...].reshape(27 * small, large)
+    unit = ones_where(iota((large, large), 0) == iota((large, large), 1))
+    out_ref[...] = dot_nt(unit, flat).astype(BF)
+
+
+def as_up(ref, out_ref, back):
+    small, large = ref.shape[1], ref.shape[2]
+    out_ref[...] = jnp.zeros(out_ref.shape, BF)
+    for p, (pr, pd, pc) in enumerate(PAIRS):
+        for n, (nr, nd, nc) in enumerate(PAIRS):
+            taps = [UP_TAP.get(key) for key in ((pd, nd), (pr, nr), (pc, nc))]
+            if None in taps:
+                continue
+            j = taps[0] * 9 + taps[1] * 3 + taps[2]
+            out_ref[p * small : (p + 1) * small, n * large : (n + 1) * large] = ref[26 - j if back else j]
+
+
+def first_weights_kernel(wh_far, wbf_far, w1_ref, w4_ref, mask_ref, wh_ref, wbf_ref, sems):
+    copies = fetch(((wh_far, wh_ref), (wbf_far, wbf_ref)), sems)
+    write_masks(mask_ref)
     for copy in copies:
         copy.wait()
-    wh_ref, wq_ref, wbh_ref, wbf_ref = here
-    w1_ref, w2_ref, w3_ref, w4_ref, up1_ref, up2_ref, up3_ref = outs[:7]
-    for ref, out, eye, back in ((wh_ref, w1_ref, 32, False), (wq_ref, w2_ref, 64, False), (wbh_ref, w3_ref, 64, True), (wbf_ref, w4_ref, 32, True)):
-        small, large = ref.shape[1], ref.shape[2]
-        if back:
-            flat = jnp.concatenate([ref[26 - k] for k in range(27)], axis=0)
-        else:
-            flat = ref[...].reshape(27 * small, large)
-        rows = lax.broadcasted_iota(jnp.int32, (eye, eye), 0)
-        cols = lax.broadcasted_iota(jnp.int32, (eye, eye), 1)
-        unit = jnp.where(rows == cols, 1.0, 0.0).astype(BF)
-        out[...] = dot_nt(unit, flat).astype(BF)
-    for ref, out, back in ((wh_ref, up1_ref, True), (wq_ref, up2_ref, True), (wbh_ref, up3_ref, False)):
-        small, large = ref.shape[1], ref.shape[2]
-        out[...] = jnp.zeros(out.shape, BF)
-        for p, (pr, pd, pc) in enumerate(PAIRS):
-            for n, (nr, nd, nc) in enumerate(PAIRS):
-                taps = [UP_TAP.get(key) for key in ((pd, nd), (pr, nr), (pc, nc))]
-                if None in taps:
-                    continue
-                j = taps[0] * 9 + taps[1] * 3 + taps[2]
-                out[p * small : (p + 1) * small, n * large : (n + 1) * large] = ref[26 - j if back else j]
+    as_conv(wh_ref, w1_ref, False)
+    as_conv(wbf_ref, w4_ref, True)
+
+
+def other_weights_kernel(wh_far, wq_far, wbh_far, after_ref, w2_ref, w3_ref, up1_ref, up2_ref, up3_ref, wh_ref, wq_ref, wbh_ref, sems):
+    copies = fetch(((wh_far, wh_ref), (wq_far, wq_ref), (wbh_far, wbh_ref)), sems)
+    for copy in copies:
+        copy.wait()
+    as_conv(wq_ref, w2_ref, False)
+    as_conv(wbh_ref, w3_ref, True)
+    as_up(wh_ref, up1_ref, True)
+    as_up(wq_ref, up2_ref, True)
+    as_up(wbh_ref, up3_ref, False)
 
 
 def roll_up(x, steps):
@@ -510,14 +522,15 @@
         flops=2 * 256 * 1024 * 4000,
         name="own",
     )(vol_rows, cot_rows)
-    weights = by_tap(w_half, True), by_tap(w_quarter, True), by_tap(w_back_half, False), by_tap(w_back_full, False)
-    w1, w2, w3, w4, up1, up2, up3, mask = call(
-        prepare_kernel,
-        [((32, 432), BF), ((64, 864), BF), ((64, 864), BF), ((32, 432), BF), ((128, 256), BF), ((256, 512), BF), ((256, 512), BF), ((8, LANES), F32)],
-        [pltpu.VMEM(weight.shape, BF) for weight in weights] + [pltpu.SemaphoreType.DMA((4,))],
-        far=(4, 0),
-        name="prepare",
-    )(*[held(weight) for weight in weights])
+    wh, wq = held(by_tap(w_half, True)), held(by_tap(w_quarter, True))
+    wbh, wbf = held(by_tap(w_back_half, False)), held(by_tap(w_back_full, False))
+    w1, w4, mask = call(
+        first_weights_kernel,
+        [((32, 432), BF), ((32, 432), BF), ((8, LANES), F32)],
+        [pltpu.VMEM(wh.shape, BF), pltpu.VMEM(wbf.shape, BF), pltpu.SemaphoreType.DMA((2,))],
+        far=(2, 0),
+        name="first_weights",
+    )(wh, wbf)
     full_window, half_rows = (5, 5, 5, 16, LANES), (2, 2, 2, 32, LANES)
     vwin, preh, half_act, half_all, half_last = call(
         half_kernel,
@@ -528,6 +541,13 @@
     cwin, pull = call(
         cotangent_kernel, [(full_window, BF), ((8, 32, LANES), F32)], flops=2 * 432 * 32 * LANES * 64, name="cotangent"
     )(main_lo, yc, *edges, spread, place, w4)
+    w2, w3, up1, up2, up3 = call(
+        other_weights_kernel,
+        [((64, 864), BF), ((64, 864), BF), ((128, 256), BF), ((256, 512), BF), ((256, 512), BF)],
+        [pltpu.VMEM(weight.shape, BF) for weight in (wh, wq, wbh)] + [pltpu.SemaphoreType.DMA((3,))],
+        far=(3, 1),
+        name="other_weights",
+    )(wh, wq, wbh, half_last)
     hwin, preq, quarter, mixed, gm, gm_all, gm_last = call(
         middle_kernel,
         [((3, 5, 3, 32, LANES), BF), ((2, 64, LANES), F32), ((64, LANES), BF), ((8, 32, LANES), BF), (half_rows, BF), ((2, 32, 1152), BF), ((32, 1152), BF)],

time: 88 us -> 88.5 us (level)
  Pallas kernels: 17.2 us -> 18.2 us
    pallas_call x1 -> x2, Pallas kernels: 1.62 us -> 2.63 us  [the longest x1 1.45 us: shards(): call(other_weights_kernel, [((64, 864), BF), ((64, 864), BF), ((128, 256)...]
  transfers between devices with their start and end apart: 17 -> 17, of which waited for: 8 -> 9; matrix products, arithmetic and copies ran while one was open for 0% -> 0% of each run, Pallas kernels for 10% -> 11%
where the time goes in v8:
time: 88.5 us; the launch traced here: 88.2 us
  starting transfers between devices  38.8 us (44%)
  waiting for transfers between devices  18.9 us (21%)
  Pallas kernels  18.2 us (21%)
  blocking collectives  10.1 us (11%)
  local copies, waits for them, and re-layouts  1.39 us (2%)
    ppermute x6, starting transfers between devices, swapped(): return lax.ppermute(value, ('row', 'col'), pairs)  18.6 us
    ppermute x8, starting transfers between devices, shifted(): lax.ppermute(value, axis, [(i, (i + steps) % count) for i in range(count)])  11.3 us
    all_to_all x1, blocking collectives, exchanged(): lax.all_to_all(value, ('row', 'col'), 0, 0, axis_index_groups=list(groups...  10.1 us
    ppermute x8, waiting for transfers between devices, shifted(): lax.ppermute(value, axis, [(i, (i + steps) % count) for i in range(count)])  7.89 us
    ppermute x6, waiting for transfers between devices, swapped(): return lax.ppermute(value, ('row', 'col'), pairs)  7.24 us
    ppermute x2, starting transfers between devices, diagonal(): return lax.ppermute(value, ('row', 'col'), pairs)  4.69 us
    all_to_all x1, starting transfers between devices, exchanged(): lax.all_to_all(value, ('row', 'col'), 0, 0, axis_index_groups=list(groups...  4.22 us
    all_to_all x1, waiting for transfers between devices, exchanged(): lax.all_to_all(value, ('row', 'col'), 0, 0, axis_index_groups=list(groups...  3.77 us
  transfers between devices with their start and end apart: 17, of which 9 were waited for; matrix products, arithmetic and copies ran while one was open for 0% of the time, Pallas kernels for 11%

profile of v8, /device:TPU:1, one launch (start us, length us, event | category | flops | bytes accessed | tf_op | source)
XLA Modules:
  0.0 88.2 jit_solution(10482540556318325057)
XLA Ops:
  0.6 2.0 %edge.1 = (bf16[256,256]{1,0:T(8,128)(2,1)S(1)}, bf16[256,1024]{1,0:T(8,128)(2,1)S(1)}, bf16[256,1024]{1,0:T(8,128)(2,1)S(1)}, bf16[128,1024]{1,0:T(8,128)(2,1)S...) custom-call(bf16[16,8,16,128]{3,2,1,0:T(8,128)(2,1)} %bitcast.35, ...), custom_call_target="tpu_custom_call" | custom-call | bytes 4000000 | tf_op jit(solution)/shard_map/edge/pallas_call | solution.py:510
  2.7 2.1 %collective-permute-start = (bf16[128,1024]{1,0:T(8,128)(2,1)S(1)}, bf16[128,1024]{1,0:T(8,128)(2,1)S(1)}, u32[]{:S(2)}, u32[]{:S(2)}) collective-permute-start(bf16[128,1024]{1,0:T(8,128)(2,1)S(1)} %get-tuple-element.51), channel_id=1, source_target_pairs={{0,32},{32,64},{64,96},{96,128},{128,160},{160,192},{192,224},{224... | collective-permute-start | bytes 786440 | tf_op jit(solution)/shard_map/ppermute | solution.py:462
  4.8 4.7 %collective-permute-start.3 = (bf16[64,128]{1,0:T(8,128)(2,1)S(1)}, bf16[64,128]{1,0:T(8,128)(2,1)S(1)}, u32[]{:S(2)}, u32[]{:S(2)}) collective-permute-start(bf16[64,128]{1,0:T(8,128)(2,1)S(1)} %get-tuple-element.57), channel_id=1, source_target_pairs={{0,33},{1,34},{2,35},{3,36},{4,37},{5,38},{6,39},{7,40},{8,41},{9,... | collective-permute-start | bytes 49160 | tf_op jit(solution)/shard_map/ppermute | solution.py:475
  9.5 3.9 %collective-permute-start.1 = (bf16[256,128]{1,0:T(8,128)(2,1)S(1)}, bf16[256,128]{1,0:T(8,128)(2,1)S(1)}, u32[]{:S(2)}, u32[]{:S(2)}) collective-permute-start(bf16[256,128]{1,0:T(8,128)(2,1)S(1)} %get-tuple-element.55), channel_id=1, source_target_pairs={{0,1},{1,2},{2,3},{3,4},{4,5},{5,6},{6,7},{7,8},{8,9},{9,10},{10,1... | collective-permute-start | bytes 196616 | tf_op jit(solution)/shard_map/ppermute | solution.py:462
  13.4 1.0 %collective-permute-start.2 = (bf16[256,128]{1,0:T(8,128)(2,1)S(1)}, bf16[256,128]{1,0:T(8,128)(2,1)S(1)}, u32[]{:S(2)}, u32[]{:S(2)}) collective-permute-start(bf16[256,128]{1,0:T(8,128)(2,1)S(1)} %get-tuple-element.56), channel_id=1, source_target_pairs={{0,31},{1,0},{2,1},{3,2},{4,3},{5,4},{6,5},{7,6},{8,7},{9,8},{10,9... | collective-permute-start | bytes 196616 | tf_op jit(solution)/shard_map/ppermute | solution.py:462
  14.3 1.4 %own.1 = (bf16[256,1536]{1,0:T(8,128)(2,1)S(1)}, bf16[256,1536]{1,0:T(8,128)(2,1)S(1)}, bf16[1024,1024]{1,0:T(8,128)(2,1)S(1)}, bf16[2,256,1536]{2,1,0:T(8,128)(2,1)S(1)}) custom-call(bf16[256,1024]{1,0:T(8,128)(2,1)S(1)} %get-tuple-element.52.vol_rows_ref, bf16[256,1024]{1,0:T(8,128)(2,1)S(1)} %get-tuple-element.53.cot_rows_ref), custom_call_target="tpu_custom_call" | custom-call | flops 2097152000 | bytes 4000000 | tf_op jit(solution)/shard_map/own/pallas_call | solution.py:519
  15.8 1.2 %first_weights.1 = (bf16[32,432]{1,0:T(8,128)(2,1)S(1)}, bf16[32,432]{1,0:T(8,128)(2,1)S(1)}, f32[8,384]{1,0:T(8,128)S(1)}) custom-call(bf16[27,16,32]{2,1,0:T(8,128)(2,1)} %bitcast.37, bf16[27,16,32]{2,1,0:T(8,128)(2,1)} %bitcast.41), custom_call_target="tpu_custom_call" | custom-call | bytes 4000000 | tf_op jit(solution)/shard_map/first_weights/pallas_call | solution.py:527
  17.0 1.6 %collective-permute-done.2.right_ref = bf16[256,128]{1,0:T(8,128)(2,1)S(1)} collective-permute-done((bf16[256,128]{1,0:T(8,128)(2,1)S(1)}, bf16[256,128]{1,0:T(8,128)(2,1)S(1)}, u32[]{:S(2)}, u32[]{:S(2)}) %collective-permute-start.2) | collective-permute-done | bytes 65568 | tf_op jit(solution)/shard_map/ppermute | solution.py:462
  18.6 1.6 %half.1 = (bf16[5,5,5,16,384]{4,3,2,1,0:T(8,128)(2,1)S(1)}, f32[2,2,2,32,384]{4,3,2,1,0:T(8,128)S(1)}, bf16[2,2,2,32,384]{4,3,2,1,0:T(8,128)(2,1)S(1)}, bf16[2,3...) custom-call(bf16[128,1024]{1,0:T(8,128)(2,1)S(1)} %collective-permute-done.main_ref, ...), custom_call_target="tpu_custom_call" | custom-call | bytes 4000000 | tf_op jit(solution)/shard_map/half/pallas_call | solution.py:535
  20.2 1.8 %collective-permute-start.6 = (bf16[2,32,1152]{2,1,0:T(8,128)(2,1)S(1)}, bf16[2,32,1152]{2,1,0:T(8,128)(2,1)S(1)}, u32[]{:S(2)}, u32[]{:S(2)}) collective-permute-start(bf16[2,32,1152]{2,1,0:T(8,128)(2,1)S(1)} %get-tuple-element.65), channel_id=1, source_target_pairs={{0,224},{32,0},{64,32},{96,64},{128,96},{160,128},{192,160},{224,1... | collective-permute-start | bytes 442376 | tf_op jit(solution)/shard_map/ppermute | solution.py:462
  22.0 1.4 %other_weights.1 = (bf16[64,864]{1,0:T(8,128)(2,1)S(1)}, bf16[64,864]{1,0:T(8,128)(2,1)S(1)}, bf16[128,256]{1,0:T(8,128)(2,1)S(1)}, bf16[256,512]{1,0:T(8,128)(2,1)S(1)}, bf16[256,512]{1,0:T(8,128)(2,1)S(1)}) custom-call(bf16[27,16,32]{2,1,0:T(8,128)(2,1)} %bitcast.38, bf16[27,32,64]{2,1,0:T(8,128)(2,1)} %bitcast.39, bf16[27,32,64]{2,1,0:T(8,128)(2,1)} %bitcast.40, ...), custom_call_target="tpu_custom_call" | custom-call | bytes 4000000 | tf_op jit(solution)/shard_map/other_weights/pallas_call | solution.py:544
  23.5 1.5 %cotangent.1 = (bf16[5,5,5,16,384]{4,3,2,1,0:T(8,128)(2,1)S(1)}, f32[8,32,384]{2,1,0:T(8,128)S(1)}) custom-call(bf16[128,1024]{1,0:T(8,128)(2,1)S(1)} %collective-permute-done.main_ref, bf16[256,1536]{1,0:T(8,128)(2,1)S(1)} %get-tuple-element.66.yc_ref, bf16[256,128]{1,0:T(8,128)(2,1)S(1)} %collective-permute-done.1.left_ref, ...), custom_call_target="tpu_custom_call" | custom-call | flops 679477248 | bytes 4000000 | tf_op jit(solution)/shard_map/cotangent/pallas_call | solution.py:541
  25.0 2.3 %collective-permute-done.5.hlo_ref = bf16[32,1152]{1,0:T(8,128)(2,1)S(1)} collective-permute-done((bf16[32,1152]{1,0:T(8,128)(2,1)S(1)}, bf16[32,1152]{1,0:T(8,128)(2,1)S(1)}, u32[]{:S(2)}, u32[]{:S(2)}) %collective-permute-start.5) | collective-permute-done | bytes 73760 | tf_op jit(solution)/shard_map/ppermute | solution.py:462
  27.3 1.3 %middle.1 = (bf16[3,5,3,32,384]{4,3,2,1,0:T(8,128)(2,1)S(1)}, f32[2,64,384]{2,1,0:T(8,128)S(1)}, bf16[64,384]{1,0:T(8,128)(2,1)S(1)}, bf16[8,32,384]{2,1,0:T(8,1...) custom-call(bf16[2,2,2,32,384]{4,3,2,1,0:T(8,128)(2,1)S(1)} %get-tup, ...), custom_call_target="tpu_custom_call" | custom-call | bytes 4000000 | tf_op jit(solution)/shard_map/middle/pallas_call | solution.py:551
  28.6 1.5 %collective-permute-start.8 = (bf16[2,32,1152]{2,1,0:T(8,128)(2,1)S(1)}, bf16[2,32,1152]{2,1,0:T(8,128)(2,1)S(1)}, u32[]{:S(2)}, u32[]{:S(2)}) collective-permute-start(bf16[2,32,1152]{2,1,0:T(8,128)(2,1)S(1)} %get-tuple-element.73), channel_id=1, source_target_pairs={{0,224},{32,0},{64,32},{96,64},{128,96},{160,128},{192,160},{224,1... | collective-permute-start | bytes 442376 | tf_op jit(solution)/shard_map/ppermute | solution.py:462
  30.3 1.1 %full_grad.1.g4_ref = f32[112,128]{1,0:T(8,128)S(1)} custom-call(bf16[5,5,5,16,384]{4,3,2,1,0:T(8,128)(2,1)S(1)} %get-tuple-element.79.cwin_ref, bf16[8,32,384]{2,1,0:T(8,128)(2,1)S(1)} %get-tuple-element.80.m_ref), custom_call_target="tpu_custom_call" | custom-call | flops 679477248 | bytes 4000000 | tf_op jit(solution)/shard_map/full_grad/pallas_call | solution.py:557
  31.5 4.0 %collective-permute-done.7.gmlo_ref = bf16[32,1152]{1,0:T(8,128)(2,1)S(1)} collective-permute-done((bf16[32,1152]{1,0:T(8,128)(2,1)S(1)}, bf16[32,1152]{1,0:T(8,128)(2,1)S(1)}, u32[]{:S(2)}, u32[]{:S(2)}) %collective-permute-start.7) | collective-permute-done | bytes 73760 | tf_op jit(solution)/shard_map/ppermute | solution.py:462
  35.5 2.6 %backward.1 = (bf16[3,2,3,32,384]{4,3,2,1,0:T(8,128)(2,1)S(1)}, bf16[32,1152]{1,0:T(8,128)(2,1)S(1)}, f32[1280,128]{1,0:T(8,128)S(1)}, bf16[640,128]{1,0:T(8,128)(2,1)S(1)}) custom-call(bf16[2,2,2,32,384]{4,3,2,1,0:T(8,128)(2,1)S(1)} %get-tuple-element.71.gm_ref, bf16[32,1152]{1,0:T(8,128)(2,1)S(1)} %collective-permute-done.7.gmlo_ref, ...), custom_call_target="tpu_custom_call" | custom-call | bytes 4000000 | tf_op jit(solution)/shard_map/backward/pallas_call | solution.py:559
  38.1 5.1 %collective-permute-start.9 = (bf16[640,128]{1,0:T(8,128)(2,1)S(1)}, bf16[640,128]{1,0:T(8,128)(2,1)S(1)}, u32[]{:S(2)}, u32[]{:S(2)}) collective-permute-start(bf16[640,128]{1,0:T(8,128)(2,1)S(1)} %get-tuple-element.84), channel_id=1, source_target_pairs={{0,1},{1,0},{2,3},{3,2},{4,5},{5,4},{6,7},{7,6},{8,9},{9,8},{10,11... | collective-permute-start | bytes 491528 | tf_op jit(solution)/shard_map/ppermute | solution.py:457
  43.1 1.0 %collective-permute-done.9.got_ref = bf16[640,128]{1,0:T(8,128)(2,1)S(1)} collective-permute-done((bf16[640,128]{1,0:T(8,128)(2,1)S(1)}, bf16[640,128]{1,0:T(8,128)(2,1)S(1)}, u32[]{:S(2)}, u32[]{:S(2)}) %collective-permute-start.9) | collective-permute-done | bytes 163872 | tf_op jit(solution)/shard_map/ppermute | solution.py:457
  44.2 10.1 %all_to_all.10 = bf16[16,40,128]{2,1,0:T(8,128)(2,1)S(1)} all-to-all(bf16[16,40,128]{2,1,0:T(8,128)(2,1)S(1)} %bitcast.34), channel_id=1, replica_groups={{0,2,32,34,64,66,96,98,128,130,160,162,192,194,224,226},{1,3,33,35,65,6..., dimensions={0} | all-to-all | bytes 327680 | tf_op jit(solution)/shard_map/all_to_all | solution.py:486
  54.4 2.5 %collective-permute-done.10 = bf16[40,128]{1,0:T(8,128)(2,1)S(1)} collective-permute-done((bf16[40,128]{1,0:T(8,128)(2,1)S(1)}, bf16[40,128]{1,0:T(8,128)(2,1)S(1)}, u32[]{:S(2)}, u32[]{:S(2)}) %collective-permute-start.10) | collective-permute-done | bytes 10272 | tf_op jit(solution)/shard_map/ppermute | solution.py:457
  56.9 4.4 %collective-permute-start.13 = (bf16[40,128]{1,0:T(8,128)(2,1)S(1)}, bf16[40,128]{1,0:T(8,128)(2,1)S(1)}, u32[]{:S(2)}, u32[]{:S(2)}) collective-permute-start(bf16[40,128]{1,0:T(8,128)(2,1)S(1)} %add_convert_fusion.1), channel_id=1, source_target_pairs={{0,24},{1,25},{2,26},{3,27},{4,28},{5,29},{6,30},{7,31},{8,16},{9,... | collective-permute-start | bytes 30728 | tf_op jit(solution)/shard_map/ppermute | solution.py:457
  61.3 3.9 %collective-permute-start.12 = (bf16[40,128]{1,0:T(8,128)(2,1)S(1)}, bf16[40,128]{1,0:T(8,128)(2,1)S(1)}, u32[]{:S(2)}, u32[]{:S(2)}) collective-permute-start(bf16[40,128]{1,0:T(8,128)(2,1)S(1)} %add_convert_fusion.1), channel_id=1, source_target_pairs={{0,16},{1,17},{2,18},{3,19},{4,20},{5,21},{6,22},{7,23},{8,24},{9,... | collective-permute-start | bytes 30728 | tf_op jit(solution)/shard_map/ppermute | solution.py:457
  66.0 1.7 %collective-permute-done.12 = bf16[40,128]{1,0:T(8,128)(2,1)S(1)} collective-permute-done((bf16[40,128]{1,0:T(8,128)(2,1)S(1)}, bf16[40,128]{1,0:T(8,128)(2,1)S(1)}, u32[]{:S(2)}, u32[]{:S(2)}) %collective-permute-start.12) | collective-permute-done | bytes 10272 | tf_op jit(solution)/shard_map/ppermute | solution.py:457
  69.4 4.2 %all-to-all-start.1 = ((bf16[16,40,128]{2,1,0:T(8,128)(2,1)}), bf16[16,40,128]{2,1,0:T(8,128)(2,1)S(1)}, u32[]{:S(2)}, u32[]{:S(2)}) async-start(bf16[16,40,128]{2,1,0:T(8,128)(2,1)} %bitcast.13), calls=%async_computation.1 | async-start | bytes 327680 | tf_op jit(solution)/shard_map/all_to_all | solution.py:486
  73.6 1.4 %copy-done.1 = bf16[5,5,5,16,384]{4,3,2,1,0:T(8,128)(2,1)S(1)} copy-done((bf16[5,5,5,16,384]{4,3,2,1,0:T(8,128)(2,1)S(1)}, bf16[5,5,5,16,384]{4,3,2,1,0:T(8,128)(2,1)}, u32[]{:S(2)}) %copy-start.1) | copy-done | bytes 1536024
  75.0 2.0 %volume.1 = bf16[16,8,16,128]{3,2,1,0:T(8,128)(2,1)} custom-call(bf16[3,2,3,32,384]{4,3,2,1,0:T(8,128)(2,1)S(1)} %get-tuple-element.87.ewin_ref, bf16[32,1152]{1,0:T(8,128)(2,1)S(1)} %collective-permute-done.14.next_ref, bf16[5,5,5,16,384]{4,3,2,1,0:T(8,128)(2,1)S(1)} %copy-done.1, bf16[128,256]{1,0:T(8,128)(2,1)S(1)} %get-tuple-element.89.up1_ref, ...), custom_call_target="tpu_custom_call" | custom-call | flops 2097152000 | bytes 4000000 | tf_op jit(solution)/shard_map/volume/pallas_call | solution.py:578
  77.0 3.8 %all-to-all-done.1 = bf16[16,40,128]{2,1,0:T(8,128)(2,1)S(1)} async-done(((bf16[16,40,128]{2,1,0:T(8,128)(2,1)}), bf16[16,40,128]{2,1,0:T(8,128)(2,1)S(1)}, u32[]{:S(2)}, u32[]{:S(2)}) %all-to-all-start.1) | async-done | bytes 163872 | tf_op jit(solution)/shard_map/all_to_all | solution.py:486
  80.8 5.2 %collective-permute-start.15 = (bf16[640,128]{1,0:T(8,128)(2,1)S(1)}, bf16[640,128]{1,0:T(8,128)(2,1)S(1)}, u32[]{:S(2)}, u32[]{:S(2)}) collective-permute-start(bf16[640,128]{1,0:T(8,128)(2,1)S(1)} %bitcast.31), channel_id=1, source_target_pairs={{0,1},{1,0},{2,3},{3,2},{4,5},{5,4},{6,7},{7,6},{8,9},{9,8},{10,11... | collective-permute-start | bytes 491528 | tf_op jit(solution)/shard_map/ppermute | solution.py:457
  86.0 1.0 %collective-permute-done.15.got_ref = bf16[640,128]{1,0:T(8,128)(2,1)S(1)} collective-permute-done((bf16[640,128]{1,0:T(8,128)(2,1)S(1)}, bf16[640,128]{1,0:T(8,128)(2,1)S(1)}, u32[]{:S(2)}, u32[]{:S(2)}) %collective-permute-start.15) | collective-permute-done | bytes 163872 | tf_op jit(solution)/shard_map/ppermute | solution.py:457
  87.0 1.2 %finish.1 = (f32[27,16,32]{2,1,0:T(8,128)}, f32[27,32,64]{2,1,0:T(8,128)}, f32[27,32,64]{2,1,0:T(8,128)}, f32[27,16,32]{2,1,0:T(8,128)}) custom-call(bf16[640,128]{1,0:T(8,128)(2,1)S(1)} %bitcast.32, bf16[640,128]{1,0:T(8,128)(2,1)S(1)} %collective-permute-done.15.got_ref), custom_call_target="tpu_custom_call" | custom-call | bytes 4000000 | tf_op jit(solution)/shard_map/finish/pallas_call | solution.py:582
  (23 shorter events, 2.7 us)
Async XLA Ops:
  2.7 15.9 %collective-permute-start = (bf16[128,1024]{1,0:T(8,128)(2,1)S(1)}, bf16[128,1024]{1,0:T(8,128)(2,1)S(1)}, u32[]{:S(2)}, u32[]{:S(2)}) collective-permute-start(bf16[128,1024]{1,0:T(8,128)(2,1)S(1)} %get-tuple-element.51), channel_id=1, source_target_pairs={{0,32},{32,64},{64,96},{96,128},{128,160},{160,192},{192,224},{224... | collective-permute-start | bytes 786440 | tf_op jit(solution)/shard_map/ppermute | solution.py:462
  4.8 12.2 %collective-permute-start.3 = (bf16[64,128]{1,0:T(8,128)(2,1)S(1)}, bf16[64,128]{1,0:T(8,128)(2,1)S(1)}, u32[]{:S(2)}, u32[]{:S(2)}) collective-permute-start(bf16[64,128]{1,0:T(8,128)(2,1)S(1)} %get-tuple-element.57), channel_id=1, source_target_pairs={{0,33},{1,34},{2,35},{3,36},{4,37},{5,38},{6,39},{7,40},{8,41},{9,... | collective-permute-start | bytes 49160 | tf_op jit(solution)/shard_map/ppermute | solution.py:475
  9.5 7.5 %collective-permute-start.4 = (bf16[64,128]{1,0:T(8,128)(2,1)S(1)}, bf16[64,128]{1,0:T(8,128)(2,1)S(1)}, u32[]{:S(2)}, u32[]{:S(2)}) collective-permute-start(bf16[64,128]{1,0:T(8,128)(2,1)S(1)} %get-tuple-element.58), channel_id=1, source_target_pairs={{0,63},{1,32},{2,33},{3,34},{4,35},{5,36},{6,37},{7,38},{8,39},{9,... | collective-permute-start | bytes 49160 | tf_op jit(solution)/shard_map/ppermute | solution.py:475
  9.5 7.5 %collective-permute-start.1 = (bf16[256,128]{1,0:T(8,128)(2,1)S(1)}, bf16[256,128]{1,0:T(8,128)(2,1)S(1)}, u32[]{:S(2)}, u32[]{:S(2)}) collective-permute-start(bf16[256,128]{1,0:T(8,128)(2,1)S(1)} %get-tuple-element.55), channel_id=1, source_target_pairs={{0,1},{1,2},{2,3},{3,4},{4,5},{5,6},{6,7},{7,8},{8,9},{9,10},{10,1... | collective-permute-start | bytes 196616 | tf_op jit(solution)/shard_map/ppermute | solution.py:462
  13.4 5.2 %collective-permute-start.2 = (bf16[256,128]{1,0:T(8,128)(2,1)S(1)}, bf16[256,128]{1,0:T(8,128)(2,1)S(1)}, u32[]{:S(2)}, u32[]{:S(2)}) collective-permute-start(bf16[256,128]{1,0:T(8,128)(2,1)S(1)} %get-tuple-element.56), channel_id=1, source_target_pairs={{0,31},{1,0},{2,1},{3,2},{4,3},{5,4},{6,5},{7,6},{8,7},{9,8},{10,9... | collective-permute-start | bytes 196616 | tf_op jit(solution)/shard_map/ppermute | solution.py:462
  20.2 7.2 %collective-permute-start.6 = (bf16[2,32,1152]{2,1,0:T(8,128)(2,1)S(1)}, bf16[2,32,1152]{2,1,0:T(8,128)(2,1)S(1)}, u32[]{:S(2)}, u32[]{:S(2)}) collective-permute-start(bf16[2,32,1152]{2,1,0:T(8,128)(2,1)S(1)} %get-tuple-element.65), channel_id=1, source_target_pairs={{0,224},{32,0},{64,32},{96,64},{128,96},{160,128},{192,160},{224,1... | collective-permute-start | bytes 442376 | tf_op jit(solution)/shard_map/ppermute | solution.py:462
  22.0 5.3 %collective-permute-start.5 = (bf16[32,1152]{1,0:T(8,128)(2,1)S(1)}, bf16[32,1152]{1,0:T(8,128)(2,1)S(1)}, u32[]{:S(2)}, u32[]{:S(2)}) collective-permute-start(bf16[32,1152]{1,0:T(8,128)(2,1)S(1)} %get-tuple-element.64.after_ref), channel_id=1, source_target_pairs={{0,32},{32,64},{64,96},{96,128},{128,160},{160,192},{192,224},{224... | collective-permute-start | bytes 221192 | tf_op jit(solution)/shard_map/ppermute | solution.py:462
  25.0 6.5 %copy-start = (bf16[5,5,5,16,384]{4,3,2,1,0:T(8,128)(2,1)}, bf16[5,5,5,16,384]{4,3,2,1,0:T(8,128)(2,1)S(1)}, u32[]{:S(2)}) copy-start(bf16[5,5,5,16,384]{4,3,2,1,0:T(8,128)(2,1)S(1)} %get-tuple-element.79.cwin_ref) | copy-start | bytes 4608004
  28.6 6.9 %collective-permute-start.8 = (bf16[2,32,1152]{2,1,0:T(8,128)(2,1)S(1)}, bf16[2,32,1152]{2,1,0:T(8,128)(2,1)S(1)}, u32[]{:S(2)}, u32[]{:S(2)}) collective-permute-start(bf16[2,32,1152]{2,1,0:T(8,128)(2,1)S(1)} %get-tuple-element.73), channel_id=1, source_target_pairs={{0,224},{32,0},{64,32},{96,64},{128,96},{160,128},{192,160},{224,1... | collective-permute-start | bytes 442376 | tf_op jit(solution)/shard_map/ppermute | solution.py:462
  30.2 5.3 %collective-permute-start.7 = (bf16[32,1152]{1,0:T(8,128)(2,1)S(1)}, bf16[32,1152]{1,0:T(8,128)(2,1)S(1)}, u32[]{:S(2)}, u32[]{:S(2)}) collective-permute-start(bf16[32,1152]{1,0:T(8,128)(2,1)S(1)} %get-tuple-element.72), channel_id=1, source_target_pairs={{0,32},{32,64},{64,96},{96,128},{128,160},{160,192},{192,224},{224... | collective-permute-start | bytes 221192 | tf_op jit(solution)/shard_map/ppermute | solution.py:462
  38.1 6.1 %collective-permute-start.9 = (bf16[640,128]{1,0:T(8,128)(2,1)S(1)}, bf16[640,128]{1,0:T(8,128)(2,1)S(1)}, u32[]{:S(2)}, u32[]{:S(2)}) collective-permute-start(bf16[640,128]{1,0:T(8,128)(2,1)S(1)} %get-tuple-element.84), channel_id=1, source_target_pairs={{0,1},{1,0},{2,3},{3,2},{4,5},{5,4},{6,7},{7,6},{8,9},{9,8},{10,11... | collective-permute-start | bytes 491528 | tf_op jit(solution)/shard_map/ppermute | solution.py:457
  54.3 2.6 %collective-permute-start.10 = (bf16[40,128]{1,0:T(8,128)(2,1)S(1)}, bf16[40,128]{1,0:T(8,128)(2,1)S(1)}, u32[]{:S(2)}, u32[]{:S(2)}) collective-permute-start(bf16[40,128]{1,0:T(8,128)(2,1)S(1)} %sum.1), channel_id=1, source_target_pairs={{0,4},{1,5},{2,6},{3,7},{4,0},{5,1},{6,2},{7,3},{8,12},{9,13},{10,... | collective-permute-start | bytes 30728 | tf_op jit(solution)/shard_map/ppermute | solution.py:457
  56.9 9.1 %collective-permute-start.13 = (bf16[40,128]{1,0:T(8,128)(2,1)S(1)}, bf16[40,128]{1,0:T(8,128)(2,1)S(1)}, u32[]{:S(2)}, u32[]{:S(2)}) collective-permute-start(bf16[40,128]{1,0:T(8,128)(2,1)S(1)} %add_convert_fusion.1), channel_id=1, source_target_pairs={{0,24},{1,25},{2,26},{3,27},{4,28},{5,29},{6,30},{7,31},{8,16},{9,... | collective-permute-start | bytes 30728 | tf_op jit(solution)/shard_map/ppermute | solution.py:457
  61.3 6.4 %collective-permute-start.12 = (bf16[40,128]{1,0:T(8,128)(2,1)S(1)}, bf16[40,128]{1,0:T(8,128)(2,1)S(1)}, u32[]{:S(2)}, u32[]{:S(2)}) collective-permute-start(bf16[40,128]{1,0:T(8,128)(2,1)S(1)} %add_convert_fusion.1), channel_id=1, source_target_pairs={{0,16},{1,17},{2,18},{3,19},{4,20},{5,21},{6,22},{7,23},{8,24},{9,... | collective-permute-start | bytes 30728 | tf_op jit(solution)/shard_map/ppermute | solution.py:457
  65.2 3.4 %collective-permute-start.11 = (bf16[40,128]{1,0:T(8,128)(2,1)S(1)}, bf16[40,128]{1,0:T(8,128)(2,1)S(1)}, u32[]{:S(2)}, u32[]{:S(2)}) collective-permute-start(bf16[40,128]{1,0:T(8,128)(2,1)S(1)} %add_convert_fusion.1), channel_id=1, source_target_pairs={{0,8},{1,9},{2,10},{3,11},{4,12},{5,13},{6,14},{7,15},{8,0},{9,1},... | collective-permute-start | bytes 30728 | tf_op jit(solution)/shard_map/ppermute | solution.py:457
  65.2 4.1 %collective-permute-start.14 = (bf16[32,1152]{1,0:T(8,128)(2,1)S(1)}, bf16[32,1152]{1,0:T(8,128)(2,1)S(1)}, u32[]{:S(2)}, u32[]{:S(2)}) collective-permute-start(bf16[32,1152]{1,0:T(8,128)(2,1)S(1)} %get-tuple-element.85), channel_id=1, source_target_pairs={{0,224},{32,0},{64,32},{96,64},{128,96},{160,128},{192,160},{224,1... | collective-permute-start | bytes 221192 | tf_op jit(solution)/shard_map/ppermute | solution.py:462
  69.4 11.4 %all-to-all-start.1 = ((bf16[16,40,128]{2,1,0:T(8,128)(2,1)}), bf16[16,40,128]{2,1,0:T(8,128)(2,1)S(1)}, u32[]{:S(2)}, u32[]{:S(2)}) async-start(bf16[16,40,128]{2,1,0:T(8,128)(2,1)} %bitcast.13), calls=%async_computation.1 | async-start | bytes 327680 | tf_op jit(solution)/shard_map/all_to_all | solution.py:486
  73.6 1.4 %copy-start.1 = (bf16[5,5,5,16,384]{4,3,2,1,0:T(8,128)(2,1)S(1)}, bf16[5,5,5,16,384]{4,3,2,1,0:T(8,128)(2,1)}, u32[]{:S(2)}) copy-start(bf16[5,5,5,16,384]{4,3,2,1,0:T(8,128)(2,1)} %copy-done) | copy-start | bytes 4608004
  80.8 6.2 %collective-permute-start.15 = (bf16[640,128]{1,0:T(8,128)(2,1)S(1)}, bf16[640,128]{1,0:T(8,128)(2,1)S(1)}, u32[]{:S(2)}, u32[]{:S(2)}) collective-permute-start(bf16[640,128]{1,0:T(8,128)(2,1)S(1)} %bitcast.31), channel_id=1, source_target_pairs={{0,1},{1,0},{2,3},{3,2},{4,5},{5,4},{6,7},{7,6},{8,9},{9,8},{10,11... | collective-permute-start | bytes 491528 | tf_op jit(solution)/shard_map/ppermute | solution.py:457

commit v9 on v8

--- a/solution.py
+++ b/solution.py
@@ -460,13 +460,6 @@
 def shifted(value, axis, steps):
     count = lax.axis_size(axis)
     return lax.ppermute(value, axis, [(i, (i + steps) % count) for i in range(count)])
-
-
-def tree_sum(terms):
-    terms = [term.astype(F32) for term in terms]
-    while len(terms) > 1:
-        terms = [low + high for low, high in zip(terms[::2], terms[1::2])]
-    return terms[0]
 
 
 def diagonal(value, row_step, col_step):
@@ -564,17 +557,14 @@
     )(gm, gm_lo, gm_hi, vwin, hwin, preh, preq, quarter, g4, mask, w3, up2)
     (part,) = call(functools.partial(fold_kernel, core), [((PACK // 2, 128), BF)], name="fold")(kept, swapped(send, 0, 1))
     gh_next = shifted(gh_first, "row", -1)
-    near = (7 & (rows - 1), 2 & (cols - 1))
-    size = 2 ** sum(bits.bit_count() for bits in near)
-    share = PACK // 2 // size
-    part = exchanged(part.reshape(size, share, 128), *near).reshape(size * share, 128)
-    (part,) = call(functools.partial(sum_kernel, size, 1), [((share, 128), BF)], name="sum")(part)
-    for steps in ((4,), (8, 16, 24)):
-        if max(steps) < cols:
-            part = tree_sum([part] + [swapped(part, 0, step) for step in steps]).astype(BF)
-    (part,) = call(functools.partial(sum_kernel, 1, size), [((size * share, 128), BF)], name="copies")(part)
+    along = [(7 & (rows - 1), 2 & (cols - 1)), (0, 28 & (cols - 1))]
+    sizes = [2 ** (r.bit_count() + c.bit_count()) for r, c in along]
+    share = PACK // 2 // sizes[0]
+    for bits, size, later in zip(along, sizes, sizes[::-1]):
+        part = exchanged(part.reshape(size, share, 128), *bits).reshape(size * share, 128)
+        (part,) = call(functools.partial(sum_kernel, size, later), [((later * share, 128), BF)], name="sum")(part)
     part, gh_next = lax.optimization_barrier((part, gh_next))
-    part = exchanged(part.reshape(size, share, 128), *near).reshape(PACK // 2, 128)
+    part = exchanged(part.reshape(sizes[0], share, 128), *along[0]).reshape(PACK // 2, 128)
     (grad_volume,) = call(
         volume_kernel, [((16, QD, 16, 128), BF)], [pltpu.VMEM((256, 4 * LANES), BF), pltpu.VMEM((3, 3, 32, LANES), BF)], flops=2 * 256 * 1024 * 4000, name="volume"
     )(ewin, gh_next, cwin, up1, spread, order)

time: 88.5 us -> 88.3 us (level)
  starting transfers between devices: 38.8 us -> 36.4 us
  waiting for transfers between devices: 18.9 us -> 20.4 us
    ppermute x6 -> x2, starting transfers between devices: 18.6 us -> 9.24 us  [swapped(): return lax.ppermute(value, ('row', 'col'), pairs)]
    all_to_all x1 -> x2, starting transfers between devices: 4.22 us -> 11.2 us  [exchanged(): lax.all_to_all(value, ('row', 'col'), 0, 0, axis_index_groups=list(groups...]
    all_to_all x1 -> x2, waiting for transfers between devices: 3.77 us -> 10.5 us  [exchanged(): lax.all_to_all(value, ('row', 'col'), 0, 0, axis_index_groups=list(groups...]
    ppermute x6 -> x2, waiting for transfers between devices: 7.24 us -> 2.06 us  [swapped(): return lax.ppermute(value, ('row', 'col'), pairs)]
  transfers between devices with their start and end apart: 17 -> 14, of which waited for: 9 -> 7; matrix products, arithmetic and copies ran while one was open for 0% -> 0% of each run, Pallas kernels for 11% -> 11%
where the time goes in v9:
time: 88.3 us; the launch traced here: 88 us
  starting transfers between devices  36.4 us (41%)
  waiting for transfers between devices  20.4 us (23%)
  Pallas kernels  18.9 us (21%)
  blocking collectives  10.1 us (11%)
  local copies, waits for them, and re-layouts  1.39 us (2%)
    all_to_all x2, starting transfers between devices, exchanged(): lax.all_to_all(value, ('row', 'col'), 0, 0, axis_index_groups=list(groups...  11.2 us
    ppermute x8, starting transfers between devices, shifted(): lax.ppermute(value, axis, [(i, (i + steps) % count) for i in range(count)])  11.2 us
    all_to_all x2, waiting for transfers between devices, exchanged(): lax.all_to_all(value, ('row', 'col'), 0, 0, axis_index_groups=list(groups...  10.5 us
    all_to_all x1, blocking collectives, exchanged(): lax.all_to_all(value, ('row', 'col'), 0, 0, axis_index_groups=list(groups...  10.1 us
    ppermute x2, starting transfers between devices, swapped(): return lax.ppermute(value, ('row', 'col'), pairs)  9.24 us
    ppermute x8, waiting for transfers between devices, shifted(): lax.ppermute(value, axis, [(i, (i + steps) % count) for i in range(count)])  7.89 us
    ppermute x2, starting transfers between devices, diagonal(): return lax.ppermute(value, ('row', 'col'), pairs)  4.69 us
    pallas_call x1, Pallas kernels, shards(): call(functools.partial(backward_kernel, core), [((3, 2, 3, 32, LANES), BF...  2.59 us
  transfers between devices with their start and end apart: 14, of which 7 were waited for; matrix products, arithmetic and copies ran while one was open for 0% of the time, Pallas kernels for 11%

profile of v9, /device:TPU:1, one launch (start us, length us, event | category | flops | bytes accessed | tf_op | source)
XLA Modules:
  0.0 88.0 jit_solution(18132007326263617152)
XLA Ops:
  0.6 2.0 %edge.1 = (bf16[256,256]{1,0:T(8,128)(2,1)S(1)}, bf16[256,1024]{1,0:T(8,128)(2,1)S(1)}, bf16[256,1024]{1,0:T(8,128)(2,1)S(1)}, bf16[128,1024]{1,0:T(8,128)(2,1)S...) custom-call(bf16[16,8,16,128]{3,2,1,0:T(8,128)(2,1)} %bitcast.38, ...), custom_call_target="tpu_custom_call" | custom-call | bytes 4000000 | tf_op jit(solution)/shard_map/edge/pallas_call | solution.py:503
  2.7 2.1 %collective-permute-start = (bf16[128,1024]{1,0:T(8,128)(2,1)S(1)}, bf16[128,1024]{1,0:T(8,128)(2,1)S(1)}, u32[]{:S(2)}, u32[]{:S(2)}) collective-permute-start(bf16[128,1024]{1,0:T(8,128)(2,1)S(1)} %get-tuple-element.51), channel_id=1, source_target_pairs={{0,32},{32,64},{64,96},{96,128},{128,160},{160,192},{192,224},{224... | collective-permute-start | bytes 786440 | tf_op jit(solution)/shard_map/ppermute | solution.py:462
  4.8 4.7 %collective-permute-start.3 = (bf16[64,128]{1,0:T(8,128)(2,1)S(1)}, bf16[64,128]{1,0:T(8,128)(2,1)S(1)}, u32[]{:S(2)}, u32[]{:S(2)}) collective-permute-start(bf16[64,128]{1,0:T(8,128)(2,1)S(1)} %get-tuple-element.57), channel_id=1, source_target_pairs={{0,33},{1,34},{2,35},{3,36},{4,37},{5,38},{6,39},{7,40},{8,41},{9,... | collective-permute-start | bytes 49160 | tf_op jit(solution)/shard_map/ppermute | solution.py:468
  9.5 3.9 %collective-permute-start.1 = (bf16[256,128]{1,0:T(8,128)(2,1)S(1)}, bf16[256,128]{1,0:T(8,128)(2,1)S(1)}, u32[]{:S(2)}, u32[]{:S(2)}) collective-permute-start(bf16[256,128]{1,0:T(8,128)(2,1)S(1)} %get-tuple-element.55), channel_id=1, source_target_pairs={{0,1},{1,2},{2,3},{3,4},{4,5},{5,6},{6,7},{7,8},{8,9},{9,10},{10,1... | collective-permute-start | bytes 196616 | tf_op jit(solution)/shard_map/ppermute | solution.py:462
  13.4 1.0 %collective-permute-start.2 = (bf16[256,128]{1,0:T(8,128)(2,1)S(1)}, bf16[256,128]{1,0:T(8,128)(2,1)S(1)}, u32[]{:S(2)}, u32[]{:S(2)}) collective-permute-start(bf16[256,128]{1,0:T(8,128)(2,1)S(1)} %get-tuple-element.56), channel_id=1, source_target_pairs={{0,31},{1,0},{2,1},{3,2},{4,3},{5,4},{6,5},{7,6},{8,7},{9,8},{10,9... | collective-permute-start | bytes 196616 | tf_op jit(solution)/shard_map/ppermute | solution.py:462
  14.3 1.4 %own.1 = (bf16[256,1536]{1,0:T(8,128)(2,1)S(1)}, bf16[256,1536]{1,0:T(8,128)(2,1)S(1)}, bf16[1024,1024]{1,0:T(8,128)(2,1)S(1)}, bf16[2,256,1536]{2,1,0:T(8,128)(2,1)S(1)}) custom-call(bf16[256,1024]{1,0:T(8,128)(2,1)S(1)} %get-tuple-element.52.vol_rows_ref, bf16[256,1024]{1,0:T(8,128)(2,1)S(1)} %get-tuple-element.53.cot_rows_ref), custom_call_target="tpu_custom_call" | custom-call | flops 2097152000 | bytes 4000000 | tf_op jit(solution)/shard_map/own/pallas_call | solution.py:512
  15.8 1.2 %first_weights.1 = (bf16[32,432]{1,0:T(8,128)(2,1)S(1)}, bf16[32,432]{1,0:T(8,128)(2,1)S(1)}, f32[8,384]{1,0:T(8,128)S(1)}) custom-call(bf16[27,16,32]{2,1,0:T(8,128)(2,1)} %bitcast.40, bf16[27,16,32]{2,1,0:T(8,128)(2,1)} %bitcast.44), custom_call_target="tpu_custom_call" | custom-call | bytes 4000000 | tf_op jit(solution)/shard_map/first_weights/pallas_call | solution.py:520
  17.0 1.6 %collective-permute-done.2.right_ref = bf16[256,128]{1,0:T(8,128)(2,1)S(1)} collective-permute-done((bf16[256,128]{1,0:T(8,128)(2,1)S(1)}, bf16[256,128]{1,0:T(8,128)(2,1)S(1)}, u32[]{:S(2)}, u32[]{:S(2)}) %collective-permute-start.2) | collective-permute-done | bytes 65568 | tf_op jit(solution)/shard_map/ppermute | solution.py:462
  18.6 1.6 %half.1 = (bf16[5,5,5,16,384]{4,3,2,1,0:T(8,128)(2,1)S(1)}, f32[2,2,2,32,384]{4,3,2,1,0:T(8,128)S(1)}, bf16[2,2,2,32,384]{4,3,2,1,0:T(8,128)(2,1)S(1)}, bf16[2,3...) custom-call(bf16[128,1024]{1,0:T(8,128)(2,1)S(1)} %collective-permute-done.main_ref, ...), custom_call_target="tpu_custom_call" | custom-call | bytes 4000000 | tf_op jit(solution)/shard_map/half/pallas_call | solution.py:528
  20.2 1.8 %collective-permute-start.6 = (bf16[2,32,1152]{2,1,0:T(8,128)(2,1)S(1)}, bf16[2,32,1152]{2,1,0:T(8,128)(2,1)S(1)}, u32[]{:S(2)}, u32[]{:S(2)}) collective-permute-start(bf16[2,32,1152]{2,1,0:T(8,128)(2,1)S(1)} %get-tuple-element.65), channel_id=1, source_target_pairs={{0,224},{32,0},{64,32},{96,64},{128,96},{160,128},{192,160},{224,1... | collective-permute-start | bytes 442376 | tf_op jit(solution)/shard_map/ppermute | solution.py:462
  22.0 1.4 %other_weights.1 = (bf16[64,864]{1,0:T(8,128)(2,1)S(1)}, bf16[64,864]{1,0:T(8,128)(2,1)S(1)}, bf16[128,256]{1,0:T(8,128)(2,1)S(1)}, bf16[256,512]{1,0:T(8,128)(2,1)S(1)}, bf16[256,512]{1,0:T(8,128)(2,1)S(1)}) custom-call(bf16[27,16,32]{2,1,0:T(8,128)(2,1)} %bitcast.41, bf16[27,32,64]{2,1,0:T(8,128)(2,1)} %bitcast.42, bf16[27,32,64]{2,1,0:T(8,128)(2,1)} %bitcast.43, ...), custom_call_target="tpu_custom_call" | custom-call | bytes 4000000 | tf_op jit(solution)/shard_map/other_weights/pallas_call | solution.py:537
  23.5 1.5 %cotangent.1 = (bf16[5,5,5,16,384]{4,3,2,1,0:T(8,128)(2,1)S(1)}, f32[8,32,384]{2,1,0:T(8,128)S(1)}) custom-call(bf16[128,1024]{1,0:T(8,128)(2,1)S(1)} %collective-permute-done.main_ref, bf16[256,1536]{1,0:T(8,128)(2,1)S(1)} %get-tuple-element.66.yc_ref, bf16[256,128]{1,0:T(8,128)(2,1)S(1)} %collective-permute-done.1.left_ref, ...), custom_call_target="tpu_custom_call" | custom-call | flops 679477248 | bytes 4000000 | tf_op jit(solution)/shard_map/cotangent/pallas_call | solution.py:534
  25.0 2.3 %collective-permute-done.5.hlo_ref = bf16[32,1152]{1,0:T(8,128)(2,1)S(1)} collective-permute-done((bf16[32,1152]{1,0:T(8,128)(2,1)S(1)}, bf16[32,1152]{1,0:T(8,128)(2,1)S(1)}, u32[]{:S(2)}, u32[]{:S(2)}) %collective-permute-start.5) | collective-permute-done | bytes 73760 | tf_op jit(solution)/shard_map/ppermute | solution.py:462
  27.3 1.3 %middle.1 = (bf16[3,5,3,32,384]{4,3,2,1,0:T(8,128)(2,1)S(1)}, f32[2,64,384]{2,1,0:T(8,128)S(1)}, bf16[64,384]{1,0:T(8,128)(2,1)S(1)}, bf16[8,32,384]{2,1,0:T(8,1...) custom-call(bf16[2,2,2,32,384]{4,3,2,1,0:T(8,128)(2,1)S(1)} %get-tup, ...), custom_call_target="tpu_custom_call" | custom-call | bytes 4000000 | tf_op jit(solution)/shard_map/middle/pallas_call | solution.py:544
  28.6 1.5 %collective-permute-start.8 = (bf16[2,32,1152]{2,1,0:T(8,128)(2,1)S(1)}, bf16[2,32,1152]{2,1,0:T(8,128)(2,1)S(1)}, u32[]{:S(2)}, u32[]{:S(2)}) collective-permute-start(bf16[2,32,1152]{2,1,0:T(8,128)(2,1)S(1)} %get-tuple-element.73), channel_id=1, source_target_pairs={{0,224},{32,0},{64,32},{96,64},{128,96},{160,128},{192,160},{224,1... | collective-permute-start | bytes 442376 | tf_op jit(solution)/shard_map/ppermute | solution.py:462
  30.3 1.1 %full_grad.1.g4_ref = f32[112,128]{1,0:T(8,128)S(1)} custom-call(bf16[5,5,5,16,384]{4,3,2,1,0:T(8,128)(2,1)S(1)} %get-tuple-element.79.cwin_ref, bf16[8,32,384]{2,1,0:T(8,128)(2,1)S(1)} %get-tuple-element.80.m_ref), custom_call_target="tpu_custom_call" | custom-call | flops 679477248 | bytes 4000000 | tf_op jit(solution)/shard_map/full_grad/pallas_call | solution.py:550
  31.5 4.0 %collective-permute-done.7.gmlo_ref = bf16[32,1152]{1,0:T(8,128)(2,1)S(1)} collective-permute-done((bf16[32,1152]{1,0:T(8,128)(2,1)S(1)}, bf16[32,1152]{1,0:T(8,128)(2,1)S(1)}, u32[]{:S(2)}, u32[]{:S(2)}) %collective-permute-start.7) | collective-permute-done | bytes 73760 | tf_op jit(solution)/shard_map/ppermute | solution.py:462
  35.5 2.6 %backward.1 = (bf16[3,2,3,32,384]{4,3,2,1,0:T(8,128)(2,1)S(1)}, bf16[32,1152]{1,0:T(8,128)(2,1)S(1)}, f32[1280,128]{1,0:T(8,128)S(1)}, bf16[640,128]{1,0:T(8,128)(2,1)S(1)}) custom-call(bf16[2,2,2,32,384]{4,3,2,1,0:T(8,128)(2,1)S(1)} %get-tuple-element.71.gm_ref, bf16[32,1152]{1,0:T(8,128)(2,1)S(1)} %collective-permute-done.7.gmlo_ref, ...), custom_call_target="tpu_custom_call" | custom-call | bytes 4000000 | tf_op jit(solution)/shard_map/backward/pallas_call | solution.py:552
  38.1 5.1 %collective-permute-start.9 = (bf16[640,128]{1,0:T(8,128)(2,1)S(1)}, bf16[640,128]{1,0:T(8,128)(2,1)S(1)}, u32[]{:S(2)}, u32[]{:S(2)}) collective-permute-start(bf16[640,128]{1,0:T(8,128)(2,1)S(1)} %get-tuple-element.84), channel_id=1, source_target_pairs={{0,1},{1,0},{2,3},{3,2},{4,5},{5,4},{6,7},{7,6},{8,9},{9,8},{10,11... | collective-permute-start | bytes 491528 | tf_op jit(solution)/shard_map/ppermute | solution.py:457
  43.1 1.0 %collective-permute-done.9.got_ref = bf16[640,128]{1,0:T(8,128)(2,1)S(1)} collective-permute-done((bf16[640,128]{1,0:T(8,128)(2,1)S(1)}, bf16[640,128]{1,0:T(8,128)(2,1)S(1)}, u32[]{:S(2)}, u32[]{:S(2)}) %collective-permute-start.9) | collective-permute-done | bytes 163872 | tf_op jit(solution)/shard_map/ppermute | solution.py:457
  44.2 10.1 %all_to_all.15 = bf16[16,40,128]{2,1,0:T(8,128)(2,1)S(1)} all-to-all(bf16[16,40,128]{2,1,0:T(8,128)(2,1)S(1)} %bitcast.36), channel_id=1, replica_groups={{0,2,32,34,64,66,96,98,128,130,160,162,192,194,224,226},{1,3,33,35,65,6..., dimensions={0} | all-to-all | bytes 327680 | tf_op jit(solution)/shard_map/all_to_all | solution.py:479
  54.9 7.7 %all-to-all-start.1 = ((bf16[8,40,128]{2,1,0:T(8,128)(2,1)}), bf16[8,40,128]{2,1,0:T(8,128)(2,1)S(1)}, u32[]{:S(2)}, u32[]{:S(2)}) async-start(bf16[8,40,128]{2,1,0:T(8,128)(2,1)} %bitcast.13), calls=%async_computation.1 | async-start | bytes 163840 | tf_op jit(solution)/shard_map/all_to_all | solution.py:479
  62.7 0.7 collective-permute-start.10
  63.4 6.8 %all-to-all-done.1 = bf16[8,40,128]{2,1,0:T(8,128)(2,1)S(1)} async-done(((bf16[8,40,128]{2,1,0:T(8,128)(2,1)}), bf16[8,40,128]{2,1,0:T(8,128)(2,1)S(1)}, u32[]{:S(2)}, u32[]{:S(2)}) %all-to-all-start.1) | async-done | bytes 81952 | tf_op jit(solution)/shard_map/all_to_all | solution.py:479
  70.2 0.7 sum.3
  70.9 3.5 %all-to-all-start.2 = ((bf16[16,40,128]{2,1,0:T(8,128)(2,1)}), bf16[16,40,128]{2,1,0:T(8,128)(2,1)S(1)}, u32[]{:S(2)}, u32[]{:S(2)}) async-start(bf16[16,40,128]{2,1,0:T(8,128)(2,1)} %bitcast.15), calls=%async_computation.2 | async-start | bytes 327680 | tf_op jit(solution)/shard_map/all_to_all | solution.py:479
  74.4 1.4 %copy-done.1 = bf16[5,5,5,16,384]{4,3,2,1,0:T(8,128)(2,1)S(1)} copy-done((bf16[5,5,5,16,384]{4,3,2,1,0:T(8,128)(2,1)S(1)}, bf16[5,5,5,16,384]{4,3,2,1,0:T(8,128)(2,1)}, u32[]{:S(2)}) %copy-start.1) | copy-done | bytes 1536024
  75.8 2.0 %volume.1 = bf16[16,8,16,128]{3,2,1,0:T(8,128)(2,1)} custom-call(bf16[3,2,3,32,384]{4,3,2,1,0:T(8,128)(2,1)S(1)} %get-tuple-element.87.ewin_ref, bf16[32,1152]{1,0:T(8,128)(2,1)S(1)} %collective-permute-done.10.next_ref, bf16[5,5,5,16,384]{4,3,2,1,0:T(8,128)(2,1)S(1)} %copy-done.1, bf16[128,256]{1,0:T(8,128)(2,1)S(1)} %get-tuple-element.89.up1_ref, ...), custom_call_target="tpu_custom_call" | custom-call | flops 2097152000 | bytes 4000000 | tf_op jit(solution)/shard_map/volume/pallas_call | solution.py:568
  77.8 3.7 %all-to-all-done.2 = bf16[16,40,128]{2,1,0:T(8,128)(2,1)S(1)} async-done(((bf16[16,40,128]{2,1,0:T(8,128)(2,1)}), bf16[16,40,128]{2,1,0:T(8,128)(2,1)S(1)}, u32[]{:S(2)}, u32[]{:S(2)}) %all-to-all-start.2) | async-done | bytes 163872 | tf_op jit(solution)/shard_map/all_to_all | solution.py:479
  81.5 4.2 %collective-permute-start.11 = (bf16[640,128]{1,0:T(8,128)(2,1)S(1)}, bf16[640,128]{1,0:T(8,128)(2,1)S(1)}, u32[]{:S(2)}, u32[]{:S(2)}) collective-permute-start(bf16[640,128]{1,0:T(8,128)(2,1)S(1)} %bitcast.33), channel_id=1, source_target_pairs={{0,1},{1,0},{2,3},{3,2},{4,5},{5,4},{6,7},{7,6},{8,9},{9,8},{10,11... | collective-permute-start | bytes 491528 | tf_op jit(solution)/shard_map/ppermute | solution.py:457
  85.7 1.0 %collective-permute-done.11.got_ref = bf16[640,128]{1,0:T(8,128)(2,1)S(1)} collective-permute-done((bf16[640,128]{1,0:T(8,128)(2,1)S(1)}, bf16[640,128]{1,0:T(8,128)(2,1)S(1)}, u32[]{:S(2)}, u32[]{:S(2)}) %collective-permute-start.11) | collective-permute-done | bytes 163872 | tf_op jit(solution)/shard_map/ppermute | solution.py:457
  86.7 1.2 %finish.1 = (f32[27,16,32]{2,1,0:T(8,128)}, f32[27,32,64]{2,1,0:T(8,128)}, f32[27,32,64]{2,1,0:T(8,128)}, f32[27,16,32]{2,1,0:T(8,128)}) custom-call(bf16[640,128]{1,0:T(8,128)(2,1)S(1)} %bitcast.34, bf16[640,128]{1,0:T(8,128)(2,1)S(1)} %collective-permute-done.11.got_ref), custom_call_target="tpu_custom_call" | custom-call | bytes 4000000 | tf_op jit(solution)/shard_map/finish/pallas_call | solution.py:572
  (15 shorter events, 0.9 us)
Async XLA Ops:
  2.7 15.9 %collective-permute-start = (bf16[128,1024]{1,0:T(8,128)(2,1)S(1)}, bf16[128,1024]{1,0:T(8,128)(2,1)S(1)}, u32[]{:S(2)}, u32[]{:S(2)}) collective-permute-start(bf16[128,1024]{1,0:T(8,128)(2,1)S(1)} %get-tuple-element.51), channel_id=1, source_target_pairs={{0,32},{32,64},{64,96},{96,128},{128,160},{160,192},{192,224},{224... | collective-permute-start | bytes 786440 | tf_op jit(solution)/shard_map/ppermute | solution.py:462
  4.8 12.2 %collective-permute-start.3 = (bf16[64,128]{1,0:T(8,128)(2,1)S(1)}, bf16[64,128]{1,0:T(8,128)(2,1)S(1)}, u32[]{:S(2)}, u32[]{:S(2)}) collective-permute-start(bf16[64,128]{1,0:T(8,128)(2,1)S(1)} %get-tuple-element.57), channel_id=1, source_target_pairs={{0,33},{1,34},{2,35},{3,36},{4,37},{5,38},{6,39},{7,40},{8,41},{9,... | collective-permute-start | bytes 49160 | tf_op jit(solution)/shard_map/ppermute | solution.py:468
  9.5 7.5 %collective-permute-start.4 = (bf16[64,128]{1,0:T(8,128)(2,1)S(1)}, bf16[64,128]{1,0:T(8,128)(2,1)S(1)}, u32[]{:S(2)}, u32[]{:S(2)}) collective-permute-start(bf16[64,128]{1,0:T(8,128)(2,1)S(1)} %get-tuple-element.58), channel_id=1, source_target_pairs={{0,63},{1,32},{2,33},{3,34},{4,35},{5,36},{6,37},{7,38},{8,39},{9,... | collective-permute-start | bytes 49160 | tf_op jit(solution)/shard_map/ppermute | solution.py:468
  9.5 7.5 %collective-permute-start.1 = (bf16[256,128]{1,0:T(8,128)(2,1)S(1)}, bf16[256,128]{1,0:T(8,128)(2,1)S(1)}, u32[]{:S(2)}, u32[]{:S(2)}) collective-permute-start(bf16[256,128]{1,0:T(8,128)(2,1)S(1)} %get-tuple-element.55), channel_id=1, source_target_pairs={{0,1},{1,2},{2,3},{3,4},{4,5},{5,6},{6,7},{7,8},{8,9},{9,10},{10,1... | collective-permute-start | bytes 196616 | tf_op jit(solution)/shard_map/ppermute | solution.py:462
  13.4 5.2 %collective-permute-start.2 = (bf16[256,128]{1,0:T(8,128)(2,1)S(1)}, bf16[256,128]{1,0:T(8,128)(2,1)S(1)}, u32[]{:S(2)}, u32[]{:S(2)}) collective-permute-start(bf16[256,128]{1,0:T(8,128)(2,1)S(1)} %get-tuple-element.56), channel_id=1, source_target_pairs={{0,31},{1,0},{2,1},{3,2},{4,3},{5,4},{6,5},{7,6},{8,7},{9,8},{10,9... | collective-permute-start | bytes 196616 | tf_op jit(solution)/shard_map/ppermute | solution.py:462
  20.2 7.2 %collective-permute-start.6 = (bf16[2,32,1152]{2,1,0:T(8,128)(2,1)S(1)}, bf16[2,32,1152]{2,1,0:T(8,128)(2,1)S(1)}, u32[]{:S(2)}, u32[]{:S(2)}) collective-permute-start(bf16[2,32,1152]{2,1,0:T(8,128)(2,1)S(1)} %get-tuple-element.65), channel_id=1, source_target_pairs={{0,224},{32,0},{64,32},{96,64},{128,96},{160,128},{192,160},{224,1... | collective-permute-start | bytes 442376 | tf_op jit(solution)/shard_map/ppermute | solution.py:462
  22.0 5.3 %collective-permute-start.5 = (bf16[32,1152]{1,0:T(8,128)(2,1)S(1)}, bf16[32,1152]{1,0:T(8,128)(2,1)S(1)}, u32[]{:S(2)}, u32[]{:S(2)}) collective-permute-start(bf16[32,1152]{1,0:T(8,128)(2,1)S(1)} %get-tuple-element.64.after_ref), channel_id=1, source_target_pairs={{0,32},{32,64},{64,96},{96,128},{128,160},{160,192},{192,224},{224... | collective-permute-start | bytes 221192 | tf_op jit(solution)/shard_map/ppermute | solution.py:462
  25.0 6.5 %copy-start = (bf16[5,5,5,16,384]{4,3,2,1,0:T(8,128)(2,1)}, bf16[5,5,5,16,384]{4,3,2,1,0:T(8,128)(2,1)S(1)}, u32[]{:S(2)}) copy-start(bf16[5,5,5,16,384]{4,3,2,1,0:T(8,128)(2,1)S(1)} %get-tuple-element.79.cwin_ref) | copy-start | bytes 4608004
  28.6 6.9 %collective-permute-start.8 = (bf16[2,32,1152]{2,1,0:T(8,128)(2,1)S(1)}, bf16[2,32,1152]{2,1,0:T(8,128)(2,1)S(1)}, u32[]{:S(2)}, u32[]{:S(2)}) collective-permute-start(bf16[2,32,1152]{2,1,0:T(8,128)(2,1)S(1)} %get-tuple-element.73), channel_id=1, source_target_pairs={{0,224},{32,0},{64,32},{96,64},{128,96},{160,128},{192,160},{224,1... | collective-permute-start | bytes 442376 | tf_op jit(solution)/shard_map/ppermute | solution.py:462
  30.2 5.3 %collective-permute-start.7 = (bf16[32,1152]{1,0:T(8,128)(2,1)S(1)}, bf16[32,1152]{1,0:T(8,128)(2,1)S(1)}, u32[]{:S(2)}, u32[]{:S(2)}) collective-permute-start(bf16[32,1152]{1,0:T(8,128)(2,1)S(1)} %get-tuple-element.72), channel_id=1, source_target_pairs={{0,32},{32,64},{64,96},{96,128},{128,160},{160,192},{192,224},{224... | collective-permute-start | bytes 221192 | tf_op jit(solution)/shard_map/ppermute | solution.py:462
  38.1 6.1 %collective-permute-start.9 = (bf16[640,128]{1,0:T(8,128)(2,1)S(1)}, bf16[640,128]{1,0:T(8,128)(2,1)S(1)}, u32[]{:S(2)}, u32[]{:S(2)}) collective-permute-start(bf16[640,128]{1,0:T(8,128)(2,1)S(1)} %get-tuple-element.84), channel_id=1, source_target_pairs={{0,1},{1,0},{2,3},{3,2},{4,5},{5,4},{6,7},{7,6},{8,9},{9,8},{10,11... | collective-permute-start | bytes 491528 | tf_op jit(solution)/shard_map/ppermute | solution.py:457
  54.9 15.2 %all-to-all-start.1 = ((bf16[8,40,128]{2,1,0:T(8,128)(2,1)}), bf16[8,40,128]{2,1,0:T(8,128)(2,1)S(1)}, u32[]{:S(2)}, u32[]{:S(2)}) async-start(bf16[8,40,128]{2,1,0:T(8,128)(2,1)} %bitcast.13), calls=%async_computation.1 | async-start | bytes 163840 | tf_op jit(solution)/shard_map/all_to_all | solution.py:479
  62.7 8.2 %collective-permute-start.10 = (bf16[32,1152]{1,0:T(8,128)(2,1)S(1)}, bf16[32,1152]{1,0:T(8,128)(2,1)S(1)}, u32[]{:S(2)}, u32[]{:S(2)}) collective-permute-start(bf16[32,1152]{1,0:T(8,128)(2,1)S(1)} %get-tuple-element.85), channel_id=1, source_target_pairs={{0,224},{32,0},{64,32},{96,64},{128,96},{160,128},{192,160},{224,1... | collective-permute-start | bytes 221192 | tf_op jit(solution)/shard_map/ppermute | solution.py:462
  70.9 10.6 %all-to-all-start.2 = ((bf16[16,40,128]{2,1,0:T(8,128)(2,1)}), bf16[16,40,128]{2,1,0:T(8,128)(2,1)S(1)}, u32[]{:S(2)}, u32[]{:S(2)}) async-start(bf16[16,40,128]{2,1,0:T(8,128)(2,1)} %bitcast.15), calls=%async_computation.2 | async-start | bytes 327680 | tf_op jit(solution)/shard_map/all_to_all | solution.py:479
  74.4 1.4 %copy-start.1 = (bf16[5,5,5,16,384]{4,3,2,1,0:T(8,128)(2,1)S(1)}, bf16[5,5,5,16,384]{4,3,2,1,0:T(8,128)(2,1)}, u32[]{:S(2)}) copy-start(bf16[5,5,5,16,384]{4,3,2,1,0:T(8,128)(2,1)} %copy-done) | copy-start | bytes 4608004
  81.5 5.2 %collective-permute-start.11 = (bf16[640,128]{1,0:T(8,128)(2,1)S(1)}, bf16[640,128]{1,0:T(8,128)(2,1)S(1)}, u32[]{:S(2)}, u32[]{:S(2)}) collective-permute-start(bf16[640,128]{1,0:T(8,128)(2,1)S(1)} %bitcast.33), channel_id=1, source_target_pairs={{0,1},{1,0},{2,3},{3,2},{4,5},{5,4},{6,7},{7,6},{8,9},{9,8},{10,11... | collective-permute-start | bytes 491528 | tf_op jit(solution)/shard_map/ppermute | solution.py:457
